TPU v7x, 32 devices: a whole 2x2x4 slice. The times are simulated.
32 devices in a mesh: parts: 2 (over y), seq: 2 (over x), wide: 4 (over z), pair: 2 (over core).
Axes of the slice: x: 2, y: 2, z: 4, core: 2. Of those that a mesh axis runs over, the one named last changes fastest.
Arguments:
- tokens: bfloat16 [128, 8192], P(('parts', 'wide'), ('seq', 'pair')), parts along dimension 0, may hold values from -6 to 6
- gate_weight: bfloat16 [8192, 26624], P(('seq', 'pair'), 'wide'), may hold values from -0.0625 to 0.0625
- up_weight: bfloat16 [8192, 26624], P(('seq', 'pair'), 'wide'), may hold values from -0.0625 to 0.0625
- down_weight: bfloat16 [26624, 8192], P('wide', ('seq', 'pair')), may hold values from -0.0390625 to 0.0390625
Outputs:
- mixed: bfloat16 [128, 8192], P(('parts', 'wide'), ('seq', 'pair')), parts along dimension 0
There are 2 independent parts, one for each index of `parts`. A program takes and returns all parts, laid end to end along the dimension named above; an argument that names none is the same for every part. Nothing has to cross between parts.
All inputs are finite; a program needn't handle non-finite values.
Results may differ from a plain program's by a relative error of at most 0.005.
Values may be sent and summed in bfloat16 or wider, within the bound.
No kernel may reach another device: no remote copies, remote signals or barrier semaphores. Data moves between devices by JAX's collectives and lax.ppermute only.
A program may use at most 192 MiB of HBM per device.

v0:
```python
import jax
import jax.numpy as jnp
from jax import lax
from jax.sharding import PartitionSpec as P


def shards(tokens, gate_weight, up_weight, down_weight):
    columns = gate_weight.shape[1]
    piece = lax.all_gather(tokens, "wide", axis=0, tiled=True)
    gate_part = jnp.dot(piece, gate_weight, preferred_element_type=jnp.float32)
    up_part = jnp.dot(piece, up_weight, preferred_element_type=jnp.float32)
    partials = jnp.concatenate([gate_part, up_part], axis=1)
    totals = lax.psum(partials, ("seq", "pair"))
    hidden = (jax.nn.silu(totals[:, :columns]) * totals[:, columns:]).astype(jnp.bfloat16)
    down_partial = jnp.dot(hidden, down_weight, preferred_element_type=jnp.float32)
    result = lax.psum_scatter(down_partial, "wide", scatter_dimension=0, tiled=True)
    return result.astype(jnp.bfloat16)


def solution(mesh):
    return jax.shard_map(
        shards,
        mesh=mesh,
        in_specs=(
            P(("parts", "wide"), ("seq", "pair")),
            P(("seq", "pair"), "wide"),
            P(("seq", "pair"), "wide"),
            P("wide", ("seq", "pair")),
        ),
        out_specs=P(("parts", "wide"), ("seq", "pair")),
        check_vma=False,
    )
```

profile of v0, /device:TPU:0, one launch (start us, length us, event | category | flops | bytes accessed | tf_op | source)
XLA Modules:
  0.0 167.0 jit_solution(12961273713358986425)
XLA Ops:
  6.5 0.0 all-reduce.2.cloned.1.call-start
  6.5 15.8 %all_gather.3 = bf16[64,2048]{1,0:T(8,128)(2,1)S(1)} all-gather(bf16[16,2048]{1,0:T(8,128)(2,1)} %param.4), channel_id=1, replica_groups=mesh['parts'=2,'seq'=2,'wide'=4,'pair'=2] {'wide'}, dimensions={0}, use_global_device_ids=true | all-gather | bytes 327680 | tf_op jit(solution)/shard_map/all_gather | solution.py:9
  22.4 11.2 %fusion.6 = f32[64,6656]{1,0:T(8,128)S(1)} fusion(bf16[64,2048]{1,0:T(8,128)(2,1)S(1)} %all_gather.3, bf16[2048,6656]{1,0:T(8,128)(2,1)} %param.6), kind=kOutput, calls=%fused_computation.7 | convolution fusion | flops 1744830464 | bytes 29229056 | tf_op jit(solution)/shard_map/dot_general | solution.py:11
  33.6 11.2 %fusion.5 = f32[64,6656]{1,0:T(8,128)S(1)} fusion(bf16[64,2048]{1,0:T(8,128)(2,1)S(1)} %all_gather.3, bf16[2048,6656]{1,0:T(8,128)(2,1)} %param.5), kind=kOutput, calls=%fused_computation.6 | convolution fusion | flops 1744830464 | bytes 29229056 | tf_op jit(solution)/shard_map/dot_general | solution.py:10
  44.8 2.0 %pad_maximum_fusion = f32[64,13312]{1,0:T(8,128)} fusion(f32[64,6656]{1,0:T(8,128)S(1)} %fusion.6, f32[64,6656]{1,0:T(8,128)S(1)} %fusion.5), kind=kLoop, calls=%fused_computation | loop fusion | flops 851968 | bytes 6815744 | tf_op jit(solution)/shard_map/concatenate | solution.py:12
  46.8 0.0 all-reduce.2.cloned.1.call-update
  46.8 0.0 reduce-scatter.2.cloned.1.call-start
  46.9 74.3 %all-reduce.2.cloned.1.call-done = f32[64,13312]{1,0:T(8,128)} async-done(((f32[64,13312]{1,0:T(8,128)}), f32[64,13312]{1,0:T(8,128)}) %all-reduce.2.cloned.1.call-update) | async-done | bytes 3407888 | tf_op jit(solution)/shard_map/psum | solution.py:13
  121.2 15.4 %fusion.1 = f32[64,2048]{1,0:T(8,128)} fusion(bf16[6656,2048]{1,0:T(8,128)(2,1)} %param.7, f32[64,13312]{1,0:T(8,128)} %all-reduce.2.cloned.1.call-done), kind=kOutput, calls=%fused_computation.3 | convolution fusion | flops 1747386368 | bytes 31195136 | tf_op jit(solution)/shard_map/dot_general | solution.py:15
  136.6 0.0 reduce-scatter.2.cloned.1.call-update
  136.7 21.9 %reduce-scatter.2.cloned.1.call-done = f32[16,2048]{1,0:T(8,128)} async-done(((f32[64,2048]{1,0:T(8,128)}), f32[16,2048]{1,0:T(8,128)}) %reduce-scatter.2.cloned.1.call-update) | async-done | bytes 131088 | tf_op jit(solution)/shard_map/reduce_scatter | solution.py:16
  158.6 1.5 convert_element_type.7
Async XLA Ops:
  6.5 114.7 %all-reduce.2.cloned.1.call-start = ((), (), s32[]{:S(2)}) async-start(), calls=%async_computation.1 | async-start | bytes 6815744 | tf_op jit(solution)/shard_map/psum | solution.py:13
  46.8 111.8 %reduce-scatter.2.cloned.1.call-start = ((), (), s32[]{:S(2)}) async-start(), calls=%async_computation.2 | async-start | bytes 655360 | tf_op jit(solution)/shard_map/reduce_scatter | solution.py:16
Sparse Core Ops, SparseCore 0:
  47.0 74.2 all-reduce.1
  136.8 21.7 reduce-scatter.1
where the time goes:
time: 167 us
  waiting for transfers between devices  96.3 us (58%)
  matrix products  37.9 us (23%)
  blocking collectives  15.8 us (9%)
  between operations  13.4 us (8%)
  other arithmetic  3.52 us (2%)
    psum x1, waiting for transfers between devices, shards(): totals = lax.psum(partials, ('seq', 'pair'))  74.3 us
    reduce_scatter x1, waiting for transfers between devices, shards(): lax.psum_scatter(down_partial, 'wide', scatter_dimension=0, tiled=True)  21.9 us
    all_gather x1, blocking collectives, shards(): piece = lax.all_gather(tokens, 'wide', axis=0, tiled=True)  15.8 us
    dot_general x1, matrix products, shards(): jnp.dot(hidden, down_weight, preferred_element_type=jnp.float32)  15.4 us
    dot_general x1, matrix products, shards(): gate_part = jnp.dot(piece, gate_weight, preferred_element_type=jnp.float32)  11.2 us
    dot_general x1, matrix products, shards(): up_part = jnp.dot(piece, up_weight, preferred_element_type=jnp.float32)  11.2 us
  transfers between devices with their start and end apart: 2, of which 2 were waited for; matrix products, arithmetic and copies ran while one was open for 0% of the time, Pallas kernels for 0%

commit v1 on v0

v1 whole, which is shorter than its diff:
```python
import functools

import jax
import jax.numpy as jnp
from jax import lax
from jax.experimental import pallas as pl
from jax.experimental.pallas import tpu as pltpu
from jax.sharding import PartitionSpec as P

BF16, F32 = jnp.bfloat16, jnp.float32
TILE = 512
SHARES = (4, 4, 3, 2)
PAIR_TYPE = F32


def on_chip():
    return pl.BlockSpec(memory_space=pltpu.VMEM)


def in_place():
    return pl.BlockSpec(memory_space=pl.ANY)


def cuts(columns):
    if columns % (TILE * sum(SHARES)):
        return [(0, columns)]
    unit = columns // sum(SHARES)
    chunks, start = [], 0
    for share in SHARES:
        chunks.append((start, share * unit))
        start += share * unit
    return chunks


def tile_of(width):
    return TILE if width % TILE == 0 else width


def copies(fetch, sources, targets, sems):
    made = []
    for at, ((axis, start, size), source, target) in enumerate(zip(fetch, sources, targets)):
        view = source.at[:, pl.ds(start, size)] if axis else source.at[pl.ds(start, size), :]
        made.append(pltpu.make_async_copy(view, target, sems.at[at]))
    return made


def call(body, operands, in_specs, outs, fetch, scratch, flops, traffic):
    fetched = []
    for array, axis, start, size in fetch:
        shape = (array.shape[0], size) if axis else (size, array.shape[1])
        fetched.append(pltpu.VMEM(shape, array.dtype))
    out = pl.pallas_call(
        body,
        out_shape=tuple(outs) + tuple(fetched),
        in_specs=list(in_specs) + [in_place()] * len(fetch),
        out_specs=tuple([on_chip()] * (len(outs) + len(fetch))),
        scratch_shapes=list(scratch) + [pltpu.SemaphoreType.DMA((max(len(fetch), 1),))],
        compiler_params=pltpu.CompilerParams(vmem_limit_bytes=12 * 2**20),
        cost_estimate=pl.CostEstimate(flops=flops, bytes_accessed=traffic, transcendentals=0),
    )(*operands, *[f[0] for f in fetch])
    return out[: len(outs)], out[len(outs) :]


def split_refs(refs, *counts):
    groups, at = [], 0
    for count in counts:
        groups.append(refs[at : at + count])
        at += count
    return groups


def load_kernel(fetch, *refs):
    sources, targets, (sems,) = split_refs(refs, len(fetch), len(fetch), 1)
    made = copies(fetch, sources, targets, sems)
    for copy in made:
        copy.start()
    for copy in made:
        copy.wait()


def gate_up_kernel(n_pair, fetch, *refs):
    (x, wg, wu), sources, (keep,), sends, targets, (res, sems) = split_refs(
        refs, 3, len(fetch), 1, n_pair - 1, len(fetch), 2
    )
    made = copies(fetch, sources, targets, sems)
    for copy in made:
        copy.start()
    me = lax.axis_index("pair")
    rows = keep.shape[1]
    width = wg.shape[1]
    tile = tile_of(width)

    @pl.loop(0, width // tile)
    def _(step):
        at = pl.ds(pl.multiple_of(step * tile, tile), tile)
        for which, weight in enumerate((wg, wu)):
            res[...] = jnp.dot(x[...], weight[:, at], preferred_element_type=F32)
            for k in range(n_pair):
                first = pl.multiple_of(lax.rem(me + k, n_pair) * rows, 16)
                target = sends[k - 1] if k else keep
                target[which, :, at] = res[pl.ds(first, rows), :].astype(target.dtype)

    for copy in made:
        copy.wait()


def pair_sum_kernel(n_pair, n_seq, *refs):
    (keep,), got, (own,), sends, _ = split_refs(refs, 1, n_pair - 1, 1, n_seq - 1, 1)
    me = lax.axis_index("seq")
    rows = own.shape[1]
    for k in range(n_seq):
        block = pl.ds(pl.multiple_of(lax.rem(me + k, n_seq) * rows, 16), rows)
        total = keep[:, block, :]
        for part in got:
            total += part[:, block, :].astype(F32)
        target = sends[k - 1] if k else own
        target[...] = total.astype(target.dtype)


def down_kernel(n_pair, n_seq, n_wide, first, last, fetch, *refs):
    pieces = n_pair * n_seq
    parts, (wd,), before, sources, outs, targets, (hidden, sems) = split_refs(
        refs, pieces, 1, 0 if first else 1, len(fetch), n_wide if last else 1, len(fetch), 2
    )
    made = copies(fetch, sources, targets, sems)
    for copy in made:
        copy.start()
    c, s = lax.axis_index("pair"), lax.axis_index("seq")
    rows = parts[0].shape[0]
    for dc in range(n_pair):
        for ds in range(n_seq):
            block = lax.rem(c + n_pair - dc, n_pair) * n_seq + lax.rem(s + n_seq - ds, n_seq)
            hidden[pl.ds(pl.multiple_of(block * rows, 16), rows), :] = parts[dc * n_seq + ds][...]
    width = wd.shape[1]
    tile = tile_of(width)

    @pl.loop(0, width // tile)
    def _(step):
        at = pl.ds(pl.multiple_of(step * tile, tile), tile)
        total = jnp.dot(hidden[...], wd[:, at], preferred_element_type=F32)
        if before:
            total += before[0][:, at]
        if last:
            share = total.shape[0] // n_wide
            for k in range(n_wide):
                place = (n_wide - k) % n_wide * share
                outs[k][:, at] = total[place : place + share].astype(outs[k].dtype)
        else:
            outs[0][:, at] = total

    for copy in made:
        copy.wait()


def shards(sizes, tokens, gate_weight, up_weight, down_weight):
    n_seq, n_wide, n_pair = sizes["seq"], sizes["wide"], sizes["pair"]

    def send(value, axis, k):
        n = sizes[axis]
        return lax.ppermute(value, axis, [(i, (i + k) % n) for i in range(n)])

    share, depth = tokens.shape
    rows = share * n_wide
    features = down_weight.shape[1]
    half, quarter = rows // n_pair, rows // n_pair // n_seq
    chunks = cuts(gate_weight.shape[1])
    size = tokens.dtype.itemsize

    def load_gate_up(j):
        if j == len(chunks):
            return [(down_weight, 0, *chunks[0])]
        return [(w, 1, *chunks[j]) for w in (gate_weight, up_weight)]

    def bytes_of(fetch):
        return sum(size * f[3] * f[0].shape[1 - f[1]] for f in fetch)

    x = jnp.concatenate([tokens] + [send(tokens, "wide", k) for k in range(1, n_wide)])

    fetch = load_gate_up(0)
    _, weights = call(
        functools.partial(load_kernel, [f[1:] for f in fetch]),
        [], [], [], fetch, [], 0, 2 * bytes_of(fetch),
    )

    hidden_parts = []
    for j, (start, width) in enumerate(chunks):
        fetch = load_gate_up(j + 1)
        outs, fetched = call(
            functools.partial(gate_up_kernel, n_pair, [f[1:] for f in fetch]),
            [x, *weights],
            [on_chip()] * 3,
            [pltpu.VMEM((2, half, width), F32)]
            + [pltpu.VMEM((2, half, width), PAIR_TYPE)] * (n_pair - 1),
            fetch,
            [pltpu.VMEM((rows, tile_of(width)), F32)],
            4 * rows * depth * width,
            2 * bytes_of(fetch),
        )
        weights = fetched
        got = [send(outs[k], "pair", k) for k in range(1, n_pair)]
        own, *sums = call(
            functools.partial(pair_sum_kernel, n_pair, n_seq),
            [outs[0], *got],
            [on_chip()] * n_pair,
            [pltpu.VMEM((2, quarter, width), F32)]
            + [pltpu.VMEM((2, quarter, width), BF16)] * (n_seq - 1),
            [], [], 0, 8 * half * width,
        )[0]
        total = own
        for k in range(1, n_seq):
            total = total + send(sums[k - 1], "seq", k).astype(F32)
        hidden = (jax.nn.silu(total[0]) * total[1]).astype(BF16)
        near = [hidden] + [send(hidden, "seq", k) for k in range(1, n_seq)]
        parts = list(near)
        for k in range(1, n_pair):
            parts += [send(part, "pair", k) for part in near]
        hidden_parts.append(parts)

    total = None
    for j, (start, width) in enumerate(chunks):
        first, last = j == 0, j == len(chunks) - 1
        fetch = [] if last else [(down_weight, 0, *chunks[j + 1])]
        if last:
            outs = [pltpu.VMEM((share, features), F32)]
            outs += [pltpu.VMEM((share, features), BF16)] * (n_wide - 1)
        else:
            outs = [pltpu.VMEM((rows, features), F32)]
        total, weights = call(
            functools.partial(down_kernel, n_pair, n_seq, n_wide, first, last, [f[1:] for f in fetch]),
            [*hidden_parts[j], *weights, *([] if first else total)],
            [on_chip()] * (n_pair * n_seq + 1 + (not first)),
            outs,
            fetch,
            [pltpu.VMEM((rows, width), BF16)],
            2 * rows * width * features,
            2 * bytes_of(fetch),
        )

    result = total[0]
    for k in range(1, n_wide):
        result = result + send(total[k], "wide", k).astype(F32)
    return result.astype(BF16)


def solution(mesh):
    return jax.shard_map(
        functools.partial(shards, dict(mesh.shape)),
        mesh=mesh,
        in_specs=(
            P(("parts", "wide"), ("seq", "pair")),
            P(("seq", "pair"), "wide"),
            P(("seq", "pair"), "wide"),
            P("wide", ("seq", "pair")),
        ),
        out_specs=P(("parts", "wide"), ("seq", "pair")),
        check_vma=False,
    )
```

time: 167 us -> 84.2 us (0.50)
  waiting for transfers between devices: 96.3 us -> 15.4 us
  matrix products: 37.9 us -> 0 us
  Pallas kernels: 0 us -> 32.5 us
  starting transfers between devices: 0.04 us -> 25.1 us
  blocking collectives: 15.8 us -> 0 us
  between operations: 13.4 us -> 0.3 us
  local copies, waits for them, and re-layouts: 0 us -> 9.65 us
  other arithmetic: 3.52 us -> 0.91 us
    psum x1 -> x0, waiting for transfers between devices: 74.3 us -> none  [shards(): totals = lax.psum(partials, ('seq', 'pair'))]
    dot_general x3 -> x0, matrix products: 37.9 us -> none  [the longest x1 15.4 us: shards(): jnp.dot(hidden, down_weight, preferred_element_type=jnp.float32)]
    pallas_call x0 -> x13, Pallas kernels: none -> 32.5 us  [call(): pl.pallas_call(body, out_shape=tuple(outs) + tuple(fetched), in_specs=lis...]
    ppermute x0 -> x26, starting transfers between devices: none -> 25.1 us  [send(): return lax.ppermute(value, axis, [(i, (i + k) % n) for i in range(n)])]
    reduce_scatter x1 -> x0, waiting for transfers between devices: 21.9 us -> none  [shards(): lax.psum_scatter(down_partial, 'wide', scatter_dimension=0, tiled=True)]
    all_gather x1 -> x0, blocking collectives: 15.8 us -> none  [shards(): piece = lax.all_gather(tokens, 'wide', axis=0, tiled=True)]
    ppermute x0 -> x26, waiting for transfers between devices: none -> 15.4 us  [send(): return lax.ppermute(value, axis, [(i, (i + k) % n) for i in range(n)])]
    unnamed x0 -> x5, local copies, waits for them, and re-layouts: none -> 9.65 us
  transfers between devices with their start and end apart: 2 -> 26, of which waited for: 2 -> 8; matrix products, arithmetic and copies ran while one was open for 0% -> 1% of each run, Pallas kernels for 0% -> 16%
where the time goes in v1:
time: 84.2 us; the launch traced here: 83.9 us
  Pallas kernels  32.5 us (39%)
  starting transfers between devices  25.1 us (30%)
  waiting for transfers between devices  15.4 us (18%)
  local copies, waits for them, and re-layouts  9.65 us (11%)
  other arithmetic  0.91 us (1%)
    pallas_call x13, Pallas kernels, call(): pl.pallas_call(body, out_shape=tuple(outs) + tuple(fetched), in_specs=lis...  32.5 us
    ppermute x26, starting transfers between devices, send(): return lax.ppermute(value, axis, [(i, (i + k) % n) for i in range(n)])  25.1 us
    ppermute x26, waiting for transfers between devices, send(): return lax.ppermute(value, axis, [(i, (i + k) % n) for i in range(n)])  15.4 us
    unnamed x5, local copies, waits for them, and re-layouts  9.65 us
  transfers between devices with their start and end apart: 26, of which 8 were waited for; matrix products, arithmetic and copies ran while one was open for 1% of the time, Pallas kernels for 16%

profile of v1, /device:TPU:0, one launch (start us, length us, event | category | flops | bytes accessed | tf_op | source)
XLA Modules:
  0.0 83.9 jit_solution(14290350156288708400)
XLA Ops:
  0.0 4.0 %collective-permute-start.1 = (bf16[16,2048]{1,0:T(8,128)(2,1)}, bf16[16,2048]{1,0:T(8,128)(2,1)S(1)}, u32[]{:S(2)}, u32[]{:S(2)}) collective-permute-start(bf16[16,2048]{1,0:T(8,128)(2,1)} %param.4), channel_id=1, source_target_pairs={{0,4},{2,6},{4,0},{6,2},{1,5},{3,7},{5,1},{7,3},{8,12},{10,14},{12... | collective-permute-start | bytes 196616 | tf_op jit(solution)/shard_map/ppermute | solution.py:160
  4.0 1.6 %collective-permute-start = (bf16[16,2048]{1,0:T(8,128)(2,1)}, bf16[16,2048]{1,0:T(8,128)(2,1)S(1)}, u32[]{:S(2)}, u32[]{:S(2)}) collective-permute-start(bf16[16,2048]{1,0:T(8,128)(2,1)} %param.4), channel_id=1, source_target_pairs={{0,2},{2,4},{4,6},{6,0},{1,3},{3,5},{5,7},{7,1},{8,10},{10,12},{12... | collective-permute-start | bytes 196616 | tf_op jit(solution)/shard_map/ppermute | solution.py:160
  5.6 2.2 %collective-permute-start.2 = (bf16[16,2048]{1,0:T(8,128)(2,1)}, bf16[16,2048]{1,0:T(8,128)(2,1)S(1)}, u32[]{:S(2)}, u32[]{:S(2)}) collective-permute-start(bf16[16,2048]{1,0:T(8,128)(2,1)} %param.4), channel_id=1, source_target_pairs={{0,6},{2,0},{4,2},{6,4},{1,7},{3,1},{5,3},{7,5},{8,14},{10,8},{12,... | collective-permute-start | bytes 196616 | tf_op jit(solution)/shard_map/ppermute | solution.py:160
  8.7 5.9 %shard_map.46 = (bf16[2048,2048]{1,0:T(8,128)(2,1)S(1)}, bf16[2048,2048]{1,0:T(8,128)(2,1)S(1)}) custom-call(bf16[2048,6656]{1,0:T(8,128)(2,1)} %refs_3_.6, bf16[2048,6656]{1,0:T(8,128)(2,1)} %refs_4_.5), custom_call_target="tpu_custom_call" | custom-call | bytes 33554432 | tf_op jit(solution)/shard_map/pallas_call | solution.py:52
  14.7 6.0 %shard_map.47 = (f32[2,32,2048]{2,1,0:T(8,128)S(1)}, f32[2,32,2048]{2,1,0:T(8,128)S(1)}, bf16[2048,2048]{1,0:T(8,128)(2,1)S(1)}, bf16[2048,2048]{1,0:T(8,128)(2,1)S(1)}) custom-call(bf16[64,2048]{1,0:T(8,128)(2,1)S(1)} %constant_dynamic-update-slice_fusion.refs_0_, bf16[2048,2048]{1,0:T(8,128)(2,1)S(1)} %get-tuple-element.40.refs_1_, ...), custom_call_target="tpu_custom_call" | custom-call | flops 1073741824 | bytes 33554432 | tf_op jit(solution)/shard_map/pallas_call | solution.py:52
  20.7 4.6 %shard_map.48 = (f32[2,32,2048]{2,1,0:T(8,128)S(1)}, f32[2,32,2048]{2,1,0:T(8,128)S(1)}, bf16[2048,1536]{1,0:T(8,128)(2,1)S(1)}, bf16[2048,1536]{1,0:T(8,128)(2,1)S(1)}) custom-call(bf16[64,2048]{1,0:T(8,128)(2,1)S(1)} %constant_dynamic-update-slice_fusion.refs_0_, bf16[2048,2048]{1,0:T(8,128)(2,1)S(1)} %get-tuple-element.42.refs_1_, ...), custom_call_target="tpu_custom_call" | custom-call | flops 1073741824 | bytes 25165824 | tf_op jit(solution)/shard_map/pallas_call | solution.py:52
  25.3 3.5 %shard_map.49 = (f32[2,32,1536]{2,1,0:T(8,128)S(1)}, f32[2,32,1536]{2,1,0:T(8,128)S(1)}, bf16[2048,1024]{1,0:T(8,128)(2,1)S(1)}, bf16[2048,1024]{1,0:T(8,128)(2,1)S(1)}) custom-call(bf16[64,2048]{1,0:T(8,128)(2,1)S(1)} %constant_dynamic-update-slice_fusion.refs_0_, bf16[2048,1536]{1,0:T(8,128)(2,1)S(1)} %get-tuple-element.44.refs_1_, ...), custom_call_target="tpu_custom_call" | custom-call | flops 805306368 | bytes 16777216 | tf_op jit(solution)/shard_map/pallas_call | solution.py:52
  28.8 3.4 %shard_map.50 = (f32[2,32,1024]{2,1,0:T(8,128)S(1)}, f32[2,32,1024]{2,1,0:T(8,128)S(1)}, bf16[2048,2048]{1,0:T(8,128)(2,1)S(1)}) custom-call(bf16[64,2048]{1,0:T(8,128)(2,1)S(1)} %constant_dynamic-update-slice_fusion.refs_0_, bf16[2048,1024]{1,0:T(8,128)(2,1)S(1)} %get-tuple-element.46.refs_1_, bf16[2048,1024]{1,0:T(8,128)(2,1)S(1)} %get-tuple-element.47.refs_2_, ...), custom_call_target="tpu_custom_call" | custom-call | flops 536870912 | bytes 16777216 | tf_op jit(solution)/shard_map/pallas_call | solution.py:52
  33.9 1.6 %collective-permute-start.4 = (bf16[2,16,1024]{2,1,0:T(8,128)(2,1)S(1)}, bf16[2,16,1024]{2,1,0:T(8,128)(2,1)S(1)}, u32[]{:S(2)}, u32[]{:S(2)}) collective-permute-start(bf16[2,16,1024]{2,1,0:T(8,128)(2,1)S(1)} %get-tuple-element.51), channel_id=1, source_target_pairs={{0,8},{8,0},{1,9},{9,1},{2,10},{10,2},{3,11},{11,3},{4,12},{12,4},... | collective-permute-start | bytes 196616 | tf_op jit(solution)/shard_map/ppermute | solution.py:160
  36.0 2.3 %collective-permute-done.4 = bf16[2,16,1024]{2,1,0:T(8,128)(2,1)S(1)} collective-permute-done((bf16[2,16,1024]{2,1,0:T(8,128)(2,1)S(1)}, bf16[2,16,1024]{2,1,0:T(8,128)(2,1)S(1)}, u32[]{:S(2)}, u32[]{:S(2)}) %collective-permute-start.4) | collective-permute-done | bytes 65568 | tf_op jit(solution)/shard_map/ppermute | solution.py:160
  38.3 1.6 %collective-permute-start.14 = (bf16[2,16,2048]{2,1,0:T(8,128)(2,1)S(1)}, bf16[2,16,2048]{2,1,0:T(8,128)(2,1)S(1)}, u32[]{:S(2)}, u32[]{:S(2)}) collective-permute-start(bf16[2,16,2048]{2,1,0:T(8,128)(2,1)S(1)} %get-tuple-element.59), channel_id=1, source_target_pairs={{0,8},{8,0},{1,9},{9,1},{2,10},{10,2},{3,11},{11,3},{4,12},{12,4},... | collective-permute-start | bytes 393224 | tf_op jit(solution)/shard_map/ppermute | solution.py:160
  40.6 1.6 %collective-permute-start.9 = (bf16[2,16,1536]{2,1,0:T(8,128)(2,1)S(1)}, bf16[2,16,1536]{2,1,0:T(8,128)(2,1)S(1)}, u32[]{:S(2)}, u32[]{:S(2)}) collective-permute-start(bf16[2,16,1536]{2,1,0:T(8,128)(2,1)S(1)} %get-tuple-element.55), channel_id=1, source_target_pairs={{0,8},{8,0},{1,9},{9,1},{2,10},{10,2},{3,11},{11,3},{4,12},{12,4},... | collective-permute-start | bytes 294920 | tf_op jit(solution)/shard_map/ppermute | solution.py:160
  42.8 2.0 %collective-permute-done.14 = bf16[2,16,2048]{2,1,0:T(8,128)(2,1)S(1)} collective-permute-done((bf16[2,16,2048]{2,1,0:T(8,128)(2,1)S(1)}, bf16[2,16,2048]{2,1,0:T(8,128)(2,1)S(1)}, u32[]{:S(2)}, u32[]{:S(2)}) %collective-permute-start.14) | collective-permute-done | bytes 131104 | tf_op jit(solution)/shard_map/ppermute | solution.py:160
  44.9 1.6 %collective-permute-start.15 = (bf16[16,2048]{1,0:T(8,128)(2,1)S(1)}, bf16[16,2048]{1,0:T(8,128)(2,1)S(1)}, u32[]{:S(2)}, u32[]{:S(2)}) collective-permute-start(bf16[16,2048]{1,0:T(8,128)(2,1)S(1)} %fusion.3.refs_0_), channel_id=1, source_target_pairs={{0,8},{8,0},{1,9},{9,1},{2,10},{10,2},{3,11},{11,3},{4,12},{12,4},... | collective-permute-start | bytes 196616 | tf_op jit(solution)/shard_map/ppermute | solution.py:160
  46.5 2.6 %collective-permute-done.19 = bf16[2,16,2048]{2,1,0:T(8,128)(2,1)S(1)} collective-permute-done((bf16[2,16,2048]{2,1,0:T(8,128)(2,1)S(1)}, bf16[2,16,2048]{2,1,0:T(8,128)(2,1)S(1)}, u32[]{:S(2)}, u32[]{:S(2)}) %collective-permute-start.19) | collective-permute-done | bytes 131104 | tf_op jit(solution)/shard_map/ppermute | solution.py:160
  49.2 1.6 %collective-permute-start.20 = (bf16[16,2048]{1,0:T(8,128)(2,1)S(1)}, bf16[16,2048]{1,0:T(8,128)(2,1)S(1)}, u32[]{:S(2)}, u32[]{:S(2)}) collective-permute-start(bf16[16,2048]{1,0:T(8,128)(2,1)S(1)} %fusion.1.refs_0_), channel_id=1, source_target_pairs={{0,8},{8,0},{1,9},{9,1},{2,10},{10,2},{3,11},{11,3},{4,12},{12,4},... | collective-permute-start | bytes 196616 | tf_op jit(solution)/shard_map/ppermute | solution.py:160
  51.4 2.1 %collective-permute-done.20.refs_1_ = bf16[16,2048]{1,0:T(8,128)(2,1)S(1)} collective-permute-done((bf16[16,2048]{1,0:T(8,128)(2,1)S(1)}, bf16[16,2048]{1,0:T(8,128)(2,1)S(1)}, u32[]{:S(2)}, u32[]{:S(2)}) %collective-permute-start.20) | collective-permute-done | bytes 65568 | tf_op jit(solution)/shard_map/ppermute | solution.py:160
  56.3 3.4 %shard_map.55 = (f32[64,2048]{1,0:T(8,128)S(1)}, bf16[2048,2048]{1,0:T(8,128)(2,1)S(1)}) custom-call(bf16[16,2048]{1,0:T(8,128)(2,1)S(1)} %fusion.1.refs_0_, bf16[16,2048]{1,0:T(8,128)(2,1)S(1)} %collective-permute-done.20.refs_1_, bf16[16,2048]{1,0:T(8,128)(2,1)S(1)} %collective-permute-done.21.refs_2_, ...), custom_call_target="tpu_custom_call" | custom-call | flops 536870912 | bytes 16777216 | tf_op jit(solution)/shard_map/pallas_call | solution.py:52
  60.3 8.8 %copy-done = bf16[6656,2048]{1,0:T(8,128)(2,1)S(1)} copy-done((bf16[6656,2048]{1,0:T(8,128)(2,1)S(1)}, bf16[6656,2048]{1,0:T(8,128)(2,1)}, u32[]{:S(2)}) %copy-start) | copy-done | bytes 27263000
  69.0 2.4 %shard_map.56 = (f32[64,2048]{1,0:T(8,128)S(1)}, bf16[1536,2048]{1,0:T(8,128)(2,1)S(1)}) custom-call(bf16[16,2048]{1,0:T(8,128)(2,1)S(1)} %fusion.3.refs_0_, bf16[16,2048]{1,0:T(8,128)(2,1)S(1)} %collective-permute-done.15.refs_1_, bf16[16,2048]{1,0:T(8,128)(2,1)S(1)} %collective-permute-done.16.refs_2_, ...), custom_call_target="tpu_custom_call" | custom-call | flops 536870912 | bytes 12582912 | tf_op jit(solution)/shard_map/pallas_call | solution.py:52
  71.5 1.9 %shard_map.57 = (f32[64,2048]{1,0:T(8,128)S(1)}, bf16[1024,2048]{1,0:T(8,128)(2,1)S(1)}) custom-call(bf16[16,1536]{1,0:T(8,128)(2,1)S(1)} %fusion.5.refs_0_, bf16[16,1536]{1,0:T(8,128)(2,1)S(1)} %collective-permute-done.10.refs_1_, bf16[16,1536]{1,0:T(8,128)(2,1)S(1)} %collective-permute-done.11.refs_2_, ...), custom_call_target="tpu_custom_call" | custom-call | flops 402653184 | bytes 8388608 | tf_op jit(solution)/shard_map/pallas_call | solution.py:52
  75.3 3.2 %collective-permute-start.25 = (bf16[16,2048]{1,0:T(8,128)(2,1)S(1)}, bf16[16,2048]{1,0:T(8,128)(2,1)S(1)}, u32[]{:S(2)}, u32[]{:S(2)}) collective-permute-start(bf16[16,2048]{1,0:T(8,128)(2,1)S(1)} %get-tuple-element.74), channel_id=1, source_target_pairs={{0,6},{2,0},{4,2},{6,4},{1,7},{3,1},{5,3},{7,5},{8,14},{10,8},{12,... | collective-permute-start | bytes 196616 | tf_op jit(solution)/shard_map/ppermute | solution.py:160
  78.5 3.0 %collective-permute-done.23 = bf16[16,2048]{1,0:T(8,128)(2,1)S(1)} collective-permute-done((bf16[16,2048]{1,0:T(8,128)(2,1)S(1)}, bf16[16,2048]{1,0:T(8,128)(2,1)S(1)}, u32[]{:S(2)}, u32[]{:S(2)}) %collective-permute-start.23) | collective-permute-done | bytes 65568 | tf_op jit(solution)/shard_map/ppermute | solution.py:160
  81.5 1.8 %collective-permute-done.24 = bf16[16,2048]{1,0:T(8,128)(2,1)S(1)} collective-permute-done((bf16[16,2048]{1,0:T(8,128)(2,1)S(1)}, bf16[16,2048]{1,0:T(8,128)(2,1)S(1)}, u32[]{:S(2)}, u32[]{:S(2)}) %collective-permute-start.24) | collective-permute-done | bytes 65568 | tf_op jit(solution)/shard_map/ppermute | solution.py:160
  (56 shorter events, 11.2 us)
Async XLA Ops:
  0.0 14.6 %collective-permute-start.1 = (bf16[16,2048]{1,0:T(8,128)(2,1)}, bf16[16,2048]{1,0:T(8,128)(2,1)S(1)}, u32[]{:S(2)}, u32[]{:S(2)}) collective-permute-start(bf16[16,2048]{1,0:T(8,128)(2,1)} %param.4), channel_id=1, source_target_pairs={{0,4},{2,6},{4,0},{6,2},{1,5},{3,7},{5,1},{7,3},{8,12},{10,14},{12... | collective-permute-start | bytes 196616 | tf_op jit(solution)/shard_map/ppermute | solution.py:160
  4.0 10.6 %collective-permute-start = (bf16[16,2048]{1,0:T(8,128)(2,1)}, bf16[16,2048]{1,0:T(8,128)(2,1)S(1)}, u32[]{:S(2)}, u32[]{:S(2)}) collective-permute-start(bf16[16,2048]{1,0:T(8,128)(2,1)} %param.4), channel_id=1, source_target_pairs={{0,2},{2,4},{4,6},{6,0},{1,3},{3,5},{5,7},{7,1},{8,10},{10,12},{12... | collective-permute-start | bytes 196616 | tf_op jit(solution)/shard_map/ppermute | solution.py:160
  5.6 9.0 %collective-permute-start.2 = (bf16[16,2048]{1,0:T(8,128)(2,1)}, bf16[16,2048]{1,0:T(8,128)(2,1)S(1)}, u32[]{:S(2)}, u32[]{:S(2)}) collective-permute-start(bf16[16,2048]{1,0:T(8,128)(2,1)} %param.4), channel_id=1, source_target_pairs={{0,6},{2,0},{4,2},{6,4},{1,7},{3,1},{5,3},{7,5},{8,14},{10,8},{12,... | collective-permute-start | bytes 196616 | tf_op jit(solution)/shard_map/ppermute | solution.py:160
  32.3 5.9 %collective-permute-start.13 = (f32[2,32,2048]{2,1,0:T(8,128)S(1)}, f32[2,32,2048]{2,1,0:T(8,128)S(1)}, u32[]{:S(2)}, u32[]{:S(2)}) collective-permute-start(f32[2,32,2048]{2,1,0:T(8,128)S(1)} %get-tuple-element.57), channel_id=1, source_target_pairs={{0,1},{1,0},{2,3},{3,2},{4,5},{5,4},{6,7},{7,6},{8,9},{9,8},{10,11... | collective-permute-start | bytes 1572872 | tf_op jit(solution)/shard_map/ppermute | solution.py:160
  33.9 4.3 %collective-permute-start.4 = (bf16[2,16,1024]{2,1,0:T(8,128)(2,1)S(1)}, bf16[2,16,1024]{2,1,0:T(8,128)(2,1)S(1)}, u32[]{:S(2)}, u32[]{:S(2)}) collective-permute-start(bf16[2,16,1024]{2,1,0:T(8,128)(2,1)S(1)} %get-tuple-element.51), channel_id=1, source_target_pairs={{0,8},{8,0},{1,9},{9,1},{2,10},{10,2},{3,11},{11,3},{4,12},{12,4},... | collective-permute-start | bytes 196616 | tf_op jit(solution)/shard_map/ppermute | solution.py:160
  35.5 6.7 %collective-permute-start.18 = (f32[2,32,2048]{2,1,0:T(8,128)S(1)}, f32[2,32,2048]{2,1,0:T(8,128)S(1)}, u32[]{:S(2)}, u32[]{:S(2)}) collective-permute-start(f32[2,32,2048]{2,1,0:T(8,128)S(1)} %get-tuple-element.61), channel_id=1, source_target_pairs={{0,1},{1,0},{2,3},{3,2},{4,5},{5,4},{6,7},{7,6},{8,9},{9,8},{10,11... | collective-permute-start | bytes 1572872 | tf_op jit(solution)/shard_map/ppermute | solution.py:160
  35.5 5.1 %collective-permute-start.8 = (f32[2,32,1536]{2,1,0:T(8,128)S(1)}, f32[2,32,1536]{2,1,0:T(8,128)S(1)}, u32[]{:S(2)}, u32[]{:S(2)}) collective-permute-start(f32[2,32,1536]{2,1,0:T(8,128)S(1)} %get-tuple-element.53), channel_id=1, source_target_pairs={{0,1},{1,0},{2,3},{3,2},{4,5},{5,4},{6,7},{7,6},{8,9},{9,8},{10,11... | collective-permute-start | bytes 1179656 | tf_op jit(solution)/shard_map/ppermute | solution.py:160
  38.3 6.5 %collective-permute-start.14 = (bf16[2,16,2048]{2,1,0:T(8,128)(2,1)S(1)}, bf16[2,16,2048]{2,1,0:T(8,128)(2,1)S(1)}, u32[]{:S(2)}, u32[]{:S(2)}) collective-permute-start(bf16[2,16,2048]{2,1,0:T(8,128)(2,1)S(1)} %get-tuple-element.59), channel_id=1, source_target_pairs={{0,8},{8,0},{1,9},{9,1},{2,10},{10,2},{3,11},{11,3},{4,12},{12,4},... | collective-permute-start | bytes 393224 | tf_op jit(solution)/shard_map/ppermute | solution.py:160
  39.9 13.7 %collective-permute-start.5 = (bf16[16,1024]{1,0:T(8,128)(2,1)S(1)}, bf16[16,1024]{1,0:T(8,128)(2,1)S(1)}, u32[]{:S(2)}, u32[]{:S(2)}) collective-permute-start(bf16[16,1024]{1,0:T(8,128)(2,1)S(1)} %fusion.7.refs_0_), channel_id=1, source_target_pairs={{0,8},{8,0},{1,9},{9,1},{2,10},{10,2},{3,11},{11,3},{4,12},{12,4},... | collective-permute-start | bytes 98312 | tf_op jit(solution)/shard_map/ppermute | solution.py:160
  40.6 10.2 %collective-permute-start.9 = (bf16[2,16,1536]{2,1,0:T(8,128)(2,1)S(1)}, bf16[2,16,1536]{2,1,0:T(8,128)(2,1)S(1)}, u32[]{:S(2)}, u32[]{:S(2)}) collective-permute-start(bf16[2,16,1536]{2,1,0:T(8,128)(2,1)S(1)} %get-tuple-element.55), channel_id=1, source_target_pairs={{0,8},{8,0},{1,9},{9,1},{2,10},{10,2},{3,11},{11,3},{4,12},{12,4},... | collective-permute-start | bytes 294920 | tf_op jit(solution)/shard_map/ppermute | solution.py:160
  42.2 6.9 %collective-permute-start.19 = (bf16[2,16,2048]{2,1,0:T(8,128)(2,1)S(1)}, bf16[2,16,2048]{2,1,0:T(8,128)(2,1)S(1)}, u32[]{:S(2)}, u32[]{:S(2)}) collective-permute-start(bf16[2,16,2048]{2,1,0:T(8,128)(2,1)S(1)} %get-tuple-element.63), channel_id=1, source_target_pairs={{0,8},{8,0},{1,9},{9,1},{2,10},{10,2},{3,11},{11,3},{4,12},{12,4},... | collective-permute-start | bytes 393224 | tf_op jit(solution)/shard_map/ppermute | solution.py:160
  44.9 6.4 %collective-permute-start.15 = (bf16[16,2048]{1,0:T(8,128)(2,1)S(1)}, bf16[16,2048]{1,0:T(8,128)(2,1)S(1)}, u32[]{:S(2)}, u32[]{:S(2)}) collective-permute-start(bf16[16,2048]{1,0:T(8,128)(2,1)S(1)} %fusion.3.refs_0_), channel_id=1, source_target_pairs={{0,8},{8,0},{1,9},{9,1},{2,10},{10,2},{3,11},{11,3},{4,12},{12,4},... | collective-permute-start | bytes 196616 | tf_op jit(solution)/shard_map/ppermute | solution.py:160
  49.2 4.3 %collective-permute-start.20 = (bf16[16,2048]{1,0:T(8,128)(2,1)S(1)}, bf16[16,2048]{1,0:T(8,128)(2,1)S(1)}, u32[]{:S(2)}, u32[]{:S(2)}) collective-permute-start(bf16[16,2048]{1,0:T(8,128)(2,1)S(1)} %fusion.1.refs_0_), channel_id=1, source_target_pairs={{0,8},{8,0},{1,9},{9,1},{2,10},{10,2},{3,11},{11,3},{4,12},{12,4},... | collective-permute-start | bytes 196616 | tf_op jit(solution)/shard_map/ppermute | solution.py:160
  50.8 9.0 %collective-permute-start.16 = (bf16[16,2048]{1,0:T(8,128)(2,1)S(1)}, bf16[16,2048]{1,0:T(8,128)(2,1)S(1)}, u32[]{:S(2)}, u32[]{:S(2)}) collective-permute-start(bf16[16,2048]{1,0:T(8,128)(2,1)S(1)} %fusion.3.refs_0_), channel_id=1, source_target_pairs={{0,1},{1,0},{2,3},{3,2},{4,5},{5,4},{6,7},{7,6},{8,9},{9,8},{10,11... | collective-permute-start | bytes 196616 | tf_op jit(solution)/shard_map/ppermute | solution.py:160
  50.9 3.3 %collective-permute-start.21 = (bf16[16,2048]{1,0:T(8,128)(2,1)S(1)}, bf16[16,2048]{1,0:T(8,128)(2,1)S(1)}, u32[]{:S(2)}, u32[]{:S(2)}) collective-permute-start(bf16[16,2048]{1,0:T(8,128)(2,1)S(1)} %fusion.1.refs_0_), channel_id=1, source_target_pairs={{0,1},{1,0},{2,3},{3,2},{4,5},{5,4},{6,7},{7,6},{8,9},{9,8},{10,11... | collective-permute-start | bytes 196616 | tf_op jit(solution)/shard_map/ppermute | solution.py:160
  51.4 8.9 %collective-permute-start.17 = (bf16[16,2048]{1,0:T(8,128)(2,1)S(1)}, bf16[16,2048]{1,0:T(8,128)(2,1)S(1)}, u32[]{:S(2)}, u32[]{:S(2)}) collective-permute-start(bf16[16,2048]{1,0:T(8,128)(2,1)S(1)} %collective-permute-done.15.refs_1_), channel_id=1, source_target_pairs={{0,1},{1,0},{2,3},{3,2},{4,5},{5,4},{6,7},{7,6},{8,9},{9,8},{10,11... | collective-permute-start | bytes 196616 | tf_op jit(solution)/shard_map/ppermute | solution.py:160
  53.6 19.8 %collective-permute-start.6 = (bf16[16,1024]{1,0:T(8,128)(2,1)S(1)}, bf16[16,1024]{1,0:T(8,128)(2,1)S(1)}, u32[]{:S(2)}, u32[]{:S(2)}) collective-permute-start(bf16[16,1024]{1,0:T(8,128)(2,1)S(1)} %fusion.7.refs_0_), channel_id=1, source_target_pairs={{0,1},{1,0},{2,3},{3,2},{4,5},{5,4},{6,7},{7,6},{8,9},{9,8},{10,11... | collective-permute-start | bytes 98312 | tf_op jit(solution)/shard_map/ppermute | solution.py:160
  54.2 19.2 %collective-permute-start.7 = (bf16[16,1024]{1,0:T(8,128)(2,1)S(1)}, bf16[16,1024]{1,0:T(8,128)(2,1)S(1)}, u32[]{:S(2)}, u32[]{:S(2)}) collective-permute-start(bf16[16,1024]{1,0:T(8,128)(2,1)S(1)} %collective-permute-done.5.refs_1_), channel_id=1, source_target_pairs={{0,1},{1,0},{2,3},{3,2},{4,5},{5,4},{6,7},{7,6},{8,9},{9,8},{10,11... | collective-permute-start | bytes 98312 | tf_op jit(solution)/shard_map/ppermute | solution.py:160
  54.8 4.9 %collective-permute-start.10 = (bf16[16,1536]{1,0:T(8,128)(2,1)S(1)}, bf16[16,1536]{1,0:T(8,128)(2,1)S(1)}, u32[]{:S(2)}, u32[]{:S(2)}) collective-permute-start(bf16[16,1536]{1,0:T(8,128)(2,1)S(1)} %fusion.5.refs_0_), channel_id=1, source_target_pairs={{0,8},{8,0},{1,9},{9,1},{2,10},{10,2},{3,11},{11,3},{4,12},{12,4},... | collective-permute-start | bytes 147464 | tf_op jit(solution)/shard_map/ppermute | solution.py:160
  59.7 11.7 %collective-permute-start.11 = (bf16[16,1536]{1,0:T(8,128)(2,1)S(1)}, bf16[16,1536]{1,0:T(8,128)(2,1)S(1)}, u32[]{:S(2)}, u32[]{:S(2)}) collective-permute-start(bf16[16,1536]{1,0:T(8,128)(2,1)S(1)} %fusion.5.refs_0_), channel_id=1, source_target_pairs={{0,1},{1,0},{2,3},{3,2},{4,5},{5,4},{6,7},{7,6},{8,9},{9,8},{10,11... | collective-permute-start | bytes 147464 | tf_op jit(solution)/shard_map/ppermute | solution.py:160
  59.8 11.7 %collective-permute-start.12 = (bf16[16,1536]{1,0:T(8,128)(2,1)S(1)}, bf16[16,1536]{1,0:T(8,128)(2,1)S(1)}, u32[]{:S(2)}, u32[]{:S(2)}) collective-permute-start(bf16[16,1536]{1,0:T(8,128)(2,1)S(1)} %collective-permute-done.10.refs_1_), channel_id=1, source_target_pairs={{0,1},{1,0},{2,3},{3,2},{4,5},{5,4},{6,7},{7,6},{8,9},{9,8},{10,11... | collective-permute-start | bytes 147464 | tf_op jit(solution)/shard_map/ppermute | solution.py:160
  74.6 6.8 %collective-permute-start.23 = (bf16[16,2048]{1,0:T(8,128)(2,1)S(1)}, bf16[16,2048]{1,0:T(8,128)(2,1)S(1)}, u32[]{:S(2)}, u32[]{:S(2)}) collective-permute-start(bf16[16,2048]{1,0:T(8,128)(2,1)S(1)} %get-tuple-element.72), channel_id=1, source_target_pairs={{0,2},{2,4},{4,6},{6,0},{1,3},{3,5},{5,7},{7,1},{8,10},{10,12},{12... | collective-permute-start | bytes 196616 | tf_op jit(solution)/shard_map/ppermute | solution.py:160
  74.7 8.6 %collective-permute-start.24 = (bf16[16,2048]{1,0:T(8,128)(2,1)S(1)}, bf16[16,2048]{1,0:T(8,128)(2,1)S(1)}, u32[]{:S(2)}, u32[]{:S(2)}) collective-permute-start(bf16[16,2048]{1,0:T(8,128)(2,1)S(1)} %get-tuple-element.73), channel_id=1, source_target_pairs={{0,4},{2,6},{4,0},{6,2},{1,5},{3,7},{5,1},{7,3},{8,12},{10,14},{12... | collective-permute-start | bytes 196616 | tf_op jit(solution)/shard_map/ppermute | solution.py:160
  75.3 8.0 %collective-permute-start.25 = (bf16[16,2048]{1,0:T(8,128)(2,1)S(1)}, bf16[16,2048]{1,0:T(8,128)(2,1)S(1)}, u32[]{:S(2)}, u32[]{:S(2)}) collective-permute-start(bf16[16,2048]{1,0:T(8,128)(2,1)S(1)} %get-tuple-element.74), channel_id=1, source_target_pairs={{0,6},{2,0},{4,2},{6,4},{1,7},{3,1},{5,3},{7,5},{8,14},{10,8},{12,... | collective-permute-start | bytes 196616 | tf_op jit(solution)/shard_map/ppermute | solution.py:160
  (3 other events, 11.6 us)

commit v2 on v0

v2 whole, which is shorter than its diff:
```python
import functools

import jax
import jax.numpy as jnp
from jax import lax
from jax.experimental import pallas as pl
from jax.experimental.pallas import tpu as pltpu
from jax.sharding import PartitionSpec as P

BF16, F32 = jnp.bfloat16, jnp.float32
TILE = 512
SHARES = (6, 4, 3)
PAIR_TYPE = F32


def on_chip():
    return pl.BlockSpec(memory_space=pltpu.VMEM)


def in_place():
    return pl.BlockSpec(memory_space=pl.ANY)


def cuts(columns):
    if columns % (TILE * sum(SHARES)):
        return [(0, columns)]
    unit = columns // sum(SHARES)
    chunks, start = [], 0
    for share in SHARES:
        chunks.append((start, share * unit))
        start += share * unit
    return chunks


def tile_of(width):
    return TILE if width % TILE == 0 else width


def copies(fetch, sources, targets, sems):
    made = []
    for at, ((axis, start, size), source, target) in enumerate(zip(fetch, sources, targets)):
        view = source.at[:, pl.ds(start, size)] if axis else source.at[pl.ds(start, size), :]
        made.append(pltpu.make_async_copy(view, target, sems.at[at]))
    return made


def call(body, operands, outs, fetch, scratch, flops, traffic, after=(), aliases=None):
    fetched = []
    for array, axis, start, size in fetch:
        shape = (array.shape[0], size) if axis else (size, array.shape[1])
        fetched.append(pltpu.VMEM(shape, array.dtype))
    n_in = len(operands)

    def kernel(*refs):
        ins, rest = refs[:n_in], refs[n_in + len(after) :]
        sources, rest = rest[: len(fetch)], rest[len(fetch) :]
        results, rest = rest[: len(outs)], rest[len(outs) :]
        targets, (*room, sems) = rest[: len(fetch)], rest[len(fetch) :]
        made = copies([f[1:] for f in fetch], sources, targets, sems)
        for copy in made:
            copy.start()
        body(ins, results, room)
        for copy in made:
            copy.wait()

    out = pl.pallas_call(
        kernel,
        out_shape=tuple(outs) + tuple(fetched),
        in_specs=[on_chip()] * n_in + [in_place()] * (len(after) + len(fetch)),
        out_specs=tuple([on_chip()] * (len(outs) + len(fetch))),
        scratch_shapes=list(scratch) + [pltpu.SemaphoreType.DMA((max(len(fetch), 1),))],
        input_output_aliases=aliases or {},
        compiler_params=pltpu.CompilerParams(vmem_limit_bytes=4 * 2**20),
        cost_estimate=pl.CostEstimate(flops=flops, bytes_accessed=traffic, transcendentals=0),
    )(*operands, *after, *[pltpu.with_memory_space_constraint(f[0], pltpu.HBM) for f in fetch])
    return out[: len(outs)], out[len(outs) :]


def load_kernel(ins, outs, room):
    pass


def pair_part_kernel(n_pair, ins, outs, room):
    x, weight = ins
    keep, *sends = outs
    (res,) = room
    me = lax.axis_index("pair")
    rows = keep.shape[0]
    width = weight.shape[1]
    tile = tile_of(width)

    @pl.loop(0, width // tile)
    def _(step):
        at = pl.ds(pl.multiple_of(step * tile, tile), tile)
        res[...] = jnp.dot(x[...], weight[:, at], preferred_element_type=F32)
        for k in range(n_pair):
            first = pl.multiple_of(lax.rem(me + k, n_pair) * rows, 16)
            target = sends[k - 1] if k else keep
            target[:, at] = res[pl.ds(first, rows), :].astype(target.dtype)


def pair_sum_kernel(ins, outs, room):
    total = ins[0][...]
    for part in ins[1:]:
        total += part[...].astype(F32)
    for out in outs:
        out[...] = total.astype(out.dtype)


def down_kernel(n_wide, first, last, ins, outs, room):
    parts, (wd, *before) = (ins[:-1], ins[-1:]) if first else (ins[:-2], ins[-2:])
    (hidden,) = room
    n_pair = len(parts)
    c, w = lax.axis_index("pair"), lax.axis_index("wide")
    rows = parts[0].shape[0]
    for k in range(n_pair):
        block = lax.rem(c + n_pair - k, n_pair)
        hidden[pl.ds(pl.multiple_of(block * rows, 16), rows), :] = parts[k][...]
    width = wd.shape[1]
    tile = tile_of(width)

    @pl.loop(0, width // tile)
    def _(step):
        at = pl.ds(pl.multiple_of(step * tile, tile), tile)
        total = jnp.dot(hidden[...], wd[:, at], preferred_element_type=F32)
        if before:
            total += before[0][:, at]
        if last:
            own, others = outs
            share = total.shape[0] // n_wide
            for k in range(n_wide):
                piece = total[k * share : (k + 1) * share]
                if k == 0:
                    own[:, at] = piece
                    piece = jnp.zeros_like(piece)
                place = pl.multiple_of(lax.rem(w + n_wide - k, n_wide) * share, 16)
                others[pl.ds(place, share), at] = piece.astype(others.dtype)
        else:
            outs[0][:, at] = total


def shards(sizes, tokens, gate_weight, up_weight, down_weight):
    n_seq, n_wide, n_pair = sizes["seq"], sizes["wide"], sizes["pair"]

    def send(value, axis, k):
        n = sizes[axis]
        return lax.ppermute(value, axis, [(i, (i + k) % n) for i in range(n)])

    share, depth = tokens.shape
    rows = share * n_wide
    features = down_weight.shape[1]
    half = rows // n_pair
    chunks = cuts(gate_weight.shape[1])
    n = len(chunks)
    size = tokens.dtype.itemsize

    def gate_of(*picks):
        return [(gate_weight, 1, *chunks[j]) for j in picks if j < n]

    def down_of(*picks):
        return [(down_weight, 0, *chunks[j]) for j in picks if j < n]

    def bytes_of(fetch):
        return sum(size * f[3] * f[0].shape[1 - f[1]] for f in fetch)

    x = jnp.concatenate([tokens] + [send(tokens, "wide", k) for k in range(1, n_wide)])

    alive = []

    def project(weight, fetch, after=()):
        width = weight.shape[1]
        outs, fetched = call(
            functools.partial(pair_part_kernel, n_pair),
            [x, weight],
            [pltpu.VMEM((half, width), F32)] + [pltpu.VMEM((half, width), PAIR_TYPE)] * (n_pair - 1),
            fetch,
            [pltpu.VMEM((rows, tile_of(width)), F32)],
            2 * rows * depth * width,
            2 * bytes_of(fetch),
            after,
        )
        got = [send(outs[k], "pair", k) for k in range(1, n_pair)]
        alive.extend(got)
        return (outs[0], *got), fetched

    def pair_sum(parts):
        shape = parts[0].shape
        return call(
            pair_sum_kernel, parts, [pltpu.VMEM(shape, F32), pltpu.VMEM(shape, BF16)],
            [], [], 0, 8 * parts[0].size,
        )[0]

    def seq_parts(sums):
        parts = [send(sums[1], "seq", k) for k in range(1, n_seq)]
        alive.extend(parts)
        return [sums[0], *parts]

    def activate(ups, gates, start, width):
        up = sum(part[:, start : start + width].astype(F32) for part in ups)
        gate = sum(part.astype(F32) for part in gates)
        return (jax.nn.silu(gate) * up).astype(BF16)

    fetch = gate_of(n - 1)
    traffic = up_weight.size * size
    _, (gate_last,) = call(load_kernel, [], [], fetch, [], 0, traffic)
    up = pltpu.with_memory_space_constraint(up_weight, pltpu.VMEM)
    ups, gate = project(up, gate_of(0) if n > 1 else [], [gate_last])
    gate = {0: gate[0] if n > 1 else None, n - 1: gate_last}
    up_sums, gate_sums, down = None, [], {}
    parts = []
    for j in range(n):
        fetch = gate_of(1) if j == 0 else []
        if j == n - 1:
            fetch = fetch + down_of(0, 1)
        after = []
        if j == 1:
            up_sums = pair_sum(ups)
            after = [up_sums[1]]
        elif j > 1:
            gate_sums.append(pair_sum(parts[j - 2]))
            after = [gate_sums[-1][1]]
        outs, fetched = project(gate[j], fetch, after)
        parts.append(outs)
        if j == 0 and n > 1:
            gate[1], *fetched = fetched
        if j == n - 1:
            down.update(zip((0, 1), fetched))
    if up_sums is None:
        up_sums = pair_sum(ups)
    for j in range(len(gate_sums), n):
        gate_sums.append(pair_sum(parts[j]))
    up_parts = seq_parts(up_sums)
    hiddens = [activate(up_parts, seq_parts(gate_sums[j]), *chunks[j]) for j in range(n)]

    total = []
    for j, (start, width) in enumerate(chunks):
        first, last = j == 0, j == n - 1
        parts = [hiddens[j]] + [send(hiddens[j], "pair", k) for k in range(1, n_pair)]
        alive.extend(parts[1:])
        if last:
            outs = [pltpu.VMEM((share, features), F32), pltpu.VMEM((rows, features), BF16)]
        else:
            outs = [pltpu.VMEM((rows, features), F32)]
        fetch = down_of(2) if j == 0 else []
        total, fetched = call(
            functools.partial(down_kernel, n_wide, first, last),
            [*parts, down[j], *total],
            outs,
            fetch,
            [pltpu.VMEM((rows, width), BF16)],
            2 * rows * width * features,
            2 * bytes_of(fetch),
            alive if last else [],
        )
        if fetch:
            down[2] = fetched[0]

    own, others = total
    others = lax.all_to_all(others, "wide", 0, 0, tiled=True)
    result = own
    for k in range(n_wide):
        result = result + others[k * share : (k + 1) * share].astype(F32)
    return result.astype(BF16)


def solution(mesh):
    return jax.shard_map(
        functools.partial(shards, dict(mesh.shape)),
        mesh=mesh,
        in_specs=(
            P(("parts", "wide"), ("seq", "pair")),
            P(("seq", "pair"), "wide"),
            P(("seq", "pair"), "wide"),
            P("wide", ("seq", "pair")),
        ),
        out_specs=P(("parts", "wide"), ("seq", "pair")),
        check_vma=False,
    )
```

time: 167 us -> 75.9 us (0.45)
  waiting for transfers between devices: 96.3 us -> 9 us
  matrix products: 37.9 us -> 0 us
  Pallas kernels: 0 us -> 28.3 us
  starting transfers between devices: 0.04 us -> 13.6 us
  between operations: 13.4 us -> 0.24 us
  local copies, waits for them, and re-layouts: 0 us -> 10.6 us
  blocking collectives: 15.8 us -> 12.8 us
  other arithmetic: 3.52 us -> 1 us
    psum x1 -> x0, waiting for transfers between devices: 74.3 us -> none  [shards(): totals = lax.psum(partials, ('seq', 'pair'))]
    dot_general x3 -> x0, matrix products: 37.9 us -> none  [the longest x1 15.4 us: shards(): jnp.dot(hidden, down_weight, preferred_element_type=jnp.float32)]
    pallas_call x0 -> x12, Pallas kernels: none -> 28.3 us  [call(): pl.pallas_call(kernel, out_shape=tuple(outs) + tuple(fetched), in_specs=[...]
    reduce_scatter x1 -> x0, waiting for transfers between devices: 21.9 us -> none  [shards(): lax.psum_scatter(down_partial, 'wide', scatter_dimension=0, tiled=True)]
    all_gather x1 -> x0, blocking collectives: 15.8 us -> none  [shards(): piece = lax.all_gather(tokens, 'wide', axis=0, tiled=True)]
    ppermute x0 -> x14, starting transfers between devices: none -> 13.6 us  [send(): return lax.ppermute(value, axis, [(i, (i + k) % n) for i in range(n)])]
    all_to_all x0 -> x1, blocking collectives: none -> 12.8 us  [shards(): others = lax.all_to_all(others, 'wide', 0, 0, tiled=True)]
    unnamed x0 -> x9, local copies, waits for them, and re-layouts: none -> 10.6 us
  transfers between devices with their start and end apart: 2 -> 14, of which waited for: 2 -> 4; matrix products, arithmetic and copies ran while one was open for 0% -> 2% of each run, Pallas kernels for 0% -> 27%
where the time goes in v2:
time: 75.9 us; the launch traced here: 75.5 us
  Pallas kernels  28.3 us (37%)
  starting transfers between devices  13.6 us (18%)
  blocking collectives  12.8 us (17%)
  local copies, waits for them, and re-layouts  10.6 us (14%)
  waiting for transfers between devices  9 us (12%)
  other arithmetic  1 us (1%)
    pallas_call x12, Pallas kernels, call(): pl.pallas_call(kernel, out_shape=tuple(outs) + tuple(fetched), in_specs=[...  28.3 us
    ppermute x14, starting transfers between devices, send(): return lax.ppermute(value, axis, [(i, (i + k) % n) for i in range(n)])  13.6 us
    all_to_all x1, blocking collectives, shards(): others = lax.all_to_all(others, 'wide', 0, 0, tiled=True)  12.8 us
    unnamed x9, local copies, waits for them, and re-layouts  10.6 us
    ppermute x14, waiting for transfers between devices, send(): return lax.ppermute(value, axis, [(i, (i + k) % n) for i in range(n)])  9 us
  transfers between devices with their start and end apart: 14, of which 4 were waited for; matrix products, arithmetic and copies ran while one was open for 2% of the time, Pallas kernels for 27%

profile of v2, /device:TPU:0, one launch (start us, length us, event | category | flops | bytes accessed | tf_op | source)
XLA Modules:
  0.0 75.5 jit_solution(13522450018572202490)
XLA Ops:
  0.0 4.0 %collective-permute-start.1 = (bf16[16,2048]{1,0:T(8,128)(2,1)}, bf16[16,2048]{1,0:T(8,128)(2,1)S(1)}, u32[]{:S(2)}, u32[]{:S(2)}) collective-permute-start(bf16[16,2048]{1,0:T(8,128)(2,1)} %param.4), channel_id=1, source_target_pairs={{0,4},{2,6},{4,0},{6,2},{1,5},{3,7},{5,1},{7,3},{8,12},{10,14},{12... | collective-permute-start | bytes 196616 | tf_op jit(solution)/shard_map/ppermute | solution.py:147
  4.0 1.6 %collective-permute-start = (bf16[16,2048]{1,0:T(8,128)(2,1)}, bf16[16,2048]{1,0:T(8,128)(2,1)S(1)}, u32[]{:S(2)}, u32[]{:S(2)}) collective-permute-start(bf16[16,2048]{1,0:T(8,128)(2,1)} %param.4), channel_id=1, source_target_pairs={{0,2},{2,4},{4,6},{6,0},{1,3},{3,5},{5,7},{7,1},{8,10},{10,12},{12... | collective-permute-start | bytes 196616 | tf_op jit(solution)/shard_map/ppermute | solution.py:147
  5.6 2.2 %collective-permute-start.2 = (bf16[16,2048]{1,0:T(8,128)(2,1)}, bf16[16,2048]{1,0:T(8,128)(2,1)S(1)}, u32[]{:S(2)}, u32[]{:S(2)}) collective-permute-start(bf16[16,2048]{1,0:T(8,128)(2,1)} %param.4), channel_id=1, source_target_pairs={{0,6},{2,0},{4,2},{6,4},{1,7},{3,1},{5,3},{7,5},{8,14},{10,8},{12,... | collective-permute-start | bytes 196616 | tf_op jit(solution)/shard_map/ppermute | solution.py:147
  7.9 0.9 %constant_dynamic-update-slice_fusion.3 = bf16[64,2048]{1,0:T(8,128)(2,1)S(1)} fusion(bf16[16,2048]{1,0:T(8,128)(2,1)} %param.4), kind=kLoop, calls=%fused_computation.15 | loop fusion | bytes 131072
  8.7 2.8 %shard_map.46.refs_2_.refs_1_ = bf16[2048,1536]{1,0:T(8,128)(2,1)S(1)} custom-call(bf16[2048,6656]{1,0:T(8,128)(2,1)} %refs_2_.1), custom_call_target="tpu_custom_call" | custom-call | bytes 27262976 | tf_op jit(solution)/shard_map/pallas_call | solution.py:66
  11.6 8.7 %copy-done = bf16[2048,6656]{1,0:T(8,128)(2,1)S(1)} copy-done((bf16[2048,6656]{1,0:T(8,128)(2,1)S(1)}, bf16[2048,6656]{1,0:T(8,128)(2,1)}, u32[]{:S(2)}) %copy-start) | copy-done | bytes 27263000
  20.4 6.4 %shard_map.47 = (f32[32,6656]{1,0:T(8,128)S(1)}, f32[32,6656]{1,0:T(8,128)S(1)}, bf16[2048,3072]{1,0:T(8,128)(2,1)S(1)}) custom-call(bf16[64,2048]{1,0:T(8,128)(2,1)S(1)} %constant_dynamic-update-slice_fusion.refs_0_, bf16[2048,6656]{1,0:T(8,128)(2,1)S(1)} %copy-done, bf16[2048,1536]{1,0:T(8,128)(2,1)S(1)} %shard_map.46.refs_2_.refs_1_, ...), custom_call_target="tpu_custom_call" | custom-call | flops 1744830464 | bytes 25165824 | tf_op jit(solution)/shard_map/pallas_call | solution.py:66
  26.9 3.5 %shard_map.48 = (f32[32,3072]{1,0:T(8,128)S(1)}, f32[32,3072]{1,0:T(8,128)S(1)}, bf16[2048,2048]{1,0:T(8,128)(2,1)S(1)}) custom-call(bf16[64,2048]{1,0:T(8,128)(2,1)S(1)} %constant_dynamic-update-slice_fusion.refs_0_, bf16[2048,3072]{1,0:T(8,128)(2,1)S(1)} %get-tuple-element.29.refs_1_, bf16[2048,6656]{1,0:T(8,128)(2,1)} %refs_2_.1), custom_call_target="tpu_custom_call" | custom-call | flops 805306368 | bytes 16777216 | tf_op jit(solution)/shard_map/pallas_call | solution.py:66
  30.3 0.6 collective-permute-start.3
  31.0 1.6 %collective-permute-start.7 = (bf16[32,6656]{1,0:T(8,128)(2,1)S(1)}, bf16[32,6656]{1,0:T(8,128)(2,1)S(1)}, u32[]{:S(2)}, u32[]{:S(2)}) collective-permute-start(bf16[32,6656]{1,0:T(8,128)(2,1)S(1)} %get-tuple-element.40.refs_2_), channel_id=1, source_target_pairs={{0,8},{8,0},{1,9},{9,1},{2,10},{10,2},{3,11},{11,3},{4,12},{12,4},... | collective-permute-start | bytes 1277960 | tf_op jit(solution)/shard_map/ppermute | solution.py:147
  32.6 2.0 %shard_map.54 = (f32[32,2048]{1,0:T(8,128)S(1)}, f32[32,2048]{1,0:T(8,128)S(1)}) custom-call(bf16[64,2048]{1,0:T(8,128)(2,1)S(1)} %constant_dynamic-update-slice_fusion.refs_0_, bf16[2048,2048]{1,0:T(8,128)(2,1)S(1)} %get-tuple-element.44.refs_1_, bf16[32,6656]{1,0:T(8,128)(2,1)S(1)} %get-tuple-element.40.refs_2_), custom_call_target="tpu_custom_call" | custom-call | flops 536870912 | tf_op jit(solution)/shard_map/pallas_call | solution.py:66
  34.8 0.9 %copy-done.2 = bf16[64,2048]{1,0:T(8,128)(2,1)S(1)} copy-done((bf16[64,2048]{1,0:T(8,128)(2,1)S(1)}, bf16[64,2048]{1,0:T(8,128)(2,1)}, u32[]{:S(2)}) %copy-start.2) | copy-done | bytes 262168
  35.7 7.0 %shard_map.50 = (f32[32,1536]{1,0:T(8,128)S(1)}, f32[32,1536]{1,0:T(8,128)S(1)}, bf16[3072,2048]{1,0:T(8,128)(2,1)S(1)}, bf16[2048,2048]{1,0:T(8,128)(2,1)S(1)}) custom-call(bf16[64,2048]{1,0:T(8,128)(2,1)S(1)} %copy-done.2, bf16[2048,1536]{1,0:T(8,128)(2,1)S(1)} %shard_map.46.refs_2_.refs_1_, bf16[32,3072]{1,0:T(8,128)(2,1)S(1)} %get-tuple-element.32.refs_2_, ...), custom_call_target="tpu_custom_call" | custom-call | flops 402653184 | bytes 41943040 | tf_op jit(solution)/shard_map/pallas_call | solution.py:66
  43.3 0.6 collective-permute-start.12
  43.9 1.5 %collective-permute-start.9 = (bf16[32,3072]{1,0:T(8,128)(2,1)S(1)}, bf16[32,3072]{1,0:T(8,128)(2,1)S(1)}, u32[]{:S(2)}, u32[]{:S(2)}) collective-permute-start(bf16[32,3072]{1,0:T(8,128)(2,1)S(1)} %get-tuple-element.32.refs_2_), channel_id=1, source_target_pairs={{0,8},{8,0},{1,9},{9,1},{2,10},{10,2},{3,11},{11,3},{4,12},{12,4},... | collective-permute-start | bytes 589832 | tf_op jit(solution)/shard_map/ppermute | solution.py:147
  45.4 0.6 collective-permute-start.5
  46.0 3.7 %collective-permute-done.12.refs_10_ = bf16[32,2048]{1,0:T(8,128)(2,1)S(1)} collective-permute-done((bf16[32,2048]{1,0:T(8,128)(2,1)S(1)}, bf16[32,2048]{1,0:T(8,128)(2,1)S(1)}, u32[]{:S(2)}, u32[]{:S(2)}) %collective-permute-start.12) | collective-permute-done | bytes 131104 | tf_op jit(solution)/shard_map/ppermute | solution.py:147
  49.9 4.0 %collective-permute-done.9.refs_9_ = bf16[32,3072]{1,0:T(8,128)(2,1)S(1)} collective-permute-done((bf16[32,3072]{1,0:T(8,128)(2,1)S(1)}, bf16[32,3072]{1,0:T(8,128)(2,1)S(1)}, u32[]{:S(2)}, u32[]{:S(2)}) %collective-permute-start.9) | collective-permute-done | bytes 196640 | tf_op jit(solution)/shard_map/ppermute | solution.py:147
  54.2 0.9 %collective-permute-done.5.refs_11_ = bf16[32,1536]{1,0:T(8,128)(2,1)S(1)} collective-permute-done((bf16[32,1536]{1,0:T(8,128)(2,1)S(1)}, bf16[32,1536]{1,0:T(8,128)(2,1)S(1)}, u32[]{:S(2)}, u32[]{:S(2)}) %collective-permute-start.5) | collective-permute-done | bytes 98336 | tf_op jit(solution)/shard_map/ppermute | solution.py:147
  55.6 2.8 %shard_map.53 = (f32[64,2048]{1,0:T(8,128)S(1)}, bf16[1536,2048]{1,0:T(8,128)(2,1)S(1)}) custom-call(bf16[32,3072]{1,0:T(8,128)(2,1)S(1)} %multiply_convert_fusion.refs_0_, bf16[32,3072]{1,0:T(8,128)(2,1)S(1)} %collective-permute-done.10.refs_1_.refs_12_, bf16[3072,2048]{1,0:T(8,128)(2,1)S(1)} %get-tuple-element.42.refs_2_, bf16[6656,2048]{1,0:T(8,128)(2,1)} %refs_3_.5), custom_call_target="tpu_custom_call" | custom-call | flops 805306368 | bytes 12582912 | tf_op jit(solution)/shard_map/pallas_call | solution.py:66
  58.4 2.0 %shard_map.56.refs_3_ = f32[64,2048]{1,0:T(8,128)S(1)} custom-call(bf16[32,2048]{1,0:T(8,128)(2,1)S(1)} %multiply_convert_fusion.1.refs_0_, bf16[32,2048]{1,0:T(8,128)(2,1)S(1)} %collective-permute-done.13.refs_1_.refs_13_, bf16[2048,2048]{1,0:T(8,128)(2,1)S(1)} %get-tuple-element.49.refs_2_, f32[64,2048]{1,0:T(8,128)S(1)} %get-tuple-element.50.refs_3_), custom_call_target="tpu_custom_call" | custom-call | flops 536870912 | tf_op jit(solution)/shard_map/pallas_call | solution.py:66
  60.4 1.6 %shard_map.57 = (f32[16,2048]{1,0:T(8,128)S(1)}, bf16[64,2048]{1,0:T(8,128)(2,1)S(1)}) custom-call(bf16[32,1536]{1,0:T(8,128)(2,1)S(1)} %multiply_convert_fusion.2.refs_0_, bf16[32,1536]{1,0:T(8,128)(2,1)S(1)} %collective-permute-done.8.refs_1_.refs_14_, bf16[1536,2048]{1,0:T(8,128)(2,1)S(1)} %get-tuple-element.43.refs_2_, ...), custom_call_target="tpu_custom_call" | custom-call | flops 402653184 | tf_op jit(solution)/shard_map/pallas_call | solution.py:66
  62.0 12.8 %all_to_all.9 = bf16[4,16,2048]{2,1,0:T(8,128)(2,1)S(1)} all-to-all(bf16[4,16,2048]{2,1,0:T(8,128)(2,1)S(1)} %bitcast.21), channel_id=1, replica_groups=mesh['parts'=2,'seq'=2,'wide'=4,'pair'=2] {'wide'}, dimensions={0} | all-to-all | bytes 524288 | tf_op jit(solution)/shard_map/all_to_all | solution.py:259
  74.8 0.7 fusion
  (31 shorter events, 1.9 us)
Async XLA Ops:
  0.0 11.6 %collective-permute-start.1 = (bf16[16,2048]{1,0:T(8,128)(2,1)}, bf16[16,2048]{1,0:T(8,128)(2,1)S(1)}, u32[]{:S(2)}, u32[]{:S(2)}) collective-permute-start(bf16[16,2048]{1,0:T(8,128)(2,1)} %param.4), channel_id=1, source_target_pairs={{0,4},{2,6},{4,0},{6,2},{1,5},{3,7},{5,1},{7,3},{8,12},{10,14},{12... | collective-permute-start | bytes 196616 | tf_op jit(solution)/shard_map/ppermute | solution.py:147
  4.0 7.5 %collective-permute-start = (bf16[16,2048]{1,0:T(8,128)(2,1)}, bf16[16,2048]{1,0:T(8,128)(2,1)S(1)}, u32[]{:S(2)}, u32[]{:S(2)}) collective-permute-start(bf16[16,2048]{1,0:T(8,128)(2,1)} %param.4), channel_id=1, source_target_pairs={{0,2},{2,4},{4,6},{6,0},{1,3},{3,5},{5,7},{7,1},{8,10},{10,12},{12... | collective-permute-start | bytes 196616 | tf_op jit(solution)/shard_map/ppermute | solution.py:147
  5.6 6.0 %collective-permute-start.2 = (bf16[16,2048]{1,0:T(8,128)(2,1)}, bf16[16,2048]{1,0:T(8,128)(2,1)S(1)}, u32[]{:S(2)}, u32[]{:S(2)}) collective-permute-start(bf16[16,2048]{1,0:T(8,128)(2,1)} %param.4), channel_id=1, source_target_pairs={{0,6},{2,0},{4,2},{6,4},{1,7},{3,1},{5,3},{7,5},{8,14},{10,8},{12,... | collective-permute-start | bytes 196616 | tf_op jit(solution)/shard_map/ppermute | solution.py:147
  11.6 8.8 %copy-start = (bf16[2048,6656]{1,0:T(8,128)(2,1)S(1)}, bf16[2048,6656]{1,0:T(8,128)(2,1)}, u32[]{:S(2)}) copy-start(bf16[2048,6656]{1,0:T(8,128)(2,1)} %refs_1_.1) | copy-start | bytes 81788928
  20.4 12.2 %copy-start.1 = (bf16[64,2048]{1,0:T(8,128)(2,1)}, bf16[64,2048]{1,0:T(8,128)(2,1)S(1)}, u32[]{:S(2)}) copy-start(bf16[64,2048]{1,0:T(8,128)(2,1)S(1)} %constant_dynamic-update-slice_fusion.refs_0_) | copy-start | bytes 786436
  26.8 4.1 %collective-permute-start.6 = (f32[32,6656]{1,0:T(8,128)S(1)}, f32[32,6656]{1,0:T(8,128)S(1)}, u32[]{:S(2)}, u32[]{:S(2)}) collective-permute-start(f32[32,6656]{1,0:T(8,128)S(1)} %get-tuple-element.38), channel_id=1, source_target_pairs={{0,1},{1,0},{2,3},{3,2},{4,5},{5,4},{6,7},{7,6},{8,9},{9,8},{10,11... | collective-permute-start | bytes 2555912 | tf_op jit(solution)/shard_map/ppermute | solution.py:147
  30.3 4.3 %collective-permute-start.3 = (f32[32,3072]{1,0:T(8,128)S(1)}, f32[32,3072]{1,0:T(8,128)S(1)}, u32[]{:S(2)}, u32[]{:S(2)}) collective-permute-start(f32[32,3072]{1,0:T(8,128)S(1)} %get-tuple-element.31), channel_id=1, source_target_pairs={{0,1},{1,0},{2,3},{3,2},{4,5},{5,4},{6,7},{7,6},{8,9},{9,8},{10,11... | collective-permute-start | bytes 1179656 | tf_op jit(solution)/shard_map/ppermute | solution.py:147
  31.0 18.7 %collective-permute-start.7 = (bf16[32,6656]{1,0:T(8,128)(2,1)S(1)}, bf16[32,6656]{1,0:T(8,128)(2,1)S(1)}, u32[]{:S(2)}, u32[]{:S(2)}) collective-permute-start(bf16[32,6656]{1,0:T(8,128)(2,1)S(1)} %get-tuple-element.40.refs_2_), channel_id=1, source_target_pairs={{0,8},{8,0},{1,9},{9,1},{2,10},{10,2},{3,11},{11,3},{4,12},{12,4},... | collective-permute-start | bytes 1277960 | tf_op jit(solution)/shard_map/ppermute | solution.py:147
  34.6 8.6 %collective-permute-start.11 = (f32[32,2048]{1,0:T(8,128)S(1)}, f32[32,2048]{1,0:T(8,128)S(1)}, u32[]{:S(2)}, u32[]{:S(2)}) collective-permute-start(f32[32,2048]{1,0:T(8,128)S(1)} %get-tuple-element.46), channel_id=1, source_target_pairs={{0,1},{1,0},{2,3},{3,2},{4,5},{5,4},{6,7},{7,6},{8,9},{9,8},{10,11... | collective-permute-start | bytes 786440 | tf_op jit(solution)/shard_map/ppermute | solution.py:147
  34.7 1.0 %copy-start.2 = (bf16[64,2048]{1,0:T(8,128)(2,1)S(1)}, bf16[64,2048]{1,0:T(8,128)(2,1)}, u32[]{:S(2)}) copy-start(bf16[64,2048]{1,0:T(8,128)(2,1)} %copy-done.1) | copy-start | bytes 786436
  42.7 2.7 %collective-permute-start.4 = (f32[32,1536]{1,0:T(8,128)S(1)}, f32[32,1536]{1,0:T(8,128)S(1)}, u32[]{:S(2)}, u32[]{:S(2)}) collective-permute-start(f32[32,1536]{1,0:T(8,128)S(1)} %get-tuple-element.34), channel_id=1, source_target_pairs={{0,1},{1,0},{2,3},{3,2},{4,5},{5,4},{6,7},{7,6},{8,9},{9,8},{10,11... | collective-permute-start | bytes 589832 | tf_op jit(solution)/shard_map/ppermute | solution.py:147
  43.3 6.4 %collective-permute-start.12 = (bf16[32,2048]{1,0:T(8,128)(2,1)S(1)}, bf16[32,2048]{1,0:T(8,128)(2,1)S(1)}, u32[]{:S(2)}, u32[]{:S(2)}) collective-permute-start(bf16[32,2048]{1,0:T(8,128)(2,1)S(1)} %get-tuple-element.48), channel_id=1, source_target_pairs={{0,8},{8,0},{1,9},{9,1},{2,10},{10,2},{3,11},{11,3},{4,12},{12,4},... | collective-permute-start | bytes 393224 | tf_op jit(solution)/shard_map/ppermute | solution.py:147
  43.9 10.0 %collective-permute-start.9 = (bf16[32,3072]{1,0:T(8,128)(2,1)S(1)}, bf16[32,3072]{1,0:T(8,128)(2,1)S(1)}, u32[]{:S(2)}, u32[]{:S(2)}) collective-permute-start(bf16[32,3072]{1,0:T(8,128)(2,1)S(1)} %get-tuple-element.32.refs_2_), channel_id=1, source_target_pairs={{0,8},{8,0},{1,9},{9,1},{2,10},{10,2},{3,11},{11,3},{4,12},{12,4},... | collective-permute-start | bytes 589832 | tf_op jit(solution)/shard_map/ppermute | solution.py:147
  45.4 9.7 %collective-permute-start.5 = (bf16[32,1536]{1,0:T(8,128)(2,1)S(1)}, bf16[32,1536]{1,0:T(8,128)(2,1)S(1)}, u32[]{:S(2)}, u32[]{:S(2)}) collective-permute-start(bf16[32,1536]{1,0:T(8,128)(2,1)S(1)} %get-tuple-element.36), channel_id=1, source_target_pairs={{0,8},{8,0},{1,9},{9,1},{2,10},{10,2},{3,11},{11,3},{4,12},{12,4},... | collective-permute-start | bytes 294920 | tf_op jit(solution)/shard_map/ppermute | solution.py:147
  49.8 8.6 %collective-permute-start.13 = (bf16[32,2048]{1,0:T(8,128)(2,1)S(1)}, bf16[32,2048]{1,0:T(8,128)(2,1)S(1)}, u32[]{:S(2)}, u32[]{:S(2)}) collective-permute-start(bf16[32,2048]{1,0:T(8,128)(2,1)S(1)} %multiply_convert_fusion.1.refs_0_), channel_id=1, source_target_pairs={{0,1},{1,0},{2,3},{3,2},{4,5},{5,4},{6,7},{7,6},{8,9},{9,8},{10,11... | collective-permute-start | bytes 393224 | tf_op jit(solution)/shard_map/ppermute | solution.py:147
  54.1 1.5 %collective-permute-start.10 = (bf16[32,3072]{1,0:T(8,128)(2,1)S(1)}, bf16[32,3072]{1,0:T(8,128)(2,1)S(1)}, u32[]{:S(2)}, u32[]{:S(2)}) collective-permute-start(bf16[32,3072]{1,0:T(8,128)(2,1)S(1)} %multiply_convert_fusion.refs_0_), channel_id=1, source_target_pairs={{0,1},{1,0},{2,3},{3,2},{4,5},{5,4},{6,7},{7,6},{8,9},{9,8},{10,11... | collective-permute-start | bytes 589832 | tf_op jit(solution)/shard_map/ppermute | solution.py:147
  55.2 5.2 %collective-permute-start.8 = (bf16[32,1536]{1,0:T(8,128)(2,1)S(1)}, bf16[32,1536]{1,0:T(8,128)(2,1)S(1)}, u32[]{:S(2)}, u32[]{:S(2)}) collective-permute-start(bf16[32,1536]{1,0:T(8,128)(2,1)S(1)} %multiply_convert_fusion.2.refs_0_), channel_id=1, source_target_pairs={{0,1},{1,0},{2,3},{3,2},{4,5},{5,4},{6,7},{7,6},{8,9},{9,8},{10,11... | collective-permute-start | bytes 294920 | tf_op jit(solution)/shard_map/ppermute | solution.py:147

commit v3 on v2

v3 whole, which is shorter than its diff:
```python
import functools

import jax
import jax.numpy as jnp
from jax import lax
from jax.experimental import pallas as pl
from jax.experimental.pallas import tpu as pltpu
from jax.sharding import PartitionSpec as P

BF16, F32 = jnp.bfloat16, jnp.float32
TILE = 512
GATE = (8, 5)
DOWN = (4, 4, 3, 2)
PAIR_TYPE = F32
COST = 1


def on_chip():
    return pl.BlockSpec(memory_space=pltpu.VMEM)


def in_place():
    return pl.BlockSpec(memory_space=pl.ANY)


def cuts(columns, shares):
    if columns % (TILE * sum(shares)):
        return [(0, columns)]
    unit = columns // sum(shares)
    chunks, start = [], 0
    for share in shares:
        chunks.append((start, share * unit))
        start += share * unit
    return chunks


def tile_of(width):
    return TILE if width % TILE == 0 else width


def copies(fetch, sources, targets, sems):
    made = []
    for at, ((axis, start, size), source, target) in enumerate(zip(fetch, sources, targets)):
        view = source.at[:, pl.ds(start, size)] if axis else source.at[pl.ds(start, size), :]
        made.append(pltpu.make_async_copy(view, target, sems.at[at]))
    return made


def call(order, body, operands, outs, fetch, scratch, flops, traffic, after=()):
    fetched = []
    for array, axis, start, size in fetch:
        shape = (array.shape[0], size) if axis else (size, array.shape[1])
        fetched.append(pltpu.VMEM(shape, array.dtype))
    n_in = len(operands)
    after = [*after, *order[-1:]]

    def kernel(*refs):
        ins, rest = refs[:n_in], refs[n_in + len(after) :]
        sources, rest = rest[: len(fetch)], rest[len(fetch) :]
        results, rest = rest[: len(outs)], rest[len(outs) :]
        targets, (*room, sems) = rest[: len(fetch)], rest[len(fetch) :]
        made = copies([f[1:] for f in fetch], sources, targets, sems)
        for copy in made:
            copy.start()
        body(ins, results, room)
        for copy in made:
            copy.wait()

    out = pl.pallas_call(
        kernel,
        out_shape=tuple(outs) + tuple(fetched),
        in_specs=[on_chip()] * n_in + [in_place()] * (len(after) + len(fetch)),
        out_specs=tuple([on_chip()] * (len(outs) + len(fetch))),
        scratch_shapes=list(scratch) + [pltpu.SemaphoreType.DMA((max(len(fetch), 1),))],
        compiler_params=pltpu.CompilerParams(vmem_limit_bytes=4 * 2**20),
        cost_estimate=pl.CostEstimate(flops=int(flops), bytes_accessed=int(traffic), transcendentals=0),
    )(*operands, *after, *[pltpu.with_memory_space_constraint(f[0], pltpu.HBM) for f in fetch])
    order.append(min(out, key=lambda array: array.size))
    return out[: len(outs)], out[len(outs) :]


def load_kernel(ins, outs, room):
    outs[0][...] = ins[0][...]


def pair_part_kernel(n_pair, chunks, ins, outs, room):
    *blocks, weight = ins
    n = len(chunks)
    keep, sends = outs[0], outs[1 : 1 + n * (n_pair - 1)]
    x = blocks[0]
    if len(outs) > 1 + len(sends):
        x = outs[-1]
        share = blocks[0].shape[0]
        for k, block in enumerate(blocks):
            x[k * share : (k + 1) * share, :] = block[...]
    (res,) = room
    me = lax.axis_index("pair")
    rows = keep.shape[0]
    for j, (start, width) in enumerate(chunks):
        tile = tile_of(width)

        @pl.loop(0, width // tile)
        def _(step, j=j, start=start, tile=tile):
            def at(offset):
                return pl.ds(pl.multiple_of(offset + step * tile, tile), tile)

            res[...] = jnp.dot(x[...], weight[:, at(start)], preferred_element_type=F32)
            for k in range(n_pair):
                block = pl.ds(pl.multiple_of(lax.rem(me + k, n_pair) * rows, 16), rows)
                target, offset = (sends[(k - 1) * n + j], 0) if k else (keep, start)
                target[:, at(offset)] = res[block, :].astype(target.dtype)


def pair_sum_kernel(chunks, ins, outs, room):
    keep, got = ins[0], ins[1:]
    n, half = len(chunks), len(outs) // 2
    for j, (start, width) in enumerate(chunks):
        at = slice(start, start + width)
        total = keep[:, at]
        for part in got[j::n]:
            total += part[...].astype(F32)
        for own in (0, half):
            out = outs[own + j] if half == n else outs[own]
            out[:, slice(0, width) if half == n else at] = total.astype(out.dtype)


def activate_kernel(start, ins, outs, room):
    at = slice(start, start + outs[0].shape[1])
    half = len(ins) // 2
    up = sum(part[:, at].astype(F32) for part in ins[:half])
    gate = sum(part[...].astype(F32) for part in ins[half:])
    outs[0][...] = (gate / (1.0 + jnp.exp(-gate)) * up).astype(BF16)


def down_kernel(n_wide, first, last, ins, outs, room):
    parts, (wd, *before) = (ins[:-1], ins[-1:]) if first else (ins[:-2], ins[-2:])
    (hidden,) = room
    n_pair = len(parts)
    c = lax.axis_index("pair")
    rows = parts[0].shape[0]
    for k in range(n_pair):
        block = lax.rem(c + n_pair - k, n_pair)
        hidden[pl.ds(pl.multiple_of(block * rows, 16), rows), :] = parts[k][...]
    width = wd.shape[1]
    tile = tile_of(width)

    @pl.loop(0, width // tile)
    def _(step):
        at = pl.ds(pl.multiple_of(step * tile, tile), tile)
        total = jnp.dot(hidden[...], wd[:, at], preferred_element_type=F32)
        if before:
            total += before[0][:, at]
        if last:
            share = total.shape[0] // n_wide
            for k in range(n_wide):
                place = (n_wide - k) % n_wide * share
                outs[k][:, at] = total[place : place + share].astype(outs[k].dtype)
        else:
            outs[0][:, at] = total


def shards(sizes, tokens, gate_weight, up_weight, down_weight):
    n_seq, n_wide, n_pair = sizes["seq"], sizes["wide"], sizes["pair"]

    def send(value, axis, k):
        n = sizes[axis]
        return lax.ppermute(value, axis, [(i, (i + k) % n) for i in range(n)])

    share, depth = tokens.shape
    rows = share * n_wide
    features = down_weight.shape[1]
    half = rows // n_pair
    loads = cuts(gate_weight.shape[1], GATE)
    chunks = cuts(down_weight.shape[0], DOWN)
    n = len(chunks)
    size = tokens.dtype.itemsize

    def gate_of(*picks):
        return [(gate_weight, 1, *loads[j]) for j in picks if j < len(loads)]

    def bytes_of(fetch):
        return sum(size * f[3] * f[0].shape[1 - f[1]] for f in fetch)

    def down_of(*picks):
        return [(down_weight, 0, *chunks[j]) for j in picks if j < n]

    order = []

    def project(blocks, weight, chunks, fetch, after=()):
        width, n = weight.shape[1], len(chunks)
        outs, fetched = call(
            order,
            functools.partial(pair_part_kernel, n_pair, chunks),
            [*blocks, weight],
            [pltpu.VMEM((half, width), F32)]
            + [pltpu.VMEM((half, wide), PAIR_TYPE) for _, wide in chunks] * (n_pair - 1)
            + [pltpu.VMEM((rows, depth), BF16)] * (len(blocks) > 1),
            fetch,
            [pltpu.VMEM((rows, tile_of(width)), F32)],
            COST * 2 * rows * depth * width,
            COST * 2 * bytes_of(fetch),
            after,
        )
        got = [send(outs[1 + (k - 1) * n + j], "pair", k) for k in range(1, n_pair) for j in range(n)]
        return (outs[0], *got), outs[-1], fetched

    def pair_sum(parts, chunks, pieces, after=()):
        outs = call(
            order, functools.partial(pair_sum_kernel, chunks), parts,
            [pltpu.VMEM((half, width), kind) for kind in (F32, BF16) for _, width in pieces],
            [], [], 0, COST * 8 * parts[0].size, after,
        )[0]
        sums = []
        for own, away in zip(outs[: len(pieces)], outs[len(pieces) :]):
            sums.append([own] + [send(away, "seq", k) for k in range(1, n_seq)])
        return sums

    def activate(ups, gates, start, width):
        (hidden,), _ = call(
            order, functools.partial(activate_kernel, start), [*ups, *gates],
            [pltpu.VMEM((half, width), BF16)], [], [], 0, COST * 8 * half * width,
        )
        got = [send(hidden, "pair", k) for k in range(1, n_pair)]
        return [hidden, *got]

    def load(array, fetch, traffic, after=()):
        (array,), fetched = call(
            order, load_kernel, [array], [pltpu.VMEM(array.shape, BF16)], fetch, [], 0, traffic, after
        )
        return array, fetched

    def multiply_down(j, parts, total):
        first, last = j == 0, j == n - 1
        width = parts[0].shape[1]
        if last:
            outs = [pltpu.VMEM((share, features), F32)]
            outs += [pltpu.VMEM((share, features), BF16)] * (n_wide - 1)
        else:
            outs = [pltpu.VMEM((rows, features), F32)]
        fetch = down_of(2) if first and n > 3 else []
        total, fetched = call(
            order,
            functools.partial(down_kernel, n_wide, first, last),
            [*parts, down[j], *total],
            outs,
            fetch,
            [pltpu.VMEM((rows, width), BF16)],
            COST * 2 * rows * width * features,
            COST * 2 * bytes_of(fetch),
        )
        if fetch:
            down[2] = fetched[0]
        return total

    tokens, early = load(tokens, [(down_weight, 0, 0, 16)], 2 * up_weight.size * size)
    blocks = [tokens] + [send(tokens, "wide", k) for k in range(1, n_wide)]
    up = pltpu.with_memory_space_constraint(up_weight, pltpu.VMEM)
    ups, x, (gate,) = project(blocks, up, chunks, gate_of(0), early)
    down = {}
    if n > 1:
        x, (down[n - 1],) = load(x, down_of(n - 1), COST * 2 * bytes_of(down_of(n - 1)))
    columns = gate_weight.shape[1]
    (ups,) = pair_sum(ups, chunks, [(0, columns)])
    gates = []
    for j, (start, width) in enumerate(loads):
        inner = [(a - start, b) for a, b in chunks if start <= a < start + width]
        last = j == len(loads) - 1
        parts, _, (weight,) = project([x], gate, inner, down_of(0) if last else gate_of(j + 1))
        if last:
            down[0] = weight
        else:
            gate = weight
        gates.append((parts, inner))
    sums = pair_sum(*gates[0], gates[0][1])
    if n > 2:
        _, (down[1],) = load(x, down_of(1), COST * 2 * bytes_of(down_of(1)))
    load(x, [], 0, ups[1:])
    for parts, inner in gates[1:]:
        sums += pair_sum(parts, inner, inner)
    hiddens = [activate(ups, sums[j], *chunks[j]) for j in range(min(n, 2))]
    total = []
    for j in range(n):
        if j and j + 1 < n:
            hiddens.append(activate(ups, sums[j + 1], *chunks[j + 1]))
        total = multiply_down(j, hiddens[j], total)

    result = total[0]
    for k in range(1, n_wide):
        result = result + send(total[k], "wide", k).astype(F32)
    return result.astype(BF16)


def solution(mesh):
    return jax.shard_map(
        functools.partial(shards, dict(mesh.shape)),
        mesh=mesh,
        in_specs=(
            P(("parts", "wide"), ("seq", "pair")),
            P(("seq", "pair"), "wide"),
            P(("seq", "pair"), "wide"),
            P("wide", ("seq", "pair")),
        ),
        out_specs=P(("parts", "wide"), ("seq", "pair")),
        check_vma=False,
    )
```

time: 75.9 us -> 64.9 us (0.86)
  blocking collectives: 12.8 us -> 0 us
  local copies, waits for them, and re-layouts: 10.6 us -> 0.84 us
  waiting for transfers between devices: 9 us -> 15.8 us
  starting transfers between devices: 13.6 us -> 18.2 us
    all_to_all x1 -> x0, blocking collectives: 12.8 us -> none  [shards(): others = lax.all_to_all(others, 'wide', 0, 0, tiled=True)]
    unnamed x9 -> x4, local copies, waits for them, and re-layouts: 10.6 us -> 0.84 us
    ppermute x14 -> x23, waiting for transfers between devices: 9 us -> 15.8 us  [send(): return lax.ppermute(value, axis, [(i, (i + k) % n) for i in range(n)])]
    ppermute x14 -> x23, starting transfers between devices: 13.6 us -> 18.2 us  [send(): return lax.ppermute(value, axis, [(i, (i + k) % n) for i in range(n)])]
    pallas_call x12 -> x18, Pallas kernels: 28.3 us -> 28.7 us  [call(): pl.pallas_call(kernel, out_shape=tuple(outs) + tuple(fetched), in_specs=[...]
  transfers between devices with their start and end apart: 14 -> 23, of which waited for: 4 -> 8; matrix products, arithmetic and copies ran while one was open for 2% -> 0% of each run, Pallas kernels for 27% -> 31%
where the time goes in v3:
time: 64.9 us; the launch traced here: 64.5 us
  Pallas kernels  28.7 us (44%)
  starting transfers between devices  18.2 us (28%)
  waiting for transfers between devices  15.8 us (24%)
  local copies, waits for them, and re-layouts  0.84 us (1%)
  other arithmetic  0.66 us (1%)
    pallas_call x18, Pallas kernels, call(): pl.pallas_call(kernel, out_shape=tuple(outs) + tuple(fetched), in_specs=[...  28.7 us
    ppermute x23, starting transfers between devices, send(): return lax.ppermute(value, axis, [(i, (i + k) % n) for i in range(n)])  18.2 us
    ppermute x23, waiting for transfers between devices, send(): return lax.ppermute(value, axis, [(i, (i + k) % n) for i in range(n)])  15.8 us
  transfers between devices with their start and end apart: 23, of which 8 were waited for; matrix products, arithmetic and copies ran while one was open for 0% of the time, Pallas kernels for 31%

profile of v3, /device:TPU:0, one launch (start us, length us, event | category | flops | bytes accessed | tf_op | source)
XLA Modules:
  0.0 64.5 jit_solution(12003028182459815509)
XLA Ops:
  0.0 0.8 %copy-done.1 = bf16[16,2048]{1,0:T(8,128)(2,1)S(1)} copy-done((bf16[16,2048]{1,0:T(8,128)(2,1)S(1)}, bf16[16,2048]{1,0:T(8,128)(2,1)}, u32[]{:S(2)}) %copy-start.1) | copy-done | bytes 65560
  0.8 1.0 %shard_map.46 = (bf16[16,2048]{1,0:T(8,128)(2,1)S(1)}, bf16[16,2048]{1,0:T(8,128)(2,1)S(1)}) custom-call(bf16[16,2048]{1,0:T(8,128)(2,1)S(1)} %copy-done.1, bf16[6656,2048]{1,0:T(8,128)(2,1)} %refs_4_.3), custom_call_target="tpu_custom_call" | custom-call | bytes 54525952 | tf_op jit(solution)/shard_map/pallas_call | solution.py:69
  1.8 5.1 %collective-permute-start.2 = (bf16[16,2048]{1,0:T(8,128)(2,1)S(1)}, bf16[16,2048]{1,0:T(8,128)(2,1)S(1)}, u32[]{:S(2)}, u32[]{:S(2)}) collective-permute-start(bf16[16,2048]{1,0:T(8,128)(2,1)S(1)} %get-tuple-element.42.refs_0_.refs_6_), channel_id=1, source_target_pairs={{0,6},{2,0},{4,2},{6,4},{1,7},{3,1},{5,3},{7,5},{8,14},{10,8},{12,... | collective-permute-start | bytes 196616 | tf_op jit(solution)/shard_map/ppermute | solution.py:167
  7.0 1.0 %collective-permute-start = (bf16[16,2048]{1,0:T(8,128)(2,1)S(1)}, bf16[16,2048]{1,0:T(8,128)(2,1)S(1)}, u32[]{:S(2)}, u32[]{:S(2)}) collective-permute-start(bf16[16,2048]{1,0:T(8,128)(2,1)S(1)} %get-tuple-element.42.refs_0_.refs_6_), channel_id=1, source_target_pairs={{0,2},{2,4},{4,6},{6,0},{1,3},{3,5},{5,7},{7,1},{8,10},{10,12},{12... | collective-permute-start | bytes 196616 | tf_op jit(solution)/shard_map/ppermute | solution.py:167
  8.0 1.5 %collective-permute-done.2.refs_3_ = bf16[16,2048]{1,0:T(8,128)(2,1)S(1)} collective-permute-done((bf16[16,2048]{1,0:T(8,128)(2,1)S(1)}, bf16[16,2048]{1,0:T(8,128)(2,1)S(1)}, u32[]{:S(2)}, u32[]{:S(2)}) %collective-permute-start.2) | collective-permute-done | bytes 65568 | tf_op jit(solution)/shard_map/ppermute | solution.py:167
  9.4 4.0 %collective-permute-done.1.refs_2_ = bf16[16,2048]{1,0:T(8,128)(2,1)S(1)} collective-permute-done((bf16[16,2048]{1,0:T(8,128)(2,1)S(1)}, bf16[16,2048]{1,0:T(8,128)(2,1)S(1)}, u32[]{:S(2)}, u32[]{:S(2)}) %collective-permute-start.1) | collective-permute-done | bytes 65568 | tf_op jit(solution)/shard_map/ppermute | solution.py:167
  13.4 6.4 %shard_map.47 = (f32[32,6656]{1,0:T(8,128)S(1)}, f32[32,2048]{1,0:T(8,128)S(1)}, f32[32,2048]{1,0:T(8,128)S(1)}, f32[32,1536]{1,0:T(8,128)S(1)}, f32[32,1024]{1,...) custom-call(bf16[16,2048]{1,0:T(8,128)(2,1)S(1)} %get-tuple-element.42.refs_0_.refs_6_, ...), custom_call_target="tpu_custom_call" | custom-call | flops 1744830464 | bytes 33554432 | tf_op jit(solution)/shard_map/pallas_call | solution.py:69
  20.9 2.2 %shard_map.48 = (bf16[64,2048]{1,0:T(8,128)(2,1)S(1)}, bf16[1024,2048]{1,0:T(8,128)(2,1)S(1)}) custom-call(bf16[64,2048]{1,0:T(8,128)(2,1)S(1)} %get-tuple-element.49.refs_0_, f32[32,1024]{1,0:T(8,128)S(1)} %get-tuple-element.48.refs_1_, bf16[6656,2048]{1,0:T(8,128)(2,1)} %refs_4_.3), custom_call_target="tpu_custom_call" | custom-call | bytes 8388608 | tf_op jit(solution)/shard_map/pallas_call | solution.py:69
  23.3 1.6 %collective-permute-start.7 = (bf16[32,6656]{1,0:T(8,128)(2,1)S(1)}, bf16[32,6656]{1,0:T(8,128)(2,1)S(1)}, u32[]{:S(2)}, u32[]{:S(2)}) collective-permute-start(bf16[32,6656]{1,0:T(8,128)(2,1)S(1)} %get-tuple-element.52), channel_id=1, source_target_pairs={{0,8},{8,0},{1,9},{9,1},{2,10},{10,2},{3,11},{11,3},{4,12},{12,4},... | collective-permute-start | bytes 1277960 | tf_op jit(solution)/shard_map/ppermute | solution.py:167
  24.9 4.1 %shard_map.50 = (f32[32,4096]{1,0:T(8,128)S(1)}, f32[32,2048]{1,0:T(8,128)S(1)}, f32[32,2048]{1,0:T(8,128)S(1)}, bf16[2048,2560]{1,0:T(8,128)(2,1)S(1)}) custom-call(bf16[64,2048]{1,0:T(8,128)(2,1)S(1)} %get-tuple-element.50.refs_5_.refs_0_, bf16[2048,4096]{1,0:T(8,128)(2,1)S(1)} %get-tuple-element.53.refs_1_, ...), custom_call_target="tpu_custom_call" | custom-call | flops 1073741824 | bytes 20971520 | tf_op jit(solution)/shard_map/pallas_call | solution.py:69
  29.5 3.4 %shard_map.51 = (f32[32,2560]{1,0:T(8,128)S(1)}, f32[32,1536]{1,0:T(8,128)S(1)}, f32[32,1024]{1,0:T(8,128)S(1)}, bf16[2048,2048]{1,0:T(8,128)(2,1)S(1)}) custom-call(bf16[64,2048]{1,0:T(8,128)(2,1)S(1)} %get-tuple-element.50.refs_5_.refs_0_, bf16[2048,2560]{1,0:T(8,128)(2,1)S(1)} %get-tuple-element.54.refs_1_, f32[32,2048]{1,0:T(8,128)S(1)} %get-tuple-element.55.refs_2_, ...), custom_call_target="tpu_custom_call" | custom-call | flops 671088640 | bytes 16777216 | tf_op jit(solution)/shard_map/pallas_call | solution.py:69
  34.2 1.5 %collective-permute-start.13 = (bf16[32,2048]{1,0:T(8,128)(2,1)S(1)}, bf16[32,2048]{1,0:T(8,128)(2,1)S(1)}, u32[]{:S(2)}, u32[]{:S(2)}) collective-permute-start(bf16[32,2048]{1,0:T(8,128)(2,1)S(1)} %get-tuple-element.66), channel_id=1, source_target_pairs={{0,8},{8,0},{1,9},{9,1},{2,10},{10,2},{3,11},{11,3},{4,12},{12,4},... | collective-permute-start | bytes 393224 | tf_op jit(solution)/shard_map/ppermute | solution.py:167
  35.7 3.4 %shard_map.53 = (bf16[64,2048]{1,0:T(8,128)(2,1)S(1)}, bf16[2048,2048]{1,0:T(8,128)(2,1)S(1)}) custom-call(bf16[64,2048]{1,0:T(8,128)(2,1)S(1)} %get-tuple-element.50.refs_5_.refs_0_, f32[32,2048]{1,0:T(8,128)S(1)} %get-tuple-element.61.refs_1_.refs_2_, bf16[6656,2048]{1,0:T(8,128)(2,1)} %refs_4_.3), custom_call_target="tpu_custom_call" | custom-call | bytes 16777216 | tf_op jit(solution)/shard_map/pallas_call | solution.py:69
  40.2 1.7 %collective-permute-done.13.refs_3_ = bf16[32,2048]{1,0:T(8,128)(2,1)S(1)} collective-permute-done((bf16[32,2048]{1,0:T(8,128)(2,1)S(1)}, bf16[32,2048]{1,0:T(8,128)(2,1)S(1)}, u32[]{:S(2)}, u32[]{:S(2)}) %collective-permute-start.13) | collective-permute-done | bytes 131104 | tf_op jit(solution)/shard_map/ppermute | solution.py:167
  42.7 2.8 %shard_map.58 = (f32[64,2048]{1,0:T(8,128)S(1)}, bf16[1536,2048]{1,0:T(8,128)(2,1)S(1)}) custom-call(bf16[32,2048]{1,0:T(8,128)(2,1)S(1)} %shard_map.56.refs_4_.refs_0_, bf16[32,2048]{1,0:T(8,128)(2,1)S(1)} %collective-permute-done.16.refs_1_, bf16[2048,2048]{1,0:T(8,128)(2,1)S(1)} %get-tuple-element.69.refs_2_, ...), custom_call_target="tpu_custom_call" | custom-call | flops 536870912 | bytes 12582912 | tf_op jit(solution)/shard_map/pallas_call | solution.py:69
  45.5 1.8 %collective-permute-done.17.refs_3_ = bf16[32,1536]{1,0:T(8,128)(2,1)S(1)} collective-permute-done((bf16[32,1536]{1,0:T(8,128)(2,1)S(1)}, bf16[32,1536]{1,0:T(8,128)(2,1)S(1)}, u32[]{:S(2)}, u32[]{:S(2)}) %collective-permute-start.17) | collective-permute-done | bytes 98336 | tf_op jit(solution)/shard_map/ppermute | solution.py:167
  48.1 2.0 %shard_map.60.refs_4_.refs_3_ = f32[64,2048]{1,0:T(8,128)S(1)} custom-call(bf16[32,2048]{1,0:T(8,128)(2,1)S(1)} %shard_map.57.refs_3_.refs_0_, bf16[32,2048]{1,0:T(8,128)(2,1)S(1)} %collective-permute-done.15.refs_1_, bf16[2048,2048]{1,0:T(8,128)(2,1)S(1)} %get-tuple-element.68.refs_2_, f32[64,2048]{1,0:T(8,128)S(1)} %get-tuple-element.70.refs_4_.refs_3_, ...), custom_call_target="tpu_custom_call" | custom-call | flops 536870912 | tf_op jit(solution)/shard_map/pallas_call | solution.py:69
  50.1 1.9 %collective-permute-done.12.refs_3_ = bf16[32,1024]{1,0:T(8,128)(2,1)S(1)} collective-permute-done((bf16[32,1024]{1,0:T(8,128)(2,1)S(1)}, bf16[32,1024]{1,0:T(8,128)(2,1)S(1)}, u32[]{:S(2)}, u32[]{:S(2)}) %collective-permute-start.12) | collective-permute-done | bytes 65568 | tf_op jit(solution)/shard_map/ppermute | solution.py:167
  52.2 1.6 %shard_map.62.refs_3_.refs_4_ = f32[64,2048]{1,0:T(8,128)S(1)} custom-call(bf16[32,1536]{1,0:T(8,128)(2,1)S(1)} %shard_map.59.refs_4_.refs_0_, bf16[32,1536]{1,0:T(8,128)(2,1)S(1)} %collective-permute-done.19.refs_1_, bf16[1536,2048]{1,0:T(8,128)(2,1)S(1)} %get-tuple-element.74.refs_2_, f32[64,2048]{1,0:T(8,128)S(1)} %shard_map.60.refs_4_.refs_3_, ...), custom_call_target="tpu_custom_call" | custom-call | flops 402653184 | tf_op jit(solution)/shard_map/pallas_call | solution.py:69
  53.8 1.2 %shard_map.63 = (f32[16,2048]{1,0:T(8,128)S(1)}, bf16[16,2048]{1,0:T(8,128)(2,1)S(1)}, bf16[16,2048]{1,0:T(8,128)(2,1)S(1)}, bf16[16,2048]{1,0:T(8,128)(2,1)S(1)}) custom-call(bf16[32,1024]{1,0:T(8,128)(2,1)S(1)} %shard_map.61.refs_4_.refs_0_, bf16[32,1024]{1,0:T(8,128)(2,1)S(1)} %collective-permute-done.18.refs_1_, ...), custom_call_target="tpu_custom_call" | custom-call | flops 268435456 | tf_op jit(solution)/shard_map/pallas_call | solution.py:69
  55.3 2.3 %collective-permute-start.21 = (bf16[16,2048]{1,0:T(8,128)(2,1)S(1)}, bf16[16,2048]{1,0:T(8,128)(2,1)S(1)}, u32[]{:S(2)}, u32[]{:S(2)}) collective-permute-start(bf16[16,2048]{1,0:T(8,128)(2,1)S(1)} %get-tuple-element.77), channel_id=1, source_target_pairs={{0,4},{2,6},{4,0},{6,2},{1,5},{3,7},{5,1},{7,3},{8,12},{10,14},{12... | collective-permute-start | bytes 196616 | tf_op jit(solution)/shard_map/ppermute | solution.py:167
  57.6 2.2 %collective-permute-start.22 = (bf16[16,2048]{1,0:T(8,128)(2,1)S(1)}, bf16[16,2048]{1,0:T(8,128)(2,1)S(1)}, u32[]{:S(2)}, u32[]{:S(2)}) collective-permute-start(bf16[16,2048]{1,0:T(8,128)(2,1)S(1)} %get-tuple-element.78), channel_id=1, source_target_pairs={{0,6},{2,0},{4,2},{6,4},{1,7},{3,1},{5,3},{7,5},{8,14},{10,8},{12,... | collective-permute-start | bytes 196616 | tf_op jit(solution)/shard_map/ppermute | solution.py:167
  59.8 2.1 %collective-permute-done.20 = bf16[16,2048]{1,0:T(8,128)(2,1)S(1)} collective-permute-done((bf16[16,2048]{1,0:T(8,128)(2,1)S(1)}, bf16[16,2048]{1,0:T(8,128)(2,1)S(1)}, u32[]{:S(2)}, u32[]{:S(2)}) %collective-permute-start.20) | collective-permute-done | bytes 65568 | tf_op jit(solution)/shard_map/ppermute | solution.py:167
  61.9 2.0 %collective-permute-done.21 = bf16[16,2048]{1,0:T(8,128)(2,1)S(1)} collective-permute-done((bf16[16,2048]{1,0:T(8,128)(2,1)S(1)}, bf16[16,2048]{1,0:T(8,128)(2,1)S(1)}, u32[]{:S(2)}, u32[]{:S(2)}) %collective-permute-start.21) | collective-permute-done | bytes 65568 | tf_op jit(solution)/shard_map/ppermute | solution.py:167
  (45 shorter events, 6.7 us)
Async XLA Ops:
  0.8 12.6 %copy-start = (bf16[2048,6656]{1,0:T(8,128)(2,1)S(1)}, bf16[2048,6656]{1,0:T(8,128)(2,1)}, u32[]{:S(2)}) copy-start(bf16[2048,6656]{1,0:T(8,128)(2,1)} %refs_4_.2) | copy-start | bytes 81788928
  1.8 7.6 %collective-permute-start.2 = (bf16[16,2048]{1,0:T(8,128)(2,1)S(1)}, bf16[16,2048]{1,0:T(8,128)(2,1)S(1)}, u32[]{:S(2)}, u32[]{:S(2)}) collective-permute-start(bf16[16,2048]{1,0:T(8,128)(2,1)S(1)} %get-tuple-element.42.refs_0_.refs_6_), channel_id=1, source_target_pairs={{0,6},{2,0},{4,2},{6,4},{1,7},{3,1},{5,3},{7,5},{8,14},{10,8},{12,... | collective-permute-start | bytes 196616 | tf_op jit(solution)/shard_map/ppermute | solution.py:167
  7.0 6.5 %collective-permute-start.1 = (bf16[16,2048]{1,0:T(8,128)(2,1)S(1)}, bf16[16,2048]{1,0:T(8,128)(2,1)S(1)}, u32[]{:S(2)}, u32[]{:S(2)}) collective-permute-start(bf16[16,2048]{1,0:T(8,128)(2,1)S(1)} %get-tuple-element.42.refs_0_.refs_6_), channel_id=1, source_target_pairs={{0,4},{2,6},{4,0},{6,2},{1,5},{3,7},{5,1},{7,3},{8,12},{10,14},{12... | collective-permute-start | bytes 196616 | tf_op jit(solution)/shard_map/ppermute | solution.py:167
  7.0 6.5 %collective-permute-start = (bf16[16,2048]{1,0:T(8,128)(2,1)S(1)}, bf16[16,2048]{1,0:T(8,128)(2,1)S(1)}, u32[]{:S(2)}, u32[]{:S(2)}) collective-permute-start(bf16[16,2048]{1,0:T(8,128)(2,1)S(1)} %get-tuple-element.42.refs_0_.refs_6_), channel_id=1, source_target_pairs={{0,2},{2,4},{4,6},{6,0},{1,3},{3,5},{5,7},{7,1},{8,10},{10,12},{12... | collective-permute-start | bytes 196616 | tf_op jit(solution)/shard_map/ppermute | solution.py:167
  19.9 3.3 %collective-permute-start.3 = (f32[32,2048]{1,0:T(8,128)S(1)}, f32[32,2048]{1,0:T(8,128)S(1)}, u32[]{:S(2)}, u32[]{:S(2)}) collective-permute-start(f32[32,2048]{1,0:T(8,128)S(1)} %get-tuple-element.45), channel_id=1, source_target_pairs={{0,1},{1,0},{2,3},{3,2},{4,5},{5,4},{6,7},{7,6},{8,9},{9,8},{10,11... | collective-permute-start | bytes 786440 | tf_op jit(solution)/shard_map/ppermute | solution.py:167
  19.9 3.2 %collective-permute-start.4 = (f32[32,2048]{1,0:T(8,128)S(1)}, f32[32,2048]{1,0:T(8,128)S(1)}, u32[]{:S(2)}, u32[]{:S(2)}) collective-permute-start(f32[32,2048]{1,0:T(8,128)S(1)} %get-tuple-element.46), channel_id=1, source_target_pairs={{0,1},{1,0},{2,3},{3,2},{4,5},{5,4},{6,7},{7,6},{8,9},{9,8},{10,11... | collective-permute-start | bytes 786440 | tf_op jit(solution)/shard_map/ppermute | solution.py:167
  20.4 2.7 %collective-permute-start.5 = (f32[32,1536]{1,0:T(8,128)S(1)}, f32[32,1536]{1,0:T(8,128)S(1)}, u32[]{:S(2)}, u32[]{:S(2)}) collective-permute-start(f32[32,1536]{1,0:T(8,128)S(1)} %get-tuple-element.47), channel_id=1, source_target_pairs={{0,1},{1,0},{2,3},{3,2},{4,5},{5,4},{6,7},{7,6},{8,9},{9,8},{10,11... | collective-permute-start | bytes 589832 | tf_op jit(solution)/shard_map/ppermute | solution.py:167
  20.5 2.6 %collective-permute-start.6 = (f32[32,1024]{1,0:T(8,128)S(1)}, f32[32,1024]{1,0:T(8,128)S(1)}, u32[]{:S(2)}, u32[]{:S(2)}) collective-permute-start(f32[32,1024]{1,0:T(8,128)S(1)} %get-tuple-element.48.refs_1_), channel_id=1, source_target_pairs={{0,1},{1,0},{2,3},{3,2},{4,5},{5,4},{6,7},{7,6},{8,9},{9,8},{10,11... | collective-permute-start | bytes 393224 | tf_op jit(solution)/shard_map/ppermute | solution.py:167
  23.3 15.7 %collective-permute-start.7 = (bf16[32,6656]{1,0:T(8,128)(2,1)S(1)}, bf16[32,6656]{1,0:T(8,128)(2,1)S(1)}, u32[]{:S(2)}, u32[]{:S(2)}) collective-permute-start(bf16[32,6656]{1,0:T(8,128)(2,1)S(1)} %get-tuple-element.52), channel_id=1, source_target_pairs={{0,8},{8,0},{1,9},{9,1},{2,10},{10,2},{3,11},{11,3},{4,12},{12,4},... | collective-permute-start | bytes 1277960 | tf_op jit(solution)/shard_map/ppermute | solution.py:167
  28.9 4.6 %collective-permute-start.11 = (f32[32,2048]{1,0:T(8,128)S(1)}, f32[32,2048]{1,0:T(8,128)S(1)}, u32[]{:S(2)}, u32[]{:S(2)}) collective-permute-start(f32[32,2048]{1,0:T(8,128)S(1)} %get-tuple-element.60), channel_id=1, source_target_pairs={{0,1},{1,0},{2,3},{3,2},{4,5},{5,4},{6,7},{7,6},{8,9},{9,8},{10,11... | collective-permute-start | bytes 786440 | tf_op jit(solution)/shard_map/ppermute | solution.py:167
  29.0 4.5 %collective-permute-start.10 = (f32[32,2048]{1,0:T(8,128)S(1)}, f32[32,2048]{1,0:T(8,128)S(1)}, u32[]{:S(2)}, u32[]{:S(2)}) collective-permute-start(f32[32,2048]{1,0:T(8,128)S(1)} %get-tuple-element.55.refs_2_), channel_id=1, source_target_pairs={{0,1},{1,0},{2,3},{3,2},{4,5},{5,4},{6,7},{7,6},{8,9},{9,8},{10,11... | collective-permute-start | bytes 786440 | tf_op jit(solution)/shard_map/ppermute | solution.py:167
  32.9 6.2 %collective-permute-start.8 = (f32[32,1536]{1,0:T(8,128)S(1)}, f32[32,1536]{1,0:T(8,128)S(1)}, u32[]{:S(2)}, u32[]{:S(2)}) collective-permute-start(f32[32,1536]{1,0:T(8,128)S(1)} %get-tuple-element.57), channel_id=1, source_target_pairs={{0,1},{1,0},{2,3},{3,2},{4,5},{5,4},{6,7},{7,6},{8,9},{9,8},{10,11... | collective-permute-start | bytes 589832 | tf_op jit(solution)/shard_map/ppermute | solution.py:167
  33.0 6.1 %collective-permute-start.9 = (f32[32,1024]{1,0:T(8,128)S(1)}, f32[32,1024]{1,0:T(8,128)S(1)}, u32[]{:S(2)}, u32[]{:S(2)}) collective-permute-start(f32[32,1024]{1,0:T(8,128)S(1)} %get-tuple-element.58.refs_3_), channel_id=1, source_target_pairs={{0,1},{1,0},{2,3},{3,2},{4,5},{5,4},{6,7},{7,6},{8,9},{9,8},{10,11... | collective-permute-start | bytes 393224 | tf_op jit(solution)/shard_map/ppermute | solution.py:167
  33.6 6.4 %collective-permute-start.14 = (bf16[32,2048]{1,0:T(8,128)(2,1)S(1)}, bf16[32,2048]{1,0:T(8,128)(2,1)S(1)}, u32[]{:S(2)}, u32[]{:S(2)}) collective-permute-start(bf16[32,2048]{1,0:T(8,128)(2,1)S(1)} %get-tuple-element.67), channel_id=1, source_target_pairs={{0,8},{8,0},{1,9},{9,1},{2,10},{10,2},{3,11},{11,3},{4,12},{12,4},... | collective-permute-start | bytes 393224 | tf_op jit(solution)/shard_map/ppermute | solution.py:167
  34.2 7.8 %collective-permute-start.13 = (bf16[32,2048]{1,0:T(8,128)(2,1)S(1)}, bf16[32,2048]{1,0:T(8,128)(2,1)S(1)}, u32[]{:S(2)}, u32[]{:S(2)}) collective-permute-start(bf16[32,2048]{1,0:T(8,128)(2,1)S(1)} %get-tuple-element.66), channel_id=1, source_target_pairs={{0,8},{8,0},{1,9},{9,1},{2,10},{10,2},{3,11},{11,3},{4,12},{12,4},... | collective-permute-start | bytes 393224 | tf_op jit(solution)/shard_map/ppermute | solution.py:167
  40.1 2.6 %collective-permute-start.16 = (bf16[32,2048]{1,0:T(8,128)(2,1)S(1)}, bf16[32,2048]{1,0:T(8,128)(2,1)S(1)}, u32[]{:S(2)}, u32[]{:S(2)}) collective-permute-start(bf16[32,2048]{1,0:T(8,128)(2,1)S(1)} %shard_map.56.refs_4_.refs_0_), channel_id=1, source_target_pairs={{0,1},{1,0},{2,3},{3,2},{4,5},{5,4},{6,7},{7,6},{8,9},{9,8},{10,11... | collective-permute-start | bytes 393224 | tf_op jit(solution)/shard_map/ppermute | solution.py:167
  42.0 6.1 %collective-permute-start.15 = (bf16[32,2048]{1,0:T(8,128)(2,1)S(1)}, bf16[32,2048]{1,0:T(8,128)(2,1)S(1)}, u32[]{:S(2)}, u32[]{:S(2)}) collective-permute-start(bf16[32,2048]{1,0:T(8,128)(2,1)S(1)} %shard_map.57.refs_3_.refs_0_), channel_id=1, source_target_pairs={{0,1},{1,0},{2,3},{3,2},{4,5},{5,4},{6,7},{7,6},{8,9},{9,8},{10,11... | collective-permute-start | bytes 393224 | tf_op jit(solution)/shard_map/ppermute | solution.py:167
  42.1 5.2 %collective-permute-start.17 = (bf16[32,1536]{1,0:T(8,128)(2,1)S(1)}, bf16[32,1536]{1,0:T(8,128)(2,1)S(1)}, u32[]{:S(2)}, u32[]{:S(2)}) collective-permute-start(bf16[32,1536]{1,0:T(8,128)(2,1)S(1)} %get-tuple-element.72), channel_id=1, source_target_pairs={{0,8},{8,0},{1,9},{9,1},{2,10},{10,2},{3,11},{11,3},{4,12},{12,4},... | collective-permute-start | bytes 294920 | tf_op jit(solution)/shard_map/ppermute | solution.py:167
  47.4 4.7 %collective-permute-start.19 = (bf16[32,1536]{1,0:T(8,128)(2,1)S(1)}, bf16[32,1536]{1,0:T(8,128)(2,1)S(1)}, u32[]{:S(2)}, u32[]{:S(2)}) collective-permute-start(bf16[32,1536]{1,0:T(8,128)(2,1)S(1)} %shard_map.59.refs_4_.refs_0_), channel_id=1, source_target_pairs={{0,1},{1,0},{2,3},{3,2},{4,5},{5,4},{6,7},{7,6},{8,9},{9,8},{10,11... | collective-permute-start | bytes 294920 | tf_op jit(solution)/shard_map/ppermute | solution.py:167
  47.5 4.5 %collective-permute-start.12 = (bf16[32,1024]{1,0:T(8,128)(2,1)S(1)}, bf16[32,1024]{1,0:T(8,128)(2,1)S(1)}, u32[]{:S(2)}, u32[]{:S(2)}) collective-permute-start(bf16[32,1024]{1,0:T(8,128)(2,1)S(1)} %get-tuple-element.64), channel_id=1, source_target_pairs={{0,8},{8,0},{1,9},{9,1},{2,10},{10,2},{3,11},{11,3},{4,12},{12,4},... | collective-permute-start | bytes 196616 | tf_op jit(solution)/shard_map/ppermute | solution.py:167
  52.1 1.7 %collective-permute-start.18 = (bf16[32,1024]{1,0:T(8,128)(2,1)S(1)}, bf16[32,1024]{1,0:T(8,128)(2,1)S(1)}, u32[]{:S(2)}, u32[]{:S(2)}) collective-permute-start(bf16[32,1024]{1,0:T(8,128)(2,1)S(1)} %shard_map.61.refs_4_.refs_0_), channel_id=1, source_target_pairs={{0,1},{1,0},{2,3},{3,2},{4,5},{5,4},{6,7},{7,6},{8,9},{9,8},{10,11... | collective-permute-start | bytes 196616 | tf_op jit(solution)/shard_map/ppermute | solution.py:167
  55.1 6.8 %collective-permute-start.20 = (bf16[16,2048]{1,0:T(8,128)(2,1)S(1)}, bf16[16,2048]{1,0:T(8,128)(2,1)S(1)}, u32[]{:S(2)}, u32[]{:S(2)}) collective-permute-start(bf16[16,2048]{1,0:T(8,128)(2,1)S(1)} %get-tuple-element.76), channel_id=1, source_target_pairs={{0,2},{2,4},{4,6},{6,0},{1,3},{3,5},{5,7},{7,1},{8,10},{10,12},{12... | collective-permute-start | bytes 196616 | tf_op jit(solution)/shard_map/ppermute | solution.py:167
  55.3 8.6 %collective-permute-start.21 = (bf16[16,2048]{1,0:T(8,128)(2,1)S(1)}, bf16[16,2048]{1,0:T(8,128)(2,1)S(1)}, u32[]{:S(2)}, u32[]{:S(2)}) collective-permute-start(bf16[16,2048]{1,0:T(8,128)(2,1)S(1)} %get-tuple-element.77), channel_id=1, source_target_pairs={{0,4},{2,6},{4,0},{6,2},{1,5},{3,7},{5,1},{7,3},{8,12},{10,14},{12... | collective-permute-start | bytes 196616 | tf_op jit(solution)/shard_map/ppermute | solution.py:167
  57.6 6.3 %collective-permute-start.22 = (bf16[16,2048]{1,0:T(8,128)(2,1)S(1)}, bf16[16,2048]{1,0:T(8,128)(2,1)S(1)}, u32[]{:S(2)}, u32[]{:S(2)}) collective-permute-start(bf16[16,2048]{1,0:T(8,128)(2,1)S(1)} %get-tuple-element.78), channel_id=1, source_target_pairs={{0,6},{2,0},{4,2},{6,4},{1,7},{3,1},{5,3},{7,5},{8,14},{10,8},{12,... | collective-permute-start | bytes 196616 | tf_op jit(solution)/shard_map/ppermute | solution.py:167
  (1 other events, 0.8 us)

commit v4 on v3

--- a/solution.py
+++ b/solution.py
@@ -13,6 +13,7 @@
 DOWN = (4, 4, 3, 2)
 PAIR_TYPE = F32
 COST = 1
+SPLIT = 2
 
 
 def on_chip():
@@ -80,7 +81,8 @@
 
 
 def load_kernel(ins, outs, room):
-    outs[0][...] = ins[0][...]
+    for source, target in zip(ins, outs):
+        target[...] = source[...]
 
 
 def pair_part_kernel(n_pair, chunks, ins, outs, room):
@@ -129,18 +131,22 @@
     half = len(ins) // 2
     up = sum(part[:, at].astype(F32) for part in ins[:half])
     gate = sum(part[...].astype(F32) for part in ins[half:])
-    outs[0][...] = (gate / (1.0 + jnp.exp(-gate)) * up).astype(BF16)
-
-
-def down_kernel(n_wide, first, last, ins, outs, room):
+    hidden = (gate / (1.0 + jnp.exp(-gate)) * up).astype(BF16)
+    rows = outs[0].shape[0]
+    for k, out in enumerate(outs):
+        out[...] = hidden[k * rows : (k + 1) * rows]
+
+
+def down_kernel(n_pair, n_wide, first, last, ins, outs, room):
     parts, (wd, *before) = (ins[:-1], ins[-1:]) if first else (ins[:-2], ins[-2:])
     (hidden,) = room
-    n_pair = len(parts)
     c = lax.axis_index("pair")
     rows = parts[0].shape[0]
-    for k in range(n_pair):
-        block = lax.rem(c + n_pair - k, n_pair)
-        hidden[pl.ds(pl.multiple_of(block * rows, 16), rows), :] = parts[k][...]
+    pieces = len(parts) // n_pair
+    for at, part in enumerate(parts):
+        k, piece = divmod(at, pieces)
+        block = lax.rem(c + n_pair - k, n_pair) * pieces + piece
+        hidden[pl.ds(pl.multiple_of(block * rows, 16), rows), :] = part[...]
     width = wd.shape[1]
     tile = tile_of(width)
 
@@ -216,12 +222,12 @@
         return sums
 
     def activate(ups, gates, start, width):
-        (hidden,), _ = call(
+        hidden, _ = call(
             order, functools.partial(activate_kernel, start), [*ups, *gates],
-            [pltpu.VMEM((half, width), BF16)], [], [], 0, COST * 8 * half * width,
+            [pltpu.VMEM((half // SPLIT, width), BF16)] * SPLIT, [], [], 0, COST * 8 * half * width,
         )
-        got = [send(hidden, "pair", k) for k in range(1, n_pair)]
-        return [hidden, *got]
+        got = [send(piece, "pair", k) for k in range(1, n_pair) for piece in hidden]
+        return [*hidden, *got]
 
     def load(array, fetch, traffic, after=()):
         (array,), fetched = call(
@@ -240,7 +246,7 @@
         fetch = down_of(2) if first and n > 3 else []
         total, fetched = call(
             order,
-            functools.partial(down_kernel, n_wide, first, last),
+            functools.partial(down_kernel, n_pair, n_wide, first, last),
             [*parts, down[j], *total],
             outs,
             fetch,
@@ -252,15 +258,18 @@
             down[2] = fetched[0]
         return total
 
-    tokens, early = load(tokens, [(down_weight, 0, 0, 16)], 2 * up_weight.size * size)
+    _, (tokens, *early) = call(
+        order, load_kernel, [], [], [(tokens, 0, 0, share), (down_weight, 0, 0, share)], [],
+        0, 2 * up_weight.size * size,
+    )
     blocks = [tokens] + [send(tokens, "wide", k) for k in range(1, n_wide)]
     up = pltpu.with_memory_space_constraint(up_weight, pltpu.VMEM)
-    ups, x, (gate,) = project(blocks, up, chunks, gate_of(0), early)
+    columns = gate_weight.shape[1]
+    ups, x, (gate,) = project(blocks, up, [(0, columns)], gate_of(0), early)
     down = {}
     if n > 1:
         x, (down[n - 1],) = load(x, down_of(n - 1), COST * 2 * bytes_of(down_of(n - 1)))
-    columns = gate_weight.shape[1]
-    (ups,) = pair_sum(ups, chunks, [(0, columns)])
+    (ups,) = pair_sum(ups, [(0, columns)], [(0, columns)])
     gates = []
     for j, (start, width) in enumerate(loads):
         inner = [(a - start, b) for a, b in chunks if start <= a < start + width]

time: 64.9 us -> 60.4 us (0.931)
  waiting for transfers between devices: 15.8 us -> 11.1 us
  starting transfers between devices: 18.2 us -> 19.3 us
  local copies, waits for them, and re-layouts: 0.84 us -> 0.01 us
    ppermute x23 -> x24, waiting for transfers between devices: 15.8 us -> 11.1 us  [send(): return lax.ppermute(value, axis, [(i, (i + k) % n) for i in range(n)])]
    ppermute x23 -> x24, starting transfers between devices: 18.2 us -> 19.3 us  [send(): return lax.ppermute(value, axis, [(i, (i + k) % n) for i in range(n)])]
    unnamed x4 -> x2, local copies, waits for them, and re-layouts: 0.84 us -> 0.01 us
  transfers between devices with their start and end apart: 23 -> 24, of which waited for: 8 -> 7; matrix products, arithmetic and copies ran while one was open for 0% -> 0% of each run, Pallas kernels for 31% -> 33%
where the time goes in v4:
time: 60.4 us; the launch traced here: 60.1 us
  Pallas kernels  28.8 us (48%)
  starting transfers between devices  19.3 us (32%)
  waiting for transfers between devices  11.1 us (18%)
  other arithmetic  0.66 us (1%)
    pallas_call x18, Pallas kernels, call(): pl.pallas_call(kernel, out_shape=tuple(outs) + tuple(fetched), in_specs=[...  28.8 us
    ppermute x24, starting transfers between devices, send(): return lax.ppermute(value, axis, [(i, (i + k) % n) for i in range(n)])  19.3 us
    ppermute x24, waiting for transfers between devices, send(): return lax.ppermute(value, axis, [(i, (i + k) % n) for i in range(n)])  11.1 us
  transfers between devices with their start and end apart: 24, of which 7 were waited for; matrix products, arithmetic and copies ran while one was open for 0% of the time, Pallas kernels for 33%

profile of v4, /device:TPU:0, one launch (start us, length us, event | category | flops | bytes accessed | tf_op | source)
XLA Modules:
  0.0 60.1 jit_solution(1086064097727795518)
XLA Ops:
  0.0 1.0 %shard_map.46 = (bf16[16,2048]{1,0:T(8,128)(2,1)S(1)}, bf16[16,2048]{1,0:T(8,128)(2,1)S(1)}) custom-call(bf16[16,2048]{1,0:T(8,128)(2,1)} %refs_0_.1, bf16[6656,2048]{1,0:T(8,128)(2,1)} %refs_6_.1), custom_call_target="tpu_custom_call" | custom-call | bytes 54525952 | tf_op jit(solution)/shard_map/pallas_call | solution.py:70
  1.0 5.1 %collective-permute-start.2 = (bf16[16,2048]{1,0:T(8,128)(2,1)S(1)}, bf16[16,2048]{1,0:T(8,128)(2,1)S(1)}, u32[]{:S(2)}, u32[]{:S(2)}) collective-permute-start(bf16[16,2048]{1,0:T(8,128)(2,1)S(1)} %get-tuple-element.47.refs_0_.refs_6_), channel_id=1, source_target_pairs={{0,6},{2,0},{4,2},{6,4},{1,7},{3,1},{5,3},{7,5},{8,14},{10,8},{12,... | collective-permute-start | bytes 196616 | tf_op jit(solution)/shard_map/ppermute | solution.py:173
  6.2 1.0 %collective-permute-start = (bf16[16,2048]{1,0:T(8,128)(2,1)S(1)}, bf16[16,2048]{1,0:T(8,128)(2,1)S(1)}, u32[]{:S(2)}, u32[]{:S(2)}) collective-permute-start(bf16[16,2048]{1,0:T(8,128)(2,1)S(1)} %get-tuple-element.47.refs_0_.refs_6_), channel_id=1, source_target_pairs={{0,2},{2,4},{4,6},{6,0},{1,3},{3,5},{5,7},{7,1},{8,10},{10,12},{12... | collective-permute-start | bytes 196616 | tf_op jit(solution)/shard_map/ppermute | solution.py:173
  7.2 1.5 %collective-permute-done.2.refs_3_ = bf16[16,2048]{1,0:T(8,128)(2,1)S(1)} collective-permute-done((bf16[16,2048]{1,0:T(8,128)(2,1)S(1)}, bf16[16,2048]{1,0:T(8,128)(2,1)S(1)}, u32[]{:S(2)}, u32[]{:S(2)}) %collective-permute-start.2) | collective-permute-done | bytes 65568 | tf_op jit(solution)/shard_map/ppermute | solution.py:173
  8.6 4.0 %collective-permute-done.1.refs_2_ = bf16[16,2048]{1,0:T(8,128)(2,1)S(1)} collective-permute-done((bf16[16,2048]{1,0:T(8,128)(2,1)S(1)}, bf16[16,2048]{1,0:T(8,128)(2,1)S(1)}, u32[]{:S(2)}, u32[]{:S(2)}) %collective-permute-start.1) | collective-permute-done | bytes 65568 | tf_op jit(solution)/shard_map/ppermute | solution.py:173
  12.6 6.4 %shard_map.47 = (f32[32,6656]{1,0:T(8,128)S(1)}, f32[32,6656]{1,0:T(8,128)S(1)}, bf16[64,2048]{1,0:T(8,128)(2,1)S(1)}, bf16[2048,4096]{1,0:T(8,128)(2,1)S(1)}) custom-call(bf16[16,2048]{1,0:T(8,128)(2,1)S(1)} %get-tuple-element.47.refs_0_.refs_6_, bf16[16,2048]{1,0:T(8,128)(2,1)S(1)} %collective-permute-done.refs_1_, ...), custom_call_target="tpu_custom_call" | custom-call | flops 1744830464 | bytes 33554432 | tf_op jit(solution)/shard_map/pallas_call | solution.py:70
  19.1 2.2 %shard_map.48 = (bf16[64,2048]{1,0:T(8,128)(2,1)S(1)}, bf16[1024,2048]{1,0:T(8,128)(2,1)S(1)}) custom-call(bf16[64,2048]{1,0:T(8,128)(2,1)S(1)} %get-tuple-element.51.refs_0_.refs_1_, bf16[64,2048]{1,0:T(8,128)(2,1)S(1)} %get-tuple-element.51.refs_0_.refs_1_, bf16[6656,2048]{1,0:T(8,128)(2,1)} %refs_6_.1), custom_call_target="tpu_custom_call" | custom-call | bytes 8388608 | tf_op jit(solution)/shard_map/pallas_call | solution.py:70
  21.6 1.6 %collective-permute-start.4 = (bf16[32,6656]{1,0:T(8,128)(2,1)S(1)}, bf16[32,6656]{1,0:T(8,128)(2,1)S(1)}, u32[]{:S(2)}, u32[]{:S(2)}) collective-permute-start(bf16[32,6656]{1,0:T(8,128)(2,1)S(1)} %get-tuple-element.54), channel_id=1, source_target_pairs={{0,8},{8,0},{1,9},{9,1},{2,10},{10,2},{3,11},{11,3},{4,12},{12,4},... | collective-permute-start | bytes 1277960 | tf_op jit(solution)/shard_map/ppermute | solution.py:173
  23.2 4.1 %shard_map.50 = (f32[32,4096]{1,0:T(8,128)S(1)}, f32[32,2048]{1,0:T(8,128)S(1)}, f32[32,2048]{1,0:T(8,128)S(1)}, bf16[2048,2560]{1,0:T(8,128)(2,1)S(1)}) custom-call(bf16[64,2048]{1,0:T(8,128)(2,1)S(1)} %get-tuple-element.52.refs_2_.refs_0_, bf16[2048,4096]{1,0:T(8,128)(2,1)S(1)} %get-tuple-element.55.refs_1_, ...), custom_call_target="tpu_custom_call" | custom-call | flops 1073741824 | bytes 20971520 | tf_op jit(solution)/shard_map/pallas_call | solution.py:70
  27.8 3.4 %shard_map.51 = (f32[32,2560]{1,0:T(8,128)S(1)}, f32[32,1536]{1,0:T(8,128)S(1)}, f32[32,1024]{1,0:T(8,128)S(1)}, bf16[2048,2048]{1,0:T(8,128)(2,1)S(1)}) custom-call(bf16[64,2048]{1,0:T(8,128)(2,1)S(1)} %get-tuple-element.52.refs_2_.refs_0_, bf16[2048,2560]{1,0:T(8,128)(2,1)S(1)} %get-tuple-element.56.refs_1_, f32[32,2048]{1,0:T(8,128)S(1)} %get-tuple-element.57.refs_2_, ...), custom_call_target="tpu_custom_call" | custom-call | flops 671088640 | bytes 16777216 | tf_op jit(solution)/shard_map/pallas_call | solution.py:70
  32.5 1.5 %collective-permute-start.10 = (bf16[32,2048]{1,0:T(8,128)(2,1)S(1)}, bf16[32,2048]{1,0:T(8,128)(2,1)S(1)}, u32[]{:S(2)}, u32[]{:S(2)}) collective-permute-start(bf16[32,2048]{1,0:T(8,128)(2,1)S(1)} %get-tuple-element.68), channel_id=1, source_target_pairs={{0,8},{8,0},{1,9},{9,1},{2,10},{10,2},{3,11},{11,3},{4,12},{12,4},... | collective-permute-start | bytes 393224 | tf_op jit(solution)/shard_map/ppermute | solution.py:173
  34.0 3.4 %shard_map.53 = (bf16[64,2048]{1,0:T(8,128)(2,1)S(1)}, bf16[2048,2048]{1,0:T(8,128)(2,1)S(1)}) custom-call(bf16[64,2048]{1,0:T(8,128)(2,1)S(1)} %get-tuple-element.52.refs_2_.refs_0_, f32[32,2048]{1,0:T(8,128)S(1)} %get-tuple-element.63.refs_1_.refs_2_, bf16[6656,2048]{1,0:T(8,128)(2,1)} %refs_6_.1), custom_call_target="tpu_custom_call" | custom-call | bytes 16777216 | tf_op jit(solution)/shard_map/pallas_call | solution.py:70
  37.5 0.8 %collective-permute-done.11.refs_3_ = bf16[32,2048]{1,0:T(8,128)(2,1)S(1)} collective-permute-done((bf16[32,2048]{1,0:T(8,128)(2,1)S(1)}, bf16[32,2048]{1,0:T(8,128)(2,1)S(1)}, u32[]{:S(2)}, u32[]{:S(2)}) %collective-permute-start.11) | collective-permute-done | bytes 131104 | tf_op jit(solution)/shard_map/ppermute | solution.py:173
  39.5 0.7 %collective-permute-done.10.refs_3_ = bf16[32,2048]{1,0:T(8,128)(2,1)S(1)} collective-permute-done((bf16[32,2048]{1,0:T(8,128)(2,1)S(1)}, bf16[32,2048]{1,0:T(8,128)(2,1)S(1)}, u32[]{:S(2)}, u32[]{:S(2)}) %collective-permute-start.10) | collective-permute-done | bytes 131104 | tf_op jit(solution)/shard_map/ppermute | solution.py:173
  40.9 0.8 %collective-permute-start.9 = (bf16[32,1024]{1,0:T(8,128)(2,1)S(1)}, bf16[32,1024]{1,0:T(8,128)(2,1)S(1)}, u32[]{:S(2)}, u32[]{:S(2)}) collective-permute-start(bf16[32,1024]{1,0:T(8,128)(2,1)S(1)} %get-tuple-element.66), channel_id=1, source_target_pairs={{0,8},{8,0},{1,9},{9,1},{2,10},{10,2},{3,11},{11,3},{4,12},{12,4},... | collective-permute-start | bytes 196616 | tf_op jit(solution)/shard_map/ppermute | solution.py:173
  41.7 2.8 %shard_map.58 = (f32[64,2048]{1,0:T(8,128)S(1)}, bf16[1536,2048]{1,0:T(8,128)(2,1)S(1)}) custom-call(bf16[16,2048]{1,0:T(8,128)(2,1)S(1)} %get-tuple-element.70.refs_4_.refs_0_, bf16[16,2048]{1,0:T(8,128)(2,1)S(1)} %get-tuple-element.74.refs_1_, bf16[16,2048]{1,0:T(8,128)(2,1)S(1)} %collective-permute-done.14.refs_2_, ...), custom_call_target="tpu_custom_call" | custom-call | flops 536870912 | bytes 12582912 | tf_op jit(solution)/shard_map/pallas_call | solution.py:70
  45.2 2.0 %shard_map.60.refs_4_.refs_5_ = f32[64,2048]{1,0:T(8,128)S(1)} custom-call(bf16[16,2048]{1,0:T(8,128)(2,1)S(1)} %get-tuple-element.71.refs_5_.refs_0_, bf16[16,2048]{1,0:T(8,128)(2,1)S(1)} %get-tuple-element.72.refs_1_, bf16[16,2048]{1,0:T(8,128)(2,1)S(1)} %collective-permute-done.12.refs_2_, bf16[16,2048]{1,0:T(8,128)(2,1)S(1)} %collective-permute-done.13.refs_3_, ...), custom_call_target="tpu_custom_call" | custom-call | flops 536870912 | tf_op jit(solution)/shard_map/pallas_call | solution.py:70
  47.9 1.6 %shard_map.62.refs_5_.refs_6_ = f32[64,2048]{1,0:T(8,128)S(1)} custom-call(bf16[16,1536]{1,0:T(8,128)(2,1)S(1)} %get-tuple-element.79.refs_6_.refs_0_, bf16[16,1536]{1,0:T(8,128)(2,1)S(1)} %get-tuple-element.83.refs_1_, bf16[16,1536]{1,0:T(8,128)(2,1)S(1)} %collective-permute-done.19.refs_2_, bf16[16,1536]{1,0:T(8,128)(2,1)S(1)} %collective-permute-done.20.refs_3_, ...), custom_call_target="tpu_custom_call" | custom-call | flops 402653184 | tf_op jit(solution)/shard_map/pallas_call | solution.py:70
  49.5 1.2 %shard_map.63 = (f32[16,2048]{1,0:T(8,128)S(1)}, bf16[16,2048]{1,0:T(8,128)(2,1)S(1)}, bf16[16,2048]{1,0:T(8,128)(2,1)S(1)}, bf16[16,2048]{1,0:T(8,128)(2,1)S(1)}) custom-call(bf16[16,1024]{1,0:T(8,128)(2,1)S(1)} %get-tuple-element.80.refs_6_.refs_0_, bf16[16,1024]{1,0:T(8,128)(2,1)S(1)} %get-tuple-element.81.refs_1_, ...), custom_call_target="tpu_custom_call" | custom-call | flops 268435456 | tf_op jit(solution)/shard_map/pallas_call | solution.py:70
  51.0 2.3 %collective-permute-start.22 = (bf16[16,2048]{1,0:T(8,128)(2,1)S(1)}, bf16[16,2048]{1,0:T(8,128)(2,1)S(1)}, u32[]{:S(2)}, u32[]{:S(2)}) collective-permute-start(bf16[16,2048]{1,0:T(8,128)(2,1)S(1)} %get-tuple-element.87), channel_id=1, source_target_pairs={{0,4},{2,6},{4,0},{6,2},{1,5},{3,7},{5,1},{7,3},{8,12},{10,14},{12... | collective-permute-start | bytes 196616 | tf_op jit(solution)/shard_map/ppermute | solution.py:173
  53.3 2.2 %collective-permute-start.23 = (bf16[16,2048]{1,0:T(8,128)(2,1)S(1)}, bf16[16,2048]{1,0:T(8,128)(2,1)S(1)}, u32[]{:S(2)}, u32[]{:S(2)}) collective-permute-start(bf16[16,2048]{1,0:T(8,128)(2,1)S(1)} %get-tuple-element.88), channel_id=1, source_target_pairs={{0,6},{2,0},{4,2},{6,4},{1,7},{3,1},{5,3},{7,5},{8,14},{10,8},{12,... | collective-permute-start | bytes 196616 | tf_op jit(solution)/shard_map/ppermute | solution.py:173
  55.5 2.1 %collective-permute-done.21 = bf16[16,2048]{1,0:T(8,128)(2,1)S(1)} collective-permute-done((bf16[16,2048]{1,0:T(8,128)(2,1)S(1)}, bf16[16,2048]{1,0:T(8,128)(2,1)S(1)}, u32[]{:S(2)}, u32[]{:S(2)}) %collective-permute-start.21) | collective-permute-done | bytes 65568 | tf_op jit(solution)/shard_map/ppermute | solution.py:173
  57.6 1.8 %collective-permute-done.22 = bf16[16,2048]{1,0:T(8,128)(2,1)S(1)} collective-permute-done((bf16[16,2048]{1,0:T(8,128)(2,1)S(1)}, bf16[16,2048]{1,0:T(8,128)(2,1)S(1)}, u32[]{:S(2)}, u32[]{:S(2)}) %collective-permute-start.22) | collective-permute-done | bytes 65568 | tf_op jit(solution)/shard_map/ppermute | solution.py:173
  59.4 0.7 %add_convert_fusion = bf16[16,2048]{1,0:T(8,128)(2,1)} fusion(bf16[16,2048]{1,0:T(8,128)(2,1)S(1)} %collective-permute-done.23, bf16[16,2048]{1,0:T(8,128)(2,1)S(1)} %collective-permute-done.22, f32[16,2048]{1,0:T(8,128)S(1)} %get-tuple-element.85, bf16[16,2048]{1,0:T(8,128)(2,1)S(1)} %collective-permute-done.21), kind=kLoop, calls=%fused_computation | loop fusion | flops 229376 | bytes 393216 | tf_op jit(solution)/shard_map/convert_element_type | solution.py:299
  (45 shorter events, 5.7 us)
Async XLA Ops:
  1.0 7.6 %collective-permute-start.2 = (bf16[16,2048]{1,0:T(8,128)(2,1)S(1)}, bf16[16,2048]{1,0:T(8,128)(2,1)S(1)}, u32[]{:S(2)}, u32[]{:S(2)}) collective-permute-start(bf16[16,2048]{1,0:T(8,128)(2,1)S(1)} %get-tuple-element.47.refs_0_.refs_6_), channel_id=1, source_target_pairs={{0,6},{2,0},{4,2},{6,4},{1,7},{3,1},{5,3},{7,5},{8,14},{10,8},{12,... | collective-permute-start | bytes 196616 | tf_op jit(solution)/shard_map/ppermute | solution.py:173
  6.1 6.5 %collective-permute-start.1 = (bf16[16,2048]{1,0:T(8,128)(2,1)S(1)}, bf16[16,2048]{1,0:T(8,128)(2,1)S(1)}, u32[]{:S(2)}, u32[]{:S(2)}) collective-permute-start(bf16[16,2048]{1,0:T(8,128)(2,1)S(1)} %get-tuple-element.47.refs_0_.refs_6_), channel_id=1, source_target_pairs={{0,4},{2,6},{4,0},{6,2},{1,5},{3,7},{5,1},{7,3},{8,12},{10,14},{12... | collective-permute-start | bytes 196616 | tf_op jit(solution)/shard_map/ppermute | solution.py:173
  6.2 6.5 %collective-permute-start = (bf16[16,2048]{1,0:T(8,128)(2,1)S(1)}, bf16[16,2048]{1,0:T(8,128)(2,1)S(1)}, u32[]{:S(2)}, u32[]{:S(2)}) collective-permute-start(bf16[16,2048]{1,0:T(8,128)(2,1)S(1)} %get-tuple-element.47.refs_0_.refs_6_), channel_id=1, source_target_pairs={{0,2},{2,4},{4,6},{6,0},{1,3},{3,5},{5,7},{7,1},{8,10},{10,12},{12... | collective-permute-start | bytes 196616 | tf_op jit(solution)/shard_map/ppermute | solution.py:173
  19.0 2.4 %collective-permute-start.3 = (f32[32,6656]{1,0:T(8,128)S(1)}, f32[32,6656]{1,0:T(8,128)S(1)}, u32[]{:S(2)}, u32[]{:S(2)}) collective-permute-start(f32[32,6656]{1,0:T(8,128)S(1)} %get-tuple-element.50), channel_id=1, source_target_pairs={{0,1},{1,0},{2,3},{3,2},{4,5},{5,4},{6,7},{7,6},{8,9},{9,8},{10,11... | collective-permute-start | bytes 2555912 | tf_op jit(solution)/shard_map/ppermute | solution.py:173
  21.6 15.7 %collective-permute-start.4 = (bf16[32,6656]{1,0:T(8,128)(2,1)S(1)}, bf16[32,6656]{1,0:T(8,128)(2,1)S(1)}, u32[]{:S(2)}, u32[]{:S(2)}) collective-permute-start(bf16[32,6656]{1,0:T(8,128)(2,1)S(1)} %get-tuple-element.54), channel_id=1, source_target_pairs={{0,8},{8,0},{1,9},{9,1},{2,10},{10,2},{3,11},{11,3},{4,12},{12,4},... | collective-permute-start | bytes 1277960 | tf_op jit(solution)/shard_map/ppermute | solution.py:173
  27.2 4.6 %collective-permute-start.8 = (f32[32,2048]{1,0:T(8,128)S(1)}, f32[32,2048]{1,0:T(8,128)S(1)}, u32[]{:S(2)}, u32[]{:S(2)}) collective-permute-start(f32[32,2048]{1,0:T(8,128)S(1)} %get-tuple-element.62), channel_id=1, source_target_pairs={{0,1},{1,0},{2,3},{3,2},{4,5},{5,4},{6,7},{7,6},{8,9},{9,8},{10,11... | collective-permute-start | bytes 786440 | tf_op jit(solution)/shard_map/ppermute | solution.py:173
  27.4 4.4 %collective-permute-start.7 = (f32[32,2048]{1,0:T(8,128)S(1)}, f32[32,2048]{1,0:T(8,128)S(1)}, u32[]{:S(2)}, u32[]{:S(2)}) collective-permute-start(f32[32,2048]{1,0:T(8,128)S(1)} %get-tuple-element.57.refs_2_), channel_id=1, source_target_pairs={{0,1},{1,0},{2,3},{3,2},{4,5},{5,4},{6,7},{7,6},{8,9},{9,8},{10,11... | collective-permute-start | bytes 786440 | tf_op jit(solution)/shard_map/ppermute | solution.py:173
  31.2 6.2 %collective-permute-start.5 = (f32[32,1536]{1,0:T(8,128)S(1)}, f32[32,1536]{1,0:T(8,128)S(1)}, u32[]{:S(2)}, u32[]{:S(2)}) collective-permute-start(f32[32,1536]{1,0:T(8,128)S(1)} %get-tuple-element.59), channel_id=1, source_target_pairs={{0,1},{1,0},{2,3},{3,2},{4,5},{5,4},{6,7},{7,6},{8,9},{9,8},{10,11... | collective-permute-start | bytes 589832 | tf_op jit(solution)/shard_map/ppermute | solution.py:173
  31.3 6.1 %collective-permute-start.6 = (f32[32,1024]{1,0:T(8,128)S(1)}, f32[32,1024]{1,0:T(8,128)S(1)}, u32[]{:S(2)}, u32[]{:S(2)}) collective-permute-start(f32[32,1024]{1,0:T(8,128)S(1)} %get-tuple-element.60.refs_3_), channel_id=1, source_target_pairs={{0,1},{1,0},{2,3},{3,2},{4,5},{5,4},{6,7},{7,6},{8,9},{9,8},{10,11... | collective-permute-start | bytes 393224 | tf_op jit(solution)/shard_map/ppermute | solution.py:173
  31.9 6.4 %collective-permute-start.11 = (bf16[32,2048]{1,0:T(8,128)(2,1)S(1)}, bf16[32,2048]{1,0:T(8,128)(2,1)S(1)}, u32[]{:S(2)}, u32[]{:S(2)}) collective-permute-start(bf16[32,2048]{1,0:T(8,128)(2,1)S(1)} %get-tuple-element.69), channel_id=1, source_target_pairs={{0,8},{8,0},{1,9},{9,1},{2,10},{10,2},{3,11},{11,3},{4,12},{12,4},... | collective-permute-start | bytes 393224 | tf_op jit(solution)/shard_map/ppermute | solution.py:173
  32.5 7.8 %collective-permute-start.10 = (bf16[32,2048]{1,0:T(8,128)(2,1)S(1)}, bf16[32,2048]{1,0:T(8,128)(2,1)S(1)}, u32[]{:S(2)}, u32[]{:S(2)}) collective-permute-start(bf16[32,2048]{1,0:T(8,128)(2,1)S(1)} %get-tuple-element.68), channel_id=1, source_target_pairs={{0,8},{8,0},{1,9},{9,1},{2,10},{10,2},{3,11},{11,3},{4,12},{12,4},... | collective-permute-start | bytes 393224 | tf_op jit(solution)/shard_map/ppermute | solution.py:173
  38.4 2.5 %collective-permute-start.15 = (bf16[16,2048]{1,0:T(8,128)(2,1)S(1)}, bf16[16,2048]{1,0:T(8,128)(2,1)S(1)}, u32[]{:S(2)}, u32[]{:S(2)}) collective-permute-start(bf16[16,2048]{1,0:T(8,128)(2,1)S(1)} %get-tuple-element.74.refs_1_), channel_id=1, source_target_pairs={{0,1},{1,0},{2,3},{3,2},{4,5},{5,4},{6,7},{7,6},{8,9},{9,8},{10,11... | collective-permute-start | bytes 196616 | tf_op jit(solution)/shard_map/ppermute | solution.py:173
  38.5 3.2 %collective-permute-start.14 = (bf16[16,2048]{1,0:T(8,128)(2,1)S(1)}, bf16[16,2048]{1,0:T(8,128)(2,1)S(1)}, u32[]{:S(2)}, u32[]{:S(2)}) collective-permute-start(bf16[16,2048]{1,0:T(8,128)(2,1)S(1)} %get-tuple-element.70.refs_4_.refs_0_), channel_id=1, source_target_pairs={{0,1},{1,0},{2,3},{3,2},{4,5},{5,4},{6,7},{7,6},{8,9},{9,8},{10,11... | collective-permute-start | bytes 196616 | tf_op jit(solution)/shard_map/ppermute | solution.py:173
  39.0 5.5 %collective-permute-start.16 = (bf16[32,1536]{1,0:T(8,128)(2,1)S(1)}, bf16[32,1536]{1,0:T(8,128)(2,1)S(1)}, u32[]{:S(2)}, u32[]{:S(2)}) collective-permute-start(bf16[32,1536]{1,0:T(8,128)(2,1)S(1)} %get-tuple-element.78), channel_id=1, source_target_pairs={{0,8},{8,0},{1,9},{9,1},{2,10},{10,2},{3,11},{11,3},{4,12},{12,4},... | collective-permute-start | bytes 294920 | tf_op jit(solution)/shard_map/ppermute | solution.py:173
  40.3 4.9 %collective-permute-start.13 = (bf16[16,2048]{1,0:T(8,128)(2,1)S(1)}, bf16[16,2048]{1,0:T(8,128)(2,1)S(1)}, u32[]{:S(2)}, u32[]{:S(2)}) collective-permute-start(bf16[16,2048]{1,0:T(8,128)(2,1)S(1)} %get-tuple-element.72.refs_1_), channel_id=1, source_target_pairs={{0,1},{1,0},{2,3},{3,2},{4,5},{5,4},{6,7},{7,6},{8,9},{9,8},{10,11... | collective-permute-start | bytes 196616 | tf_op jit(solution)/shard_map/ppermute | solution.py:173
  40.4 4.8 %collective-permute-start.12 = (bf16[16,2048]{1,0:T(8,128)(2,1)S(1)}, bf16[16,2048]{1,0:T(8,128)(2,1)S(1)}, u32[]{:S(2)}, u32[]{:S(2)}) collective-permute-start(bf16[16,2048]{1,0:T(8,128)(2,1)S(1)} %get-tuple-element.71.refs_5_.refs_0_), channel_id=1, source_target_pairs={{0,1},{1,0},{2,3},{3,2},{4,5},{5,4},{6,7},{7,6},{8,9},{9,8},{10,11... | collective-permute-start | bytes 196616 | tf_op jit(solution)/shard_map/ppermute | solution.py:173
  40.9 6.3 %collective-permute-start.9 = (bf16[32,1024]{1,0:T(8,128)(2,1)S(1)}, bf16[32,1024]{1,0:T(8,128)(2,1)S(1)}, u32[]{:S(2)}, u32[]{:S(2)}) collective-permute-start(bf16[32,1024]{1,0:T(8,128)(2,1)S(1)} %get-tuple-element.66), channel_id=1, source_target_pairs={{0,8},{8,0},{1,9},{9,1},{2,10},{10,2},{3,11},{11,3},{4,12},{12,4},... | collective-permute-start | bytes 196616 | tf_op jit(solution)/shard_map/ppermute | solution.py:173
  44.6 3.2 %collective-permute-start.20 = (bf16[16,1536]{1,0:T(8,128)(2,1)S(1)}, bf16[16,1536]{1,0:T(8,128)(2,1)S(1)}, u32[]{:S(2)}, u32[]{:S(2)}) collective-permute-start(bf16[16,1536]{1,0:T(8,128)(2,1)S(1)} %get-tuple-element.83.refs_1_), channel_id=1, source_target_pairs={{0,1},{1,0},{2,3},{3,2},{4,5},{5,4},{6,7},{7,6},{8,9},{9,8},{10,11... | collective-permute-start | bytes 147464 | tf_op jit(solution)/shard_map/ppermute | solution.py:173
  44.7 3.2 %collective-permute-start.19 = (bf16[16,1536]{1,0:T(8,128)(2,1)S(1)}, bf16[16,1536]{1,0:T(8,128)(2,1)S(1)}, u32[]{:S(2)}, u32[]{:S(2)}) collective-permute-start(bf16[16,1536]{1,0:T(8,128)(2,1)S(1)} %get-tuple-element.79.refs_6_.refs_0_), channel_id=1, source_target_pairs={{0,1},{1,0},{2,3},{3,2},{4,5},{5,4},{6,7},{7,6},{8,9},{9,8},{10,11... | collective-permute-start | bytes 147464 | tf_op jit(solution)/shard_map/ppermute | solution.py:173
  47.3 2.2 %collective-permute-start.18 = (bf16[16,1024]{1,0:T(8,128)(2,1)S(1)}, bf16[16,1024]{1,0:T(8,128)(2,1)S(1)}, u32[]{:S(2)}, u32[]{:S(2)}) collective-permute-start(bf16[16,1024]{1,0:T(8,128)(2,1)S(1)} %get-tuple-element.81.refs_1_), channel_id=1, source_target_pairs={{0,1},{1,0},{2,3},{3,2},{4,5},{5,4},{6,7},{7,6},{8,9},{9,8},{10,11... | collective-permute-start | bytes 98312 | tf_op jit(solution)/shard_map/ppermute | solution.py:173
  47.5 2.1 %collective-permute-start.17 = (bf16[16,1024]{1,0:T(8,128)(2,1)S(1)}, bf16[16,1024]{1,0:T(8,128)(2,1)S(1)}, u32[]{:S(2)}, u32[]{:S(2)}) collective-permute-start(bf16[16,1024]{1,0:T(8,128)(2,1)S(1)} %get-tuple-element.80.refs_6_.refs_0_), channel_id=1, source_target_pairs={{0,1},{1,0},{2,3},{3,2},{4,5},{5,4},{6,7},{7,6},{8,9},{9,8},{10,11... | collective-permute-start | bytes 98312 | tf_op jit(solution)/shard_map/ppermute | solution.py:173
  50.8 6.8 %collective-permute-start.21 = (bf16[16,2048]{1,0:T(8,128)(2,1)S(1)}, bf16[16,2048]{1,0:T(8,128)(2,1)S(1)}, u32[]{:S(2)}, u32[]{:S(2)}) collective-permute-start(bf16[16,2048]{1,0:T(8,128)(2,1)S(1)} %get-tuple-element.86), channel_id=1, source_target_pairs={{0,2},{2,4},{4,6},{6,0},{1,3},{3,5},{5,7},{7,1},{8,10},{10,12},{12... | collective-permute-start | bytes 196616 | tf_op jit(solution)/shard_map/ppermute | solution.py:173
  51.0 8.4 %collective-permute-start.22 = (bf16[16,2048]{1,0:T(8,128)(2,1)S(1)}, bf16[16,2048]{1,0:T(8,128)(2,1)S(1)}, u32[]{:S(2)}, u32[]{:S(2)}) collective-permute-start(bf16[16,2048]{1,0:T(8,128)(2,1)S(1)} %get-tuple-element.87), channel_id=1, source_target_pairs={{0,4},{2,6},{4,0},{6,2},{1,5},{3,7},{5,1},{7,3},{8,12},{10,14},{12... | collective-permute-start | bytes 196616 | tf_op jit(solution)/shard_map/ppermute | solution.py:173
  53.3 6.1 %collective-permute-start.23 = (bf16[16,2048]{1,0:T(8,128)(2,1)S(1)}, bf16[16,2048]{1,0:T(8,128)(2,1)S(1)}, u32[]{:S(2)}, u32[]{:S(2)}) collective-permute-start(bf16[16,2048]{1,0:T(8,128)(2,1)S(1)} %get-tuple-element.88), channel_id=1, source_target_pairs={{0,6},{2,0},{4,2},{6,4},{1,7},{3,1},{5,3},{7,5},{8,14},{10,8},{12,... | collective-permute-start | bytes 196616 | tf_op jit(solution)/shard_map/ppermute | solution.py:173
  (1 other events, 12.6 us)

commit v5 on v4

--- a/solution.py
+++ b/solution.py
@@ -159,7 +159,7 @@
         if last:
             share = total.shape[0] // n_wide
             for k in range(n_wide):
-                place = (n_wide - k) % n_wide * share
+                place = (k if n_wide & (n_wide - 1) == 0 else (n_wide - k) % n_wide) * share
                 outs[k][:, at] = total[place : place + share].astype(outs[k].dtype)
         else:
             outs[0][:, at] = total
@@ -170,7 +170,8 @@
 
     def send(value, axis, k):
         n = sizes[axis]
-        return lax.ppermute(value, axis, [(i, (i + k) % n) for i in range(n)])
+        paired = axis == "wide" and n & (n - 1) == 0
+        return lax.ppermute(value, axis, [(i, i ^ k if paired else (i + k) % n) for i in range(n)])
 
     share, depth = tokens.shape
     rows = share * n_wide
@@ -243,20 +244,16 @@
             outs += [pltpu.VMEM((share, features), BF16)] * (n_wide - 1)
         else:
             outs = [pltpu.VMEM((rows, features), F32)]
-        fetch = down_of(2) if first and n > 3 else []
-        total, fetched = call(
+        return call(
             order,
             functools.partial(down_kernel, n_pair, n_wide, first, last),
             [*parts, down[j], *total],
             outs,
-            fetch,
+            [],
             [pltpu.VMEM((rows, width), BF16)],
             COST * 2 * rows * width * features,
-            COST * 2 * bytes_of(fetch),
-        )
-        if fetch:
-            down[2] = fetched[0]
-        return total
+            0,
+        )[0]
 
     _, (tokens, *early) = call(
         order, load_kernel, [], [], [(tokens, 0, 0, share), (down_weight, 0, 0, share)], [],
@@ -266,11 +263,7 @@
     up = pltpu.with_memory_space_constraint(up_weight, pltpu.VMEM)
     columns = gate_weight.shape[1]
     ups, x, (gate,) = project(blocks, up, [(0, columns)], gate_of(0), early)
-    down = {}
-    if n > 1:
-        x, (down[n - 1],) = load(x, down_of(n - 1), COST * 2 * bytes_of(down_of(n - 1)))
-    (ups,) = pair_sum(ups, [(0, columns)], [(0, columns)])
-    gates = []
+    down, gates = {}, []
     for j, (start, width) in enumerate(loads):
         inner = [(a - start, b) for a, b in chunks if start <= a < start + width]
         last = j == len(loads) - 1
@@ -280,9 +273,13 @@
         else:
             gate = weight
         gates.append((parts, inner))
+        if j == 0:
+            (ups,) = pair_sum(ups, [(0, columns)], [(0, columns)])
     sums = pair_sum(*gates[0], gates[0][1])
-    if n > 2:
-        _, (down[1],) = load(x, down_of(1), COST * 2 * bytes_of(down_of(1)))
+    if n > 1:
+        late = list(range(1, n))
+        _, more = load(x, down_of(*late), COST * 2 * bytes_of(down_of(*late)))
+        down.update(zip(late, more))
     load(x, [], 0, ups[1:])
     for parts, inner in gates[1:]:
         sums += pair_sum(parts, inner, inner)

time: 60.4 us -> 61.2 us (1.013)
  starting transfers between devices: 19.3 us -> 20.3 us
    ppermute x24, starting transfers between devices: 19.3 us -> 20.3 us  [send(): lax.ppermute(value, axis, [(i, i ^ k if paired else (i + k) % n) for i in...]
    pallas_call x18 -> x17, Pallas kernels: 28.8 us -> 28.8 us  [call(): pl.pallas_call(kernel, out_shape=tuple(outs) + tuple(fetched), in_specs=[...]
  transfers between devices with their start and end apart: 24 -> 24, of which waited for: 7 -> 6; matrix products, arithmetic and copies ran while one was open for 0% -> 0% of each run, Pallas kernels for 33% -> 33%
where the time goes in v5:
time: 61.2 us; the launch traced here: 61 us
  Pallas kernels  28.8 us (47%)
  starting transfers between devices  20.3 us (33%)
  waiting for transfers between devices  11 us (18%)
  other arithmetic  0.66 us (1%)
    pallas_call x17, Pallas kernels, call(): pl.pallas_call(kernel, out_shape=tuple(outs) + tuple(fetched), in_specs=[...  28.8 us
    ppermute x24, starting transfers between devices, send(): lax.ppermute(value, axis, [(i, i ^ k if paired else (i + k) % n) for i in...  20.3 us
    ppermute x24, waiting for transfers between devices, send(): lax.ppermute(value, axis, [(i, i ^ k if paired else (i + k) % n) for i in...  11 us
  transfers between devices with their start and end apart: 24, of which 6 were waited for; matrix products, arithmetic and copies ran while one was open for 0% of the time, Pallas kernels for 33%

profile of v5, /device:TPU:0, one launch (start us, length us, event | category | flops | bytes accessed | tf_op | source)
XLA Modules:
  0.0 61.0 jit_solution(5675093889485938226)
XLA Ops:
  0.0 1.0 %shard_map.46 = (bf16[16,2048]{1,0:T(8,128)(2,1)S(1)}, bf16[16,2048]{1,0:T(8,128)(2,1)S(1)}) custom-call(bf16[16,2048]{1,0:T(8,128)(2,1)} %refs_0_.1, bf16[6656,2048]{1,0:T(8,128)(2,1)} %refs_4_.3), custom_call_target="tpu_custom_call" | custom-call | bytes 54525952 | tf_op jit(solution)/shard_map/pallas_call | solution.py:70
  1.0 5.1 %collective-permute-start.2 = (bf16[16,2048]{1,0:T(8,128)(2,1)S(1)}, bf16[16,2048]{1,0:T(8,128)(2,1)S(1)}, u32[]{:S(2)}, u32[]{:S(2)}) collective-permute-start(bf16[16,2048]{1,0:T(8,128)(2,1)S(1)} %get-tuple-element.45.refs_0_.refs_6_), channel_id=1, source_target_pairs={{0,6},{2,4},{4,2},{6,0},{1,7},{3,5},{5,3},{7,1},{8,14},{10,12},{12... | collective-permute-start | bytes 196616 | tf_op jit(solution)/shard_map/ppermute | solution.py:174
  6.2 0.6 %collective-permute-start = (bf16[16,2048]{1,0:T(8,128)(2,1)S(1)}, bf16[16,2048]{1,0:T(8,128)(2,1)S(1)}, u32[]{:S(2)}, u32[]{:S(2)}) collective-permute-start(bf16[16,2048]{1,0:T(8,128)(2,1)S(1)} %get-tuple-element.45.refs_0_.refs_6_), channel_id=1, source_target_pairs={{0,2},{2,0},{4,6},{6,4},{1,3},{3,1},{5,7},{7,5},{8,10},{10,8},{12,... | collective-permute-start | bytes 196616 | tf_op jit(solution)/shard_map/ppermute | solution.py:174
  6.8 1.9 %collective-permute-done.2.refs_3_ = bf16[16,2048]{1,0:T(8,128)(2,1)S(1)} collective-permute-done((bf16[16,2048]{1,0:T(8,128)(2,1)S(1)}, bf16[16,2048]{1,0:T(8,128)(2,1)S(1)}, u32[]{:S(2)}, u32[]{:S(2)}) %collective-permute-start.2) | collective-permute-done | bytes 65568 | tf_op jit(solution)/shard_map/ppermute | solution.py:174
  8.7 3.0 %collective-permute-done.1.refs_2_ = bf16[16,2048]{1,0:T(8,128)(2,1)S(1)} collective-permute-done((bf16[16,2048]{1,0:T(8,128)(2,1)S(1)}, bf16[16,2048]{1,0:T(8,128)(2,1)S(1)}, u32[]{:S(2)}, u32[]{:S(2)}) %collective-permute-start.1) | collective-permute-done | bytes 65568 | tf_op jit(solution)/shard_map/ppermute | solution.py:174
  11.8 6.4 %shard_map.47 = (f32[32,6656]{1,0:T(8,128)S(1)}, f32[32,6656]{1,0:T(8,128)S(1)}, bf16[64,2048]{1,0:T(8,128)(2,1)S(1)}, bf16[2048,4096]{1,0:T(8,128)(2,1)S(1)}) custom-call(bf16[16,2048]{1,0:T(8,128)(2,1)S(1)} %get-tuple-element.45.refs_0_.refs_6_, bf16[16,2048]{1,0:T(8,128)(2,1)S(1)} %collective-permute-done.refs_1_, ...), custom_call_target="tpu_custom_call" | custom-call | flops 1744830464 | bytes 33554432 | tf_op jit(solution)/shard_map/pallas_call | solution.py:70
  18.3 4.1 %shard_map.48 = (f32[32,4096]{1,0:T(8,128)S(1)}, f32[32,2048]{1,0:T(8,128)S(1)}, f32[32,2048]{1,0:T(8,128)S(1)}, bf16[2048,2560]{1,0:T(8,128)(2,1)S(1)}) custom-call(bf16[64,2048]{1,0:T(8,128)(2,1)S(1)} %get-tuple-element.49.refs_0_.refs_2_, bf16[2048,4096]{1,0:T(8,128)(2,1)S(1)} %get-tuple-element.50.refs_1_, ...), custom_call_target="tpu_custom_call" | custom-call | flops 1073741824 | bytes 20971520 | tf_op jit(solution)/shard_map/pallas_call | solution.py:70
  22.5 1.6 %collective-permute-start.4 = (bf16[32,6656]{1,0:T(8,128)(2,1)S(1)}, bf16[32,6656]{1,0:T(8,128)(2,1)S(1)}, u32[]{:S(2)}, u32[]{:S(2)}) collective-permute-start(bf16[32,6656]{1,0:T(8,128)(2,1)S(1)} %get-tuple-element.53), channel_id=1, source_target_pairs={{0,8},{8,0},{1,9},{9,1},{2,10},{10,2},{3,11},{11,3},{4,12},{12,4},... | collective-permute-start | bytes 1277960 | tf_op jit(solution)/shard_map/ppermute | solution.py:174
  24.5 3.4 %shard_map.50 = (f32[32,2560]{1,0:T(8,128)S(1)}, f32[32,1536]{1,0:T(8,128)S(1)}, f32[32,1024]{1,0:T(8,128)S(1)}, bf16[2048,2048]{1,0:T(8,128)(2,1)S(1)}) custom-call(bf16[64,2048]{1,0:T(8,128)(2,1)S(1)} %get-tuple-element.49.refs_0_.refs_2_, bf16[2048,2560]{1,0:T(8,128)(2,1)S(1)} %get-tuple-element.54.refs_1_, ...), custom_call_target="tpu_custom_call" | custom-call | flops 671088640 | bytes 16777216 | tf_op jit(solution)/shard_map/pallas_call | solution.py:70
  29.2 1.5 %collective-permute-start.10 = (bf16[32,2048]{1,0:T(8,128)(2,1)S(1)}, bf16[32,2048]{1,0:T(8,128)(2,1)S(1)}, u32[]{:S(2)}, u32[]{:S(2)}) collective-permute-start(bf16[32,2048]{1,0:T(8,128)(2,1)S(1)} %get-tuple-element.65), channel_id=1, source_target_pairs={{0,8},{8,0},{1,9},{9,1},{2,10},{10,2},{3,11},{11,3},{4,12},{12,4},... | collective-permute-start | bytes 393224 | tf_op jit(solution)/shard_map/ppermute | solution.py:174
  30.7 6.4 %shard_map.52 = (bf16[64,2048]{1,0:T(8,128)(2,1)S(1)}, bf16[2048,2048]{1,0:T(8,128)(2,1)S(1)}, bf16[1536,2048]{1,0:T(8,128)(2,1)S(1)}, bf16[1024,2048]{1,0:T(8,128)(2,1)S(1)}) custom-call(bf16[64,2048]{1,0:T(8,128)(2,1)S(1)} %get-tuple-element.49.refs_0_.refs_2_, f32[32,2048]{1,0:T(8,128)S(1)} %get-tuple-element.60.refs_1_.refs_2_, ...), custom_call_target="tpu_custom_call" | custom-call | bytes 37748736 | tf_op jit(solution)/shard_map/pallas_call | solution.py:70
  37.2 0.7 %collective-permute-done.11.refs_3_ = bf16[32,2048]{1,0:T(8,128)(2,1)S(1)} collective-permute-done((bf16[32,2048]{1,0:T(8,128)(2,1)S(1)}, bf16[32,2048]{1,0:T(8,128)(2,1)S(1)}, u32[]{:S(2)}, u32[]{:S(2)}) %collective-permute-start.11) | collective-permute-done | bytes 131104 | tf_op jit(solution)/shard_map/ppermute | solution.py:174
  38.7 1.5 %collective-permute-start.16 = (bf16[32,1536]{1,0:T(8,128)(2,1)S(1)}, bf16[32,1536]{1,0:T(8,128)(2,1)S(1)}, u32[]{:S(2)}, u32[]{:S(2)}) collective-permute-start(bf16[32,1536]{1,0:T(8,128)(2,1)S(1)} %get-tuple-element.74), channel_id=1, source_target_pairs={{0,8},{8,0},{1,9},{9,1},{2,10},{10,2},{3,11},{11,3},{4,12},{12,4},... | collective-permute-start | bytes 294920 | tf_op jit(solution)/shard_map/ppermute | solution.py:174
  41.1 1.5 %collective-permute-start.9 = (bf16[32,1024]{1,0:T(8,128)(2,1)S(1)}, bf16[32,1024]{1,0:T(8,128)(2,1)S(1)}, u32[]{:S(2)}, u32[]{:S(2)}) collective-permute-start(bf16[32,1024]{1,0:T(8,128)(2,1)S(1)} %get-tuple-element.63), channel_id=1, source_target_pairs={{0,8},{8,0},{1,9},{9,1},{2,10},{10,2},{3,11},{11,3},{4,12},{12,4},... | collective-permute-start | bytes 196616 | tf_op jit(solution)/shard_map/ppermute | solution.py:174
  42.6 2.0 %shard_map.57.refs_4_.refs_5_ = f32[64,2048]{1,0:T(8,128)S(1)} custom-call(bf16[16,2048]{1,0:T(8,128)(2,1)S(1)} %get-tuple-element.67.refs_4_.refs_0_, bf16[16,2048]{1,0:T(8,128)(2,1)S(1)} %get-tuple-element.71.refs_1_, bf16[16,2048]{1,0:T(8,128)(2,1)S(1)} %collective-permute-done.14.refs_2_, bf16[16,2048]{1,0:T(8,128)(2,1)S(1)} %collective-permute-done.15.refs_3_, ...), custom_call_target="tpu_custom_call" | custom-call | flops 536870912 | tf_op jit(solution)/shard_map/pallas_call | solution.py:70
  45.2 2.0 %shard_map.59.refs_4_.refs_5_ = f32[64,2048]{1,0:T(8,128)S(1)} custom-call(bf16[16,2048]{1,0:T(8,128)(2,1)S(1)} %get-tuple-element.68.refs_5_.refs_0_, bf16[16,2048]{1,0:T(8,128)(2,1)S(1)} %get-tuple-element.69.refs_1_, bf16[16,2048]{1,0:T(8,128)(2,1)S(1)} %collective-permute-done.12.refs_2_, bf16[16,2048]{1,0:T(8,128)(2,1)S(1)} %collective-permute-done.13.refs_3_, ...), custom_call_target="tpu_custom_call" | custom-call | flops 536870912 | tf_op jit(solution)/shard_map/pallas_call | solution.py:70
  47.9 1.6 %shard_map.61.refs_5_.refs_6_ = f32[64,2048]{1,0:T(8,128)S(1)} custom-call(bf16[16,1536]{1,0:T(8,128)(2,1)S(1)} %get-tuple-element.75.refs_6_.refs_0_, bf16[16,1536]{1,0:T(8,128)(2,1)S(1)} %get-tuple-element.79.refs_1_, bf16[16,1536]{1,0:T(8,128)(2,1)S(1)} %collective-permute-done.19.refs_2_, bf16[16,1536]{1,0:T(8,128)(2,1)S(1)} %collective-permute-done.20.refs_3_, ...), custom_call_target="tpu_custom_call" | custom-call | flops 402653184 | tf_op jit(solution)/shard_map/pallas_call | solution.py:70
  49.5 1.2 %shard_map.62 = (f32[16,2048]{1,0:T(8,128)S(1)}, bf16[16,2048]{1,0:T(8,128)(2,1)S(1)}, bf16[16,2048]{1,0:T(8,128)(2,1)S(1)}, bf16[16,2048]{1,0:T(8,128)(2,1)S(1)}) custom-call(bf16[16,1024]{1,0:T(8,128)(2,1)S(1)} %get-tuple-element.76.refs_6_.refs_0_, bf16[16,1024]{1,0:T(8,128)(2,1)S(1)} %get-tuple-element.77.refs_1_, ...), custom_call_target="tpu_custom_call" | custom-call | flops 268435456 | tf_op jit(solution)/shard_map/pallas_call | solution.py:70
  50.8 1.1 %collective-permute-start.21 = (bf16[16,2048]{1,0:T(8,128)(2,1)S(1)}, bf16[16,2048]{1,0:T(8,128)(2,1)S(1)}, u32[]{:S(2)}, u32[]{:S(2)}) collective-permute-start(bf16[16,2048]{1,0:T(8,128)(2,1)S(1)} %get-tuple-element.82), channel_id=1, source_target_pairs={{0,2},{2,0},{4,6},{6,4},{1,3},{3,1},{5,7},{7,5},{8,10},{10,8},{12,... | collective-permute-start | bytes 196616 | tf_op jit(solution)/shard_map/ppermute | solution.py:174
  51.9 2.2 %collective-permute-start.22 = (bf16[16,2048]{1,0:T(8,128)(2,1)S(1)}, bf16[16,2048]{1,0:T(8,128)(2,1)S(1)}, u32[]{:S(2)}, u32[]{:S(2)}) collective-permute-start(bf16[16,2048]{1,0:T(8,128)(2,1)S(1)} %get-tuple-element.83), channel_id=1, source_target_pairs={{0,4},{2,6},{4,0},{6,2},{1,5},{3,7},{5,1},{7,3},{8,12},{10,14},{12... | collective-permute-start | bytes 196616 | tf_op jit(solution)/shard_map/ppermute | solution.py:174
  54.1 1.1 %collective-permute-start.23 = (bf16[16,2048]{1,0:T(8,128)(2,1)S(1)}, bf16[16,2048]{1,0:T(8,128)(2,1)S(1)}, u32[]{:S(2)}, u32[]{:S(2)}) collective-permute-start(bf16[16,2048]{1,0:T(8,128)(2,1)S(1)} %get-tuple-element.84), channel_id=1, source_target_pairs={{0,6},{2,4},{4,2},{6,0},{1,7},{3,5},{5,3},{7,1},{8,14},{10,12},{12... | collective-permute-start | bytes 196616 | tf_op jit(solution)/shard_map/ppermute | solution.py:174
  55.2 4.2 %collective-permute-done.22 = bf16[16,2048]{1,0:T(8,128)(2,1)S(1)} collective-permute-done((bf16[16,2048]{1,0:T(8,128)(2,1)S(1)}, bf16[16,2048]{1,0:T(8,128)(2,1)S(1)}, u32[]{:S(2)}, u32[]{:S(2)}) %collective-permute-start.22) | collective-permute-done | bytes 65568 | tf_op jit(solution)/shard_map/ppermute | solution.py:174
  59.4 0.9 %collective-permute-done.23 = bf16[16,2048]{1,0:T(8,128)(2,1)S(1)} collective-permute-done((bf16[16,2048]{1,0:T(8,128)(2,1)S(1)}, bf16[16,2048]{1,0:T(8,128)(2,1)S(1)}, u32[]{:S(2)}, u32[]{:S(2)}) %collective-permute-start.23) | collective-permute-done | bytes 65568 | tf_op jit(solution)/shard_map/ppermute | solution.py:174
  60.3 0.7 %add_convert_fusion = bf16[16,2048]{1,0:T(8,128)(2,1)} fusion(bf16[16,2048]{1,0:T(8,128)(2,1)S(1)} %collective-permute-done.23, bf16[16,2048]{1,0:T(8,128)(2,1)S(1)} %collective-permute-done.22, f32[16,2048]{1,0:T(8,128)S(1)} %get-tuple-element.81, bf16[16,2048]{1,0:T(8,128)(2,1)S(1)} %collective-permute-done.21), kind=kLoop, calls=%fused_computation | loop fusion | flops 229376 | bytes 393216 | tf_op jit(solution)/shard_map/convert_element_type | solution.py:296
  (44 shorter events, 5.0 us)
Async XLA Ops:
  1.0 7.7 %collective-permute-start.2 = (bf16[16,2048]{1,0:T(8,128)(2,1)S(1)}, bf16[16,2048]{1,0:T(8,128)(2,1)S(1)}, u32[]{:S(2)}, u32[]{:S(2)}) collective-permute-start(bf16[16,2048]{1,0:T(8,128)(2,1)S(1)} %get-tuple-element.45.refs_0_.refs_6_), channel_id=1, source_target_pairs={{0,6},{2,4},{4,2},{6,0},{1,7},{3,5},{5,3},{7,1},{8,14},{10,12},{12... | collective-permute-start | bytes 196616 | tf_op jit(solution)/shard_map/ppermute | solution.py:174
  6.2 5.6 %collective-permute-start.1 = (bf16[16,2048]{1,0:T(8,128)(2,1)S(1)}, bf16[16,2048]{1,0:T(8,128)(2,1)S(1)}, u32[]{:S(2)}, u32[]{:S(2)}) collective-permute-start(bf16[16,2048]{1,0:T(8,128)(2,1)S(1)} %get-tuple-element.45.refs_0_.refs_6_), channel_id=1, source_target_pairs={{0,4},{2,6},{4,0},{6,2},{1,5},{3,7},{5,1},{7,3},{8,12},{10,14},{12... | collective-permute-start | bytes 196616 | tf_op jit(solution)/shard_map/ppermute | solution.py:174
  6.2 5.6 %collective-permute-start = (bf16[16,2048]{1,0:T(8,128)(2,1)S(1)}, bf16[16,2048]{1,0:T(8,128)(2,1)S(1)}, u32[]{:S(2)}, u32[]{:S(2)}) collective-permute-start(bf16[16,2048]{1,0:T(8,128)(2,1)S(1)} %get-tuple-element.45.refs_0_.refs_6_), channel_id=1, source_target_pairs={{0,2},{2,0},{4,6},{6,4},{1,3},{3,1},{5,7},{7,5},{8,10},{10,8},{12,... | collective-permute-start | bytes 196616 | tf_op jit(solution)/shard_map/ppermute | solution.py:174
  18.2 4.1 %collective-permute-start.3 = (f32[32,6656]{1,0:T(8,128)S(1)}, f32[32,6656]{1,0:T(8,128)S(1)}, u32[]{:S(2)}, u32[]{:S(2)}) collective-permute-start(f32[32,6656]{1,0:T(8,128)S(1)} %get-tuple-element.48), channel_id=1, source_target_pairs={{0,1},{1,0},{2,3},{3,2},{4,5},{5,4},{6,7},{7,6},{8,9},{9,8},{10,11... | collective-permute-start | bytes 2555912 | tf_op jit(solution)/shard_map/ppermute | solution.py:174
  22.5 14.6 %collective-permute-start.4 = (bf16[32,6656]{1,0:T(8,128)(2,1)S(1)}, bf16[32,6656]{1,0:T(8,128)(2,1)S(1)}, u32[]{:S(2)}, u32[]{:S(2)}) collective-permute-start(bf16[32,6656]{1,0:T(8,128)(2,1)S(1)} %get-tuple-element.53), channel_id=1, source_target_pairs={{0,8},{8,0},{1,9},{9,1},{2,10},{10,2},{3,11},{11,3},{4,12},{12,4},... | collective-permute-start | bytes 1277960 | tf_op jit(solution)/shard_map/ppermute | solution.py:174
  24.0 4.5 %collective-permute-start.8 = (f32[32,2048]{1,0:T(8,128)S(1)}, f32[32,2048]{1,0:T(8,128)S(1)}, u32[]{:S(2)}, u32[]{:S(2)}) collective-permute-start(f32[32,2048]{1,0:T(8,128)S(1)} %get-tuple-element.59), channel_id=1, source_target_pairs={{0,1},{1,0},{2,3},{3,2},{4,5},{5,4},{6,7},{7,6},{8,9},{9,8},{10,11... | collective-permute-start | bytes 786440 | tf_op jit(solution)/shard_map/ppermute | solution.py:174
  24.2 4.3 %collective-permute-start.7 = (f32[32,2048]{1,0:T(8,128)S(1)}, f32[32,2048]{1,0:T(8,128)S(1)}, u32[]{:S(2)}, u32[]{:S(2)}) collective-permute-start(f32[32,2048]{1,0:T(8,128)S(1)} %get-tuple-element.51.refs_2_), channel_id=1, source_target_pairs={{0,1},{1,0},{2,3},{3,2},{4,5},{5,4},{6,7},{7,6},{8,9},{9,8},{10,11... | collective-permute-start | bytes 786440 | tf_op jit(solution)/shard_map/ppermute | solution.py:174
  27.9 9.2 %collective-permute-start.5 = (f32[32,1536]{1,0:T(8,128)S(1)}, f32[32,1536]{1,0:T(8,128)S(1)}, u32[]{:S(2)}, u32[]{:S(2)}) collective-permute-start(f32[32,1536]{1,0:T(8,128)S(1)} %get-tuple-element.56), channel_id=1, source_target_pairs={{0,1},{1,0},{2,3},{3,2},{4,5},{5,4},{6,7},{7,6},{8,9},{9,8},{10,11... | collective-permute-start | bytes 589832 | tf_op jit(solution)/shard_map/ppermute | solution.py:174
  28.2 8.9 %collective-permute-start.6 = (f32[32,1024]{1,0:T(8,128)S(1)}, f32[32,1024]{1,0:T(8,128)S(1)}, u32[]{:S(2)}, u32[]{:S(2)}) collective-permute-start(f32[32,1024]{1,0:T(8,128)S(1)} %get-tuple-element.57.refs_3_), channel_id=1, source_target_pairs={{0,1},{1,0},{2,3},{3,2},{4,5},{5,4},{6,7},{7,6},{8,9},{9,8},{10,11... | collective-permute-start | bytes 393224 | tf_op jit(solution)/shard_map/ppermute | solution.py:174
  28.6 9.4 %collective-permute-start.11 = (bf16[32,2048]{1,0:T(8,128)(2,1)S(1)}, bf16[32,2048]{1,0:T(8,128)(2,1)S(1)}, u32[]{:S(2)}, u32[]{:S(2)}) collective-permute-start(bf16[32,2048]{1,0:T(8,128)(2,1)S(1)} %get-tuple-element.66), channel_id=1, source_target_pairs={{0,8},{8,0},{1,9},{9,1},{2,10},{10,2},{3,11},{11,3},{4,12},{12,4},... | collective-permute-start | bytes 393224 | tf_op jit(solution)/shard_map/ppermute | solution.py:174
  29.2 11.2 %collective-permute-start.10 = (bf16[32,2048]{1,0:T(8,128)(2,1)S(1)}, bf16[32,2048]{1,0:T(8,128)(2,1)S(1)}, u32[]{:S(2)}, u32[]{:S(2)}) collective-permute-start(bf16[32,2048]{1,0:T(8,128)(2,1)S(1)} %get-tuple-element.65), channel_id=1, source_target_pairs={{0,8},{8,0},{1,9},{9,1},{2,10},{10,2},{3,11},{11,3},{4,12},{12,4},... | collective-permute-start | bytes 393224 | tf_op jit(solution)/shard_map/ppermute | solution.py:174
  38.1 3.0 %collective-permute-start.15 = (bf16[16,2048]{1,0:T(8,128)(2,1)S(1)}, bf16[16,2048]{1,0:T(8,128)(2,1)S(1)}, u32[]{:S(2)}, u32[]{:S(2)}) collective-permute-start(bf16[16,2048]{1,0:T(8,128)(2,1)S(1)} %get-tuple-element.71.refs_1_), channel_id=1, source_target_pairs={{0,1},{1,0},{2,3},{3,2},{4,5},{5,4},{6,7},{7,6},{8,9},{9,8},{10,11... | collective-permute-start | bytes 196616 | tf_op jit(solution)/shard_map/ppermute | solution.py:174
  38.2 4.4 %collective-permute-start.14 = (bf16[16,2048]{1,0:T(8,128)(2,1)S(1)}, bf16[16,2048]{1,0:T(8,128)(2,1)S(1)}, u32[]{:S(2)}, u32[]{:S(2)}) collective-permute-start(bf16[16,2048]{1,0:T(8,128)(2,1)S(1)} %get-tuple-element.67.refs_4_.refs_0_), channel_id=1, source_target_pairs={{0,1},{1,0},{2,3},{3,2},{4,5},{5,4},{6,7},{7,6},{8,9},{9,8},{10,11... | collective-permute-start | bytes 196616 | tf_op jit(solution)/shard_map/ppermute | solution.py:174
  38.7 5.9 %collective-permute-start.16 = (bf16[32,1536]{1,0:T(8,128)(2,1)S(1)}, bf16[32,1536]{1,0:T(8,128)(2,1)S(1)}, u32[]{:S(2)}, u32[]{:S(2)}) collective-permute-start(bf16[32,1536]{1,0:T(8,128)(2,1)S(1)} %get-tuple-element.74), channel_id=1, source_target_pairs={{0,8},{8,0},{1,9},{9,1},{2,10},{10,2},{3,11},{11,3},{4,12},{12,4},... | collective-permute-start | bytes 294920 | tf_op jit(solution)/shard_map/ppermute | solution.py:174
  40.5 4.8 %collective-permute-start.13 = (bf16[16,2048]{1,0:T(8,128)(2,1)S(1)}, bf16[16,2048]{1,0:T(8,128)(2,1)S(1)}, u32[]{:S(2)}, u32[]{:S(2)}) collective-permute-start(bf16[16,2048]{1,0:T(8,128)(2,1)S(1)} %get-tuple-element.69.refs_1_), channel_id=1, source_target_pairs={{0,1},{1,0},{2,3},{3,2},{4,5},{5,4},{6,7},{7,6},{8,9},{9,8},{10,11... | collective-permute-start | bytes 196616 | tf_op jit(solution)/shard_map/ppermute | solution.py:174
  40.6 4.7 %collective-permute-start.12 = (bf16[16,2048]{1,0:T(8,128)(2,1)S(1)}, bf16[16,2048]{1,0:T(8,128)(2,1)S(1)}, u32[]{:S(2)}, u32[]{:S(2)}) collective-permute-start(bf16[16,2048]{1,0:T(8,128)(2,1)S(1)} %get-tuple-element.68.refs_5_.refs_0_), channel_id=1, source_target_pairs={{0,1},{1,0},{2,3},{3,2},{4,5},{5,4},{6,7},{7,6},{8,9},{9,8},{10,11... | collective-permute-start | bytes 196616 | tf_op jit(solution)/shard_map/ppermute | solution.py:174
  41.1 6.2 %collective-permute-start.9 = (bf16[32,1024]{1,0:T(8,128)(2,1)S(1)}, bf16[32,1024]{1,0:T(8,128)(2,1)S(1)}, u32[]{:S(2)}, u32[]{:S(2)}) collective-permute-start(bf16[32,1024]{1,0:T(8,128)(2,1)S(1)} %get-tuple-element.63), channel_id=1, source_target_pairs={{0,8},{8,0},{1,9},{9,1},{2,10},{10,2},{3,11},{11,3},{4,12},{12,4},... | collective-permute-start | bytes 196616 | tf_op jit(solution)/shard_map/ppermute | solution.py:174
  44.7 3.2 %collective-permute-start.20 = (bf16[16,1536]{1,0:T(8,128)(2,1)S(1)}, bf16[16,1536]{1,0:T(8,128)(2,1)S(1)}, u32[]{:S(2)}, u32[]{:S(2)}) collective-permute-start(bf16[16,1536]{1,0:T(8,128)(2,1)S(1)} %get-tuple-element.79.refs_1_), channel_id=1, source_target_pairs={{0,1},{1,0},{2,3},{3,2},{4,5},{5,4},{6,7},{7,6},{8,9},{9,8},{10,11... | collective-permute-start | bytes 147464 | tf_op jit(solution)/shard_map/ppermute | solution.py:174
  44.7 3.2 %collective-permute-start.19 = (bf16[16,1536]{1,0:T(8,128)(2,1)S(1)}, bf16[16,1536]{1,0:T(8,128)(2,1)S(1)}, u32[]{:S(2)}, u32[]{:S(2)}) collective-permute-start(bf16[16,1536]{1,0:T(8,128)(2,1)S(1)} %get-tuple-element.75.refs_6_.refs_0_), channel_id=1, source_target_pairs={{0,1},{1,0},{2,3},{3,2},{4,5},{5,4},{6,7},{7,6},{8,9},{9,8},{10,11... | collective-permute-start | bytes 147464 | tf_op jit(solution)/shard_map/ppermute | solution.py:174
  47.3 2.2 %collective-permute-start.18 = (bf16[16,1024]{1,0:T(8,128)(2,1)S(1)}, bf16[16,1024]{1,0:T(8,128)(2,1)S(1)}, u32[]{:S(2)}, u32[]{:S(2)}) collective-permute-start(bf16[16,1024]{1,0:T(8,128)(2,1)S(1)} %get-tuple-element.77.refs_1_), channel_id=1, source_target_pairs={{0,1},{1,0},{2,3},{3,2},{4,5},{5,4},{6,7},{7,6},{8,9},{9,8},{10,11... | collective-permute-start | bytes 98312 | tf_op jit(solution)/shard_map/ppermute | solution.py:174
  47.5 2.1 %collective-permute-start.17 = (bf16[16,1024]{1,0:T(8,128)(2,1)S(1)}, bf16[16,1024]{1,0:T(8,128)(2,1)S(1)}, u32[]{:S(2)}, u32[]{:S(2)}) collective-permute-start(bf16[16,1024]{1,0:T(8,128)(2,1)S(1)} %get-tuple-element.76.refs_6_.refs_0_), channel_id=1, source_target_pairs={{0,1},{1,0},{2,3},{3,2},{4,5},{5,4},{6,7},{7,6},{8,9},{9,8},{10,11... | collective-permute-start | bytes 98312 | tf_op jit(solution)/shard_map/ppermute | solution.py:174
  50.8 4.5 %collective-permute-start.21 = (bf16[16,2048]{1,0:T(8,128)(2,1)S(1)}, bf16[16,2048]{1,0:T(8,128)(2,1)S(1)}, u32[]{:S(2)}, u32[]{:S(2)}) collective-permute-start(bf16[16,2048]{1,0:T(8,128)(2,1)S(1)} %get-tuple-element.82), channel_id=1, source_target_pairs={{0,2},{2,0},{4,6},{6,4},{1,3},{3,1},{5,7},{7,5},{8,10},{10,8},{12,... | collective-permute-start | bytes 196616 | tf_op jit(solution)/shard_map/ppermute | solution.py:174
  51.9 7.5 %collective-permute-start.22 = (bf16[16,2048]{1,0:T(8,128)(2,1)S(1)}, bf16[16,2048]{1,0:T(8,128)(2,1)S(1)}, u32[]{:S(2)}, u32[]{:S(2)}) collective-permute-start(bf16[16,2048]{1,0:T(8,128)(2,1)S(1)} %get-tuple-element.83), channel_id=1, source_target_pairs={{0,4},{2,6},{4,0},{6,2},{1,5},{3,7},{5,1},{7,3},{8,12},{10,14},{12... | collective-permute-start | bytes 196616 | tf_op jit(solution)/shard_map/ppermute | solution.py:174
  54.1 6.2 %collective-permute-start.23 = (bf16[16,2048]{1,0:T(8,128)(2,1)S(1)}, bf16[16,2048]{1,0:T(8,128)(2,1)S(1)}, u32[]{:S(2)}, u32[]{:S(2)}) collective-permute-start(bf16[16,2048]{1,0:T(8,128)(2,1)S(1)} %get-tuple-element.84), channel_id=1, source_target_pairs={{0,6},{2,4},{4,2},{6,0},{1,7},{3,5},{5,3},{7,1},{8,14},{10,12},{12... | collective-permute-start | bytes 196616 | tf_op jit(solution)/shard_map/ppermute | solution.py:174
  (1 other events, 11.8 us)

commit v6 on v5

--- a/solution.py
+++ b/solution.py
@@ -9,8 +9,8 @@
 
 BF16, F32 = jnp.bfloat16, jnp.float32
 TILE = 512
-GATE = (8, 5)
-DOWN = (4, 4, 3, 2)
+GATE = (9, 4)
+DOWN = (4, 5, 4)
 PAIR_TYPE = F32
 COST = 1
 SPLIT = 2
@@ -275,14 +275,14 @@
         gates.append((parts, inner))
         if j == 0:
             (ups,) = pair_sum(ups, [(0, columns)], [(0, columns)])
-    sums = pair_sum(*gates[0], gates[0][1])
+    sums = []
+    for parts, inner in gates:
+        sums += pair_sum(parts, inner, inner)
     if n > 1:
         late = list(range(1, n))
-        _, more = load(x, down_of(*late), COST * 2 * bytes_of(down_of(*late)))
+        _, more = load(x, down_of(*late), 0)
         down.update(zip(late, more))
     load(x, [], 0, ups[1:])
-    for parts, inner in gates[1:]:
-        sums += pair_sum(parts, inner, inner)
     hiddens = [activate(ups, sums[j], *chunks[j]) for j in range(min(n, 2))]
     total = []
     for j in range(n):

time: 61.2 us -> 60.7 us (level)
  starting transfers between devices: 20.3 us -> 17.4 us
  waiting for transfers between devices: 11 us -> 13.6 us
    ppermute x24 -> x20, starting transfers between devices: 20.3 us -> 17.4 us  [send(): lax.ppermute(value, axis, [(i, i ^ k if paired else (i + k) % n) for i in...]
    ppermute x24 -> x20, waiting for transfers between devices: 11 us -> 13.6 us  [send(): lax.ppermute(value, axis, [(i, i ^ k if paired else (i + k) % n) for i in...]
    pallas_call x17 -> x15, Pallas kernels: 28.8 us -> 28.6 us  [call(): pl.pallas_call(kernel, out_shape=tuple(outs) + tuple(fetched), in_specs=[...]
  transfers between devices with their start and end apart: 24 -> 20, of which waited for: 6 -> 6; matrix products, arithmetic and copies ran while one was open for 0% -> 0% of each run, Pallas kernels for 33% -> 32%
where the time goes in v6:
time: 60.7 us; the launch traced here: 60.5 us
  Pallas kernels  28.6 us (47%)
  starting transfers between devices  17.4 us (29%)
  waiting for transfers between devices  13.6 us (22%)
  other arithmetic  0.67 us (1%)
    pallas_call x15, Pallas kernels, call(): pl.pallas_call(kernel, out_shape=tuple(outs) + tuple(fetched), in_specs=[...  28.6 us
    ppermute x20, starting transfers between devices, send(): lax.ppermute(value, axis, [(i, i ^ k if paired else (i + k) % n) for i in...  17.4 us
    ppermute x20, waiting for transfers between devices, send(): lax.ppermute(value, axis, [(i, i ^ k if paired else (i + k) % n) for i in...  13.6 us
  transfers between devices with their start and end apart: 20, of which 6 were waited for; matrix products, arithmetic and copies ran while one was open for 0% of the time, Pallas kernels for 32%

profile of v6, /device:TPU:0, one launch (start us, length us, event | category | flops | bytes accessed | tf_op | source)
XLA Modules:
  0.0 60.5 jit_solution(13277670058987673860)
XLA Ops:
  0.0 1.0 %shard_map.46 = (bf16[16,2048]{1,0:T(8,128)(2,1)S(1)}, bf16[16,2048]{1,0:T(8,128)(2,1)S(1)}) custom-call(bf16[16,2048]{1,0:T(8,128)(2,1)} %refs_0_.1, bf16[6656,2048]{1,0:T(8,128)(2,1)} %refs_3_.5), custom_call_target="tpu_custom_call" | custom-call | bytes 54525952 | tf_op jit(solution)/shard_map/pallas_call | solution.py:70
  1.0 5.1 %collective-permute-start.2 = (bf16[16,2048]{1,0:T(8,128)(2,1)S(1)}, bf16[16,2048]{1,0:T(8,128)(2,1)S(1)}, u32[]{:S(2)}, u32[]{:S(2)}) collective-permute-start(bf16[16,2048]{1,0:T(8,128)(2,1)S(1)} %get-tuple-element.39.refs_0_.refs_6_), channel_id=1, source_target_pairs={{0,6},{2,4},{4,2},{6,0},{1,7},{3,5},{5,3},{7,1},{8,14},{10,12},{12... | collective-permute-start | bytes 196616 | tf_op jit(solution)/shard_map/ppermute | solution.py:174
  6.2 0.6 %collective-permute-start = (bf16[16,2048]{1,0:T(8,128)(2,1)S(1)}, bf16[16,2048]{1,0:T(8,128)(2,1)S(1)}, u32[]{:S(2)}, u32[]{:S(2)}) collective-permute-start(bf16[16,2048]{1,0:T(8,128)(2,1)S(1)} %get-tuple-element.39.refs_0_.refs_6_), channel_id=1, source_target_pairs={{0,2},{2,0},{4,6},{6,4},{1,3},{3,1},{5,7},{7,5},{8,10},{10,8},{12,... | collective-permute-start | bytes 196616 | tf_op jit(solution)/shard_map/ppermute | solution.py:174
  6.8 1.9 %collective-permute-done.2.refs_3_ = bf16[16,2048]{1,0:T(8,128)(2,1)S(1)} collective-permute-done((bf16[16,2048]{1,0:T(8,128)(2,1)S(1)}, bf16[16,2048]{1,0:T(8,128)(2,1)S(1)}, u32[]{:S(2)}, u32[]{:S(2)}) %collective-permute-start.2) | collective-permute-done | bytes 65568 | tf_op jit(solution)/shard_map/ppermute | solution.py:174
  8.7 3.0 %collective-permute-done.1.refs_2_ = bf16[16,2048]{1,0:T(8,128)(2,1)S(1)} collective-permute-done((bf16[16,2048]{1,0:T(8,128)(2,1)S(1)}, bf16[16,2048]{1,0:T(8,128)(2,1)S(1)}, u32[]{:S(2)}, u32[]{:S(2)}) %collective-permute-start.1) | collective-permute-done | bytes 65568 | tf_op jit(solution)/shard_map/ppermute | solution.py:174
  11.8 6.5 %shard_map.47 = (f32[32,6656]{1,0:T(8,128)S(1)}, f32[32,6656]{1,0:T(8,128)S(1)}, bf16[64,2048]{1,0:T(8,128)(2,1)S(1)}, bf16[2048,4608]{1,0:T(8,128)(2,1)S(1)}) custom-call(bf16[16,2048]{1,0:T(8,128)(2,1)S(1)} %get-tuple-element.39.refs_0_.refs_6_, bf16[16,2048]{1,0:T(8,128)(2,1)S(1)} %collective-permute-done.refs_1_, ...), custom_call_target="tpu_custom_call" | custom-call | flops 1744830464 | bytes 37748736 | tf_op jit(solution)/shard_map/pallas_call | solution.py:70
  18.3 4.4 %shard_map.48 = (f32[32,4608]{1,0:T(8,128)S(1)}, f32[32,2048]{1,0:T(8,128)S(1)}, f32[32,2560]{1,0:T(8,128)S(1)}, bf16[2048,2048]{1,0:T(8,128)(2,1)S(1)}) custom-call(bf16[64,2048]{1,0:T(8,128)(2,1)S(1)} %get-tuple-element.43.refs_0_.refs_2_, bf16[2048,4608]{1,0:T(8,128)(2,1)S(1)} %get-tuple-element.44.refs_1_, ...), custom_call_target="tpu_custom_call" | custom-call | flops 1207959552 | bytes 16777216 | tf_op jit(solution)/shard_map/pallas_call | solution.py:70
  23.4 1.6 %collective-permute-start.4 = (bf16[32,6656]{1,0:T(8,128)(2,1)S(1)}, bf16[32,6656]{1,0:T(8,128)(2,1)S(1)}, u32[]{:S(2)}, u32[]{:S(2)}) collective-permute-start(bf16[32,6656]{1,0:T(8,128)(2,1)S(1)} %get-tuple-element.47), channel_id=1, source_target_pairs={{0,8},{8,0},{1,9},{9,1},{2,10},{10,2},{3,11},{11,3},{4,12},{12,4},... | collective-permute-start | bytes 1277960 | tf_op jit(solution)/shard_map/ppermute | solution.py:174
  25.0 3.4 %shard_map.50 = (f32[32,2048]{1,0:T(8,128)S(1)}, f32[32,2048]{1,0:T(8,128)S(1)}, bf16[2048,2048]{1,0:T(8,128)(2,1)S(1)}) custom-call(bf16[64,2048]{1,0:T(8,128)(2,1)S(1)} %get-tuple-element.43.refs_0_.refs_2_, bf16[2048,2048]{1,0:T(8,128)(2,1)S(1)} %get-tuple-element.48.refs_1_, f32[32,6656]{1,0:T(8,128)S(1)} %get-tuple-element.46.refs_2_.refs_0_, ...), custom_call_target="tpu_custom_call" | custom-call | flops 536870912 | bytes 16777216 | tf_op jit(solution)/shard_map/pallas_call | solution.py:70
  29.1 0.6 collective-permute-start.9
  29.7 1.5 %collective-permute-start.12 = (bf16[32,2560]{1,0:T(8,128)(2,1)S(1)}, bf16[32,2560]{1,0:T(8,128)(2,1)S(1)}, u32[]{:S(2)}, u32[]{:S(2)}) collective-permute-start(bf16[32,2560]{1,0:T(8,128)(2,1)S(1)} %get-tuple-element.62), channel_id=1, source_target_pairs={{0,8},{8,0},{1,9},{9,1},{2,10},{10,2},{3,11},{11,3},{4,12},{12,4},... | collective-permute-start | bytes 491528 | tf_op jit(solution)/shard_map/ppermute | solution.py:174
  31.2 0.6 collective-permute-start.8
  31.8 6.4 %shard_map.53 = (bf16[64,2048]{1,0:T(8,128)(2,1)S(1)}, bf16[2560,2048]{1,0:T(8,128)(2,1)S(1)}, bf16[2048,2048]{1,0:T(8,128)(2,1)S(1)}) custom-call(bf16[64,2048]{1,0:T(8,128)(2,1)S(1)} %get-tuple-element.43.refs_0_.refs_2_, f32[32,2048]{1,0:T(8,128)S(1)} %get-tuple-element.54.refs_1_.refs_2_, bf16[6656,2048]{1,0:T(8,128)(2,1)} %refs_3_.5, ...), custom_call_target="tpu_custom_call" | custom-call | tf_op jit(solution)/shard_map/pallas_call | solution.py:70
  38.3 0.7 %collective-permute-done.9.refs_3_ = bf16[32,2048]{1,0:T(8,128)(2,1)S(1)} collective-permute-done((bf16[32,2048]{1,0:T(8,128)(2,1)S(1)}, bf16[32,2048]{1,0:T(8,128)(2,1)S(1)}, u32[]{:S(2)}, u32[]{:S(2)}) %collective-permute-start.9) | collective-permute-done | bytes 131104 | tf_op jit(solution)/shard_map/ppermute | solution.py:174
  39.7 2.8 %collective-permute-done.12.refs_3_ = bf16[32,2560]{1,0:T(8,128)(2,1)S(1)} collective-permute-done((bf16[32,2560]{1,0:T(8,128)(2,1)S(1)}, bf16[32,2560]{1,0:T(8,128)(2,1)S(1)}, u32[]{:S(2)}, u32[]{:S(2)}) %collective-permute-start.12) | collective-permute-done | bytes 163872 | tf_op jit(solution)/shard_map/ppermute | solution.py:174
  43.2 2.0 %shard_map.57.refs_4_.refs_5_ = f32[64,2048]{1,0:T(8,128)S(1)} custom-call(bf16[16,2048]{1,0:T(8,128)(2,1)S(1)} %get-tuple-element.58.refs_4_.refs_0_, bf16[16,2048]{1,0:T(8,128)(2,1)S(1)} %get-tuple-element.59.refs_1_, bf16[16,2048]{1,0:T(8,128)(2,1)S(1)} %collective-permute-done.10.refs_2_, bf16[16,2048]{1,0:T(8,128)(2,1)S(1)} %collective-permute-done.11.refs_3_, ...), custom_call_target="tpu_custom_call" | custom-call | flops 536870912 | tf_op jit(solution)/shard_map/pallas_call | solution.py:70
  45.9 2.3 %shard_map.59.refs_5_.refs_6_ = f32[64,2048]{1,0:T(8,128)S(1)} custom-call(bf16[16,2560]{1,0:T(8,128)(2,1)S(1)} %get-tuple-element.63.refs_5_.refs_0_, bf16[16,2560]{1,0:T(8,128)(2,1)S(1)} %get-tuple-element.67.refs_1_, bf16[16,2560]{1,0:T(8,128)(2,1)S(1)} %collective-permute-done.15.refs_2_, bf16[16,2560]{1,0:T(8,128)(2,1)S(1)} %collective-permute-done.16.refs_3_, ...), custom_call_target="tpu_custom_call" | custom-call | flops 671088640 | tf_op jit(solution)/shard_map/pallas_call | solution.py:70
  48.3 2.0 %shard_map.60 = (f32[16,2048]{1,0:T(8,128)S(1)}, bf16[16,2048]{1,0:T(8,128)(2,1)S(1)}, bf16[16,2048]{1,0:T(8,128)(2,1)S(1)}, bf16[16,2048]{1,0:T(8,128)(2,1)S(1)}) custom-call(bf16[16,2048]{1,0:T(8,128)(2,1)S(1)} %get-tuple-element.64.refs_6_.refs_0_, bf16[16,2048]{1,0:T(8,128)(2,1)S(1)} %get-tuple-element.65.refs_1_, ...), custom_call_target="tpu_custom_call" | custom-call | flops 536870912 | tf_op jit(solution)/shard_map/pallas_call | solution.py:70
  50.3 1.1 %collective-permute-start.17 = (bf16[16,2048]{1,0:T(8,128)(2,1)S(1)}, bf16[16,2048]{1,0:T(8,128)(2,1)S(1)}, u32[]{:S(2)}, u32[]{:S(2)}) collective-permute-start(bf16[16,2048]{1,0:T(8,128)(2,1)S(1)} %get-tuple-element.70), channel_id=1, source_target_pairs={{0,2},{2,0},{4,6},{6,4},{1,3},{3,1},{5,7},{7,5},{8,10},{10,8},{12,... | collective-permute-start | bytes 196616 | tf_op jit(solution)/shard_map/ppermute | solution.py:174
  51.4 2.2 %collective-permute-start.18 = (bf16[16,2048]{1,0:T(8,128)(2,1)S(1)}, bf16[16,2048]{1,0:T(8,128)(2,1)S(1)}, u32[]{:S(2)}, u32[]{:S(2)}) collective-permute-start(bf16[16,2048]{1,0:T(8,128)(2,1)S(1)} %get-tuple-element.71), channel_id=1, source_target_pairs={{0,4},{2,6},{4,0},{6,2},{1,5},{3,7},{5,1},{7,3},{8,12},{10,14},{12... | collective-permute-start | bytes 196616 | tf_op jit(solution)/shard_map/ppermute | solution.py:174
  53.6 1.1 %collective-permute-start.19 = (bf16[16,2048]{1,0:T(8,128)(2,1)S(1)}, bf16[16,2048]{1,0:T(8,128)(2,1)S(1)}, u32[]{:S(2)}, u32[]{:S(2)}) collective-permute-start(bf16[16,2048]{1,0:T(8,128)(2,1)S(1)} %get-tuple-element.72), channel_id=1, source_target_pairs={{0,6},{2,4},{4,2},{6,0},{1,7},{3,5},{5,3},{7,1},{8,14},{10,12},{12... | collective-permute-start | bytes 196616 | tf_op jit(solution)/shard_map/ppermute | solution.py:174
  54.8 4.2 %collective-permute-done.18 = bf16[16,2048]{1,0:T(8,128)(2,1)S(1)} collective-permute-done((bf16[16,2048]{1,0:T(8,128)(2,1)S(1)}, bf16[16,2048]{1,0:T(8,128)(2,1)S(1)}, u32[]{:S(2)}, u32[]{:S(2)}) %collective-permute-start.18) | collective-permute-done | bytes 65568 | tf_op jit(solution)/shard_map/ppermute | solution.py:174
  59.0 0.9 %collective-permute-done.19 = bf16[16,2048]{1,0:T(8,128)(2,1)S(1)} collective-permute-done((bf16[16,2048]{1,0:T(8,128)(2,1)S(1)}, bf16[16,2048]{1,0:T(8,128)(2,1)S(1)}, u32[]{:S(2)}, u32[]{:S(2)}) %collective-permute-start.19) | collective-permute-done | bytes 65568 | tf_op jit(solution)/shard_map/ppermute | solution.py:174
  59.8 0.7 %add_convert_fusion = bf16[16,2048]{1,0:T(8,128)(2,1)} fusion(bf16[16,2048]{1,0:T(8,128)(2,1)S(1)} %collective-permute-done.19, bf16[16,2048]{1,0:T(8,128)(2,1)S(1)} %collective-permute-done.18, f32[16,2048]{1,0:T(8,128)S(1)} %get-tuple-element.69, bf16[16,2048]{1,0:T(8,128)(2,1)S(1)} %collective-permute-done.17), kind=kLoop, calls=%fused_computation | loop fusion | flops 229376 | bytes 393216 | tf_op jit(solution)/shard_map/convert_element_type | solution.py:296
  (34 shorter events, 3.6 us)
Async XLA Ops:
  0.0 11.8 %copy-start = (bf16[2048,6656]{1,0:T(8,128)(2,1)S(1)}, bf16[2048,6656]{1,0:T(8,128)(2,1)}, u32[]{:S(2)}) copy-start(bf16[2048,6656]{1,0:T(8,128)(2,1)} %refs_4_.1) | copy-start | bytes 81788928
  1.0 7.7 %collective-permute-start.2 = (bf16[16,2048]{1,0:T(8,128)(2,1)S(1)}, bf16[16,2048]{1,0:T(8,128)(2,1)S(1)}, u32[]{:S(2)}, u32[]{:S(2)}) collective-permute-start(bf16[16,2048]{1,0:T(8,128)(2,1)S(1)} %get-tuple-element.39.refs_0_.refs_6_), channel_id=1, source_target_pairs={{0,6},{2,4},{4,2},{6,0},{1,7},{3,5},{5,3},{7,1},{8,14},{10,12},{12... | collective-permute-start | bytes 196616 | tf_op jit(solution)/shard_map/ppermute | solution.py:174
  6.2 5.6 %collective-permute-start.1 = (bf16[16,2048]{1,0:T(8,128)(2,1)S(1)}, bf16[16,2048]{1,0:T(8,128)(2,1)S(1)}, u32[]{:S(2)}, u32[]{:S(2)}) collective-permute-start(bf16[16,2048]{1,0:T(8,128)(2,1)S(1)} %get-tuple-element.39.refs_0_.refs_6_), channel_id=1, source_target_pairs={{0,4},{2,6},{4,0},{6,2},{1,5},{3,7},{5,1},{7,3},{8,12},{10,14},{12... | collective-permute-start | bytes 196616 | tf_op jit(solution)/shard_map/ppermute | solution.py:174
  6.2 5.6 %collective-permute-start = (bf16[16,2048]{1,0:T(8,128)(2,1)S(1)}, bf16[16,2048]{1,0:T(8,128)(2,1)S(1)}, u32[]{:S(2)}, u32[]{:S(2)}) collective-permute-start(bf16[16,2048]{1,0:T(8,128)(2,1)S(1)} %get-tuple-element.39.refs_0_.refs_6_), channel_id=1, source_target_pairs={{0,2},{2,0},{4,6},{6,4},{1,3},{3,1},{5,7},{7,5},{8,10},{10,8},{12,... | collective-permute-start | bytes 196616 | tf_op jit(solution)/shard_map/ppermute | solution.py:174
  18.2 5.1 %collective-permute-start.3 = (f32[32,6656]{1,0:T(8,128)S(1)}, f32[32,6656]{1,0:T(8,128)S(1)}, u32[]{:S(2)}, u32[]{:S(2)}) collective-permute-start(f32[32,6656]{1,0:T(8,128)S(1)} %get-tuple-element.42), channel_id=1, source_target_pairs={{0,1},{1,0},{2,3},{3,2},{4,5},{5,4},{6,7},{7,6},{8,9},{9,8},{10,11... | collective-permute-start | bytes 2555912 | tf_op jit(solution)/shard_map/ppermute | solution.py:174
  22.8 6.2 %collective-permute-start.7 = (f32[32,2560]{1,0:T(8,128)S(1)}, f32[32,2560]{1,0:T(8,128)S(1)}, u32[]{:S(2)}, u32[]{:S(2)}) collective-permute-start(f32[32,2560]{1,0:T(8,128)S(1)} %get-tuple-element.52), channel_id=1, source_target_pairs={{0,1},{1,0},{2,3},{3,2},{4,5},{5,4},{6,7},{7,6},{8,9},{9,8},{10,11... | collective-permute-start | bytes 983048 | tf_op jit(solution)/shard_map/ppermute | solution.py:174
  23.4 14.8 %collective-permute-start.4 = (bf16[32,6656]{1,0:T(8,128)(2,1)S(1)}, bf16[32,6656]{1,0:T(8,128)(2,1)S(1)}, u32[]{:S(2)}, u32[]{:S(2)}) collective-permute-start(bf16[32,6656]{1,0:T(8,128)(2,1)S(1)} %get-tuple-element.47), channel_id=1, source_target_pairs={{0,8},{8,0},{1,9},{9,1},{2,10},{10,2},{3,11},{11,3},{4,12},{12,4},... | collective-permute-start | bytes 1277960 | tf_op jit(solution)/shard_map/ppermute | solution.py:174
  25.0 4.0 %collective-permute-start.6 = (f32[32,2048]{1,0:T(8,128)S(1)}, f32[32,2048]{1,0:T(8,128)S(1)}, u32[]{:S(2)}, u32[]{:S(2)}) collective-permute-start(f32[32,2048]{1,0:T(8,128)S(1)} %get-tuple-element.45.refs_2_), channel_id=1, source_target_pairs={{0,1},{1,0},{2,3},{3,2},{4,5},{5,4},{6,7},{7,6},{8,9},{9,8},{10,11... | collective-permute-start | bytes 786440 | tf_op jit(solution)/shard_map/ppermute | solution.py:174
  28.4 2.8 %collective-permute-start.5 = (f32[32,2048]{1,0:T(8,128)S(1)}, f32[32,2048]{1,0:T(8,128)S(1)}, u32[]{:S(2)}, u32[]{:S(2)}) collective-permute-start(f32[32,2048]{1,0:T(8,128)S(1)} %get-tuple-element.50), channel_id=1, source_target_pairs={{0,1},{1,0},{2,3},{3,2},{4,5},{5,4},{6,7},{7,6},{8,9},{9,8},{10,11... | collective-permute-start | bytes 786440 | tf_op jit(solution)/shard_map/ppermute | solution.py:174
  29.1 9.9 %collective-permute-start.9 = (bf16[32,2048]{1,0:T(8,128)(2,1)S(1)}, bf16[32,2048]{1,0:T(8,128)(2,1)S(1)}, u32[]{:S(2)}, u32[]{:S(2)}) collective-permute-start(bf16[32,2048]{1,0:T(8,128)(2,1)S(1)} %get-tuple-element.56), channel_id=1, source_target_pairs={{0,8},{8,0},{1,9},{9,1},{2,10},{10,2},{3,11},{11,3},{4,12},{12,4},... | collective-permute-start | bytes 393224 | tf_op jit(solution)/shard_map/ppermute | solution.py:174
  29.7 12.8 %collective-permute-start.12 = (bf16[32,2560]{1,0:T(8,128)(2,1)S(1)}, bf16[32,2560]{1,0:T(8,128)(2,1)S(1)}, u32[]{:S(2)}, u32[]{:S(2)}) collective-permute-start(bf16[32,2560]{1,0:T(8,128)(2,1)S(1)} %get-tuple-element.62), channel_id=1, source_target_pairs={{0,8},{8,0},{1,9},{9,1},{2,10},{10,2},{3,11},{11,3},{4,12},{12,4},... | collective-permute-start | bytes 491528 | tf_op jit(solution)/shard_map/ppermute | solution.py:174
  31.2 14.0 %collective-permute-start.8 = (bf16[32,2048]{1,0:T(8,128)(2,1)S(1)}, bf16[32,2048]{1,0:T(8,128)(2,1)S(1)}, u32[]{:S(2)}, u32[]{:S(2)}) collective-permute-start(bf16[32,2048]{1,0:T(8,128)(2,1)S(1)} %get-tuple-element.55), channel_id=1, source_target_pairs={{0,8},{8,0},{1,9},{9,1},{2,10},{10,2},{3,11},{11,3},{4,12},{12,4},... | collective-permute-start | bytes 393224 | tf_op jit(solution)/shard_map/ppermute | solution.py:174
  39.1 4.1 %collective-permute-start.11 = (bf16[16,2048]{1,0:T(8,128)(2,1)S(1)}, bf16[16,2048]{1,0:T(8,128)(2,1)S(1)}, u32[]{:S(2)}, u32[]{:S(2)}) collective-permute-start(bf16[16,2048]{1,0:T(8,128)(2,1)S(1)} %get-tuple-element.59.refs_1_), channel_id=1, source_target_pairs={{0,1},{1,0},{2,3},{3,2},{4,5},{5,4},{6,7},{7,6},{8,9},{9,8},{10,11... | collective-permute-start | bytes 196616 | tf_op jit(solution)/shard_map/ppermute | solution.py:174
  39.2 4.0 %collective-permute-start.10 = (bf16[16,2048]{1,0:T(8,128)(2,1)S(1)}, bf16[16,2048]{1,0:T(8,128)(2,1)S(1)}, u32[]{:S(2)}, u32[]{:S(2)}) collective-permute-start(bf16[16,2048]{1,0:T(8,128)(2,1)S(1)} %get-tuple-element.58.refs_4_.refs_0_), channel_id=1, source_target_pairs={{0,1},{1,0},{2,3},{3,2},{4,5},{5,4},{6,7},{7,6},{8,9},{9,8},{10,11... | collective-permute-start | bytes 196616 | tf_op jit(solution)/shard_map/ppermute | solution.py:174
  42.7 3.3 %collective-permute-start.16 = (bf16[16,2560]{1,0:T(8,128)(2,1)S(1)}, bf16[16,2560]{1,0:T(8,128)(2,1)S(1)}, u32[]{:S(2)}, u32[]{:S(2)}) collective-permute-start(bf16[16,2560]{1,0:T(8,128)(2,1)S(1)} %get-tuple-element.67.refs_1_), channel_id=1, source_target_pairs={{0,1},{1,0},{2,3},{3,2},{4,5},{5,4},{6,7},{7,6},{8,9},{9,8},{10,11... | collective-permute-start | bytes 245768 | tf_op jit(solution)/shard_map/ppermute | solution.py:174
  42.7 3.2 %collective-permute-start.15 = (bf16[16,2560]{1,0:T(8,128)(2,1)S(1)}, bf16[16,2560]{1,0:T(8,128)(2,1)S(1)}, u32[]{:S(2)}, u32[]{:S(2)}) collective-permute-start(bf16[16,2560]{1,0:T(8,128)(2,1)S(1)} %get-tuple-element.63.refs_5_.refs_0_), channel_id=1, source_target_pairs={{0,1},{1,0},{2,3},{3,2},{4,5},{5,4},{6,7},{7,6},{8,9},{9,8},{10,11... | collective-permute-start | bytes 245768 | tf_op jit(solution)/shard_map/ppermute | solution.py:174
  45.4 2.9 %collective-permute-start.14 = (bf16[16,2048]{1,0:T(8,128)(2,1)S(1)}, bf16[16,2048]{1,0:T(8,128)(2,1)S(1)}, u32[]{:S(2)}, u32[]{:S(2)}) collective-permute-start(bf16[16,2048]{1,0:T(8,128)(2,1)S(1)} %get-tuple-element.65.refs_1_), channel_id=1, source_target_pairs={{0,1},{1,0},{2,3},{3,2},{4,5},{5,4},{6,7},{7,6},{8,9},{9,8},{10,11... | collective-permute-start | bytes 196616 | tf_op jit(solution)/shard_map/ppermute | solution.py:174
  45.5 2.8 %collective-permute-start.13 = (bf16[16,2048]{1,0:T(8,128)(2,1)S(1)}, bf16[16,2048]{1,0:T(8,128)(2,1)S(1)}, u32[]{:S(2)}, u32[]{:S(2)}) collective-permute-start(bf16[16,2048]{1,0:T(8,128)(2,1)S(1)} %get-tuple-element.64.refs_6_.refs_0_), channel_id=1, source_target_pairs={{0,1},{1,0},{2,3},{3,2},{4,5},{5,4},{6,7},{7,6},{8,9},{9,8},{10,11... | collective-permute-start | bytes 196616 | tf_op jit(solution)/shard_map/ppermute | solution.py:174
  50.3 4.5 %collective-permute-start.17 = (bf16[16,2048]{1,0:T(8,128)(2,1)S(1)}, bf16[16,2048]{1,0:T(8,128)(2,1)S(1)}, u32[]{:S(2)}, u32[]{:S(2)}) collective-permute-start(bf16[16,2048]{1,0:T(8,128)(2,1)S(1)} %get-tuple-element.70), channel_id=1, source_target_pairs={{0,2},{2,0},{4,6},{6,4},{1,3},{3,1},{5,7},{7,5},{8,10},{10,8},{12,... | collective-permute-start | bytes 196616 | tf_op jit(solution)/shard_map/ppermute | solution.py:174
  51.4 7.5 %collective-permute-start.18 = (bf16[16,2048]{1,0:T(8,128)(2,1)S(1)}, bf16[16,2048]{1,0:T(8,128)(2,1)S(1)}, u32[]{:S(2)}, u32[]{:S(2)}) collective-permute-start(bf16[16,2048]{1,0:T(8,128)(2,1)S(1)} %get-tuple-element.71), channel_id=1, source_target_pairs={{0,4},{2,6},{4,0},{6,2},{1,5},{3,7},{5,1},{7,3},{8,12},{10,14},{12... | collective-permute-start | bytes 196616 | tf_op jit(solution)/shard_map/ppermute | solution.py:174
  53.6 6.2 %collective-permute-start.19 = (bf16[16,2048]{1,0:T(8,128)(2,1)S(1)}, bf16[16,2048]{1,0:T(8,128)(2,1)S(1)}, u32[]{:S(2)}, u32[]{:S(2)}) collective-permute-start(bf16[16,2048]{1,0:T(8,128)(2,1)S(1)} %get-tuple-element.72), channel_id=1, source_target_pairs={{0,6},{2,4},{4,2},{6,0},{1,7},{3,5},{5,3},{7,1},{8,14},{10,12},{12... | collective-permute-start | bytes 196616 | tf_op jit(solution)/shard_map/ppermute | solution.py:174

commit v7 on v6

--- a/solution.py
+++ b/solution.py
@@ -9,9 +9,10 @@
 
 BF16, F32 = jnp.bfloat16, jnp.float32
 TILE = 512
-GATE = (9, 4)
-DOWN = (4, 5, 4)
-PAIR_TYPE = F32
+GATE = (4, 4, 5)
+UP = (7, 6)
+DOWN = (4, 4, 5)
+PAIR_TYPE = BF16
 COST = 1
 SPLIT = 2
 
@@ -47,9 +48,10 @@
     return made
 
 
-def call(order, body, operands, outs, fetch, scratch, flops, traffic, after=()):
+def call(order, body, operands, outs, fetch, scratch, flops, traffic, after=(), carry=()):
     fetched = []
-    for array, axis, start, size in fetch:
+    moves = [*fetch, *((operands[-1], *move) for move in carry)]
+    for array, axis, start, size in moves:
         shape = (array.shape[0], size) if axis else (size, array.shape[1])
         fetched.append(pltpu.VMEM(shape, array.dtype))
     n_in = len(operands)
@@ -57,10 +59,10 @@
 
     def kernel(*refs):
         ins, rest = refs[:n_in], refs[n_in + len(after) :]
-        sources, rest = rest[: len(fetch)], rest[len(fetch) :]
+        sources, rest = [*rest[: len(fetch)], *[ins[-1] for _ in carry]], rest[len(fetch) :]
         results, rest = rest[: len(outs)], rest[len(outs) :]
-        targets, (*room, sems) = rest[: len(fetch)], rest[len(fetch) :]
-        made = copies([f[1:] for f in fetch], sources, targets, sems)
+        targets, (*room, sems) = rest[: len(moves)], rest[len(moves) :]
+        made = copies([move[1:] for move in moves], sources, targets, sems)
         for copy in made:
             copy.start()
         body(ins, results, room)
@@ -71,8 +73,8 @@
         kernel,
         out_shape=tuple(outs) + tuple(fetched),
         in_specs=[on_chip()] * n_in + [in_place()] * (len(after) + len(fetch)),
-        out_specs=tuple([on_chip()] * (len(outs) + len(fetch))),
-        scratch_shapes=list(scratch) + [pltpu.SemaphoreType.DMA((max(len(fetch), 1),))],
+        out_specs=tuple([on_chip()] * (len(outs) + len(moves))),
+        scratch_shapes=list(scratch) + [pltpu.SemaphoreType.DMA((max(len(moves), 1),))],
         compiler_params=pltpu.CompilerParams(vmem_limit_bytes=4 * 2**20),
         cost_estimate=pl.CostEstimate(flops=int(flops), bytes_accessed=int(traffic), transcendentals=0),
     )(*operands, *after, *[pltpu.with_memory_space_constraint(f[0], pltpu.HBM) for f in fetch])
@@ -85,8 +87,8 @@
         target[...] = source[...]
 
 
-def pair_part_kernel(n_pair, chunks, ins, outs, room):
-    *blocks, weight = ins
+def pair_part_kernel(n_pair, chunks, n_weights, ins, outs, room):
+    blocks, weights = ins[:-n_weights], ins[-n_weights:]
     n = len(chunks)
     keep, sends = outs[0], outs[1 : 1 + n * (n_pair - 1)]
     x = blocks[0]
@@ -98,19 +100,26 @@
     (res,) = room
     me = lax.axis_index("pair")
     rows = keep.shape[0]
-    for j, (start, width) in enumerate(chunks):
-        tile = tile_of(width)
-
-        @pl.loop(0, width // tile)
-        def _(step, j=j, start=start, tile=tile):
-            def at(offset):
-                return pl.ds(pl.multiple_of(offset + step * tile, tile), tile)
-
-            res[...] = jnp.dot(x[...], weight[:, at(start)], preferred_element_type=F32)
-            for k in range(n_pair):
-                block = pl.ds(pl.multiple_of(lax.rem(me + k, n_pair) * rows, 16), rows)
-                target, offset = (sends[(k - 1) * n + j], 0) if k else (keep, start)
-                target[:, at(offset)] = res[block, :].astype(target.dtype)
+    start = 0
+    for weight in weights:
+        for j, (first, width) in enumerate(chunks):
+            low, high = max(start, first), min(start + weight.shape[1], first + width)
+            if low >= high:
+                continue
+            tile = tile_of(high - low)
+
+            @pl.loop(0, (high - low) // tile)
+            def _(step, weight=weight, tile=tile, j=j, low=low, first=first, start=start):
+                def at(offset):
+                    return pl.ds(pl.multiple_of(offset + step * tile, tile), tile)
+
+                res[...] = jnp.dot(x[...], weight[:, at(low - start)], preferred_element_type=F32)
+                for k in range(n_pair):
+                    block = pl.ds(pl.multiple_of(lax.rem(me + k, n_pair) * rows, 16), rows)
+                    target, offset = (sends[(k - 1) * n + j], low - first) if k else (keep, low)
+                    target[:, at(offset)] = res[block, :].astype(target.dtype)
+
+        start += weight.shape[1]
 
 
 def pair_sum_kernel(chunks, ins, outs, room):
@@ -126,11 +135,22 @@
             out[:, slice(0, width) if half == n else at] = total.astype(out.dtype)
 
 
-def activate_kernel(start, ins, outs, room):
-    at = slice(start, start + outs[0].shape[1])
-    half = len(ins) // 2
-    up = sum(part[:, at].astype(F32) for part in ins[:half])
-    gate = sum(part[...].astype(F32) for part in ins[half:])
+def pair_join_kernel(widths, ins, outs, room):
+    count, start = len(ins) // len(widths), 0
+    for j, width in enumerate(widths):
+        total = sum(part[...].astype(F32) for part in ins[j * count : (j + 1) * count])
+        for out in outs:
+            out[:, start : start + width] = total.astype(out.dtype)
+        start += width
+
+
+def activate_kernel(slices, ins, outs, room):
+    n_parts = len(ins) // (len(slices) + 1)
+    pieces = []
+    for j, at in enumerate(slices):
+        pieces.append(sum(part[:, at].astype(F32) for part in ins[j * n_parts : (j + 1) * n_parts]))
+    up = pieces[0] if len(pieces) == 1 else jnp.concatenate(pieces, axis=1)
+    gate = sum(part[...].astype(F32) for part in ins[len(slices) * n_parts :])
     hidden = (gate / (1.0 + jnp.exp(-gate)) * up).astype(BF16)
     rows = outs[0].shape[0]
     for k, out in enumerate(outs):
@@ -193,12 +213,12 @@
 
     order = []
 
-    def project(blocks, weight, chunks, fetch, after=()):
-        width, n = weight.shape[1], len(chunks)
+    def project(blocks, weights, chunks, fetch, after=(), carry=()):
+        width, n = sum(width for _, width in chunks), len(chunks)
         outs, fetched = call(
             order,
-            functools.partial(pair_part_kernel, n_pair, chunks),
-            [*blocks, weight],
+            functools.partial(pair_part_kernel, n_pair, chunks, len(weights)),
+            [*blocks, *weights],
             [pltpu.VMEM((half, width), F32)]
             + [pltpu.VMEM((half, wide), PAIR_TYPE) for _, wide in chunks] * (n_pair - 1)
             + [pltpu.VMEM((rows, depth), BF16)] * (len(blocks) > 1),
@@ -207,6 +227,7 @@
             COST * 2 * rows * depth * width,
             COST * 2 * bytes_of(fetch),
             after,
+            carry,
         )
         got = [send(outs[1 + (k - 1) * n + j], "pair", k) for k in range(1, n_pair) for j in range(n)]
         return (outs[0], *got), outs[-1], fetched
@@ -222,9 +243,16 @@
             sums.append([own] + [send(away, "seq", k) for k in range(1, n_seq)])
         return sums
 
-    def activate(ups, gates, start, width):
+    def activate(j):
+        start, width = chunks[j]
+        slices, parts = [], []
+        for (first, wide), up in zip(spans, ups):
+            low, high = max(start, first), min(start + width, first + wide)
+            if low < high:
+                slices.append(slice(low - first, high - first))
+                parts += up
         hidden, _ = call(
-            order, functools.partial(activate_kernel, start), [*ups, *gates],
+            order, functools.partial(activate_kernel, slices), [*parts, *sums[j]],
             [pltpu.VMEM((half // SPLIT, width), BF16)] * SPLIT, [], [], 0, COST * 8 * half * width,
         )
         got = [send(piece, "pair", k) for k in range(1, n_pair) for piece in hidden]
@@ -261,37 +289,44 @@
     )
     blocks = [tokens] + [send(tokens, "wide", k) for k in range(1, n_wide)]
     up = pltpu.with_memory_space_constraint(up_weight, pltpu.VMEM)
-    columns = gate_weight.shape[1]
-    ups, x, (gate,) = project(blocks, up, [(0, columns)], gate_of(0), early)
-    down, gates = {}, []
-    for j, (start, width) in enumerate(loads):
-        inner = [(a - start, b) for a, b in chunks if start <= a < start + width]
-        last = j == len(loads) - 1
-        parts, _, (weight,) = project([x], gate, inner, down_of(0) if last else gate_of(j + 1))
-        if last:
-            down[0] = weight
-        else:
-            gate = weight
-        gates.append((parts, inner))
-        if j == 0:
-            (ups,) = pair_sum(ups, [(0, columns)], [(0, columns)])
-    sums = []
-    for parts, inner in gates:
-        sums += pair_sum(parts, inner, inner)
+    spans = cuts(up_weight.shape[1], UP)
+    ups, gate, down, sums = [], [], {}, []
+    if n == 1:
+        parts, x, gate = project(blocks, [up], spans, gate_of(0), early)
+        ups = pair_sum(parts, spans, spans)
+        parts, _, (down[0],) = project([x], gate, chunks, down_of(0))
+        sums = pair_sum(parts, chunks, chunks)
+    else:
+        parts, x, (gate_0, rest) = project(blocks, [up], spans[:1], gate_of(0), early, [(1, *spans[1])])
+        more, _, (gate_1,) = project([x], [rest], [(0, spans[1][1])], gate_of(1))
+        columns = up_weight.shape[1]
+        (own, away), _ = call(
+            order, functools.partial(pair_join_kernel, [width for _, width in spans]), [*parts, *more],
+            [pltpu.VMEM((half, columns), F32), pltpu.VMEM((half, columns), BF16)],
+            [], [], 0, COST * 8 * half * columns,
+        )
+        ups.append([own] + [send(away, "seq", k) for k in range(1, n_seq)])
+        spans = [(0, columns)]
+        edge = loads[2][0]
+        inner = [chunk for chunk in chunks if chunk[0] < edge]
+        parts, _, (gate_2,) = project([x], [gate_0, gate_1], inner, gate_of(2))
+        rest = [(start - edge, width) for start, width in chunks if start >= edge]
+        more, _, (down[0],) = project([x], [gate_2], rest, down_of(0))
+        sums = pair_sum(parts, inner, inner) + pair_sum(more, rest, rest)
     if n > 1:
         late = list(range(1, n))
         _, more = load(x, down_of(*late), 0)
         down.update(zip(late, more))
-    load(x, [], 0, ups[1:])
-    hiddens = [activate(ups, sums[j], *chunks[j]) for j in range(min(n, 2))]
+    load(x, [], 0, [part for up in ups for part in up[1:]])
+    hiddens = [activate(j) for j in range(min(n, 2))]
     total = []
     for j in range(n):
         if j and j + 1 < n:
-            hiddens.append(activate(ups, sums[j + 1], *chunks[j + 1]))
+            hiddens.append(activate(j + 1))
         total = multiply_down(j, hiddens[j], total)
 
     result = total[0]
-    for k in range(1, n_wide):
+    for k in reversed(range(1, n_wide)):
         result = result + send(total[k], "wide", k).astype(F32)
     return result.astype(BF16)
 

time: 60.7 us -> 60.2 us (level)
  waiting for transfers between devices: 13.6 us -> 10.9 us
  Pallas kernels: 28.6 us -> 30.7 us
    ppermute x20 -> x21, waiting for transfers between devices: 13.6 us -> 10.9 us  [send(): lax.ppermute(value, axis, [(i, i ^ k if paired else (i + k) % n) for i in...]
    pallas_call x15 -> x16, Pallas kernels: 28.6 us -> 30.7 us  [call(): pl.pallas_call(kernel, out_shape=tuple(outs) + tuple(fetched), in_specs=[...]
    ppermute x20 -> x21, starting transfers between devices: 17.4 us -> 17.5 us  [send(): lax.ppermute(value, axis, [(i, i ^ k if paired else (i + k) % n) for i in...]
  transfers between devices with their start and end apart: 20 -> 21, of which waited for: 6 -> 6; matrix products, arithmetic and copies ran while one was open for 0% -> 0% of each run, Pallas kernels for 32% -> 36%
where the time goes in v7:
time: 60.2 us; the launch traced here: 60 us
  Pallas kernels  30.7 us (51%)
  starting transfers between devices  17.5 us (29%)
  waiting for transfers between devices  10.9 us (18%)
  other arithmetic  0.66 us (1%)
    pallas_call x16, Pallas kernels, call(): pl.pallas_call(kernel, out_shape=tuple(outs) + tuple(fetched), in_specs=[...  30.7 us
    ppermute x21, starting transfers between devices, send(): lax.ppermute(value, axis, [(i, i ^ k if paired else (i + k) % n) for i in...  17.5 us
    ppermute x21, waiting for transfers between devices, send(): lax.ppermute(value, axis, [(i, i ^ k if paired else (i + k) % n) for i in...  10.9 us
  transfers between devices with their start and end apart: 21, of which 6 were waited for; matrix products, arithmetic and copies ran while one was open for 0% of the time, Pallas kernels for 36%

profile of v7, /device:TPU:0, one launch (start us, length us, event | category | flops | bytes accessed | tf_op | source)
XLA Modules:
  0.0 60.0 jit_solution(13163229463353052986)
XLA Ops:
  0.0 1.0 %shard_map.46 = (bf16[16,2048]{1,0:T(8,128)(2,1)S(1)}, bf16[16,2048]{1,0:T(8,128)(2,1)S(1)}) custom-call(bf16[16,2048]{1,0:T(8,128)(2,1)} %refs_0_.1, bf16[6656,2048]{1,0:T(8,128)(2,1)} %refs_3_.5), custom_call_target="tpu_custom_call" | custom-call | bytes 54525952 | tf_op jit(solution)/shard_map/pallas_call | solution.py:72
  1.0 5.1 %collective-permute-start.2 = (bf16[16,2048]{1,0:T(8,128)(2,1)S(1)}, bf16[16,2048]{1,0:T(8,128)(2,1)S(1)}, u32[]{:S(2)}, u32[]{:S(2)}) collective-permute-start(bf16[16,2048]{1,0:T(8,128)(2,1)S(1)} %get-tuple-element.43.refs_0_.refs_6_), channel_id=1, source_target_pairs={{0,6},{2,4},{4,2},{6,0},{1,7},{3,5},{5,3},{7,1},{8,14},{10,12},{12... | collective-permute-start | bytes 196616 | tf_op jit(solution)/shard_map/ppermute | solution.py:194
  6.2 0.6 %collective-permute-start = (bf16[16,2048]{1,0:T(8,128)(2,1)S(1)}, bf16[16,2048]{1,0:T(8,128)(2,1)S(1)}, u32[]{:S(2)}, u32[]{:S(2)}) collective-permute-start(bf16[16,2048]{1,0:T(8,128)(2,1)S(1)} %get-tuple-element.43.refs_0_.refs_6_), channel_id=1, source_target_pairs={{0,2},{2,0},{4,6},{6,4},{1,3},{3,1},{5,7},{7,5},{8,10},{10,8},{12,... | collective-permute-start | bytes 196616 | tf_op jit(solution)/shard_map/ppermute | solution.py:194
  6.8 1.9 %collective-permute-done.2.refs_3_ = bf16[16,2048]{1,0:T(8,128)(2,1)S(1)} collective-permute-done((bf16[16,2048]{1,0:T(8,128)(2,1)S(1)}, bf16[16,2048]{1,0:T(8,128)(2,1)S(1)}, u32[]{:S(2)}, u32[]{:S(2)}) %collective-permute-start.2) | collective-permute-done | bytes 65568 | tf_op jit(solution)/shard_map/ppermute | solution.py:194
  8.7 3.0 %collective-permute-done.1.refs_2_ = bf16[16,2048]{1,0:T(8,128)(2,1)S(1)} collective-permute-done((bf16[16,2048]{1,0:T(8,128)(2,1)S(1)}, bf16[16,2048]{1,0:T(8,128)(2,1)S(1)}, u32[]{:S(2)}, u32[]{:S(2)}) %collective-permute-start.1) | collective-permute-done | bytes 65568 | tf_op jit(solution)/shard_map/ppermute | solution.py:194
  11.8 5.5 %shard_map.47 = (f32[32,3584]{1,0:T(8,128)S(1)}, bf16[32,3584]{1,0:T(8,128)(2,1)S(1)}, bf16[64,2048]{1,0:T(8,128)(2,1)S(1)}, bf16[2048,2048]{1,0:T(8,128)(2,1)S(1)}, bf16[2048,3072]{1,0:T(8,128)(2,1)S(1)}) custom-call(bf16[16,2048]{1,0:T(8,128)(2,1)S(1)} %get-tuple-element.43.refs_0_.refs_6_, bf16[16,2048]{1,0:T(8,128)(2,1)S(1)} %collective-permute-done.refs_1_, ...), custom_call_target="tpu_custom_call" | custom-call | flops 939524096 | bytes 16777216 | tf_op jit(solution)/shard_map/pallas_call | solution.py:72
  17.3 3.4 %shard_map.48 = (f32[32,3072]{1,0:T(8,128)S(1)}, bf16[32,3072]{1,0:T(8,128)(2,1)S(1)}, bf16[2048,2048]{1,0:T(8,128)(2,1)S(1)}) custom-call(bf16[64,2048]{1,0:T(8,128)(2,1)S(1)} %get-tuple-element.47.refs_0_, bf16[2048,3072]{1,0:T(8,128)(2,1)S(1)} %get-tuple-element.48.refs_1_, f32[32,3584]{1,0:T(8,128)S(1)} %get-tuple-element.45.refs_2_.refs_0_, ...), custom_call_target="tpu_custom_call" | custom-call | flops 805306368 | bytes 16777216 | tf_op jit(solution)/shard_map/pallas_call | solution.py:72
  20.7 0.6 collective-permute-start.4
  21.3 1.1 %collective-permute-done.4.refs_3_ = bf16[32,3072]{1,0:T(8,128)(2,1)S(1)} collective-permute-done((bf16[32,3072]{1,0:T(8,128)(2,1)S(1)}, bf16[32,3072]{1,0:T(8,128)(2,1)S(1)}, u32[]{:S(2)}, u32[]{:S(2)}) %collective-permute-start.4) | collective-permute-done | bytes 196640 | tf_op jit(solution)/shard_map/ppermute | solution.py:194
  22.5 1.6 %collective-permute-start.5 = (bf16[32,6656]{1,0:T(8,128)(2,1)S(1)}, bf16[32,6656]{1,0:T(8,128)(2,1)S(1)}, u32[]{:S(2)}, u32[]{:S(2)}) collective-permute-start(bf16[32,6656]{1,0:T(8,128)(2,1)S(1)} %get-tuple-element.52), channel_id=1, source_target_pairs={{0,8},{8,0},{1,9},{9,1},{2,10},{10,2},{3,11},{11,3},{4,12},{12,4},... | collective-permute-start | bytes 1277960 | tf_op jit(solution)/shard_map/ppermute | solution.py:194
  24.1 4.1 %shard_map.50 = (f32[32,4096]{1,0:T(8,128)S(1)}, bf16[32,2048]{1,0:T(8,128)(2,1)S(1)}, bf16[32,2048]{1,0:T(8,128)(2,1)S(1)}, bf16[2048,2560]{1,0:T(8,128)(2,1)S(1)}) custom-call(bf16[64,2048]{1,0:T(8,128)(2,1)S(1)} %get-tuple-element.47.refs_0_, bf16[2048,2048]{1,0:T(8,128)(2,1)S(1)} %get-tuple-element.53.refs_1_, ...), custom_call_target="tpu_custom_call" | custom-call | flops 1073741824 | bytes 20971520 | tf_op jit(solution)/shard_map/pallas_call | solution.py:72
  28.7 3.4 %shard_map.51 = (f32[32,2560]{1,0:T(8,128)S(1)}, bf16[32,2560]{1,0:T(8,128)(2,1)S(1)}, bf16[2048,2048]{1,0:T(8,128)(2,1)S(1)}) custom-call(bf16[64,2048]{1,0:T(8,128)(2,1)S(1)} %get-tuple-element.47.refs_0_, bf16[2048,2560]{1,0:T(8,128)(2,1)S(1)} %get-tuple-element.55.refs_1_, bf16[32,2048]{1,0:T(8,128)(2,1)S(1)} %get-tuple-element.56.refs_2_, ...), custom_call_target="tpu_custom_call" | custom-call | flops 671088640 | bytes 16777216 | tf_op jit(solution)/shard_map/pallas_call | solution.py:72
  32.3 0.6 collective-permute-start.10
  32.9 1.5 %collective-permute-start.13 = (bf16[32,2048]{1,0:T(8,128)(2,1)S(1)}, bf16[32,2048]{1,0:T(8,128)(2,1)S(1)}, u32[]{:S(2)}, u32[]{:S(2)}) collective-permute-start(bf16[32,2048]{1,0:T(8,128)(2,1)S(1)} %get-tuple-element.70), channel_id=1, source_target_pairs={{0,8},{8,0},{1,9},{9,1},{2,10},{10,2},{3,11},{11,3},{4,12},{12,4},... | collective-permute-start | bytes 393224 | tf_op jit(solution)/shard_map/ppermute | solution.py:194
  34.5 0.6 collective-permute-start.9
  35.1 6.4 %shard_map.54 = (bf16[64,2048]{1,0:T(8,128)(2,1)S(1)}, bf16[2048,2048]{1,0:T(8,128)(2,1)S(1)}, bf16[2560,2048]{1,0:T(8,128)(2,1)S(1)}) custom-call(bf16[64,2048]{1,0:T(8,128)(2,1)S(1)} %get-tuple-element.47.refs_0_, f32[32,2560]{1,0:T(8,128)S(1)} %get-tuple-element.62.refs_1_.refs_2_, bf16[6656,2048]{1,0:T(8,128)(2,1)} %refs_3_.5, bf16[6656,2048]{1,0:T(8,128)(2,1)} %refs_3_.5), custom_call_target="tpu_custom_call" | custom-call | tf_op jit(solution)/shard_map/pallas_call | solution.py:72
  43.2 2.0 %shard_map.58.refs_4_.refs_5_ = f32[64,2048]{1,0:T(8,128)S(1)} custom-call(bf16[16,2048]{1,0:T(8,128)(2,1)S(1)} %get-tuple-element.66.refs_4_.refs_0_, bf16[16,2048]{1,0:T(8,128)(2,1)S(1)} %get-tuple-element.67.refs_1_, bf16[16,2048]{1,0:T(8,128)(2,1)S(1)} %collective-permute-done.11.refs_2_, bf16[16,2048]{1,0:T(8,128)(2,1)S(1)} %collective-permute-done.12.refs_3_, ...), custom_call_target="tpu_custom_call" | custom-call | flops 536870912 | tf_op jit(solution)/shard_map/pallas_call | solution.py:72
  45.9 2.0 %shard_map.60.refs_5_.refs_6_ = f32[64,2048]{1,0:T(8,128)S(1)} custom-call(bf16[16,2048]{1,0:T(8,128)(2,1)S(1)} %get-tuple-element.71.refs_5_.refs_0_, bf16[16,2048]{1,0:T(8,128)(2,1)S(1)} %get-tuple-element.75.refs_1_, bf16[16,2048]{1,0:T(8,128)(2,1)S(1)} %collective-permute-done.16.refs_2_, bf16[16,2048]{1,0:T(8,128)(2,1)S(1)} %collective-permute-done.17.refs_3_, ...), custom_call_target="tpu_custom_call" | custom-call | flops 536870912 | tf_op jit(solution)/shard_map/pallas_call | solution.py:72
  47.9 2.3 %shard_map.61 = (f32[16,2048]{1,0:T(8,128)S(1)}, bf16[16,2048]{1,0:T(8,128)(2,1)S(1)}, bf16[16,2048]{1,0:T(8,128)(2,1)S(1)}, bf16[16,2048]{1,0:T(8,128)(2,1)S(1)}) custom-call(bf16[16,2560]{1,0:T(8,128)(2,1)S(1)} %get-tuple-element.72.refs_6_.refs_0_, bf16[16,2560]{1,0:T(8,128)(2,1)S(1)} %get-tuple-element.73.refs_1_, ...), custom_call_target="tpu_custom_call" | custom-call | flops 671088640 | tf_op jit(solution)/shard_map/pallas_call | solution.py:72
  50.2 2.8 %collective-permute-start.18 = (bf16[16,2048]{1,0:T(8,128)(2,1)S(1)}, bf16[16,2048]{1,0:T(8,128)(2,1)S(1)}, u32[]{:S(2)}, u32[]{:S(2)}) collective-permute-start(bf16[16,2048]{1,0:T(8,128)(2,1)S(1)} %get-tuple-element.78), channel_id=1, source_target_pairs={{0,6},{2,4},{4,2},{6,0},{1,7},{3,5},{5,3},{7,1},{8,14},{10,12},{12... | collective-permute-start | bytes 196616 | tf_op jit(solution)/shard_map/ppermute | solution.py:194
  53.0 1.7 %collective-permute-start.20 = (bf16[16,2048]{1,0:T(8,128)(2,1)S(1)}, bf16[16,2048]{1,0:T(8,128)(2,1)S(1)}, u32[]{:S(2)}, u32[]{:S(2)}) collective-permute-start(bf16[16,2048]{1,0:T(8,128)(2,1)S(1)} %get-tuple-element.80), channel_id=1, source_target_pairs={{0,2},{2,0},{4,6},{6,4},{1,3},{3,1},{5,7},{7,5},{8,10},{10,8},{12,... | collective-permute-start | bytes 196616 | tf_op jit(solution)/shard_map/ppermute | solution.py:194
  54.7 2.4 %collective-permute-done.18 = bf16[16,2048]{1,0:T(8,128)(2,1)S(1)} collective-permute-done((bf16[16,2048]{1,0:T(8,128)(2,1)S(1)}, bf16[16,2048]{1,0:T(8,128)(2,1)S(1)}, u32[]{:S(2)}, u32[]{:S(2)}) %collective-permute-start.18) | collective-permute-done | bytes 65568 | tf_op jit(solution)/shard_map/ppermute | solution.py:194
  57.1 2.2 %collective-permute-done.19 = bf16[16,2048]{1,0:T(8,128)(2,1)S(1)} collective-permute-done((bf16[16,2048]{1,0:T(8,128)(2,1)S(1)}, bf16[16,2048]{1,0:T(8,128)(2,1)S(1)}, u32[]{:S(2)}, u32[]{:S(2)}) %collective-permute-start.19) | collective-permute-done | bytes 65568 | tf_op jit(solution)/shard_map/ppermute | solution.py:194
  59.3 0.7 %add_convert_fusion = bf16[16,2048]{1,0:T(8,128)(2,1)} fusion(bf16[16,2048]{1,0:T(8,128)(2,1)S(1)} %collective-permute-done.20, bf16[16,2048]{1,0:T(8,128)(2,1)S(1)} %collective-permute-done.19, f32[16,2048]{1,0:T(8,128)S(1)} %get-tuple-element.77, bf16[16,2048]{1,0:T(8,128)(2,1)S(1)} %collective-permute-done.18), kind=kLoop, calls=%fused_computation | loop fusion | flops 229376 | bytes 393216 | tf_op jit(solution)/shard_map/convert_element_type | solution.py:331
  (37 shorter events, 3.4 us)
Async XLA Ops:
  0.0 11.8 %copy-start = (bf16[2048,6656]{1,0:T(8,128)(2,1)S(1)}, bf16[2048,6656]{1,0:T(8,128)(2,1)}, u32[]{:S(2)}) copy-start(bf16[2048,6656]{1,0:T(8,128)(2,1)} %refs_4_.2) | copy-start | bytes 81788928
  1.0 7.7 %collective-permute-start.2 = (bf16[16,2048]{1,0:T(8,128)(2,1)S(1)}, bf16[16,2048]{1,0:T(8,128)(2,1)S(1)}, u32[]{:S(2)}, u32[]{:S(2)}) collective-permute-start(bf16[16,2048]{1,0:T(8,128)(2,1)S(1)} %get-tuple-element.43.refs_0_.refs_6_), channel_id=1, source_target_pairs={{0,6},{2,4},{4,2},{6,0},{1,7},{3,5},{5,3},{7,1},{8,14},{10,12},{12... | collective-permute-start | bytes 196616 | tf_op jit(solution)/shard_map/ppermute | solution.py:194
  6.2 5.6 %collective-permute-start.1 = (bf16[16,2048]{1,0:T(8,128)(2,1)S(1)}, bf16[16,2048]{1,0:T(8,128)(2,1)S(1)}, u32[]{:S(2)}, u32[]{:S(2)}) collective-permute-start(bf16[16,2048]{1,0:T(8,128)(2,1)S(1)} %get-tuple-element.43.refs_0_.refs_6_), channel_id=1, source_target_pairs={{0,4},{2,6},{4,0},{6,2},{1,5},{3,7},{5,1},{7,3},{8,12},{10,14},{12... | collective-permute-start | bytes 196616 | tf_op jit(solution)/shard_map/ppermute | solution.py:194
  6.2 5.6 %collective-permute-start = (bf16[16,2048]{1,0:T(8,128)(2,1)S(1)}, bf16[16,2048]{1,0:T(8,128)(2,1)S(1)}, u32[]{:S(2)}, u32[]{:S(2)}) collective-permute-start(bf16[16,2048]{1,0:T(8,128)(2,1)S(1)} %get-tuple-element.43.refs_0_.refs_6_), channel_id=1, source_target_pairs={{0,2},{2,0},{4,6},{6,4},{1,3},{3,1},{5,7},{7,5},{8,10},{10,8},{12,... | collective-permute-start | bytes 196616 | tf_op jit(solution)/shard_map/ppermute | solution.py:194
  17.3 5.1 %collective-permute-start.3 = (bf16[32,3584]{1,0:T(8,128)(2,1)S(1)}, bf16[32,3584]{1,0:T(8,128)(2,1)S(1)}, u32[]{:S(2)}, u32[]{:S(2)}) collective-permute-start(bf16[32,3584]{1,0:T(8,128)(2,1)S(1)} %get-tuple-element.46), channel_id=1, source_target_pairs={{0,1},{1,0},{2,3},{3,2},{4,5},{5,4},{6,7},{7,6},{8,9},{9,8},{10,11... | collective-permute-start | bytes 688136 | tf_op jit(solution)/shard_map/ppermute | solution.py:194
  20.7 1.6 %collective-permute-start.4 = (bf16[32,3072]{1,0:T(8,128)(2,1)S(1)}, bf16[32,3072]{1,0:T(8,128)(2,1)S(1)}, u32[]{:S(2)}, u32[]{:S(2)}) collective-permute-start(bf16[32,3072]{1,0:T(8,128)(2,1)S(1)} %get-tuple-element.50), channel_id=1, source_target_pairs={{0,1},{1,0},{2,3},{3,2},{4,5},{5,4},{6,7},{7,6},{8,9},{9,8},{10,11... | collective-permute-start | bytes 589832 | tf_op jit(solution)/shard_map/ppermute | solution.py:194
  22.5 19.0 %collective-permute-start.5 = (bf16[32,6656]{1,0:T(8,128)(2,1)S(1)}, bf16[32,6656]{1,0:T(8,128)(2,1)S(1)}, u32[]{:S(2)}, u32[]{:S(2)}) collective-permute-start(bf16[32,6656]{1,0:T(8,128)(2,1)S(1)} %get-tuple-element.52), channel_id=1, source_target_pairs={{0,8},{8,0},{1,9},{9,1},{2,10},{10,2},{3,11},{11,3},{4,12},{12,4},... | collective-permute-start | bytes 1277960 | tf_op jit(solution)/shard_map/ppermute | solution.py:194
  28.1 4.1 %collective-permute-start.8 = (bf16[32,2048]{1,0:T(8,128)(2,1)S(1)}, bf16[32,2048]{1,0:T(8,128)(2,1)S(1)}, u32[]{:S(2)}, u32[]{:S(2)}) collective-permute-start(bf16[32,2048]{1,0:T(8,128)(2,1)S(1)} %get-tuple-element.60), channel_id=1, source_target_pairs={{0,1},{1,0},{2,3},{3,2},{4,5},{5,4},{6,7},{7,6},{8,9},{9,8},{10,11... | collective-permute-start | bytes 393224 | tf_op jit(solution)/shard_map/ppermute | solution.py:194
  28.3 4.0 %collective-permute-start.7 = (bf16[32,2048]{1,0:T(8,128)(2,1)S(1)}, bf16[32,2048]{1,0:T(8,128)(2,1)S(1)}, u32[]{:S(2)}, u32[]{:S(2)}) collective-permute-start(bf16[32,2048]{1,0:T(8,128)(2,1)S(1)} %get-tuple-element.56.refs_2_), channel_id=1, source_target_pairs={{0,1},{1,0},{2,3},{3,2},{4,5},{5,4},{6,7},{7,6},{8,9},{9,8},{10,11... | collective-permute-start | bytes 393224 | tf_op jit(solution)/shard_map/ppermute | solution.py:194
  32.1 2.3 %collective-permute-start.6 = (bf16[32,2560]{1,0:T(8,128)(2,1)S(1)}, bf16[32,2560]{1,0:T(8,128)(2,1)S(1)}, u32[]{:S(2)}, u32[]{:S(2)}) collective-permute-start(bf16[32,2560]{1,0:T(8,128)(2,1)S(1)} %get-tuple-element.58), channel_id=1, source_target_pairs={{0,1},{1,0},{2,3},{3,2},{4,5},{5,4},{6,7},{7,6},{8,9},{9,8},{10,11... | collective-permute-start | bytes 491528 | tf_op jit(solution)/shard_map/ppermute | solution.py:194
  32.3 9.2 %collective-permute-start.10 = (bf16[32,2048]{1,0:T(8,128)(2,1)S(1)}, bf16[32,2048]{1,0:T(8,128)(2,1)S(1)}, u32[]{:S(2)}, u32[]{:S(2)}) collective-permute-start(bf16[32,2048]{1,0:T(8,128)(2,1)S(1)} %get-tuple-element.64), channel_id=1, source_target_pairs={{0,8},{8,0},{1,9},{9,1},{2,10},{10,2},{3,11},{11,3},{4,12},{12,4},... | collective-permute-start | bytes 393224 | tf_op jit(solution)/shard_map/ppermute | solution.py:194
  32.9 9.3 %collective-permute-start.13 = (bf16[32,2048]{1,0:T(8,128)(2,1)S(1)}, bf16[32,2048]{1,0:T(8,128)(2,1)S(1)}, u32[]{:S(2)}, u32[]{:S(2)}) collective-permute-start(bf16[32,2048]{1,0:T(8,128)(2,1)S(1)} %get-tuple-element.70), channel_id=1, source_target_pairs={{0,8},{8,0},{1,9},{9,1},{2,10},{10,2},{3,11},{11,3},{4,12},{12,4},... | collective-permute-start | bytes 393224 | tf_op jit(solution)/shard_map/ppermute | solution.py:194
  34.5 10.6 %collective-permute-start.9 = (bf16[32,2560]{1,0:T(8,128)(2,1)S(1)}, bf16[32,2560]{1,0:T(8,128)(2,1)S(1)}, u32[]{:S(2)}, u32[]{:S(2)}) collective-permute-start(bf16[32,2560]{1,0:T(8,128)(2,1)S(1)} %get-tuple-element.63), channel_id=1, source_target_pairs={{0,8},{8,0},{1,9},{9,1},{2,10},{10,2},{3,11},{11,3},{4,12},{12,4},... | collective-permute-start | bytes 491528 | tf_op jit(solution)/shard_map/ppermute | solution.py:194
  41.7 1.3 %collective-permute-start.12 = (bf16[16,2048]{1,0:T(8,128)(2,1)S(1)}, bf16[16,2048]{1,0:T(8,128)(2,1)S(1)}, u32[]{:S(2)}, u32[]{:S(2)}) collective-permute-start(bf16[16,2048]{1,0:T(8,128)(2,1)S(1)} %get-tuple-element.67.refs_1_), channel_id=1, source_target_pairs={{0,1},{1,0},{2,3},{3,2},{4,5},{5,4},{6,7},{7,6},{8,9},{9,8},{10,11... | collective-permute-start | bytes 196616 | tf_op jit(solution)/shard_map/ppermute | solution.py:194
  41.8 1.4 %collective-permute-start.11 = (bf16[16,2048]{1,0:T(8,128)(2,1)S(1)}, bf16[16,2048]{1,0:T(8,128)(2,1)S(1)}, u32[]{:S(2)}, u32[]{:S(2)}) collective-permute-start(bf16[16,2048]{1,0:T(8,128)(2,1)S(1)} %get-tuple-element.66.refs_4_.refs_0_), channel_id=1, source_target_pairs={{0,1},{1,0},{2,3},{3,2},{4,5},{5,4},{6,7},{7,6},{8,9},{9,8},{10,11... | collective-permute-start | bytes 196616 | tf_op jit(solution)/shard_map/ppermute | solution.py:194
  42.4 3.5 %collective-permute-start.17 = (bf16[16,2048]{1,0:T(8,128)(2,1)S(1)}, bf16[16,2048]{1,0:T(8,128)(2,1)S(1)}, u32[]{:S(2)}, u32[]{:S(2)}) collective-permute-start(bf16[16,2048]{1,0:T(8,128)(2,1)S(1)} %get-tuple-element.75.refs_1_), channel_id=1, source_target_pairs={{0,1},{1,0},{2,3},{3,2},{4,5},{5,4},{6,7},{7,6},{8,9},{9,8},{10,11... | collective-permute-start | bytes 196616 | tf_op jit(solution)/shard_map/ppermute | solution.py:194
  42.5 3.4 %collective-permute-start.16 = (bf16[16,2048]{1,0:T(8,128)(2,1)S(1)}, bf16[16,2048]{1,0:T(8,128)(2,1)S(1)}, u32[]{:S(2)}, u32[]{:S(2)}) collective-permute-start(bf16[16,2048]{1,0:T(8,128)(2,1)S(1)} %get-tuple-element.71.refs_5_.refs_0_), channel_id=1, source_target_pairs={{0,1},{1,0},{2,3},{3,2},{4,5},{5,4},{6,7},{7,6},{8,9},{9,8},{10,11... | collective-permute-start | bytes 196616 | tf_op jit(solution)/shard_map/ppermute | solution.py:194
  45.3 2.6 %collective-permute-start.15 = (bf16[16,2560]{1,0:T(8,128)(2,1)S(1)}, bf16[16,2560]{1,0:T(8,128)(2,1)S(1)}, u32[]{:S(2)}, u32[]{:S(2)}) collective-permute-start(bf16[16,2560]{1,0:T(8,128)(2,1)S(1)} %get-tuple-element.73.refs_1_), channel_id=1, source_target_pairs={{0,1},{1,0},{2,3},{3,2},{4,5},{5,4},{6,7},{7,6},{8,9},{9,8},{10,11... | collective-permute-start | bytes 245768 | tf_op jit(solution)/shard_map/ppermute | solution.py:194
  45.7 2.2 %collective-permute-start.14 = (bf16[16,2560]{1,0:T(8,128)(2,1)S(1)}, bf16[16,2560]{1,0:T(8,128)(2,1)S(1)}, u32[]{:S(2)}, u32[]{:S(2)}) collective-permute-start(bf16[16,2560]{1,0:T(8,128)(2,1)S(1)} %get-tuple-element.72.refs_6_.refs_0_), channel_id=1, source_target_pairs={{0,1},{1,0},{2,3},{3,2},{4,5},{5,4},{6,7},{7,6},{8,9},{9,8},{10,11... | collective-permute-start | bytes 245768 | tf_op jit(solution)/shard_map/ppermute | solution.py:194
  50.2 6.9 %collective-permute-start.18 = (bf16[16,2048]{1,0:T(8,128)(2,1)S(1)}, bf16[16,2048]{1,0:T(8,128)(2,1)S(1)}, u32[]{:S(2)}, u32[]{:S(2)}) collective-permute-start(bf16[16,2048]{1,0:T(8,128)(2,1)S(1)} %get-tuple-element.78), channel_id=1, source_target_pairs={{0,6},{2,4},{4,2},{6,0},{1,7},{3,5},{5,3},{7,1},{8,14},{10,12},{12... | collective-permute-start | bytes 196616 | tf_op jit(solution)/shard_map/ppermute | solution.py:194
  53.0 6.3 %collective-permute-start.19 = (bf16[16,2048]{1,0:T(8,128)(2,1)S(1)}, bf16[16,2048]{1,0:T(8,128)(2,1)S(1)}, u32[]{:S(2)}, u32[]{:S(2)}) collective-permute-start(bf16[16,2048]{1,0:T(8,128)(2,1)S(1)} %get-tuple-element.79), channel_id=1, source_target_pairs={{0,4},{2,6},{4,0},{6,2},{1,5},{3,7},{5,1},{7,3},{8,12},{10,14},{12... | collective-permute-start | bytes 196616 | tf_op jit(solution)/shard_map/ppermute | solution.py:194
  53.0 6.3 %collective-permute-start.20 = (bf16[16,2048]{1,0:T(8,128)(2,1)S(1)}, bf16[16,2048]{1,0:T(8,128)(2,1)S(1)}, u32[]{:S(2)}, u32[]{:S(2)}) collective-permute-start(bf16[16,2048]{1,0:T(8,128)(2,1)S(1)} %get-tuple-element.80), channel_id=1, source_target_pairs={{0,2},{2,0},{4,6},{6,4},{1,3},{3,1},{5,7},{7,5},{8,10},{10,8},{12,... | collective-permute-start | bytes 196616 | tf_op jit(solution)/shard_map/ppermute | solution.py:194

commit v8 on v6

--- a/solution.py
+++ b/solution.py
@@ -9,9 +9,9 @@
 
 BF16, F32 = jnp.bfloat16, jnp.float32
 TILE = 512
-GATE = (9, 4)
-DOWN = (4, 5, 4)
-PAIR_TYPE = F32
+GATE = (8, 5)
+DOWN = (4, 4, 5)
+PAIR_TYPE = BF16
 COST = 1
 SPLIT = 2
 
@@ -263,6 +263,7 @@
     up = pltpu.with_memory_space_constraint(up_weight, pltpu.VMEM)
     columns = gate_weight.shape[1]
     ups, x, (gate,) = project(blocks, up, [(0, columns)], gate_of(0), early)
+    (ups,) = pair_sum(ups, [(0, columns)], [(0, columns)])
     down, gates = {}, []
     for j, (start, width) in enumerate(loads):
         inner = [(a - start, b) for a, b in chunks if start <= a < start + width]
@@ -273,8 +274,6 @@
         else:
             gate = weight
         gates.append((parts, inner))
-        if j == 0:
-            (ups,) = pair_sum(ups, [(0, columns)], [(0, columns)])
     sums = []
     for parts, inner in gates:
         sums += pair_sum(parts, inner, inner)
@@ -291,7 +290,7 @@
         total = multiply_down(j, hiddens[j], total)
 
     result = total[0]
-    for k in range(1, n_wide):
+    for k in reversed(range(1, n_wide)):
         result = result + send(total[k], "wide", k).astype(F32)
     return result.astype(BF16)
 

time: 60.7 us -> 57.9 us (0.954)
  waiting for transfers between devices: 13.6 us -> 11.6 us
    ppermute x20, waiting for transfers between devices: 13.6 us -> 11.6 us  [send(): lax.ppermute(value, axis, [(i, i ^ k if paired else (i + k) % n) for i in...]
where the time goes in v8:
time: 57.9 us; the launch traced here: 57.7 us
  Pallas kernels  28.2 us (49%)
  starting transfers between devices  17 us (29%)
  waiting for transfers between devices  11.6 us (20%)
  other arithmetic  0.66 us (1%)
    pallas_call x15, Pallas kernels, call(): pl.pallas_call(kernel, out_shape=tuple(outs) + tuple(fetched), in_specs=[...  28.2 us
    ppermute x20, starting transfers between devices, send(): lax.ppermute(value, axis, [(i, i ^ k if paired else (i + k) % n) for i in...  17 us
    ppermute x20, waiting for transfers between devices, send(): lax.ppermute(value, axis, [(i, i ^ k if paired else (i + k) % n) for i in...  11.6 us
  transfers between devices with their start and end apart: 20, of which 6 were waited for; matrix products, arithmetic and copies ran while one was open for 0% of the time, Pallas kernels for 32%

profile of v8, /device:TPU:0, one launch (start us, length us, event | category | flops | bytes accessed | tf_op | source)
XLA Modules:
  0.0 57.7 jit_solution(6263851614721377808)
XLA Ops:
  0.0 1.0 %shard_map.46 = (bf16[16,2048]{1,0:T(8,128)(2,1)S(1)}, bf16[16,2048]{1,0:T(8,128)(2,1)S(1)}) custom-call(bf16[16,2048]{1,0:T(8,128)(2,1)} %refs_0_.1, bf16[6656,2048]{1,0:T(8,128)(2,1)} %refs_3_.5), custom_call_target="tpu_custom_call" | custom-call | bytes 54525952 | tf_op jit(solution)/shard_map/pallas_call | solution.py:70
  1.0 5.1 %collective-permute-start.2 = (bf16[16,2048]{1,0:T(8,128)(2,1)S(1)}, bf16[16,2048]{1,0:T(8,128)(2,1)S(1)}, u32[]{:S(2)}, u32[]{:S(2)}) collective-permute-start(bf16[16,2048]{1,0:T(8,128)(2,1)S(1)} %get-tuple-element.39.refs_0_.refs_6_), channel_id=1, source_target_pairs={{0,6},{2,4},{4,2},{6,0},{1,7},{3,5},{5,3},{7,1},{8,14},{10,12},{12... | collective-permute-start | bytes 196616 | tf_op jit(solution)/shard_map/ppermute | solution.py:174
  6.2 0.6 %collective-permute-start = (bf16[16,2048]{1,0:T(8,128)(2,1)S(1)}, bf16[16,2048]{1,0:T(8,128)(2,1)S(1)}, u32[]{:S(2)}, u32[]{:S(2)}) collective-permute-start(bf16[16,2048]{1,0:T(8,128)(2,1)S(1)} %get-tuple-element.39.refs_0_.refs_6_), channel_id=1, source_target_pairs={{0,2},{2,0},{4,6},{6,4},{1,3},{3,1},{5,7},{7,5},{8,10},{10,8},{12,... | collective-permute-start | bytes 196616 | tf_op jit(solution)/shard_map/ppermute | solution.py:174
  6.8 1.9 %collective-permute-done.2.refs_3_ = bf16[16,2048]{1,0:T(8,128)(2,1)S(1)} collective-permute-done((bf16[16,2048]{1,0:T(8,128)(2,1)S(1)}, bf16[16,2048]{1,0:T(8,128)(2,1)S(1)}, u32[]{:S(2)}, u32[]{:S(2)}) %collective-permute-start.2) | collective-permute-done | bytes 65568 | tf_op jit(solution)/shard_map/ppermute | solution.py:174
  8.7 3.0 %collective-permute-done.1.refs_2_ = bf16[16,2048]{1,0:T(8,128)(2,1)S(1)} collective-permute-done((bf16[16,2048]{1,0:T(8,128)(2,1)S(1)}, bf16[16,2048]{1,0:T(8,128)(2,1)S(1)}, u32[]{:S(2)}, u32[]{:S(2)}) %collective-permute-start.1) | collective-permute-done | bytes 65568 | tf_op jit(solution)/shard_map/ppermute | solution.py:174
  11.8 6.4 %shard_map.47 = (f32[32,6656]{1,0:T(8,128)S(1)}, bf16[32,6656]{1,0:T(8,128)(2,1)S(1)}, bf16[64,2048]{1,0:T(8,128)(2,1)S(1)}, bf16[2048,4096]{1,0:T(8,128)(2,1)S(1)}) custom-call(bf16[16,2048]{1,0:T(8,128)(2,1)S(1)} %get-tuple-element.39.refs_0_.refs_6_, bf16[16,2048]{1,0:T(8,128)(2,1)S(1)} %collective-permute-done.refs_1_, ...), custom_call_target="tpu_custom_call" | custom-call | flops 1744830464 | bytes 33554432 | tf_op jit(solution)/shard_map/pallas_call | solution.py:70
  18.3 1.8 %collective-permute-done.3.refs_1_ = bf16[32,6656]{1,0:T(8,128)(2,1)S(1)} collective-permute-done((bf16[32,6656]{1,0:T(8,128)(2,1)S(1)}, bf16[32,6656]{1,0:T(8,128)(2,1)S(1)}, u32[]{:S(2)}, u32[]{:S(2)}) %collective-permute-start.3) | collective-permute-done | bytes 426016 | tf_op jit(solution)/shard_map/ppermute | solution.py:174
  20.2 1.6 %collective-permute-start.4 = (bf16[32,6656]{1,0:T(8,128)(2,1)S(1)}, bf16[32,6656]{1,0:T(8,128)(2,1)S(1)}, u32[]{:S(2)}, u32[]{:S(2)}) collective-permute-start(bf16[32,6656]{1,0:T(8,128)(2,1)S(1)} %get-tuple-element.45), channel_id=1, source_target_pairs={{0,8},{8,0},{1,9},{9,1},{2,10},{10,2},{3,11},{11,3},{4,12},{12,4},... | collective-permute-start | bytes 1277960 | tf_op jit(solution)/shard_map/ppermute | solution.py:174
  21.7 4.1 %shard_map.49 = (f32[32,4096]{1,0:T(8,128)S(1)}, bf16[32,2048]{1,0:T(8,128)(2,1)S(1)}, bf16[32,2048]{1,0:T(8,128)(2,1)S(1)}, bf16[2048,2560]{1,0:T(8,128)(2,1)S(1)}) custom-call(bf16[64,2048]{1,0:T(8,128)(2,1)S(1)} %get-tuple-element.43.refs_2_.refs_0_, bf16[2048,4096]{1,0:T(8,128)(2,1)S(1)} %get-tuple-element.46.refs_1_, ...), custom_call_target="tpu_custom_call" | custom-call | flops 1073741824 | bytes 20971520 | tf_op jit(solution)/shard_map/pallas_call | solution.py:70
  25.9 0.5 collective-permute-start.6
  26.4 3.4 %shard_map.50 = (f32[32,2560]{1,0:T(8,128)S(1)}, bf16[32,2560]{1,0:T(8,128)(2,1)S(1)}, bf16[2048,2048]{1,0:T(8,128)(2,1)S(1)}) custom-call(bf16[64,2048]{1,0:T(8,128)(2,1)S(1)} %get-tuple-element.43.refs_2_.refs_0_, bf16[2048,2560]{1,0:T(8,128)(2,1)S(1)} %get-tuple-element.47.refs_1_, bf16[32,2048]{1,0:T(8,128)(2,1)S(1)} %get-tuple-element.48.refs_2_, ...), custom_call_target="tpu_custom_call" | custom-call | flops 671088640 | bytes 16777216 | tf_op jit(solution)/shard_map/pallas_call | solution.py:70
  30.0 0.6 %collective-permute-start.9 = (bf16[32,2048]{1,0:T(8,128)(2,1)S(1)}, bf16[32,2048]{1,0:T(8,128)(2,1)S(1)}, u32[]{:S(2)}, u32[]{:S(2)}) collective-permute-start(bf16[32,2048]{1,0:T(8,128)(2,1)S(1)} %get-tuple-element.56), channel_id=1, source_target_pairs={{0,8},{8,0},{1,9},{9,1},{2,10},{10,2},{3,11},{11,3},{4,12},{12,4},... | collective-permute-start | bytes 393224 | tf_op jit(solution)/shard_map/ppermute | solution.py:174
  30.6 1.5 %collective-permute-start.12 = (bf16[32,2048]{1,0:T(8,128)(2,1)S(1)}, bf16[32,2048]{1,0:T(8,128)(2,1)S(1)}, u32[]{:S(2)}, u32[]{:S(2)}) collective-permute-start(bf16[32,2048]{1,0:T(8,128)(2,1)S(1)} %get-tuple-element.62), channel_id=1, source_target_pairs={{0,8},{8,0},{1,9},{9,1},{2,10},{10,2},{3,11},{11,3},{4,12},{12,4},... | collective-permute-start | bytes 393224 | tf_op jit(solution)/shard_map/ppermute | solution.py:174
  32.2 0.6 %collective-permute-start.8 = (bf16[32,2560]{1,0:T(8,128)(2,1)S(1)}, bf16[32,2560]{1,0:T(8,128)(2,1)S(1)}, u32[]{:S(2)}, u32[]{:S(2)}) collective-permute-start(bf16[32,2560]{1,0:T(8,128)(2,1)S(1)} %get-tuple-element.55), channel_id=1, source_target_pairs={{0,8},{8,0},{1,9},{9,1},{2,10},{10,2},{3,11},{11,3},{4,12},{12,4},... | collective-permute-start | bytes 491528 | tf_op jit(solution)/shard_map/ppermute | solution.py:174
  32.8 6.4 %shard_map.53 = (bf16[64,2048]{1,0:T(8,128)(2,1)S(1)}, bf16[2048,2048]{1,0:T(8,128)(2,1)S(1)}, bf16[2560,2048]{1,0:T(8,128)(2,1)S(1)}) custom-call(bf16[64,2048]{1,0:T(8,128)(2,1)S(1)} %get-tuple-element.43.refs_2_.refs_0_, f32[32,2560]{1,0:T(8,128)S(1)} %get-tuple-element.54.refs_1_.refs_2_, bf16[6656,2048]{1,0:T(8,128)(2,1)} %refs_3_.5, ...), custom_call_target="tpu_custom_call" | custom-call | tf_op jit(solution)/shard_map/pallas_call | solution.py:70
  39.4 0.5 collective-permute-start.10
  40.8 2.0 %shard_map.57.refs_4_.refs_5_ = f32[64,2048]{1,0:T(8,128)S(1)} custom-call(bf16[16,2048]{1,0:T(8,128)(2,1)S(1)} %get-tuple-element.58.refs_4_.refs_0_, bf16[16,2048]{1,0:T(8,128)(2,1)S(1)} %get-tuple-element.59.refs_1_, bf16[16,2048]{1,0:T(8,128)(2,1)S(1)} %collective-permute-done.10.refs_2_, bf16[16,2048]{1,0:T(8,128)(2,1)S(1)} %collective-permute-done.11.refs_3_, ...), custom_call_target="tpu_custom_call" | custom-call | flops 536870912 | tf_op jit(solution)/shard_map/pallas_call | solution.py:70
  43.5 2.0 %shard_map.59.refs_5_.refs_6_ = f32[64,2048]{1,0:T(8,128)S(1)} custom-call(bf16[16,2048]{1,0:T(8,128)(2,1)S(1)} %get-tuple-element.63.refs_5_.refs_0_, bf16[16,2048]{1,0:T(8,128)(2,1)S(1)} %get-tuple-element.67.refs_1_, bf16[16,2048]{1,0:T(8,128)(2,1)S(1)} %collective-permute-done.15.refs_2_, bf16[16,2048]{1,0:T(8,128)(2,1)S(1)} %collective-permute-done.16.refs_3_, ...), custom_call_target="tpu_custom_call" | custom-call | flops 536870912 | tf_op jit(solution)/shard_map/pallas_call | solution.py:70
  45.6 2.3 %shard_map.60 = (f32[16,2048]{1,0:T(8,128)S(1)}, bf16[16,2048]{1,0:T(8,128)(2,1)S(1)}, bf16[16,2048]{1,0:T(8,128)(2,1)S(1)}, bf16[16,2048]{1,0:T(8,128)(2,1)S(1)}) custom-call(bf16[16,2560]{1,0:T(8,128)(2,1)S(1)} %get-tuple-element.64.refs_6_.refs_0_, bf16[16,2560]{1,0:T(8,128)(2,1)S(1)} %get-tuple-element.65.refs_1_, ...), custom_call_target="tpu_custom_call" | custom-call | flops 671088640 | tf_op jit(solution)/shard_map/pallas_call | solution.py:70
  47.9 2.8 %collective-permute-start.17 = (bf16[16,2048]{1,0:T(8,128)(2,1)S(1)}, bf16[16,2048]{1,0:T(8,128)(2,1)S(1)}, u32[]{:S(2)}, u32[]{:S(2)}) collective-permute-start(bf16[16,2048]{1,0:T(8,128)(2,1)S(1)} %get-tuple-element.70), channel_id=1, source_target_pairs={{0,6},{2,4},{4,2},{6,0},{1,7},{3,5},{5,3},{7,1},{8,14},{10,12},{12... | collective-permute-start | bytes 196616 | tf_op jit(solution)/shard_map/ppermute | solution.py:174
  50.7 1.7 %collective-permute-start.19 = (bf16[16,2048]{1,0:T(8,128)(2,1)S(1)}, bf16[16,2048]{1,0:T(8,128)(2,1)S(1)}, u32[]{:S(2)}, u32[]{:S(2)}) collective-permute-start(bf16[16,2048]{1,0:T(8,128)(2,1)S(1)} %get-tuple-element.72), channel_id=1, source_target_pairs={{0,2},{2,0},{4,6},{6,4},{1,3},{3,1},{5,7},{7,5},{8,10},{10,8},{12,... | collective-permute-start | bytes 196616 | tf_op jit(solution)/shard_map/ppermute | solution.py:174
  52.4 2.4 %collective-permute-done.17 = bf16[16,2048]{1,0:T(8,128)(2,1)S(1)} collective-permute-done((bf16[16,2048]{1,0:T(8,128)(2,1)S(1)}, bf16[16,2048]{1,0:T(8,128)(2,1)S(1)}, u32[]{:S(2)}, u32[]{:S(2)}) %collective-permute-start.17) | collective-permute-done | bytes 65568 | tf_op jit(solution)/shard_map/ppermute | solution.py:174
  54.8 2.2 %collective-permute-done.18 = bf16[16,2048]{1,0:T(8,128)(2,1)S(1)} collective-permute-done((bf16[16,2048]{1,0:T(8,128)(2,1)S(1)}, bf16[16,2048]{1,0:T(8,128)(2,1)S(1)}, u32[]{:S(2)}, u32[]{:S(2)}) %collective-permute-start.18) | collective-permute-done | bytes 65568 | tf_op jit(solution)/shard_map/ppermute | solution.py:174
  57.0 0.7 %add_convert_fusion = bf16[16,2048]{1,0:T(8,128)(2,1)} fusion(bf16[16,2048]{1,0:T(8,128)(2,1)S(1)} %collective-permute-done.19, bf16[16,2048]{1,0:T(8,128)(2,1)S(1)} %collective-permute-done.18, f32[16,2048]{1,0:T(8,128)S(1)} %get-tuple-element.69, bf16[16,2048]{1,0:T(8,128)(2,1)S(1)} %collective-permute-done.17), kind=kLoop, calls=%fused_computation | loop fusion | flops 229376 | bytes 393216 | tf_op jit(solution)/shard_map/convert_element_type | solution.py:295
  (34 shorter events, 2.4 us)
Async XLA Ops:
  0.0 11.8 %copy-start = (bf16[2048,6656]{1,0:T(8,128)(2,1)S(1)}, bf16[2048,6656]{1,0:T(8,128)(2,1)}, u32[]{:S(2)}) copy-start(bf16[2048,6656]{1,0:T(8,128)(2,1)} %refs_4_.1) | copy-start | bytes 81788928
  1.0 7.7 %collective-permute-start.2 = (bf16[16,2048]{1,0:T(8,128)(2,1)S(1)}, bf16[16,2048]{1,0:T(8,128)(2,1)S(1)}, u32[]{:S(2)}, u32[]{:S(2)}) collective-permute-start(bf16[16,2048]{1,0:T(8,128)(2,1)S(1)} %get-tuple-element.39.refs_0_.refs_6_), channel_id=1, source_target_pairs={{0,6},{2,4},{4,2},{6,0},{1,7},{3,5},{5,3},{7,1},{8,14},{10,12},{12... | collective-permute-start | bytes 196616 | tf_op jit(solution)/shard_map/ppermute | solution.py:174
  6.2 5.6 %collective-permute-start.1 = (bf16[16,2048]{1,0:T(8,128)(2,1)S(1)}, bf16[16,2048]{1,0:T(8,128)(2,1)S(1)}, u32[]{:S(2)}, u32[]{:S(2)}) collective-permute-start(bf16[16,2048]{1,0:T(8,128)(2,1)S(1)} %get-tuple-element.39.refs_0_.refs_6_), channel_id=1, source_target_pairs={{0,4},{2,6},{4,0},{6,2},{1,5},{3,7},{5,1},{7,3},{8,12},{10,14},{12... | collective-permute-start | bytes 196616 | tf_op jit(solution)/shard_map/ppermute | solution.py:174
  6.2 5.6 %collective-permute-start = (bf16[16,2048]{1,0:T(8,128)(2,1)S(1)}, bf16[16,2048]{1,0:T(8,128)(2,1)S(1)}, u32[]{:S(2)}, u32[]{:S(2)}) collective-permute-start(bf16[16,2048]{1,0:T(8,128)(2,1)S(1)} %get-tuple-element.39.refs_0_.refs_6_), channel_id=1, source_target_pairs={{0,2},{2,0},{4,6},{6,4},{1,3},{3,1},{5,7},{7,5},{8,10},{10,8},{12,... | collective-permute-start | bytes 196616 | tf_op jit(solution)/shard_map/ppermute | solution.py:174
  18.2 1.8 %collective-permute-start.3 = (bf16[32,6656]{1,0:T(8,128)(2,1)S(1)}, bf16[32,6656]{1,0:T(8,128)(2,1)S(1)}, u32[]{:S(2)}, u32[]{:S(2)}) collective-permute-start(bf16[32,6656]{1,0:T(8,128)(2,1)S(1)} %get-tuple-element.42), channel_id=1, source_target_pairs={{0,1},{1,0},{2,3},{3,2},{4,5},{5,4},{6,7},{7,6},{8,9},{9,8},{10,11... | collective-permute-start | bytes 1277960 | tf_op jit(solution)/shard_map/ppermute | solution.py:174
  20.2 19.0 %collective-permute-start.4 = (bf16[32,6656]{1,0:T(8,128)(2,1)S(1)}, bf16[32,6656]{1,0:T(8,128)(2,1)S(1)}, u32[]{:S(2)}, u32[]{:S(2)}) collective-permute-start(bf16[32,6656]{1,0:T(8,128)(2,1)S(1)} %get-tuple-element.45), channel_id=1, source_target_pairs={{0,8},{8,0},{1,9},{9,1},{2,10},{10,2},{3,11},{11,3},{4,12},{12,4},... | collective-permute-start | bytes 1277960 | tf_op jit(solution)/shard_map/ppermute | solution.py:174
  25.8 4.1 %collective-permute-start.7 = (bf16[32,2048]{1,0:T(8,128)(2,1)S(1)}, bf16[32,2048]{1,0:T(8,128)(2,1)S(1)}, u32[]{:S(2)}, u32[]{:S(2)}) collective-permute-start(bf16[32,2048]{1,0:T(8,128)(2,1)S(1)} %get-tuple-element.52), channel_id=1, source_target_pairs={{0,1},{1,0},{2,3},{3,2},{4,5},{5,4},{6,7},{7,6},{8,9},{9,8},{10,11... | collective-permute-start | bytes 393224 | tf_op jit(solution)/shard_map/ppermute | solution.py:174
  25.9 4.0 %collective-permute-start.6 = (bf16[32,2048]{1,0:T(8,128)(2,1)S(1)}, bf16[32,2048]{1,0:T(8,128)(2,1)S(1)}, u32[]{:S(2)}, u32[]{:S(2)}) collective-permute-start(bf16[32,2048]{1,0:T(8,128)(2,1)S(1)} %get-tuple-element.48.refs_2_), channel_id=1, source_target_pairs={{0,1},{1,0},{2,3},{3,2},{4,5},{5,4},{6,7},{7,6},{8,9},{9,8},{10,11... | collective-permute-start | bytes 393224 | tf_op jit(solution)/shard_map/ppermute | solution.py:174
  29.8 2.3 %collective-permute-start.5 = (bf16[32,2560]{1,0:T(8,128)(2,1)S(1)}, bf16[32,2560]{1,0:T(8,128)(2,1)S(1)}, u32[]{:S(2)}, u32[]{:S(2)}) collective-permute-start(bf16[32,2560]{1,0:T(8,128)(2,1)S(1)} %get-tuple-element.50), channel_id=1, source_target_pairs={{0,1},{1,0},{2,3},{3,2},{4,5},{5,4},{6,7},{7,6},{8,9},{9,8},{10,11... | collective-permute-start | bytes 491528 | tf_op jit(solution)/shard_map/ppermute | solution.py:174
  30.0 9.2 %collective-permute-start.9 = (bf16[32,2048]{1,0:T(8,128)(2,1)S(1)}, bf16[32,2048]{1,0:T(8,128)(2,1)S(1)}, u32[]{:S(2)}, u32[]{:S(2)}) collective-permute-start(bf16[32,2048]{1,0:T(8,128)(2,1)S(1)} %get-tuple-element.56), channel_id=1, source_target_pairs={{0,8},{8,0},{1,9},{9,1},{2,10},{10,2},{3,11},{11,3},{4,12},{12,4},... | collective-permute-start | bytes 393224 | tf_op jit(solution)/shard_map/ppermute | solution.py:174
  30.6 9.3 %collective-permute-start.12 = (bf16[32,2048]{1,0:T(8,128)(2,1)S(1)}, bf16[32,2048]{1,0:T(8,128)(2,1)S(1)}, u32[]{:S(2)}, u32[]{:S(2)}) collective-permute-start(bf16[32,2048]{1,0:T(8,128)(2,1)S(1)} %get-tuple-element.62), channel_id=1, source_target_pairs={{0,8},{8,0},{1,9},{9,1},{2,10},{10,2},{3,11},{11,3},{4,12},{12,4},... | collective-permute-start | bytes 393224 | tf_op jit(solution)/shard_map/ppermute | solution.py:174
  32.2 10.6 %collective-permute-start.8 = (bf16[32,2560]{1,0:T(8,128)(2,1)S(1)}, bf16[32,2560]{1,0:T(8,128)(2,1)S(1)}, u32[]{:S(2)}, u32[]{:S(2)}) collective-permute-start(bf16[32,2560]{1,0:T(8,128)(2,1)S(1)} %get-tuple-element.55), channel_id=1, source_target_pairs={{0,8},{8,0},{1,9},{9,1},{2,10},{10,2},{3,11},{11,3},{4,12},{12,4},... | collective-permute-start | bytes 491528 | tf_op jit(solution)/shard_map/ppermute | solution.py:174
  39.3 1.3 %collective-permute-start.11 = (bf16[16,2048]{1,0:T(8,128)(2,1)S(1)}, bf16[16,2048]{1,0:T(8,128)(2,1)S(1)}, u32[]{:S(2)}, u32[]{:S(2)}) collective-permute-start(bf16[16,2048]{1,0:T(8,128)(2,1)S(1)} %get-tuple-element.59.refs_1_), channel_id=1, source_target_pairs={{0,1},{1,0},{2,3},{3,2},{4,5},{5,4},{6,7},{7,6},{8,9},{9,8},{10,11... | collective-permute-start | bytes 196616 | tf_op jit(solution)/shard_map/ppermute | solution.py:174
  39.4 1.4 %collective-permute-start.10 = (bf16[16,2048]{1,0:T(8,128)(2,1)S(1)}, bf16[16,2048]{1,0:T(8,128)(2,1)S(1)}, u32[]{:S(2)}, u32[]{:S(2)}) collective-permute-start(bf16[16,2048]{1,0:T(8,128)(2,1)S(1)} %get-tuple-element.58.refs_4_.refs_0_), channel_id=1, source_target_pairs={{0,1},{1,0},{2,3},{3,2},{4,5},{5,4},{6,7},{7,6},{8,9},{9,8},{10,11... | collective-permute-start | bytes 196616 | tf_op jit(solution)/shard_map/ppermute | solution.py:174
  40.0 3.5 %collective-permute-start.16 = (bf16[16,2048]{1,0:T(8,128)(2,1)S(1)}, bf16[16,2048]{1,0:T(8,128)(2,1)S(1)}, u32[]{:S(2)}, u32[]{:S(2)}) collective-permute-start(bf16[16,2048]{1,0:T(8,128)(2,1)S(1)} %get-tuple-element.67.refs_1_), channel_id=1, source_target_pairs={{0,1},{1,0},{2,3},{3,2},{4,5},{5,4},{6,7},{7,6},{8,9},{9,8},{10,11... | collective-permute-start | bytes 196616 | tf_op jit(solution)/shard_map/ppermute | solution.py:174
  40.2 3.4 %collective-permute-start.15 = (bf16[16,2048]{1,0:T(8,128)(2,1)S(1)}, bf16[16,2048]{1,0:T(8,128)(2,1)S(1)}, u32[]{:S(2)}, u32[]{:S(2)}) collective-permute-start(bf16[16,2048]{1,0:T(8,128)(2,1)S(1)} %get-tuple-element.63.refs_5_.refs_0_), channel_id=1, source_target_pairs={{0,1},{1,0},{2,3},{3,2},{4,5},{5,4},{6,7},{7,6},{8,9},{9,8},{10,11... | collective-permute-start | bytes 196616 | tf_op jit(solution)/shard_map/ppermute | solution.py:174
  43.0 2.6 %collective-permute-start.14 = (bf16[16,2560]{1,0:T(8,128)(2,1)S(1)}, bf16[16,2560]{1,0:T(8,128)(2,1)S(1)}, u32[]{:S(2)}, u32[]{:S(2)}) collective-permute-start(bf16[16,2560]{1,0:T(8,128)(2,1)S(1)} %get-tuple-element.65.refs_1_), channel_id=1, source_target_pairs={{0,1},{1,0},{2,3},{3,2},{4,5},{5,4},{6,7},{7,6},{8,9},{9,8},{10,11... | collective-permute-start | bytes 245768 | tf_op jit(solution)/shard_map/ppermute | solution.py:174
  43.4 2.2 %collective-permute-start.13 = (bf16[16,2560]{1,0:T(8,128)(2,1)S(1)}, bf16[16,2560]{1,0:T(8,128)(2,1)S(1)}, u32[]{:S(2)}, u32[]{:S(2)}) collective-permute-start(bf16[16,2560]{1,0:T(8,128)(2,1)S(1)} %get-tuple-element.64.refs_6_.refs_0_), channel_id=1, source_target_pairs={{0,1},{1,0},{2,3},{3,2},{4,5},{5,4},{6,7},{7,6},{8,9},{9,8},{10,11... | collective-permute-start | bytes 245768 | tf_op jit(solution)/shard_map/ppermute | solution.py:174
  47.9 6.9 %collective-permute-start.17 = (bf16[16,2048]{1,0:T(8,128)(2,1)S(1)}, bf16[16,2048]{1,0:T(8,128)(2,1)S(1)}, u32[]{:S(2)}, u32[]{:S(2)}) collective-permute-start(bf16[16,2048]{1,0:T(8,128)(2,1)S(1)} %get-tuple-element.70), channel_id=1, source_target_pairs={{0,6},{2,4},{4,2},{6,0},{1,7},{3,5},{5,3},{7,1},{8,14},{10,12},{12... | collective-permute-start | bytes 196616 | tf_op jit(solution)/shard_map/ppermute | solution.py:174
  50.7 6.3 %collective-permute-start.18 = (bf16[16,2048]{1,0:T(8,128)(2,1)S(1)}, bf16[16,2048]{1,0:T(8,128)(2,1)S(1)}, u32[]{:S(2)}, u32[]{:S(2)}) collective-permute-start(bf16[16,2048]{1,0:T(8,128)(2,1)S(1)} %get-tuple-element.71), channel_id=1, source_target_pairs={{0,4},{2,6},{4,0},{6,2},{1,5},{3,7},{5,1},{7,3},{8,12},{10,14},{12... | collective-permute-start | bytes 196616 | tf_op jit(solution)/shard_map/ppermute | solution.py:174
  50.7 6.3 %collective-permute-start.19 = (bf16[16,2048]{1,0:T(8,128)(2,1)S(1)}, bf16[16,2048]{1,0:T(8,128)(2,1)S(1)}, u32[]{:S(2)}, u32[]{:S(2)}) collective-permute-start(bf16[16,2048]{1,0:T(8,128)(2,1)S(1)} %get-tuple-element.72), channel_id=1, source_target_pairs={{0,2},{2,0},{4,6},{6,4},{1,3},{3,1},{5,7},{7,5},{8,10},{10,8},{12,... | collective-permute-start | bytes 196616 | tf_op jit(solution)/shard_map/ppermute | solution.py:174

commit v9 on v8

--- a/solution.py
+++ b/solution.py
@@ -9,10 +9,11 @@
 
 BF16, F32 = jnp.bfloat16, jnp.float32
 TILE = 512
-GATE = (8, 5)
-DOWN = (4, 4, 5)
+GATE = (8, 2, 3)
+DOWN = (5, 5, 3)
+DOWN_LOADS = dict(gate=((0, 3),), rest=((3, 1),), late=((4, 1), (5, 5), (10, 3)))
 PAIR_TYPE = BF16
-COST = 1
+COST = 0.05
 SPLIT = 2
 
 
@@ -85,8 +86,8 @@
         target[...] = source[...]
 
 
-def pair_part_kernel(n_pair, chunks, ins, outs, room):
-    *blocks, weight = ins
+def pair_part_kernel(n_pair, chunks, n_weights, ins, outs, room):
+    blocks, weights = ins[:-n_weights], ins[-n_weights:]
     n = len(chunks)
     keep, sends = outs[0], outs[1 : 1 + n * (n_pair - 1)]
     x = blocks[0]
@@ -98,19 +99,26 @@
     (res,) = room
     me = lax.axis_index("pair")
     rows = keep.shape[0]
-    for j, (start, width) in enumerate(chunks):
-        tile = tile_of(width)
-
-        @pl.loop(0, width // tile)
-        def _(step, j=j, start=start, tile=tile):
-            def at(offset):
-                return pl.ds(pl.multiple_of(offset + step * tile, tile), tile)
-
-            res[...] = jnp.dot(x[...], weight[:, at(start)], preferred_element_type=F32)
-            for k in range(n_pair):
-                block = pl.ds(pl.multiple_of(lax.rem(me + k, n_pair) * rows, 16), rows)
-                target, offset = (sends[(k - 1) * n + j], 0) if k else (keep, start)
-                target[:, at(offset)] = res[block, :].astype(target.dtype)
+    start = 0
+    for weight in weights:
+        for j, (first, width) in enumerate(chunks):
+            low, high = max(start, first), min(start + weight.shape[1], first + width)
+            if low >= high:
+                continue
+            tile = tile_of(high - low)
+
+            @pl.loop(0, (high - low) // tile)
+            def _(step, weight=weight, tile=tile, j=j, low=low, first=first, start=start):
+                def at(offset):
+                    return pl.ds(pl.multiple_of(offset + step * tile, tile), tile)
+
+                res[...] = jnp.dot(x[...], weight[:, at(low - start)], preferred_element_type=F32)
+                for k in range(n_pair):
+                    block = pl.ds(pl.multiple_of(lax.rem(me + k, n_pair) * rows, 16), rows)
+                    target, offset = (sends[(k - 1) * n + j], low - first) if k else (keep, low)
+                    target[:, at(offset)] = res[block, :].astype(target.dtype)
+
+        start += weight.shape[1]
 
 
 def pair_sum_kernel(chunks, ins, outs, room):
@@ -126,6 +134,23 @@
             out[:, slice(0, width) if half == n else at] = total.astype(out.dtype)
 
 
+def pair_join_kernel(counts, ins, outs, room):
+    n_outs, at, chunk = len(outs) // 2, 0, 0
+    received = (len(ins) - len(counts)) // sum(counts)
+    for count in counts:
+        own, got = ins[at], ins[at + 1 : at + 1 + received * count]
+        start = 0
+        for j in range(count):
+            width = outs[chunk].shape[1]
+            total = own[:, start : start + width]
+            for part in got[j::count]:
+                total += part[...].astype(F32)
+            outs[chunk][...] = total
+            outs[n_outs + chunk][...] = total.astype(BF16)
+            start, chunk = start + width, chunk + 1
+        at += 1 + len(got)
+
+
 def activate_kernel(start, ins, outs, room):
     at = slice(start, start + outs[0].shape[1])
     half = len(ins) // 2
@@ -137,8 +162,10 @@
         out[...] = hidden[k * rows : (k + 1) * rows]
 
 
-def down_kernel(n_pair, n_wide, first, last, ins, outs, room):
-    parts, (wd, *before) = (ins[:-1], ins[-1:]) if first else (ins[:-2], ins[-2:])
+def down_kernel(n_pair, n_wide, n_weights, first, last, ins, outs, room):
+    before = ins[-1:] if not first else []
+    ins = ins[: len(ins) - len(before)]
+    parts, weights = ins[:-n_weights], ins[-n_weights:]
     (hidden,) = room
     c = lax.axis_index("pair")
     rows = parts[0].shape[0]
@@ -147,13 +174,17 @@
         k, piece = divmod(at, pieces)
         block = lax.rem(c + n_pair - k, n_pair) * pieces + piece
         hidden[pl.ds(pl.multiple_of(block * rows, 16), rows), :] = part[...]
-    width = wd.shape[1]
+    width = weights[0].shape[1]
     tile = tile_of(width)
 
     @pl.loop(0, width // tile)
     def _(step):
         at = pl.ds(pl.multiple_of(step * tile, tile), tile)
-        total = jnp.dot(hidden[...], wd[:, at], preferred_element_type=F32)
+        total, start = 0, 0
+        for weight in weights:
+            deep = slice(start, start + weight.shape[0])
+            total += jnp.dot(hidden[:, deep], weight[:, at], preferred_element_type=F32)
+            start += weight.shape[0]
         if before:
             total += before[0][:, at]
         if last:
@@ -182,23 +213,29 @@
     n = len(chunks)
     size = tokens.dtype.itemsize
 
-    def gate_of(*picks):
-        return [(gate_weight, 1, *loads[j]) for j in picks if j < len(loads)]
-
     def bytes_of(fetch):
         return sum(size * f[3] * f[0].shape[1 - f[1]] for f in fetch)
 
-    def down_of(*picks):
-        return [(down_weight, 0, *chunks[j]) for j in picks if j < n]
+    unit = gate_weight.shape[1] // sum(GATE)
+
+    def gate_of(j):
+        return [(gate_weight, 1, *loads[j])]
+
+    def down_of(name):
+        return [(down_weight, 0, start * unit, count * unit) for start, count in DOWN_LOADS[name]]
+
+    def keep(name, fetched):
+        for (start, _), array in zip(DOWN_LOADS[name], fetched):
+            down[start * unit] = array
 
     order = []
 
-    def project(blocks, weight, chunks, fetch, after=()):
-        width, n = weight.shape[1], len(chunks)
+    def project(blocks, weights, chunks, fetch, after=()):
+        width, n = sum(width for _, width in chunks), len(chunks)
         outs, fetched = call(
             order,
-            functools.partial(pair_part_kernel, n_pair, chunks),
-            [*blocks, weight],
+            functools.partial(pair_part_kernel, n_pair, chunks, len(weights)),
+            [*blocks, *weights],
             [pltpu.VMEM((half, width), F32)]
             + [pltpu.VMEM((half, wide), PAIR_TYPE) for _, wide in chunks] * (n_pair - 1)
             + [pltpu.VMEM((rows, depth), BF16)] * (len(blocks) > 1),
@@ -222,6 +259,19 @@
             sums.append([own] + [send(away, "seq", k) for k in range(1, n_seq)])
         return sums
 
+    def pair_join(groups):
+        widths = [width for _, inner in groups for _, width in inner]
+        outs = call(
+            order, functools.partial(pair_join_kernel, [len(inner) for _, inner in groups]),
+            [part for parts, _ in groups for part in parts],
+            [pltpu.VMEM((half, width), kind) for kind in (F32, BF16) for width in widths],
+            [], [], 0, COST * 8 * half * sum(widths),
+        )[0]
+        sums = []
+        for own, away in zip(outs[: len(widths)], outs[len(widths) :]):
+            sums.append([own] + [send(away, "seq", k) for k in range(1, n_seq)])
+        return sums
+
     def activate(ups, gates, start, width):
         hidden, _ = call(
             order, functools.partial(activate_kernel, start), [*ups, *gates],
@@ -238,7 +288,8 @@
 
     def multiply_down(j, parts, total):
         first, last = j == 0, j == n - 1
-        width = parts[0].shape[1]
+        start, width = chunks[j]
+        weights = [down[at] for at in sorted(down) if start <= at < start + width]
         if last:
             outs = [pltpu.VMEM((share, features), F32)]
             outs += [pltpu.VMEM((share, features), BF16)] * (n_wide - 1)
@@ -246,8 +297,8 @@
             outs = [pltpu.VMEM((rows, features), F32)]
         return call(
             order,
-            functools.partial(down_kernel, n_pair, n_wide, first, last),
-            [*parts, down[j], *total],
+            functools.partial(down_kernel, n_pair, n_wide, len(weights), first, last),
+            [*parts, *weights, *total],
             outs,
             [],
             [pltpu.VMEM((rows, width), BF16)],
@@ -262,25 +313,26 @@
     blocks = [tokens] + [send(tokens, "wide", k) for k in range(1, n_wide)]
     up = pltpu.with_memory_space_constraint(up_weight, pltpu.VMEM)
     columns = gate_weight.shape[1]
-    ups, x, (gate,) = project(blocks, up, [(0, columns)], gate_of(0), early)
-    (ups,) = pair_sum(ups, [(0, columns)], [(0, columns)])
-    down, gates = {}, []
-    for j, (start, width) in enumerate(loads):
-        inner = [(a - start, b) for a, b in chunks if start <= a < start + width]
-        last = j == len(loads) - 1
-        parts, _, (weight,) = project([x], gate, inner, down_of(0) if last else gate_of(j + 1))
-        if last:
-            down[0] = weight
-        else:
-            gate = weight
-        gates.append((parts, inner))
-    sums = []
-    for parts, inner in gates:
-        sums += pair_sum(parts, inner, inner)
-    if n > 1:
-        late = list(range(1, n))
-        _, more = load(x, down_of(*late), 0)
-        down.update(zip(late, more))
+    down, whole = {}, [(0, columns)]
+    if n == 1:
+        ups, x, gate = project(blocks, [up], whole, gate_of(0), early)
+        (ups,) = pair_sum(ups, whole, whole)
+        parts, _, (down[0],) = project([x], gate, chunks, [(down_weight, 0, 0, columns)])
+        sums = pair_sum(parts, chunks, chunks)
+    else:
+        ups, x, first = project(blocks, [up], whole, gate_of(0), early)
+        x, second = load(x, gate_of(1), COST * 2 * bytes_of(gate_of(1)))
+        (ups,) = pair_sum(ups, whole, whole)
+        edge = loads[2][0]
+        inner = [chunk for chunk in chunks if chunk[0] < edge]
+        parts, _, (third, *more) = project([x], [*first, *second], inner, gate_of(2) + down_of("gate"))
+        keep("gate", more)
+        outer = [(start - edge, width) for start, width in chunks if start >= edge]
+        others, _, more = project([x], [third], outer, down_of("rest"))
+        keep("rest", more)
+        sums = pair_join([(parts, inner), (others, outer)])
+        _, more = load(x, down_of("late"), 0)
+        keep("late", more)
     load(x, [], 0, ups[1:])
     hiddens = [activate(ups, sums[j], *chunks[j]) for j in range(min(n, 2))]
     total = []

time: 57.9 us -> 59.7 us (1.031)
  Pallas kernels: 28.2 us -> 29.7 us
    pallas_call x15, Pallas kernels: 28.2 us -> 29.7 us  [call(): pl.pallas_call(kernel, out_shape=tuple(outs) + tuple(fetched), in_specs=[...]
  transfers between devices with their start and end apart: 20 -> 20, of which waited for: 6 -> 7; matrix products, arithmetic and copies ran while one was open for 0% -> 0% of each run, Pallas kernels for 32% -> 34%
where the time goes in v9:
time: 59.7 us; the launch traced here: 59.5 us
  Pallas kernels  29.7 us (50%)
  starting transfers between devices  16.9 us (28%)
  waiting for transfers between devices  12 us (20%)
  other arithmetic  0.66 us (1%)
    pallas_call x15, Pallas kernels, call(): pl.pallas_call(kernel, out_shape=tuple(outs) + tuple(fetched), in_specs=[...  29.7 us
    ppermute x20, starting transfers between devices, send(): lax.ppermute(value, axis, [(i, i ^ k if paired else (i + k) % n) for i in...  16.9 us
    ppermute x20, waiting for transfers between devices, send(): lax.ppermute(value, axis, [(i, i ^ k if paired else (i + k) % n) for i in...  12 us
  transfers between devices with their start and end apart: 20, of which 7 were waited for; matrix products, arithmetic and copies ran while one was open for 0% of the time, Pallas kernels for 34%

profile of v9, /device:TPU:0, one launch (start us, length us, event | category | flops | bytes accessed | tf_op | source)
XLA Modules:
  0.0 59.5 jit_solution(12030060488406780530)
XLA Ops:
  0.0 1.0 %shard_map.46 = (bf16[16,2048]{1,0:T(8,128)(2,1)S(1)}, bf16[16,2048]{1,0:T(8,128)(2,1)S(1)}) custom-call(bf16[16,2048]{1,0:T(8,128)(2,1)} %refs_0_.1, bf16[6656,2048]{1,0:T(8,128)(2,1)} %refs_4_.5), custom_call_target="tpu_custom_call" | custom-call | bytes 54525952 | tf_op jit(solution)/shard_map/pallas_call | solution.py:71
  1.0 3.1 %collective-permute-start = (bf16[16,2048]{1,0:T(8,128)(2,1)S(1)}, bf16[16,2048]{1,0:T(8,128)(2,1)S(1)}, u32[]{:S(2)}, u32[]{:S(2)}) collective-permute-start(bf16[16,2048]{1,0:T(8,128)(2,1)S(1)} %get-tuple-element.43.refs_0_.refs_6_), channel_id=1, source_target_pairs={{0,2},{2,0},{4,6},{6,4},{1,3},{3,1},{5,7},{7,5},{8,10},{10,8},{12,... | collective-permute-start | bytes 196616 | tf_op jit(solution)/shard_map/ppermute | solution.py:205
  4.1 2.6 %collective-permute-start.1 = (bf16[16,2048]{1,0:T(8,128)(2,1)S(1)}, bf16[16,2048]{1,0:T(8,128)(2,1)S(1)}, u32[]{:S(2)}, u32[]{:S(2)}) collective-permute-start(bf16[16,2048]{1,0:T(8,128)(2,1)S(1)} %get-tuple-element.43.refs_0_.refs_6_), channel_id=1, source_target_pairs={{0,4},{2,6},{4,0},{6,2},{1,5},{3,7},{5,1},{7,3},{8,12},{10,14},{12... | collective-permute-start | bytes 196616 | tf_op jit(solution)/shard_map/ppermute | solution.py:205
  6.7 4.7 %collective-permute-done.1.refs_2_ = bf16[16,2048]{1,0:T(8,128)(2,1)S(1)} collective-permute-done((bf16[16,2048]{1,0:T(8,128)(2,1)S(1)}, bf16[16,2048]{1,0:T(8,128)(2,1)S(1)}, u32[]{:S(2)}, u32[]{:S(2)}) %collective-permute-start.1) | collective-permute-done | bytes 65568 | tf_op jit(solution)/shard_map/ppermute | solution.py:205
  11.4 1.4 %collective-permute-done.2.refs_3_ = bf16[16,2048]{1,0:T(8,128)(2,1)S(1)} collective-permute-done((bf16[16,2048]{1,0:T(8,128)(2,1)S(1)}, bf16[16,2048]{1,0:T(8,128)(2,1)S(1)}, u32[]{:S(2)}, u32[]{:S(2)}) %collective-permute-start.2) | collective-permute-done | bytes 65568 | tf_op jit(solution)/shard_map/ppermute | solution.py:205
  12.8 6.4 %shard_map.47 = (f32[32,6656]{1,0:T(8,128)S(1)}, bf16[32,6656]{1,0:T(8,128)(2,1)S(1)}, bf16[64,2048]{1,0:T(8,128)(2,1)S(1)}, bf16[2048,4096]{1,0:T(8,128)(2,1)S(1)}) custom-call(bf16[16,2048]{1,0:T(8,128)(2,1)S(1)} %get-tuple-element.43.refs_0_.refs_6_, bf16[16,2048]{1,0:T(8,128)(2,1)S(1)} %collective-permute-done.refs_1_, ...), custom_call_target="tpu_custom_call" | custom-call | flops 87241520 | bytes 1677721 | tf_op jit(solution)/shard_map/pallas_call | solution.py:71
  19.3 2.2 %shard_map.48 = (bf16[64,2048]{1,0:T(8,128)(2,1)S(1)}, bf16[2048,1024]{1,0:T(8,128)(2,1)S(1)}) custom-call(bf16[64,2048]{1,0:T(8,128)(2,1)S(1)} %get-tuple-element.47.refs_0_.refs_1_, bf16[64,2048]{1,0:T(8,128)(2,1)S(1)} %get-tuple-element.47.refs_0_.refs_1_, bf16[2048,6656]{1,0:T(8,128)(2,1)} %refs_4_.4), custom_call_target="tpu_custom_call" | custom-call | bytes 419430 | tf_op jit(solution)/shard_map/pallas_call | solution.py:71
  21.7 1.6 %collective-permute-start.4 = (bf16[32,6656]{1,0:T(8,128)(2,1)S(1)}, bf16[32,6656]{1,0:T(8,128)(2,1)S(1)}, u32[]{:S(2)}, u32[]{:S(2)}) collective-permute-start(bf16[32,6656]{1,0:T(8,128)(2,1)S(1)} %get-tuple-element.50), channel_id=1, source_target_pairs={{0,8},{8,0},{1,9},{9,1},{2,10},{10,2},{3,11},{11,3},{4,12},{12,4},... | collective-permute-start | bytes 1277960 | tf_op jit(solution)/shard_map/ppermute | solution.py:205
  23.2 5.1 %shard_map.50 = (f32[32,5120]{1,0:T(8,128)S(1)}, bf16[32,2560]{1,0:T(8,128)(2,1)S(1)}, bf16[32,2560]{1,0:T(8,128)(2,1)S(1)}, bf16[2048,1536]{1,0:T(8,128)(2,1)S(1)}, bf16[1536,2048]{1,0:T(8,128)(2,1)S(1)}) custom-call(bf16[64,2048]{1,0:T(8,128)(2,1)S(1)} %get-tuple-element.48.refs_2_.refs_0_, bf16[2048,4096]{1,0:T(8,128)(2,1)S(1)} %get-tuple-element.51.refs_1_, ...), custom_call_target="tpu_custom_call" | custom-call | flops 67108864 | bytes 1258291 | tf_op jit(solution)/shard_map/pallas_call | solution.py:71
  28.9 1.6 %shard_map.51 = (f32[32,1536]{1,0:T(8,128)S(1)}, bf16[32,1536]{1,0:T(8,128)(2,1)S(1)}, bf16[512,2048]{1,0:T(8,128)(2,1)S(1)}) custom-call(bf16[64,2048]{1,0:T(8,128)(2,1)S(1)} %get-tuple-element.48.refs_2_.refs_0_, bf16[2048,1536]{1,0:T(8,128)(2,1)S(1)} %get-tuple-element.56.refs_1_, bf16[32,2560]{1,0:T(8,128)(2,1)S(1)} %get-tuple-element.54.refs_2_, ...), custom_call_target="tpu_custom_call" | custom-call | flops 20132660 | bytes 209715 | tf_op jit(solution)/shard_map/pallas_call | solution.py:71
  30.8 1.1 %collective-permute-done.7.refs_4_ = bf16[32,1536]{1,0:T(8,128)(2,1)S(1)} collective-permute-done((bf16[32,1536]{1,0:T(8,128)(2,1)S(1)}, bf16[32,1536]{1,0:T(8,128)(2,1)S(1)}, u32[]{:S(2)}, u32[]{:S(2)}) %collective-permute-start.7) | collective-permute-done | bytes 98336 | tf_op jit(solution)/shard_map/ppermute | solution.py:205
  32.0 0.6 %collective-permute-start.9 = (bf16[32,2560]{1,0:T(8,128)(2,1)S(1)}, bf16[32,2560]{1,0:T(8,128)(2,1)S(1)}, u32[]{:S(2)}, u32[]{:S(2)}) collective-permute-start(bf16[32,2560]{1,0:T(8,128)(2,1)S(1)} %get-tuple-element.62), channel_id=1, source_target_pairs={{0,8},{8,0},{1,9},{9,1},{2,10},{10,2},{3,11},{11,3},{4,12},{12,4},... | collective-permute-start | bytes 491528 | tf_op jit(solution)/shard_map/ppermute | solution.py:205
  32.6 1.5 %collective-permute-start.12 = (bf16[32,2560]{1,0:T(8,128)(2,1)S(1)}, bf16[32,2560]{1,0:T(8,128)(2,1)S(1)}, u32[]{:S(2)}, u32[]{:S(2)}) collective-permute-start(bf16[32,2560]{1,0:T(8,128)(2,1)S(1)} %get-tuple-element.70), channel_id=1, source_target_pairs={{0,8},{8,0},{1,9},{9,1},{2,10},{10,2},{3,11},{11,3},{4,12},{12,4},... | collective-permute-start | bytes 491528 | tf_op jit(solution)/shard_map/ppermute | solution.py:205
  34.6 6.4 %shard_map.53 = (bf16[64,2048]{1,0:T(8,128)(2,1)S(1)}, bf16[512,2048]{1,0:T(8,128)(2,1)S(1)}, bf16[2560,2048]{1,0:T(8,128)(2,1)S(1)}, bf16[1536,2048]{1,0:T(8,128)(2,1)S(1)}) custom-call(bf16[64,2048]{1,0:T(8,128)(2,1)S(1)} %get-tuple-element.48.refs_2_.refs_0_, f32[32,1536]{1,0:T(8,128)S(1)} %get-tuple-element.59.refs_1_.refs_2_, ...), custom_call_target="tpu_custom_call" | custom-call | tf_op jit(solution)/shard_map/pallas_call | solution.py:71
  41.8 0.8 %collective-permute-done.12.refs_3_ = bf16[32,2560]{1,0:T(8,128)(2,1)S(1)} collective-permute-done((bf16[32,2560]{1,0:T(8,128)(2,1)S(1)}, bf16[32,2560]{1,0:T(8,128)(2,1)S(1)}, u32[]{:S(2)}, u32[]{:S(2)}) %collective-permute-start.12) | collective-permute-done | bytes 163872 | tf_op jit(solution)/shard_map/ppermute | solution.py:205
  43.3 2.3 %shard_map.57.refs_4_.refs_5_ = f32[64,2048]{1,0:T(8,128)S(1)} custom-call(bf16[16,2560]{1,0:T(8,128)(2,1)S(1)} %get-tuple-element.64.refs_4_.refs_0_, bf16[16,2560]{1,0:T(8,128)(2,1)S(1)} %get-tuple-element.65.refs_1_, bf16[16,2560]{1,0:T(8,128)(2,1)S(1)} %collective-permute-done.10.refs_2_, bf16[16,2560]{1,0:T(8,128)(2,1)S(1)} %collective-permute-done.11.refs_3_, ...), custom_call_target="tpu_custom_call" | custom-call | flops 33554432 | tf_op jit(solution)/shard_map/pallas_call | solution.py:71
  46.4 2.3 %shard_map.59.refs_5_.refs_6_ = f32[64,2048]{1,0:T(8,128)S(1)} custom-call(bf16[16,2560]{1,0:T(8,128)(2,1)S(1)} %get-tuple-element.71.refs_7_.refs_0_, bf16[16,2560]{1,0:T(8,128)(2,1)S(1)} %get-tuple-element.75.refs_1_, bf16[16,2560]{1,0:T(8,128)(2,1)S(1)} %collective-permute-done.15.refs_2_, bf16[16,2560]{1,0:T(8,128)(2,1)S(1)} %collective-permute-done.16.refs_3_, ...), custom_call_target="tpu_custom_call" | custom-call | flops 33554432 | tf_op jit(solution)/shard_map/pallas_call | solution.py:71
  48.7 1.6 %shard_map.60 = (f32[16,2048]{1,0:T(8,128)S(1)}, bf16[16,2048]{1,0:T(8,128)(2,1)S(1)}, bf16[16,2048]{1,0:T(8,128)(2,1)S(1)}, bf16[16,2048]{1,0:T(8,128)(2,1)S(1)}) custom-call(bf16[16,1536]{1,0:T(8,128)(2,1)S(1)} %get-tuple-element.72.refs_6_.refs_0_, bf16[16,1536]{1,0:T(8,128)(2,1)S(1)} %get-tuple-element.73.refs_1_, ...), custom_call_target="tpu_custom_call" | custom-call | flops 20132660 | tf_op jit(solution)/shard_map/pallas_call | solution.py:71
  50.4 2.3 %collective-permute-start.18 = (bf16[16,2048]{1,0:T(8,128)(2,1)S(1)}, bf16[16,2048]{1,0:T(8,128)(2,1)S(1)}, u32[]{:S(2)}, u32[]{:S(2)}) collective-permute-start(bf16[16,2048]{1,0:T(8,128)(2,1)S(1)} %get-tuple-element.79), channel_id=1, source_target_pairs={{0,4},{2,6},{4,0},{6,2},{1,5},{3,7},{5,1},{7,3},{8,12},{10,14},{12... | collective-permute-start | bytes 196616 | tf_op jit(solution)/shard_map/ppermute | solution.py:205
  52.7 2.0 %collective-permute-start.17 = (bf16[16,2048]{1,0:T(8,128)(2,1)S(1)}, bf16[16,2048]{1,0:T(8,128)(2,1)S(1)}, u32[]{:S(2)}, u32[]{:S(2)}) collective-permute-start(bf16[16,2048]{1,0:T(8,128)(2,1)S(1)} %get-tuple-element.78), channel_id=1, source_target_pairs={{0,6},{2,4},{4,2},{6,0},{1,7},{3,5},{5,3},{7,1},{8,14},{10,12},{12... | collective-permute-start | bytes 196616 | tf_op jit(solution)/shard_map/ppermute | solution.py:205
  54.8 1.0 %collective-permute-done.19 = bf16[16,2048]{1,0:T(8,128)(2,1)S(1)} collective-permute-done((bf16[16,2048]{1,0:T(8,128)(2,1)S(1)}, bf16[16,2048]{1,0:T(8,128)(2,1)S(1)}, u32[]{:S(2)}, u32[]{:S(2)}) %collective-permute-start.19) | collective-permute-done | bytes 65568 | tf_op jit(solution)/shard_map/ppermute | solution.py:205
  55.8 2.3 %collective-permute-done.18 = bf16[16,2048]{1,0:T(8,128)(2,1)S(1)} collective-permute-done((bf16[16,2048]{1,0:T(8,128)(2,1)S(1)}, bf16[16,2048]{1,0:T(8,128)(2,1)S(1)}, u32[]{:S(2)}, u32[]{:S(2)}) %collective-permute-start.18) | collective-permute-done | bytes 65568 | tf_op jit(solution)/shard_map/ppermute | solution.py:205
  58.1 0.8 %collective-permute-done.17 = bf16[16,2048]{1,0:T(8,128)(2,1)S(1)} collective-permute-done((bf16[16,2048]{1,0:T(8,128)(2,1)S(1)}, bf16[16,2048]{1,0:T(8,128)(2,1)S(1)}, u32[]{:S(2)}, u32[]{:S(2)}) %collective-permute-start.17) | collective-permute-done | bytes 65568 | tf_op jit(solution)/shard_map/ppermute | solution.py:205
  58.9 0.7 %add_convert_fusion = bf16[16,2048]{1,0:T(8,128)(2,1)} fusion(bf16[16,2048]{1,0:T(8,128)(2,1)S(1)} %collective-permute-done.19, bf16[16,2048]{1,0:T(8,128)(2,1)S(1)} %collective-permute-done.18, f32[16,2048]{1,0:T(8,128)S(1)} %get-tuple-element.77, bf16[16,2048]{1,0:T(8,128)(2,1)S(1)} %collective-permute-done.17), kind=kLoop, calls=%fused_computation | loop fusion | flops 229376 | bytes 393216 | tf_op jit(solution)/shard_map/convert_element_type | solution.py:347
  (34 shorter events, 4.0 us)
Async XLA Ops:
  0.0 12.8 %copy-start = (bf16[2048,6656]{1,0:T(8,128)(2,1)S(1)}, bf16[2048,6656]{1,0:T(8,128)(2,1)}, u32[]{:S(2)}) copy-start(bf16[2048,6656]{1,0:T(8,128)(2,1)} %refs_4_.3) | copy-start | bytes 81788928
  1.0 5.7 %collective-permute-start = (bf16[16,2048]{1,0:T(8,128)(2,1)S(1)}, bf16[16,2048]{1,0:T(8,128)(2,1)S(1)}, u32[]{:S(2)}, u32[]{:S(2)}) collective-permute-start(bf16[16,2048]{1,0:T(8,128)(2,1)S(1)} %get-tuple-element.43.refs_0_.refs_6_), channel_id=1, source_target_pairs={{0,2},{2,0},{4,6},{6,4},{1,3},{3,1},{5,7},{7,5},{8,10},{10,8},{12,... | collective-permute-start | bytes 196616 | tf_op jit(solution)/shard_map/ppermute | solution.py:205
  4.1 7.3 %collective-permute-start.1 = (bf16[16,2048]{1,0:T(8,128)(2,1)S(1)}, bf16[16,2048]{1,0:T(8,128)(2,1)S(1)}, u32[]{:S(2)}, u32[]{:S(2)}) collective-permute-start(bf16[16,2048]{1,0:T(8,128)(2,1)S(1)} %get-tuple-element.43.refs_0_.refs_6_), channel_id=1, source_target_pairs={{0,4},{2,6},{4,0},{6,2},{1,5},{3,7},{5,1},{7,3},{8,12},{10,14},{12... | collective-permute-start | bytes 196616 | tf_op jit(solution)/shard_map/ppermute | solution.py:205
  6.7 6.1 %collective-permute-start.2 = (bf16[16,2048]{1,0:T(8,128)(2,1)S(1)}, bf16[16,2048]{1,0:T(8,128)(2,1)S(1)}, u32[]{:S(2)}, u32[]{:S(2)}) collective-permute-start(bf16[16,2048]{1,0:T(8,128)(2,1)S(1)} %get-tuple-element.43.refs_0_.refs_6_), channel_id=1, source_target_pairs={{0,6},{2,4},{4,2},{6,0},{1,7},{3,5},{5,3},{7,1},{8,14},{10,12},{12... | collective-permute-start | bytes 196616 | tf_op jit(solution)/shard_map/ppermute | solution.py:205
  19.2 2.3 %collective-permute-start.3 = (bf16[32,6656]{1,0:T(8,128)(2,1)S(1)}, bf16[32,6656]{1,0:T(8,128)(2,1)S(1)}, u32[]{:S(2)}, u32[]{:S(2)}) collective-permute-start(bf16[32,6656]{1,0:T(8,128)(2,1)S(1)} %get-tuple-element.46), channel_id=1, source_target_pairs={{0,1},{1,0},{2,3},{3,2},{4,5},{5,4},{6,7},{7,6},{8,9},{9,8},{10,11... | collective-permute-start | bytes 1277960 | tf_op jit(solution)/shard_map/ppermute | solution.py:205
  21.7 19.4 %collective-permute-start.4 = (bf16[32,6656]{1,0:T(8,128)(2,1)S(1)}, bf16[32,6656]{1,0:T(8,128)(2,1)S(1)}, u32[]{:S(2)}, u32[]{:S(2)}) collective-permute-start(bf16[32,6656]{1,0:T(8,128)(2,1)S(1)} %get-tuple-element.50), channel_id=1, source_target_pairs={{0,8},{8,0},{1,9},{9,1},{2,10},{10,2},{3,11},{11,3},{4,12},{12,4},... | collective-permute-start | bytes 1277960 | tf_op jit(solution)/shard_map/ppermute | solution.py:205
  28.3 3.6 %collective-permute-start.5 = (bf16[32,2560]{1,0:T(8,128)(2,1)S(1)}, bf16[32,2560]{1,0:T(8,128)(2,1)S(1)}, u32[]{:S(2)}, u32[]{:S(2)}) collective-permute-start(bf16[32,2560]{1,0:T(8,128)(2,1)S(1)} %get-tuple-element.54.refs_2_), channel_id=1, source_target_pairs={{0,1},{1,0},{2,3},{3,2},{4,5},{5,4},{6,7},{7,6},{8,9},{9,8},{10,11... | collective-permute-start | bytes 491528 | tf_op jit(solution)/shard_map/ppermute | solution.py:205
  28.6 3.3 %collective-permute-start.6 = (bf16[32,2560]{1,0:T(8,128)(2,1)S(1)}, bf16[32,2560]{1,0:T(8,128)(2,1)S(1)}, u32[]{:S(2)}, u32[]{:S(2)}) collective-permute-start(bf16[32,2560]{1,0:T(8,128)(2,1)S(1)} %get-tuple-element.55), channel_id=1, source_target_pairs={{0,1},{1,0},{2,3},{3,2},{4,5},{5,4},{6,7},{7,6},{8,9},{9,8},{10,11... | collective-permute-start | bytes 491528 | tf_op jit(solution)/shard_map/ppermute | solution.py:205
  30.5 1.4 %collective-permute-start.7 = (bf16[32,1536]{1,0:T(8,128)(2,1)S(1)}, bf16[32,1536]{1,0:T(8,128)(2,1)S(1)}, u32[]{:S(2)}, u32[]{:S(2)}) collective-permute-start(bf16[32,1536]{1,0:T(8,128)(2,1)S(1)} %get-tuple-element.58), channel_id=1, source_target_pairs={{0,1},{1,0},{2,3},{3,2},{4,5},{5,4},{6,7},{7,6},{8,9},{9,8},{10,11... | collective-permute-start | bytes 294920 | tf_op jit(solution)/shard_map/ppermute | solution.py:205
  32.0 9.1 %collective-permute-start.9 = (bf16[32,2560]{1,0:T(8,128)(2,1)S(1)}, bf16[32,2560]{1,0:T(8,128)(2,1)S(1)}, u32[]{:S(2)}, u32[]{:S(2)}) collective-permute-start(bf16[32,2560]{1,0:T(8,128)(2,1)S(1)} %get-tuple-element.62), channel_id=1, source_target_pairs={{0,8},{8,0},{1,9},{9,1},{2,10},{10,2},{3,11},{11,3},{4,12},{12,4},... | collective-permute-start | bytes 491528 | tf_op jit(solution)/shard_map/ppermute | solution.py:205
  32.6 10.0 %collective-permute-start.12 = (bf16[32,2560]{1,0:T(8,128)(2,1)S(1)}, bf16[32,2560]{1,0:T(8,128)(2,1)S(1)}, u32[]{:S(2)}, u32[]{:S(2)}) collective-permute-start(bf16[32,2560]{1,0:T(8,128)(2,1)S(1)} %get-tuple-element.70), channel_id=1, source_target_pairs={{0,8},{8,0},{1,9},{9,1},{2,10},{10,2},{3,11},{11,3},{4,12},{12,4},... | collective-permute-start | bytes 491528 | tf_op jit(solution)/shard_map/ppermute | solution.py:205
  34.1 11.6 %collective-permute-start.8 = (bf16[32,1536]{1,0:T(8,128)(2,1)S(1)}, bf16[32,1536]{1,0:T(8,128)(2,1)S(1)}, u32[]{:S(2)}, u32[]{:S(2)}) collective-permute-start(bf16[32,1536]{1,0:T(8,128)(2,1)S(1)} %get-tuple-element.60), channel_id=1, source_target_pairs={{0,8},{8,0},{1,9},{9,1},{2,10},{10,2},{3,11},{11,3},{4,12},{12,4},... | collective-permute-start | bytes 294920 | tf_op jit(solution)/shard_map/ppermute | solution.py:205
  41.3 2.1 %collective-permute-start.10 = (bf16[16,2560]{1,0:T(8,128)(2,1)S(1)}, bf16[16,2560]{1,0:T(8,128)(2,1)S(1)}, u32[]{:S(2)}, u32[]{:S(2)}) collective-permute-start(bf16[16,2560]{1,0:T(8,128)(2,1)S(1)} %get-tuple-element.64.refs_4_.refs_0_), channel_id=1, source_target_pairs={{0,1},{1,0},{2,3},{3,2},{4,5},{5,4},{6,7},{7,6},{8,9},{9,8},{10,11... | collective-permute-start | bytes 245768 | tf_op jit(solution)/shard_map/ppermute | solution.py:205
  41.3 2.0 %collective-permute-start.11 = (bf16[16,2560]{1,0:T(8,128)(2,1)S(1)}, bf16[16,2560]{1,0:T(8,128)(2,1)S(1)}, u32[]{:S(2)}, u32[]{:S(2)}) collective-permute-start(bf16[16,2560]{1,0:T(8,128)(2,1)S(1)} %get-tuple-element.65.refs_1_), channel_id=1, source_target_pairs={{0,1},{1,0},{2,3},{3,2},{4,5},{5,4},{6,7},{7,6},{8,9},{9,8},{10,11... | collective-permute-start | bytes 245768 | tf_op jit(solution)/shard_map/ppermute | solution.py:205
  42.7 3.6 %collective-permute-start.15 = (bf16[16,2560]{1,0:T(8,128)(2,1)S(1)}, bf16[16,2560]{1,0:T(8,128)(2,1)S(1)}, u32[]{:S(2)}, u32[]{:S(2)}) collective-permute-start(bf16[16,2560]{1,0:T(8,128)(2,1)S(1)} %get-tuple-element.71.refs_7_.refs_0_), channel_id=1, source_target_pairs={{0,1},{1,0},{2,3},{3,2},{4,5},{5,4},{6,7},{7,6},{8,9},{9,8},{10,11... | collective-permute-start | bytes 245768 | tf_op jit(solution)/shard_map/ppermute | solution.py:205
  42.8 3.5 %collective-permute-start.16 = (bf16[16,2560]{1,0:T(8,128)(2,1)S(1)}, bf16[16,2560]{1,0:T(8,128)(2,1)S(1)}, u32[]{:S(2)}, u32[]{:S(2)}) collective-permute-start(bf16[16,2560]{1,0:T(8,128)(2,1)S(1)} %get-tuple-element.75.refs_1_), channel_id=1, source_target_pairs={{0,1},{1,0},{2,3},{3,2},{4,5},{5,4},{6,7},{7,6},{8,9},{9,8},{10,11... | collective-permute-start | bytes 245768 | tf_op jit(solution)/shard_map/ppermute | solution.py:205
  45.8 2.9 %collective-permute-start.13 = (bf16[16,1536]{1,0:T(8,128)(2,1)S(1)}, bf16[16,1536]{1,0:T(8,128)(2,1)S(1)}, u32[]{:S(2)}, u32[]{:S(2)}) collective-permute-start(bf16[16,1536]{1,0:T(8,128)(2,1)S(1)} %get-tuple-element.72.refs_6_.refs_0_), channel_id=1, source_target_pairs={{0,1},{1,0},{2,3},{3,2},{4,5},{5,4},{6,7},{7,6},{8,9},{9,8},{10,11... | collective-permute-start | bytes 147464 | tf_op jit(solution)/shard_map/ppermute | solution.py:205
  45.9 2.8 %collective-permute-start.14 = (bf16[16,1536]{1,0:T(8,128)(2,1)S(1)}, bf16[16,1536]{1,0:T(8,128)(2,1)S(1)}, u32[]{:S(2)}, u32[]{:S(2)}) collective-permute-start(bf16[16,1536]{1,0:T(8,128)(2,1)S(1)} %get-tuple-element.73.refs_1_), channel_id=1, source_target_pairs={{0,1},{1,0},{2,3},{3,2},{4,5},{5,4},{6,7},{7,6},{8,9},{9,8},{10,11... | collective-permute-start | bytes 147464 | tf_op jit(solution)/shard_map/ppermute | solution.py:205
  50.3 5.5 %collective-permute-start.19 = (bf16[16,2048]{1,0:T(8,128)(2,1)S(1)}, bf16[16,2048]{1,0:T(8,128)(2,1)S(1)}, u32[]{:S(2)}, u32[]{:S(2)}) collective-permute-start(bf16[16,2048]{1,0:T(8,128)(2,1)S(1)} %get-tuple-element.80), channel_id=1, source_target_pairs={{0,2},{2,0},{4,6},{6,4},{1,3},{3,1},{5,7},{7,5},{8,10},{10,8},{12,... | collective-permute-start | bytes 196616 | tf_op jit(solution)/shard_map/ppermute | solution.py:205
  50.4 7.7 %collective-permute-start.18 = (bf16[16,2048]{1,0:T(8,128)(2,1)S(1)}, bf16[16,2048]{1,0:T(8,128)(2,1)S(1)}, u32[]{:S(2)}, u32[]{:S(2)}) collective-permute-start(bf16[16,2048]{1,0:T(8,128)(2,1)S(1)} %get-tuple-element.79), channel_id=1, source_target_pairs={{0,4},{2,6},{4,0},{6,2},{1,5},{3,7},{5,1},{7,3},{8,12},{10,14},{12... | collective-permute-start | bytes 196616 | tf_op jit(solution)/shard_map/ppermute | solution.py:205
  52.7 6.1 %collective-permute-start.17 = (bf16[16,2048]{1,0:T(8,128)(2,1)S(1)}, bf16[16,2048]{1,0:T(8,128)(2,1)S(1)}, u32[]{:S(2)}, u32[]{:S(2)}) collective-permute-start(bf16[16,2048]{1,0:T(8,128)(2,1)S(1)} %get-tuple-element.78), channel_id=1, source_target_pairs={{0,6},{2,4},{4,2},{6,0},{1,7},{3,5},{5,3},{7,1},{8,14},{10,12},{12... | collective-permute-start | bytes 196616 | tf_op jit(solution)/shard_map/ppermute | solution.py:205

commit v10 on v9

--- a/solution.py
+++ b/solution.py
@@ -9,11 +9,11 @@
 
 BF16, F32 = jnp.bfloat16, jnp.float32
 TILE = 512
-GATE = (8, 2, 3)
-DOWN = (5, 5, 3)
-DOWN_LOADS = dict(gate=((0, 3),), rest=((3, 1),), late=((4, 1), (5, 5), (10, 3)))
+GATE = (8, 5)
+DOWN = (4, 4, 5)
+DOWN_LOADS = dict(wait=((0, 1),), gate=(), late=((1, 3), (4, 4), (8, 1)), first=((9, 2),), second=((11, 2),))
 PAIR_TYPE = BF16
-COST = 0.05
+COST = 1
 SPLIT = 2
 
 
@@ -295,16 +295,21 @@
             outs += [pltpu.VMEM((share, features), BF16)] * (n_wide - 1)
         else:
             outs = [pltpu.VMEM((rows, features), F32)]
-        return call(
+        name = ("first", "second", "")[min(j, 2)]
+        fetch = down_of(name) if n > 1 and name else []
+        total, more = call(
             order,
             functools.partial(down_kernel, n_pair, n_wide, len(weights), first, last),
             [*parts, *weights, *total],
             outs,
-            [],
+            fetch,
             [pltpu.VMEM((rows, width), BF16)],
             COST * 2 * rows * width * features,
-            0,
-        )[0]
+            COST * 2 * bytes_of(fetch),
+        )
+        if fetch:
+            keep(name, more)
+        return total
 
     _, (tokens, *early) = call(
         order, load_kernel, [], [], [(tokens, 0, 0, share), (down_weight, 0, 0, share)], [],
@@ -321,16 +326,16 @@
         sums = pair_sum(parts, chunks, chunks)
     else:
         ups, x, first = project(blocks, [up], whole, gate_of(0), early)
-        x, second = load(x, gate_of(1), COST * 2 * bytes_of(gate_of(1)))
+        x, more = load(x, down_of("wait"), COST * 2 * bytes_of(down_of("wait")))
+        keep("wait", more)
         (ups,) = pair_sum(ups, whole, whole)
-        edge = loads[2][0]
+        edge = loads[1][0]
         inner = [chunk for chunk in chunks if chunk[0] < edge]
-        parts, _, (third, *more) = project([x], [*first, *second], inner, gate_of(2) + down_of("gate"))
+        parts, _, (second, *more) = project([x], first, inner, gate_of(1) + down_of("gate"))
         keep("gate", more)
         outer = [(start - edge, width) for start, width in chunks if start >= edge]
-        others, _, more = project([x], [third], outer, down_of("rest"))
-        keep("rest", more)
-        sums = pair_join([(parts, inner), (others, outer)])
+        others, _, _ = project([x], [second], outer, [])
+        sums = pair_sum(parts, inner, inner) + pair_sum(others, outer, outer)
         _, more = load(x, down_of("late"), 0)
         keep("late", more)
     load(x, [], 0, ups[1:])

time: 59.7 us -> 56.9 us (0.953)
  waiting for transfers between devices: 12 us -> 9.98 us
  Pallas kernels: 29.7 us -> 28.8 us
    ppermute x20, waiting for transfers between devices: 12 us -> 9.98 us  [send(): lax.ppermute(value, axis, [(i, i ^ k if paired else (i + k) % n) for i in...]
    pallas_call x15 -> x16, Pallas kernels: 29.7 us -> 28.8 us  [call(): pl.pallas_call(kernel, out_shape=tuple(outs) + tuple(fetched), in_specs=[...]
  transfers between devices with their start and end apart: 20 -> 20, of which waited for: 7 -> 6; matrix products, arithmetic and copies ran while one was open for 0% -> 0% of each run, Pallas kernels for 34% -> 33%
where the time goes in v10:
time: 56.9 us; the launch traced here: 56.7 us
  Pallas kernels  28.8 us (51%)
  starting transfers between devices  17 us (30%)
  waiting for transfers between devices  9.98 us (18%)
  other arithmetic  0.66 us (1%)
    pallas_call x16, Pallas kernels, call(): pl.pallas_call(kernel, out_shape=tuple(outs) + tuple(fetched), in_specs=[...  28.8 us
    ppermute x20, starting transfers between devices, send(): lax.ppermute(value, axis, [(i, i ^ k if paired else (i + k) % n) for i in...  17 us
    ppermute x20, waiting for transfers between devices, send(): lax.ppermute(value, axis, [(i, i ^ k if paired else (i + k) % n) for i in...  9.98 us
  transfers between devices with their start and end apart: 20, of which 6 were waited for; matrix products, arithmetic and copies ran while one was open for 0% of the time, Pallas kernels for 33%

profile of v10, /device:TPU:0, one launch (start us, length us, event | category | flops | bytes accessed | tf_op | source)
XLA Modules:
  0.0 56.7 jit_solution(12811391479450149745)
XLA Ops:
  0.0 1.0 %shard_map.46 = (bf16[16,2048]{1,0:T(8,128)(2,1)S(1)}, bf16[16,2048]{1,0:T(8,128)(2,1)S(1)}) custom-call(bf16[16,2048]{1,0:T(8,128)(2,1)} %refs_0_.1, bf16[6656,2048]{1,0:T(8,128)(2,1)} %refs_7_.5), custom_call_target="tpu_custom_call" | custom-call | bytes 54525952 | tf_op jit(solution)/shard_map/pallas_call | solution.py:71
  1.0 5.1 %collective-permute-start.2 = (bf16[16,2048]{1,0:T(8,128)(2,1)S(1)}, bf16[16,2048]{1,0:T(8,128)(2,1)S(1)}, u32[]{:S(2)}, u32[]{:S(2)}) collective-permute-start(bf16[16,2048]{1,0:T(8,128)(2,1)S(1)} %get-tuple-element.45.refs_0_.refs_6_), channel_id=1, source_target_pairs={{0,6},{2,4},{4,2},{6,0},{1,7},{3,5},{5,3},{7,1},{8,14},{10,12},{12... | collective-permute-start | bytes 196616 | tf_op jit(solution)/shard_map/ppermute | solution.py:205
  6.2 0.6 %collective-permute-start = (bf16[16,2048]{1,0:T(8,128)(2,1)S(1)}, bf16[16,2048]{1,0:T(8,128)(2,1)S(1)}, u32[]{:S(2)}, u32[]{:S(2)}) collective-permute-start(bf16[16,2048]{1,0:T(8,128)(2,1)S(1)} %get-tuple-element.45.refs_0_.refs_6_), channel_id=1, source_target_pairs={{0,2},{2,0},{4,6},{6,4},{1,3},{3,1},{5,7},{7,5},{8,10},{10,8},{12,... | collective-permute-start | bytes 196616 | tf_op jit(solution)/shard_map/ppermute | solution.py:205
  6.8 1.9 %collective-permute-done.2.refs_3_ = bf16[16,2048]{1,0:T(8,128)(2,1)S(1)} collective-permute-done((bf16[16,2048]{1,0:T(8,128)(2,1)S(1)}, bf16[16,2048]{1,0:T(8,128)(2,1)S(1)}, u32[]{:S(2)}, u32[]{:S(2)}) %collective-permute-start.2) | collective-permute-done | bytes 65568 | tf_op jit(solution)/shard_map/ppermute | solution.py:205
  8.7 3.0 %collective-permute-done.1.refs_2_ = bf16[16,2048]{1,0:T(8,128)(2,1)S(1)} collective-permute-done((bf16[16,2048]{1,0:T(8,128)(2,1)S(1)}, bf16[16,2048]{1,0:T(8,128)(2,1)S(1)}, u32[]{:S(2)}, u32[]{:S(2)}) %collective-permute-start.1) | collective-permute-done | bytes 65568 | tf_op jit(solution)/shard_map/ppermute | solution.py:205
  11.8 6.4 %shard_map.47 = (f32[32,6656]{1,0:T(8,128)S(1)}, bf16[32,6656]{1,0:T(8,128)(2,1)S(1)}, bf16[64,2048]{1,0:T(8,128)(2,1)S(1)}, bf16[2048,4096]{1,0:T(8,128)(2,1)S(1)}) custom-call(bf16[16,2048]{1,0:T(8,128)(2,1)S(1)} %get-tuple-element.45.refs_0_.refs_6_, bf16[16,2048]{1,0:T(8,128)(2,1)S(1)} %collective-permute-done.refs_1_, ...), custom_call_target="tpu_custom_call" | custom-call | flops 1744830464 | bytes 33554432 | tf_op jit(solution)/shard_map/pallas_call | solution.py:71
  18.3 1.6 %shard_map.48 = (bf16[64,2048]{1,0:T(8,128)(2,1)S(1)}, bf16[512,2048]{1,0:T(8,128)(2,1)S(1)}) custom-call(bf16[64,2048]{1,0:T(8,128)(2,1)S(1)} %get-tuple-element.49.refs_0_.refs_1_, bf16[64,2048]{1,0:T(8,128)(2,1)S(1)} %get-tuple-element.49.refs_0_.refs_1_, bf16[6656,2048]{1,0:T(8,128)(2,1)} %refs_7_.5), custom_call_target="tpu_custom_call" | custom-call | bytes 4194304 | tf_op jit(solution)/shard_map/pallas_call | solution.py:71
  20.2 1.6 %collective-permute-start.4 = (bf16[32,6656]{1,0:T(8,128)(2,1)S(1)}, bf16[32,6656]{1,0:T(8,128)(2,1)S(1)}, u32[]{:S(2)}, u32[]{:S(2)}) collective-permute-start(bf16[32,6656]{1,0:T(8,128)(2,1)S(1)} %get-tuple-element.52), channel_id=1, source_target_pairs={{0,8},{8,0},{1,9},{9,1},{2,10},{10,2},{3,11},{11,3},{4,12},{12,4},... | collective-permute-start | bytes 1277960 | tf_op jit(solution)/shard_map/ppermute | solution.py:205
  21.8 4.1 %shard_map.50 = (f32[32,4096]{1,0:T(8,128)S(1)}, bf16[32,2048]{1,0:T(8,128)(2,1)S(1)}, bf16[32,2048]{1,0:T(8,128)(2,1)S(1)}, bf16[2048,2560]{1,0:T(8,128)(2,1)S(1)}) custom-call(bf16[64,2048]{1,0:T(8,128)(2,1)S(1)} %get-tuple-element.50.refs_2_.refs_0_, bf16[2048,4096]{1,0:T(8,128)(2,1)S(1)} %get-tuple-element.53.refs_1_, ...), custom_call_target="tpu_custom_call" | custom-call | flops 1073741824 | bytes 20971520 | tf_op jit(solution)/shard_map/pallas_call | solution.py:71
  25.9 0.4 collective-permute-start.6
  26.4 2.5 %shard_map.51 = (f32[32,2560]{1,0:T(8,128)S(1)}, bf16[32,2560]{1,0:T(8,128)(2,1)S(1)}) custom-call(bf16[64,2048]{1,0:T(8,128)(2,1)S(1)} %get-tuple-element.50.refs_2_.refs_0_, bf16[2048,2560]{1,0:T(8,128)(2,1)S(1)} %get-tuple-element.54.refs_1_, bf16[32,2048]{1,0:T(8,128)(2,1)S(1)} %get-tuple-element.55.refs_2_), custom_call_target="tpu_custom_call" | custom-call | flops 671088640 | tf_op jit(solution)/shard_map/pallas_call | solution.py:71
  29.1 0.6 %collective-permute-start.9 = (bf16[32,2048]{1,0:T(8,128)(2,1)S(1)}, bf16[32,2048]{1,0:T(8,128)(2,1)S(1)}, u32[]{:S(2)}, u32[]{:S(2)}) collective-permute-start(bf16[32,2048]{1,0:T(8,128)(2,1)S(1)} %get-tuple-element.63), channel_id=1, source_target_pairs={{0,8},{8,0},{1,9},{9,1},{2,10},{10,2},{3,11},{11,3},{4,12},{12,4},... | collective-permute-start | bytes 393224 | tf_op jit(solution)/shard_map/ppermute | solution.py:205
  29.7 1.5 %collective-permute-start.12 = (bf16[32,2048]{1,0:T(8,128)(2,1)S(1)}, bf16[32,2048]{1,0:T(8,128)(2,1)S(1)}, u32[]{:S(2)}, u32[]{:S(2)}) collective-permute-start(bf16[32,2048]{1,0:T(8,128)(2,1)S(1)} %get-tuple-element.70), channel_id=1, source_target_pairs={{0,8},{8,0},{1,9},{9,1},{2,10},{10,2},{3,11},{11,3},{4,12},{12,4},... | collective-permute-start | bytes 393224 | tf_op jit(solution)/shard_map/ppermute | solution.py:205
  31.3 0.6 %collective-permute-start.8 = (bf16[32,2560]{1,0:T(8,128)(2,1)S(1)}, bf16[32,2560]{1,0:T(8,128)(2,1)S(1)}, u32[]{:S(2)}, u32[]{:S(2)}) collective-permute-start(bf16[32,2560]{1,0:T(8,128)(2,1)S(1)} %get-tuple-element.62), channel_id=1, source_target_pairs={{0,8},{8,0},{1,9},{9,1},{2,10},{10,2},{3,11},{11,3},{4,12},{12,4},... | collective-permute-start | bytes 491528 | tf_op jit(solution)/shard_map/ppermute | solution.py:205
  31.9 5.8 %shard_map.54 = (bf16[64,2048]{1,0:T(8,128)(2,1)S(1)}, bf16[1536,2048]{1,0:T(8,128)(2,1)S(1)}, bf16[2048,2048]{1,0:T(8,128)(2,1)S(1)}, bf16[512,2048]{1,0:T(8,128)(2,1)S(1)}) custom-call(bf16[64,2048]{1,0:T(8,128)(2,1)S(1)} %get-tuple-element.50.refs_2_.refs_0_, f32[32,2560]{1,0:T(8,128)S(1)} %get-tuple-element.61.refs_1_.refs_2_, ...), custom_call_target="tpu_custom_call" | custom-call | tf_op jit(solution)/shard_map/pallas_call | solution.py:71
  38.0 0.5 collective-permute-start.10
  39.4 2.2 %shard_map.58 = (f32[64,2048]{1,0:T(8,128)S(1)}, bf16[1024,2048]{1,0:T(8,128)(2,1)S(1)}) custom-call(bf16[16,2048]{1,0:T(8,128)(2,1)S(1)} %get-tuple-element.65.refs_4_.refs_0_, bf16[16,2048]{1,0:T(8,128)(2,1)S(1)} %get-tuple-element.66.refs_1_, bf16[16,2048]{1,0:T(8,128)(2,1)S(1)} %collective-permute-done.10.refs_2_, ...), custom_call_target="tpu_custom_call" | custom-call | flops 536870912 | bytes 8388608 | tf_op jit(solution)/shard_map/pallas_call | solution.py:71
  42.3 2.2 %shard_map.60 = (f32[64,2048]{1,0:T(8,128)S(1)}, bf16[1024,2048]{1,0:T(8,128)(2,1)S(1)}) custom-call(bf16[16,2048]{1,0:T(8,128)(2,1)S(1)} %get-tuple-element.71.refs_6_.refs_0_, bf16[16,2048]{1,0:T(8,128)(2,1)S(1)} %get-tuple-element.77.refs_1_, bf16[16,2048]{1,0:T(8,128)(2,1)S(1)} %collective-permute-done.15.refs_2_, ...), custom_call_target="tpu_custom_call" | custom-call | flops 536870912 | bytes 8388608 | tf_op jit(solution)/shard_map/pallas_call | solution.py:71
  44.5 2.3 %shard_map.61 = (f32[16,2048]{1,0:T(8,128)S(1)}, bf16[16,2048]{1,0:T(8,128)(2,1)S(1)}, bf16[16,2048]{1,0:T(8,128)(2,1)S(1)}, bf16[16,2048]{1,0:T(8,128)(2,1)S(1)}) custom-call(bf16[16,2560]{1,0:T(8,128)(2,1)S(1)} %get-tuple-element.73.refs_6_.refs_0_, bf16[16,2560]{1,0:T(8,128)(2,1)S(1)} %get-tuple-element.74.refs_1_, ...), custom_call_target="tpu_custom_call" | custom-call | flops 671088640 | tf_op jit(solution)/shard_map/pallas_call | solution.py:71
  46.9 2.8 %collective-permute-start.17 = (bf16[16,2048]{1,0:T(8,128)(2,1)S(1)}, bf16[16,2048]{1,0:T(8,128)(2,1)S(1)}, u32[]{:S(2)}, u32[]{:S(2)}) collective-permute-start(bf16[16,2048]{1,0:T(8,128)(2,1)S(1)} %get-tuple-element.82), channel_id=1, source_target_pairs={{0,6},{2,4},{4,2},{6,0},{1,7},{3,5},{5,3},{7,1},{8,14},{10,12},{12... | collective-permute-start | bytes 196616 | tf_op jit(solution)/shard_map/ppermute | solution.py:205
  49.7 1.7 %collective-permute-start.19 = (bf16[16,2048]{1,0:T(8,128)(2,1)S(1)}, bf16[16,2048]{1,0:T(8,128)(2,1)S(1)}, u32[]{:S(2)}, u32[]{:S(2)}) collective-permute-start(bf16[16,2048]{1,0:T(8,128)(2,1)S(1)} %get-tuple-element.84), channel_id=1, source_target_pairs={{0,2},{2,0},{4,6},{6,4},{1,3},{3,1},{5,7},{7,5},{8,10},{10,8},{12,... | collective-permute-start | bytes 196616 | tf_op jit(solution)/shard_map/ppermute | solution.py:205
  51.3 2.4 %collective-permute-done.17 = bf16[16,2048]{1,0:T(8,128)(2,1)S(1)} collective-permute-done((bf16[16,2048]{1,0:T(8,128)(2,1)S(1)}, bf16[16,2048]{1,0:T(8,128)(2,1)S(1)}, u32[]{:S(2)}, u32[]{:S(2)}) %collective-permute-start.17) | collective-permute-done | bytes 65568 | tf_op jit(solution)/shard_map/ppermute | solution.py:205
  53.8 2.2 %collective-permute-done.18 = bf16[16,2048]{1,0:T(8,128)(2,1)S(1)} collective-permute-done((bf16[16,2048]{1,0:T(8,128)(2,1)S(1)}, bf16[16,2048]{1,0:T(8,128)(2,1)S(1)}, u32[]{:S(2)}, u32[]{:S(2)}) %collective-permute-start.18) | collective-permute-done | bytes 65568 | tf_op jit(solution)/shard_map/ppermute | solution.py:205
  56.0 0.7 %add_convert_fusion = bf16[16,2048]{1,0:T(8,128)(2,1)} fusion(bf16[16,2048]{1,0:T(8,128)(2,1)S(1)} %collective-permute-done.19, bf16[16,2048]{1,0:T(8,128)(2,1)S(1)} %collective-permute-done.18, f32[16,2048]{1,0:T(8,128)S(1)} %get-tuple-element.81, bf16[16,2048]{1,0:T(8,128)(2,1)S(1)} %collective-permute-done.17), kind=kLoop, calls=%fused_computation | loop fusion | flops 229376 | bytes 393216 | tf_op jit(solution)/shard_map/convert_element_type | solution.py:352
  (35 shorter events, 2.6 us)
Async XLA Ops:
  0.0 11.8 %copy-start = (bf16[2048,6656]{1,0:T(8,128)(2,1)S(1)}, bf16[2048,6656]{1,0:T(8,128)(2,1)}, u32[]{:S(2)}) copy-start(bf16[2048,6656]{1,0:T(8,128)(2,1)} %refs_4_.2) | copy-start | bytes 81788928
  1.0 7.7 %collective-permute-start.2 = (bf16[16,2048]{1,0:T(8,128)(2,1)S(1)}, bf16[16,2048]{1,0:T(8,128)(2,1)S(1)}, u32[]{:S(2)}, u32[]{:S(2)}) collective-permute-start(bf16[16,2048]{1,0:T(8,128)(2,1)S(1)} %get-tuple-element.45.refs_0_.refs_6_), channel_id=1, source_target_pairs={{0,6},{2,4},{4,2},{6,0},{1,7},{3,5},{5,3},{7,1},{8,14},{10,12},{12... | collective-permute-start | bytes 196616 | tf_op jit(solution)/shard_map/ppermute | solution.py:205
  6.2 5.6 %collective-permute-start.1 = (bf16[16,2048]{1,0:T(8,128)(2,1)S(1)}, bf16[16,2048]{1,0:T(8,128)(2,1)S(1)}, u32[]{:S(2)}, u32[]{:S(2)}) collective-permute-start(bf16[16,2048]{1,0:T(8,128)(2,1)S(1)} %get-tuple-element.45.refs_0_.refs_6_), channel_id=1, source_target_pairs={{0,4},{2,6},{4,0},{6,2},{1,5},{3,7},{5,1},{7,3},{8,12},{10,14},{12... | collective-permute-start | bytes 196616 | tf_op jit(solution)/shard_map/ppermute | solution.py:205
  6.2 5.6 %collective-permute-start = (bf16[16,2048]{1,0:T(8,128)(2,1)S(1)}, bf16[16,2048]{1,0:T(8,128)(2,1)S(1)}, u32[]{:S(2)}, u32[]{:S(2)}) collective-permute-start(bf16[16,2048]{1,0:T(8,128)(2,1)S(1)} %get-tuple-element.45.refs_0_.refs_6_), channel_id=1, source_target_pairs={{0,2},{2,0},{4,6},{6,4},{1,3},{3,1},{5,7},{7,5},{8,10},{10,8},{12,... | collective-permute-start | bytes 196616 | tf_op jit(solution)/shard_map/ppermute | solution.py:205
  18.2 1.8 %collective-permute-start.3 = (bf16[32,6656]{1,0:T(8,128)(2,1)S(1)}, bf16[32,6656]{1,0:T(8,128)(2,1)S(1)}, u32[]{:S(2)}, u32[]{:S(2)}) collective-permute-start(bf16[32,6656]{1,0:T(8,128)(2,1)S(1)} %get-tuple-element.48), channel_id=1, source_target_pairs={{0,1},{1,0},{2,3},{3,2},{4,5},{5,4},{6,7},{7,6},{8,9},{9,8},{10,11... | collective-permute-start | bytes 1277960 | tf_op jit(solution)/shard_map/ppermute | solution.py:205
  20.2 17.5 %collective-permute-start.4 = (bf16[32,6656]{1,0:T(8,128)(2,1)S(1)}, bf16[32,6656]{1,0:T(8,128)(2,1)S(1)}, u32[]{:S(2)}, u32[]{:S(2)}) collective-permute-start(bf16[32,6656]{1,0:T(8,128)(2,1)S(1)} %get-tuple-element.52), channel_id=1, source_target_pairs={{0,8},{8,0},{1,9},{9,1},{2,10},{10,2},{3,11},{11,3},{4,12},{12,4},... | collective-permute-start | bytes 1277960 | tf_op jit(solution)/shard_map/ppermute | solution.py:205
  25.8 3.2 %collective-permute-start.7 = (bf16[32,2048]{1,0:T(8,128)(2,1)S(1)}, bf16[32,2048]{1,0:T(8,128)(2,1)S(1)}, u32[]{:S(2)}, u32[]{:S(2)}) collective-permute-start(bf16[32,2048]{1,0:T(8,128)(2,1)S(1)} %get-tuple-element.59), channel_id=1, source_target_pairs={{0,1},{1,0},{2,3},{3,2},{4,5},{5,4},{6,7},{7,6},{8,9},{9,8},{10,11... | collective-permute-start | bytes 393224 | tf_op jit(solution)/shard_map/ppermute | solution.py:205
  25.9 3.1 %collective-permute-start.6 = (bf16[32,2048]{1,0:T(8,128)(2,1)S(1)}, bf16[32,2048]{1,0:T(8,128)(2,1)S(1)}, u32[]{:S(2)}, u32[]{:S(2)}) collective-permute-start(bf16[32,2048]{1,0:T(8,128)(2,1)S(1)} %get-tuple-element.55.refs_2_), channel_id=1, source_target_pairs={{0,1},{1,0},{2,3},{3,2},{4,5},{5,4},{6,7},{7,6},{8,9},{9,8},{10,11... | collective-permute-start | bytes 393224 | tf_op jit(solution)/shard_map/ppermute | solution.py:205
  28.9 2.3 %collective-permute-start.5 = (bf16[32,2560]{1,0:T(8,128)(2,1)S(1)}, bf16[32,2560]{1,0:T(8,128)(2,1)S(1)}, u32[]{:S(2)}, u32[]{:S(2)}) collective-permute-start(bf16[32,2560]{1,0:T(8,128)(2,1)S(1)} %get-tuple-element.57), channel_id=1, source_target_pairs={{0,1},{1,0},{2,3},{3,2},{4,5},{5,4},{6,7},{7,6},{8,9},{9,8},{10,11... | collective-permute-start | bytes 491528 | tf_op jit(solution)/shard_map/ppermute | solution.py:205
  29.1 8.6 %collective-permute-start.9 = (bf16[32,2048]{1,0:T(8,128)(2,1)S(1)}, bf16[32,2048]{1,0:T(8,128)(2,1)S(1)}, u32[]{:S(2)}, u32[]{:S(2)}) collective-permute-start(bf16[32,2048]{1,0:T(8,128)(2,1)S(1)} %get-tuple-element.63), channel_id=1, source_target_pairs={{0,8},{8,0},{1,9},{9,1},{2,10},{10,2},{3,11},{11,3},{4,12},{12,4},... | collective-permute-start | bytes 393224 | tf_op jit(solution)/shard_map/ppermute | solution.py:205
  29.7 8.8 %collective-permute-start.12 = (bf16[32,2048]{1,0:T(8,128)(2,1)S(1)}, bf16[32,2048]{1,0:T(8,128)(2,1)S(1)}, u32[]{:S(2)}, u32[]{:S(2)}) collective-permute-start(bf16[32,2048]{1,0:T(8,128)(2,1)S(1)} %get-tuple-element.70), channel_id=1, source_target_pairs={{0,8},{8,0},{1,9},{9,1},{2,10},{10,2},{3,11},{11,3},{4,12},{12,4},... | collective-permute-start | bytes 393224 | tf_op jit(solution)/shard_map/ppermute | solution.py:205
  31.3 10.3 %collective-permute-start.8 = (bf16[32,2560]{1,0:T(8,128)(2,1)S(1)}, bf16[32,2560]{1,0:T(8,128)(2,1)S(1)}, u32[]{:S(2)}, u32[]{:S(2)}) collective-permute-start(bf16[32,2560]{1,0:T(8,128)(2,1)S(1)} %get-tuple-element.62), channel_id=1, source_target_pairs={{0,8},{8,0},{1,9},{9,1},{2,10},{10,2},{3,11},{11,3},{4,12},{12,4},... | collective-permute-start | bytes 491528 | tf_op jit(solution)/shard_map/ppermute | solution.py:205
  37.9 1.3 %collective-permute-start.11 = (bf16[16,2048]{1,0:T(8,128)(2,1)S(1)}, bf16[16,2048]{1,0:T(8,128)(2,1)S(1)}, u32[]{:S(2)}, u32[]{:S(2)}) collective-permute-start(bf16[16,2048]{1,0:T(8,128)(2,1)S(1)} %get-tuple-element.66.refs_1_), channel_id=1, source_target_pairs={{0,1},{1,0},{2,3},{3,2},{4,5},{5,4},{6,7},{7,6},{8,9},{9,8},{10,11... | collective-permute-start | bytes 196616 | tf_op jit(solution)/shard_map/ppermute | solution.py:205
  38.0 1.4 %collective-permute-start.10 = (bf16[16,2048]{1,0:T(8,128)(2,1)S(1)}, bf16[16,2048]{1,0:T(8,128)(2,1)S(1)}, u32[]{:S(2)}, u32[]{:S(2)}) collective-permute-start(bf16[16,2048]{1,0:T(8,128)(2,1)S(1)} %get-tuple-element.65.refs_4_.refs_0_), channel_id=1, source_target_pairs={{0,1},{1,0},{2,3},{3,2},{4,5},{5,4},{6,7},{7,6},{8,9},{9,8},{10,11... | collective-permute-start | bytes 196616 | tf_op jit(solution)/shard_map/ppermute | solution.py:205
  38.6 3.7 %collective-permute-start.16 = (bf16[16,2048]{1,0:T(8,128)(2,1)S(1)}, bf16[16,2048]{1,0:T(8,128)(2,1)S(1)}, u32[]{:S(2)}, u32[]{:S(2)}) collective-permute-start(bf16[16,2048]{1,0:T(8,128)(2,1)S(1)} %get-tuple-element.77.refs_1_), channel_id=1, source_target_pairs={{0,1},{1,0},{2,3},{3,2},{4,5},{5,4},{6,7},{7,6},{8,9},{9,8},{10,11... | collective-permute-start | bytes 196616 | tf_op jit(solution)/shard_map/ppermute | solution.py:205
  38.7 3.6 %collective-permute-start.15 = (bf16[16,2048]{1,0:T(8,128)(2,1)S(1)}, bf16[16,2048]{1,0:T(8,128)(2,1)S(1)}, u32[]{:S(2)}, u32[]{:S(2)}) collective-permute-start(bf16[16,2048]{1,0:T(8,128)(2,1)S(1)} %get-tuple-element.71.refs_6_.refs_0_), channel_id=1, source_target_pairs={{0,1},{1,0},{2,3},{3,2},{4,5},{5,4},{6,7},{7,6},{8,9},{9,8},{10,11... | collective-permute-start | bytes 196616 | tf_op jit(solution)/shard_map/ppermute | solution.py:205
  41.7 2.8 %collective-permute-start.14 = (bf16[16,2560]{1,0:T(8,128)(2,1)S(1)}, bf16[16,2560]{1,0:T(8,128)(2,1)S(1)}, u32[]{:S(2)}, u32[]{:S(2)}) collective-permute-start(bf16[16,2560]{1,0:T(8,128)(2,1)S(1)} %get-tuple-element.74.refs_1_), channel_id=1, source_target_pairs={{0,1},{1,0},{2,3},{3,2},{4,5},{5,4},{6,7},{7,6},{8,9},{9,8},{10,11... | collective-permute-start | bytes 245768 | tf_op jit(solution)/shard_map/ppermute | solution.py:205
  42.1 2.4 %collective-permute-start.13 = (bf16[16,2560]{1,0:T(8,128)(2,1)S(1)}, bf16[16,2560]{1,0:T(8,128)(2,1)S(1)}, u32[]{:S(2)}, u32[]{:S(2)}) collective-permute-start(bf16[16,2560]{1,0:T(8,128)(2,1)S(1)} %get-tuple-element.73.refs_6_.refs_0_), channel_id=1, source_target_pairs={{0,1},{1,0},{2,3},{3,2},{4,5},{5,4},{6,7},{7,6},{8,9},{9,8},{10,11... | collective-permute-start | bytes 245768 | tf_op jit(solution)/shard_map/ppermute | solution.py:205
  46.9 6.9 %collective-permute-start.17 = (bf16[16,2048]{1,0:T(8,128)(2,1)S(1)}, bf16[16,2048]{1,0:T(8,128)(2,1)S(1)}, u32[]{:S(2)}, u32[]{:S(2)}) collective-permute-start(bf16[16,2048]{1,0:T(8,128)(2,1)S(1)} %get-tuple-element.82), channel_id=1, source_target_pairs={{0,6},{2,4},{4,2},{6,0},{1,7},{3,5},{5,3},{7,1},{8,14},{10,12},{12... | collective-permute-start | bytes 196616 | tf_op jit(solution)/shard_map/ppermute | solution.py:205
  49.7 6.3 %collective-permute-start.18 = (bf16[16,2048]{1,0:T(8,128)(2,1)S(1)}, bf16[16,2048]{1,0:T(8,128)(2,1)S(1)}, u32[]{:S(2)}, u32[]{:S(2)}) collective-permute-start(bf16[16,2048]{1,0:T(8,128)(2,1)S(1)} %get-tuple-element.83), channel_id=1, source_target_pairs={{0,4},{2,6},{4,0},{6,2},{1,5},{3,7},{5,1},{7,3},{8,12},{10,14},{12... | collective-permute-start | bytes 196616 | tf_op jit(solution)/shard_map/ppermute | solution.py:205
  49.7 6.3 %collective-permute-start.19 = (bf16[16,2048]{1,0:T(8,128)(2,1)S(1)}, bf16[16,2048]{1,0:T(8,128)(2,1)S(1)}, u32[]{:S(2)}, u32[]{:S(2)}) collective-permute-start(bf16[16,2048]{1,0:T(8,128)(2,1)S(1)} %get-tuple-element.84), channel_id=1, source_target_pairs={{0,2},{2,0},{4,6},{6,4},{1,3},{3,1},{5,7},{7,5},{8,10},{10,8},{12,... | collective-permute-start | bytes 196616 | tf_op jit(solution)/shard_map/ppermute | solution.py:205

commit v11 on v10

--- a/solution.py
+++ b/solution.py
@@ -9,9 +9,9 @@
 
 BF16, F32 = jnp.bfloat16, jnp.float32
 TILE = 512
-GATE = (8, 5)
-DOWN = (4, 4, 5)
-DOWN_LOADS = dict(wait=((0, 1),), gate=(), late=((1, 3), (4, 4), (8, 1)), first=((9, 2),), second=((11, 2),))
+GATE = (9, 4)
+DOWN = (5, 4, 4)
+DOWN_LOADS = dict(wait=((0, 1),), gate=((1, 1),), late=((2, 3), (5, 4)), first=((9, 2),), second=((11, 2),))
 PAIR_TYPE = BF16
 COST = 1
 SPLIT = 2
@@ -121,34 +121,19 @@
         start += weight.shape[1]
 
 
-def pair_sum_kernel(chunks, ins, outs, room):
+def pair_sum_kernel(chunks, pieces, ins, outs, room):
     keep, got = ins[0], ins[1:]
-    n, half = len(chunks), len(outs) // 2
-    for j, (start, width) in enumerate(chunks):
-        at = slice(start, start + width)
-        total = keep[:, at]
-        for part in got[j::n]:
-            total += part[...].astype(F32)
-        for own in (0, half):
-            out = outs[own + j] if half == n else outs[own]
-            out[:, slice(0, width) if half == n else at] = total.astype(out.dtype)
-
-
-def pair_join_kernel(counts, ins, outs, room):
-    n_outs, at, chunk = len(outs) // 2, 0, 0
-    received = (len(ins) - len(counts)) // sum(counts)
-    for count in counts:
-        own, got = ins[at], ins[at + 1 : at + 1 + received * count]
-        start = 0
-        for j in range(count):
-            width = outs[chunk].shape[1]
-            total = own[:, start : start + width]
-            for part in got[j::count]:
-                total += part[...].astype(F32)
-            outs[chunk][...] = total
-            outs[n_outs + chunk][...] = total.astype(BF16)
-            start, chunk = start + width, chunk + 1
-        at += 1 + len(got)
+    n, half = len(chunks), len(pieces)
+    for j, (first, wide) in enumerate(chunks):
+        for k, (start, width) in enumerate(pieces):
+            low, high = max(first, start), min(first + wide, start + width)
+            if low >= high:
+                continue
+            total = keep[:, low:high]
+            for part in got[j::n]:
+                total += part[:, low - first : high - first].astype(F32)
+            for out in (outs[k], outs[half + k]):
+                out[:, low - start : high - start] = total.astype(out.dtype)
 
 
 def activate_kernel(start, ins, outs, room):
@@ -250,7 +235,7 @@
 
     def pair_sum(parts, chunks, pieces, after=()):
         outs = call(
-            order, functools.partial(pair_sum_kernel, chunks), parts,
+            order, functools.partial(pair_sum_kernel, chunks, pieces), parts,
             [pltpu.VMEM((half, width), kind) for kind in (F32, BF16) for _, width in pieces],
             [], [], 0, COST * 8 * parts[0].size, after,
         )[0]
@@ -259,23 +244,11 @@
             sums.append([own] + [send(away, "seq", k) for k in range(1, n_seq)])
         return sums
 
-    def pair_join(groups):
-        widths = [width for _, inner in groups for _, width in inner]
-        outs = call(
-            order, functools.partial(pair_join_kernel, [len(inner) for _, inner in groups]),
-            [part for parts, _ in groups for part in parts],
-            [pltpu.VMEM((half, width), kind) for kind in (F32, BF16) for width in widths],
-            [], [], 0, COST * 8 * half * sum(widths),
-        )[0]
-        sums = []
-        for own, away in zip(outs[: len(widths)], outs[len(widths) :]):
-            sums.append([own] + [send(away, "seq", k) for k in range(1, n_seq)])
-        return sums
-
     def activate(ups, gates, start, width):
+        split = SPLIT if start == 0 else 1
         hidden, _ = call(
             order, functools.partial(activate_kernel, start), [*ups, *gates],
-            [pltpu.VMEM((half // SPLIT, width), BF16)] * SPLIT, [], [], 0, COST * 8 * half * width,
+            [pltpu.VMEM((half // split, width), BF16)] * split, [], [], 0, COST * 8 * half * width,
         )
         got = [send(piece, "pair", k) for k in range(1, n_pair) for piece in hidden]
         return [*hidden, *got]

time: 56.9 us -> 57.3 us (level)
  waiting for transfers between devices: 9.98 us -> 11.5 us
  Pallas kernels: 28.8 us -> 28 us
    ppermute x20 -> x18, waiting for transfers between devices: 9.98 us -> 11.5 us  [send(): lax.ppermute(value, axis, [(i, i ^ k if paired else (i + k) % n) for i in...]
    pallas_call x16, Pallas kernels: 28.8 us -> 28 us  [call(): pl.pallas_call(kernel, out_shape=tuple(outs) + tuple(fetched), in_specs=[...]
    ppermute x20 -> x18, starting transfers between devices: 17 us -> 16.7 us  [send(): lax.ppermute(value, axis, [(i, i ^ k if paired else (i + k) % n) for i in...]
  transfers between devices with their start and end apart: 20 -> 18, of which waited for: 6 -> 6; matrix products, arithmetic and copies ran while one was open for 0% -> 0% of each run, Pallas kernels for 33% -> 32%
where the time goes in v11:
time: 57.3 us; the launch traced here: 57.1 us
  Pallas kernels  28 us (49%)
  starting transfers between devices  16.7 us (29%)
  waiting for transfers between devices  11.5 us (20%)
  other arithmetic  0.66 us (1%)
    pallas_call x16, Pallas kernels, call(): pl.pallas_call(kernel, out_shape=tuple(outs) + tuple(fetched), in_specs=[...  28 us
    ppermute x18, starting transfers between devices, send(): lax.ppermute(value, axis, [(i, i ^ k if paired else (i + k) % n) for i in...  16.7 us
    ppermute x18, waiting for transfers between devices, send(): lax.ppermute(value, axis, [(i, i ^ k if paired else (i + k) % n) for i in...  11.5 us
  transfers between devices with their start and end apart: 18, of which 6 were waited for; matrix products, arithmetic and copies ran while one was open for 0% of the time, Pallas kernels for 32%

profile of v11, /device:TPU:0, one launch (start us, length us, event | category | flops | bytes accessed | tf_op | source)
XLA Modules:
  0.0 57.1 jit_solution(1899809809778953686)
XLA Ops:
  0.0 1.0 %shard_map.46 = (bf16[16,2048]{1,0:T(8,128)(2,1)S(1)}, bf16[16,2048]{1,0:T(8,128)(2,1)S(1)}) custom-call(bf16[16,2048]{1,0:T(8,128)(2,1)} %refs_0_.1, bf16[6656,2048]{1,0:T(8,128)(2,1)} %refs_5_.1), custom_call_target="tpu_custom_call" | custom-call | bytes 54525952 | tf_op jit(solution)/shard_map/pallas_call | solution.py:71
  1.0 5.1 %collective-permute-start.2 = (bf16[16,2048]{1,0:T(8,128)(2,1)S(1)}, bf16[16,2048]{1,0:T(8,128)(2,1)S(1)}, u32[]{:S(2)}, u32[]{:S(2)}) collective-permute-start(bf16[16,2048]{1,0:T(8,128)(2,1)S(1)} %get-tuple-element.41.refs_0_.refs_6_), channel_id=1, source_target_pairs={{0,6},{2,4},{4,2},{6,0},{1,7},{3,5},{5,3},{7,1},{8,14},{10,12},{12... | collective-permute-start | bytes 196616 | tf_op jit(solution)/shard_map/ppermute | solution.py:190
  6.2 0.6 %collective-permute-start = (bf16[16,2048]{1,0:T(8,128)(2,1)S(1)}, bf16[16,2048]{1,0:T(8,128)(2,1)S(1)}, u32[]{:S(2)}, u32[]{:S(2)}) collective-permute-start(bf16[16,2048]{1,0:T(8,128)(2,1)S(1)} %get-tuple-element.41.refs_0_.refs_6_), channel_id=1, source_target_pairs={{0,2},{2,0},{4,6},{6,4},{1,3},{3,1},{5,7},{7,5},{8,10},{10,8},{12,... | collective-permute-start | bytes 196616 | tf_op jit(solution)/shard_map/ppermute | solution.py:190
  6.8 1.9 %collective-permute-done.2.refs_3_ = bf16[16,2048]{1,0:T(8,128)(2,1)S(1)} collective-permute-done((bf16[16,2048]{1,0:T(8,128)(2,1)S(1)}, bf16[16,2048]{1,0:T(8,128)(2,1)S(1)}, u32[]{:S(2)}, u32[]{:S(2)}) %collective-permute-start.2) | collective-permute-done | bytes 65568 | tf_op jit(solution)/shard_map/ppermute | solution.py:190
  8.7 3.0 %collective-permute-done.1.refs_2_ = bf16[16,2048]{1,0:T(8,128)(2,1)S(1)} collective-permute-done((bf16[16,2048]{1,0:T(8,128)(2,1)S(1)}, bf16[16,2048]{1,0:T(8,128)(2,1)S(1)}, u32[]{:S(2)}, u32[]{:S(2)}) %collective-permute-start.1) | collective-permute-done | bytes 65568 | tf_op jit(solution)/shard_map/ppermute | solution.py:190
  11.8 6.5 %shard_map.47 = (f32[32,6656]{1,0:T(8,128)S(1)}, bf16[32,6656]{1,0:T(8,128)(2,1)S(1)}, bf16[64,2048]{1,0:T(8,128)(2,1)S(1)}, bf16[2048,4608]{1,0:T(8,128)(2,1)S(1)}) custom-call(bf16[16,2048]{1,0:T(8,128)(2,1)S(1)} %get-tuple-element.41.refs_0_.refs_6_, bf16[16,2048]{1,0:T(8,128)(2,1)S(1)} %collective-permute-done.refs_1_, ...), custom_call_target="tpu_custom_call" | custom-call | flops 1744830464 | bytes 37748736 | tf_op jit(solution)/shard_map/pallas_call | solution.py:71
  18.3 1.6 %shard_map.48 = (bf16[64,2048]{1,0:T(8,128)(2,1)S(1)}, bf16[512,2048]{1,0:T(8,128)(2,1)S(1)}) custom-call(bf16[64,2048]{1,0:T(8,128)(2,1)S(1)} %get-tuple-element.45.refs_0_.refs_1_, bf16[64,2048]{1,0:T(8,128)(2,1)S(1)} %get-tuple-element.45.refs_0_.refs_1_, bf16[6656,2048]{1,0:T(8,128)(2,1)} %refs_5_.1), custom_call_target="tpu_custom_call" | custom-call | bytes 4194304 | tf_op jit(solution)/shard_map/pallas_call | solution.py:71
  20.2 1.6 %collective-permute-start.4 = (bf16[32,6656]{1,0:T(8,128)(2,1)S(1)}, bf16[32,6656]{1,0:T(8,128)(2,1)S(1)}, u32[]{:S(2)}, u32[]{:S(2)}) collective-permute-start(bf16[32,6656]{1,0:T(8,128)(2,1)S(1)} %get-tuple-element.48), channel_id=1, source_target_pairs={{0,8},{8,0},{1,9},{9,1},{2,10},{10,2},{3,11},{11,3},{4,12},{12,4},... | collective-permute-start | bytes 1277960 | tf_op jit(solution)/shard_map/ppermute | solution.py:190
  21.8 4.5 %shard_map.50 = (f32[32,4608]{1,0:T(8,128)S(1)}, bf16[32,2560]{1,0:T(8,128)(2,1)S(1)}, bf16[32,2048]{1,0:T(8,128)(2,1)S(1)}, bf16[2048,2048]{1,0:T(8,128)(2,1)S(1)}, bf16[512,2048]{1,0:T(8,128)(2,1)S(1)}) custom-call(bf16[64,2048]{1,0:T(8,128)(2,1)S(1)} %get-tuple-element.46.refs_2_.refs_0_, bf16[2048,4608]{1,0:T(8,128)(2,1)S(1)} %get-tuple-element.49.refs_1_, ...), custom_call_target="tpu_custom_call" | custom-call | flops 1207959552 | bytes 20971520 | tf_op jit(solution)/shard_map/pallas_call | solution.py:71
  26.4 0.4 collective-permute-start.7
  26.8 2.0 %shard_map.51 = (f32[32,2048]{1,0:T(8,128)S(1)}, bf16[32,2048]{1,0:T(8,128)(2,1)S(1)}) custom-call(bf16[64,2048]{1,0:T(8,128)(2,1)S(1)} %get-tuple-element.46.refs_2_.refs_0_, bf16[2048,2048]{1,0:T(8,128)(2,1)S(1)} %get-tuple-element.50.refs_1_, bf16[32,2048]{1,0:T(8,128)(2,1)S(1)} %get-tuple-element.51.refs_2_), custom_call_target="tpu_custom_call" | custom-call | flops 536870912 | tf_op jit(solution)/shard_map/pallas_call | solution.py:71
  29.0 0.6 %collective-permute-start.9 = (bf16[32,2560]{1,0:T(8,128)(2,1)S(1)}, bf16[32,2560]{1,0:T(8,128)(2,1)S(1)}, u32[]{:S(2)}, u32[]{:S(2)}) collective-permute-start(bf16[32,2560]{1,0:T(8,128)(2,1)S(1)} %get-tuple-element.60), channel_id=1, source_target_pairs={{0,8},{8,0},{1,9},{9,1},{2,10},{10,2},{3,11},{11,3},{4,12},{12,4},... | collective-permute-start | bytes 491528 | tf_op jit(solution)/shard_map/ppermute | solution.py:190
  29.6 1.5 %collective-permute-start.12 = (bf16[32,2048]{1,0:T(8,128)(2,1)S(1)}, bf16[32,2048]{1,0:T(8,128)(2,1)S(1)}, u32[]{:S(2)}, u32[]{:S(2)}) collective-permute-start(bf16[32,2048]{1,0:T(8,128)(2,1)S(1)} %get-tuple-element.67), channel_id=1, source_target_pairs={{0,8},{8,0},{1,9},{9,1},{2,10},{10,2},{3,11},{11,3},{4,12},{12,4},... | collective-permute-start | bytes 393224 | tf_op jit(solution)/shard_map/ppermute | solution.py:190
  31.1 5.2 %shard_map.54 = (bf16[64,2048]{1,0:T(8,128)(2,1)S(1)}, bf16[1536,2048]{1,0:T(8,128)(2,1)S(1)}, bf16[2048,2048]{1,0:T(8,128)(2,1)S(1)}) custom-call(bf16[64,2048]{1,0:T(8,128)(2,1)S(1)} %get-tuple-element.46.refs_2_.refs_0_, f32[32,2048]{1,0:T(8,128)S(1)} %get-tuple-element.57.refs_1_.refs_2_, bf16[6656,2048]{1,0:T(8,128)(2,1)} %refs_5_.1, ...), custom_call_target="tpu_custom_call" | custom-call | tf_op jit(solution)/shard_map/pallas_call | solution.py:71
  37.2 1.5 %collective-permute-start.8 = (bf16[32,2048]{1,0:T(8,128)(2,1)S(1)}, bf16[32,2048]{1,0:T(8,128)(2,1)S(1)}, u32[]{:S(2)}, u32[]{:S(2)}) collective-permute-start(bf16[32,2048]{1,0:T(8,128)(2,1)S(1)} %get-tuple-element.58), channel_id=1, source_target_pairs={{0,8},{8,0},{1,9},{9,1},{2,10},{10,2},{3,11},{11,3},{4,12},{12,4},... | collective-permute-start | bytes 393224 | tf_op jit(solution)/shard_map/ppermute | solution.py:190
  38.9 2.3 %shard_map.58 = (f32[64,2048]{1,0:T(8,128)S(1)}, bf16[1024,2048]{1,0:T(8,128)(2,1)S(1)}) custom-call(bf16[16,2560]{1,0:T(8,128)(2,1)S(1)} %get-tuple-element.62.refs_4_.refs_0_, bf16[16,2560]{1,0:T(8,128)(2,1)S(1)} %get-tuple-element.63.refs_1_, bf16[16,2560]{1,0:T(8,128)(2,1)S(1)} %collective-permute-done.10.refs_2_, ...), custom_call_target="tpu_custom_call" | custom-call | flops 671088640 | bytes 8388608 | tf_op jit(solution)/shard_map/pallas_call | solution.py:71
  41.2 1.5 %collective-permute-done.8.refs_3_ = bf16[32,2048]{1,0:T(8,128)(2,1)S(1)} collective-permute-done((bf16[32,2048]{1,0:T(8,128)(2,1)S(1)}, bf16[32,2048]{1,0:T(8,128)(2,1)S(1)}, u32[]{:S(2)}, u32[]{:S(2)}) %collective-permute-start.8) | collective-permute-done | bytes 131104 | tf_op jit(solution)/shard_map/ppermute | solution.py:190
  43.0 2.2 %shard_map.60 = (f32[64,2048]{1,0:T(8,128)S(1)}, bf16[1024,2048]{1,0:T(8,128)(2,1)S(1)}) custom-call(bf16[32,2048]{1,0:T(8,128)(2,1)S(1)} %shard_map.57.refs_7_.refs_0_, bf16[32,2048]{1,0:T(8,128)(2,1)S(1)} %collective-permute-done.14.refs_1_, bf16[2048,2048]{1,0:T(8,128)(2,1)S(1)} %get-tuple-element.70.refs_2_, ...), custom_call_target="tpu_custom_call" | custom-call | flops 536870912 | bytes 8388608 | tf_op jit(solution)/shard_map/pallas_call | solution.py:71
  45.2 2.0 %shard_map.61 = (f32[16,2048]{1,0:T(8,128)S(1)}, bf16[16,2048]{1,0:T(8,128)(2,1)S(1)}, bf16[16,2048]{1,0:T(8,128)(2,1)S(1)}, bf16[16,2048]{1,0:T(8,128)(2,1)S(1)}) custom-call(bf16[32,2048]{1,0:T(8,128)(2,1)S(1)} %shard_map.59.refs_4_.refs_0_, bf16[32,2048]{1,0:T(8,128)(2,1)S(1)} %collective-permute-done.13.refs_1_, ...), custom_call_target="tpu_custom_call" | custom-call | flops 536870912 | tf_op jit(solution)/shard_map/pallas_call | solution.py:71
  47.2 2.8 %collective-permute-start.15 = (bf16[16,2048]{1,0:T(8,128)(2,1)S(1)}, bf16[16,2048]{1,0:T(8,128)(2,1)S(1)}, u32[]{:S(2)}, u32[]{:S(2)}) collective-permute-start(bf16[16,2048]{1,0:T(8,128)(2,1)S(1)} %get-tuple-element.74), channel_id=1, source_target_pairs={{0,6},{2,4},{4,2},{6,0},{1,7},{3,5},{5,3},{7,1},{8,14},{10,12},{12... | collective-permute-start | bytes 196616 | tf_op jit(solution)/shard_map/ppermute | solution.py:190
  50.0 1.7 %collective-permute-start.17 = (bf16[16,2048]{1,0:T(8,128)(2,1)S(1)}, bf16[16,2048]{1,0:T(8,128)(2,1)S(1)}, u32[]{:S(2)}, u32[]{:S(2)}) collective-permute-start(bf16[16,2048]{1,0:T(8,128)(2,1)S(1)} %get-tuple-element.76), channel_id=1, source_target_pairs={{0,2},{2,0},{4,6},{6,4},{1,3},{3,1},{5,7},{7,5},{8,10},{10,8},{12,... | collective-permute-start | bytes 196616 | tf_op jit(solution)/shard_map/ppermute | solution.py:190
  51.6 2.4 %collective-permute-done.15 = bf16[16,2048]{1,0:T(8,128)(2,1)S(1)} collective-permute-done((bf16[16,2048]{1,0:T(8,128)(2,1)S(1)}, bf16[16,2048]{1,0:T(8,128)(2,1)S(1)}, u32[]{:S(2)}, u32[]{:S(2)}) %collective-permute-start.15) | collective-permute-done | bytes 65568 | tf_op jit(solution)/shard_map/ppermute | solution.py:190
  54.0 2.4 %collective-permute-done.16 = bf16[16,2048]{1,0:T(8,128)(2,1)S(1)} collective-permute-done((bf16[16,2048]{1,0:T(8,128)(2,1)S(1)}, bf16[16,2048]{1,0:T(8,128)(2,1)S(1)}, u32[]{:S(2)}, u32[]{:S(2)}) %collective-permute-start.16) | collective-permute-done | bytes 65568 | tf_op jit(solution)/shard_map/ppermute | solution.py:190
  56.4 0.7 %add_convert_fusion = bf16[16,2048]{1,0:T(8,128)(2,1)} fusion(bf16[16,2048]{1,0:T(8,128)(2,1)S(1)} %collective-permute-done.17, bf16[16,2048]{1,0:T(8,128)(2,1)S(1)} %collective-permute-done.16, f32[16,2048]{1,0:T(8,128)S(1)} %get-tuple-element.73, bf16[16,2048]{1,0:T(8,128)(2,1)S(1)} %collective-permute-done.15), kind=kLoop, calls=%fused_computation | loop fusion | flops 229376 | bytes 393216 | tf_op jit(solution)/shard_map/convert_element_type | solution.py:325
  (31 shorter events, 1.8 us)
Async XLA Ops:
  0.0 11.8 %copy-start = (bf16[2048,6656]{1,0:T(8,128)(2,1)S(1)}, bf16[2048,6656]{1,0:T(8,128)(2,1)}, u32[]{:S(2)}) copy-start(bf16[2048,6656]{1,0:T(8,128)(2,1)} %refs_4_.2) | copy-start | bytes 81788928
  1.0 7.7 %collective-permute-start.2 = (bf16[16,2048]{1,0:T(8,128)(2,1)S(1)}, bf16[16,2048]{1,0:T(8,128)(2,1)S(1)}, u32[]{:S(2)}, u32[]{:S(2)}) collective-permute-start(bf16[16,2048]{1,0:T(8,128)(2,1)S(1)} %get-tuple-element.41.refs_0_.refs_6_), channel_id=1, source_target_pairs={{0,6},{2,4},{4,2},{6,0},{1,7},{3,5},{5,3},{7,1},{8,14},{10,12},{12... | collective-permute-start | bytes 196616 | tf_op jit(solution)/shard_map/ppermute | solution.py:190
  6.2 5.6 %collective-permute-start.1 = (bf16[16,2048]{1,0:T(8,128)(2,1)S(1)}, bf16[16,2048]{1,0:T(8,128)(2,1)S(1)}, u32[]{:S(2)}, u32[]{:S(2)}) collective-permute-start(bf16[16,2048]{1,0:T(8,128)(2,1)S(1)} %get-tuple-element.41.refs_0_.refs_6_), channel_id=1, source_target_pairs={{0,4},{2,6},{4,0},{6,2},{1,5},{3,7},{5,1},{7,3},{8,12},{10,14},{12... | collective-permute-start | bytes 196616 | tf_op jit(solution)/shard_map/ppermute | solution.py:190
  6.2 5.6 %collective-permute-start = (bf16[16,2048]{1,0:T(8,128)(2,1)S(1)}, bf16[16,2048]{1,0:T(8,128)(2,1)S(1)}, u32[]{:S(2)}, u32[]{:S(2)}) collective-permute-start(bf16[16,2048]{1,0:T(8,128)(2,1)S(1)} %get-tuple-element.41.refs_0_.refs_6_), channel_id=1, source_target_pairs={{0,2},{2,0},{4,6},{6,4},{1,3},{3,1},{5,7},{7,5},{8,10},{10,8},{12,... | collective-permute-start | bytes 196616 | tf_op jit(solution)/shard_map/ppermute | solution.py:190
  18.2 1.8 %collective-permute-start.3 = (bf16[32,6656]{1,0:T(8,128)(2,1)S(1)}, bf16[32,6656]{1,0:T(8,128)(2,1)S(1)}, u32[]{:S(2)}, u32[]{:S(2)}) collective-permute-start(bf16[32,6656]{1,0:T(8,128)(2,1)S(1)} %get-tuple-element.44), channel_id=1, source_target_pairs={{0,1},{1,0},{2,3},{3,2},{4,5},{5,4},{6,7},{7,6},{8,9},{9,8},{10,11... | collective-permute-start | bytes 1277960 | tf_op jit(solution)/shard_map/ppermute | solution.py:190
  20.2 16.1 %collective-permute-start.4 = (bf16[32,6656]{1,0:T(8,128)(2,1)S(1)}, bf16[32,6656]{1,0:T(8,128)(2,1)S(1)}, u32[]{:S(2)}, u32[]{:S(2)}) collective-permute-start(bf16[32,6656]{1,0:T(8,128)(2,1)S(1)} %get-tuple-element.48), channel_id=1, source_target_pairs={{0,8},{8,0},{1,9},{9,1},{2,10},{10,2},{3,11},{11,3},{4,12},{12,4},... | collective-permute-start | bytes 1277960 | tf_op jit(solution)/shard_map/ppermute | solution.py:190
  26.2 2.6 %collective-permute-start.6 = (bf16[32,2560]{1,0:T(8,128)(2,1)S(1)}, bf16[32,2560]{1,0:T(8,128)(2,1)S(1)}, u32[]{:S(2)}, u32[]{:S(2)}) collective-permute-start(bf16[32,2560]{1,0:T(8,128)(2,1)S(1)} %get-tuple-element.55), channel_id=1, source_target_pairs={{0,1},{1,0},{2,3},{3,2},{4,5},{5,4},{6,7},{7,6},{8,9},{9,8},{10,11... | collective-permute-start | bytes 491528 | tf_op jit(solution)/shard_map/ppermute | solution.py:190
  26.4 2.5 %collective-permute-start.7 = (bf16[32,2048]{1,0:T(8,128)(2,1)S(1)}, bf16[32,2048]{1,0:T(8,128)(2,1)S(1)}, u32[]{:S(2)}, u32[]{:S(2)}) collective-permute-start(bf16[32,2048]{1,0:T(8,128)(2,1)S(1)} %get-tuple-element.51.refs_2_), channel_id=1, source_target_pairs={{0,1},{1,0},{2,3},{3,2},{4,5},{5,4},{6,7},{7,6},{8,9},{9,8},{10,11... | collective-permute-start | bytes 393224 | tf_op jit(solution)/shard_map/ppermute | solution.py:190
  29.0 7.5 %collective-permute-start.9 = (bf16[32,2560]{1,0:T(8,128)(2,1)S(1)}, bf16[32,2560]{1,0:T(8,128)(2,1)S(1)}, u32[]{:S(2)}, u32[]{:S(2)}) collective-permute-start(bf16[32,2560]{1,0:T(8,128)(2,1)S(1)} %get-tuple-element.60), channel_id=1, source_target_pairs={{0,8},{8,0},{1,9},{9,1},{2,10},{10,2},{3,11},{11,3},{4,12},{12,4},... | collective-permute-start | bytes 491528 | tf_op jit(solution)/shard_map/ppermute | solution.py:190
  29.6 1.5 %collective-permute-start.5 = (bf16[32,2048]{1,0:T(8,128)(2,1)S(1)}, bf16[32,2048]{1,0:T(8,128)(2,1)S(1)}, u32[]{:S(2)}, u32[]{:S(2)}) collective-permute-start(bf16[32,2048]{1,0:T(8,128)(2,1)S(1)} %get-tuple-element.53), channel_id=1, source_target_pairs={{0,1},{1,0},{2,3},{3,2},{4,5},{5,4},{6,7},{7,6},{8,9},{9,8},{10,11... | collective-permute-start | bytes 393224 | tf_op jit(solution)/shard_map/ppermute | solution.py:190
  29.6 9.1 %collective-permute-start.12 = (bf16[32,2048]{1,0:T(8,128)(2,1)S(1)}, bf16[32,2048]{1,0:T(8,128)(2,1)S(1)}, u32[]{:S(2)}, u32[]{:S(2)}) collective-permute-start(bf16[32,2048]{1,0:T(8,128)(2,1)S(1)} %get-tuple-element.67), channel_id=1, source_target_pairs={{0,8},{8,0},{1,9},{9,1},{2,10},{10,2},{3,11},{11,3},{4,12},{12,4},... | collective-permute-start | bytes 393224 | tf_op jit(solution)/shard_map/ppermute | solution.py:190
  36.6 2.3 %collective-permute-start.11 = (bf16[16,2560]{1,0:T(8,128)(2,1)S(1)}, bf16[16,2560]{1,0:T(8,128)(2,1)S(1)}, u32[]{:S(2)}, u32[]{:S(2)}) collective-permute-start(bf16[16,2560]{1,0:T(8,128)(2,1)S(1)} %get-tuple-element.63.refs_1_), channel_id=1, source_target_pairs={{0,1},{1,0},{2,3},{3,2},{4,5},{5,4},{6,7},{7,6},{8,9},{9,8},{10,11... | collective-permute-start | bytes 245768 | tf_op jit(solution)/shard_map/ppermute | solution.py:190
  36.8 2.0 %collective-permute-start.10 = (bf16[16,2560]{1,0:T(8,128)(2,1)S(1)}, bf16[16,2560]{1,0:T(8,128)(2,1)S(1)}, u32[]{:S(2)}, u32[]{:S(2)}) collective-permute-start(bf16[16,2560]{1,0:T(8,128)(2,1)S(1)} %get-tuple-element.62.refs_4_.refs_0_), channel_id=1, source_target_pairs={{0,1},{1,0},{2,3},{3,2},{4,5},{5,4},{6,7},{7,6},{8,9},{9,8},{10,11... | collective-permute-start | bytes 245768 | tf_op jit(solution)/shard_map/ppermute | solution.py:190
  37.2 5.6 %collective-permute-start.8 = (bf16[32,2048]{1,0:T(8,128)(2,1)S(1)}, bf16[32,2048]{1,0:T(8,128)(2,1)S(1)}, u32[]{:S(2)}, u32[]{:S(2)}) collective-permute-start(bf16[32,2048]{1,0:T(8,128)(2,1)S(1)} %get-tuple-element.58), channel_id=1, source_target_pairs={{0,8},{8,0},{1,9},{9,1},{2,10},{10,2},{3,11},{11,3},{4,12},{12,4},... | collective-permute-start | bytes 393224 | tf_op jit(solution)/shard_map/ppermute | solution.py:190
  38.8 4.2 %collective-permute-start.14 = (bf16[32,2048]{1,0:T(8,128)(2,1)S(1)}, bf16[32,2048]{1,0:T(8,128)(2,1)S(1)}, u32[]{:S(2)}, u32[]{:S(2)}) collective-permute-start(bf16[32,2048]{1,0:T(8,128)(2,1)S(1)} %shard_map.57.refs_7_.refs_0_), channel_id=1, source_target_pairs={{0,1},{1,0},{2,3},{3,2},{4,5},{5,4},{6,7},{7,6},{8,9},{9,8},{10,11... | collective-permute-start | bytes 393224 | tf_op jit(solution)/shard_map/ppermute | solution.py:190
  42.9 2.3 %collective-permute-start.13 = (bf16[32,2048]{1,0:T(8,128)(2,1)S(1)}, bf16[32,2048]{1,0:T(8,128)(2,1)S(1)}, u32[]{:S(2)}, u32[]{:S(2)}) collective-permute-start(bf16[32,2048]{1,0:T(8,128)(2,1)S(1)} %shard_map.59.refs_4_.refs_0_), channel_id=1, source_target_pairs={{0,1},{1,0},{2,3},{3,2},{4,5},{5,4},{6,7},{7,6},{8,9},{9,8},{10,11... | collective-permute-start | bytes 393224 | tf_op jit(solution)/shard_map/ppermute | solution.py:190
  47.2 6.9 %collective-permute-start.15 = (bf16[16,2048]{1,0:T(8,128)(2,1)S(1)}, bf16[16,2048]{1,0:T(8,128)(2,1)S(1)}, u32[]{:S(2)}, u32[]{:S(2)}) collective-permute-start(bf16[16,2048]{1,0:T(8,128)(2,1)S(1)} %get-tuple-element.74), channel_id=1, source_target_pairs={{0,6},{2,4},{4,2},{6,0},{1,7},{3,5},{5,3},{7,1},{8,14},{10,12},{12... | collective-permute-start | bytes 196616 | tf_op jit(solution)/shard_map/ppermute | solution.py:190
  50.0 6.4 %collective-permute-start.16 = (bf16[16,2048]{1,0:T(8,128)(2,1)S(1)}, bf16[16,2048]{1,0:T(8,128)(2,1)S(1)}, u32[]{:S(2)}, u32[]{:S(2)}) collective-permute-start(bf16[16,2048]{1,0:T(8,128)(2,1)S(1)} %get-tuple-element.75), channel_id=1, source_target_pairs={{0,4},{2,6},{4,0},{6,2},{1,5},{3,7},{5,1},{7,3},{8,12},{10,14},{12... | collective-permute-start | bytes 196616 | tf_op jit(solution)/shard_map/ppermute | solution.py:190
  50.0 6.4 %collective-permute-start.17 = (bf16[16,2048]{1,0:T(8,128)(2,1)S(1)}, bf16[16,2048]{1,0:T(8,128)(2,1)S(1)}, u32[]{:S(2)}, u32[]{:S(2)}) collective-permute-start(bf16[16,2048]{1,0:T(8,128)(2,1)S(1)} %get-tuple-element.76), channel_id=1, source_target_pairs={{0,2},{2,0},{4,6},{6,4},{1,3},{3,1},{5,7},{7,5},{8,10},{10,8},{12,... | collective-permute-start | bytes 196616 | tf_op jit(solution)/shard_map/ppermute | solution.py:190

commit v12 on v11

--- a/solution.py
+++ b/solution.py
@@ -9,9 +9,9 @@
 
 BF16, F32 = jnp.bfloat16, jnp.float32
 TILE = 512
-GATE = (9, 4)
-DOWN = (5, 4, 4)
-DOWN_LOADS = dict(wait=((0, 1),), gate=((1, 1),), late=((2, 3), (5, 4)), first=((9, 2),), second=((11, 2),))
+GATE = (8, 5)
+DOWN = (4, 4, 5)
+DOWN_LOADS = dict(wait=((0, 1),), rest=((1, 2),), late=((3, 1), (4, 4), (8, 1)), first=((9, 2),), second=((11, 2),))
 PAIR_TYPE = BF16
 COST = 1
 SPLIT = 2
@@ -304,10 +304,10 @@
         (ups,) = pair_sum(ups, whole, whole)
         edge = loads[1][0]
         inner = [chunk for chunk in chunks if chunk[0] < edge]
-        parts, _, (second, *more) = project([x], first, inner, gate_of(1) + down_of("gate"))
-        keep("gate", more)
+        parts, _, (second,) = project([x], first, inner, gate_of(1))
         outer = [(start - edge, width) for start, width in chunks if start >= edge]
-        others, _, _ = project([x], [second], outer, [])
+        others, _, more = project([x], [second], outer, down_of("rest"))
+        keep("rest", more)
         sums = pair_sum(parts, inner, inner) + pair_sum(others, outer, outer)
         _, more = load(x, down_of("late"), 0)
         keep("late", more)

time: 57.3 us -> 56.4 us (0.984)
  starting transfers between devices: 16.7 us -> 16 us
    ppermute x18, starting transfers between devices: 16.7 us -> 16 us  [send(): lax.ppermute(value, axis, [(i, i ^ k if paired else (i + k) % n) for i in...]
  transfers between devices with their start and end apart: 18 -> 18, of which waited for: 6 -> 7; matrix products, arithmetic and copies ran while one was open for 0% -> 0% of each run, Pallas kernels for 32% -> 32%
where the time goes in v12:
time: 56.4 us; the launch traced here: 56.2 us
  Pallas kernels  27.7 us (49%)
  starting transfers between devices  16 us (28%)
  waiting for transfers between devices  11.7 us (21%)
  other arithmetic  0.66 us (1%)
    pallas_call x16, Pallas kernels, call(): pl.pallas_call(kernel, out_shape=tuple(outs) + tuple(fetched), in_specs=[...  27.7 us
    ppermute x18, starting transfers between devices, send(): lax.ppermute(value, axis, [(i, i ^ k if paired else (i + k) % n) for i in...  16 us
    ppermute x18, waiting for transfers between devices, send(): lax.ppermute(value, axis, [(i, i ^ k if paired else (i + k) % n) for i in...  11.7 us
  transfers between devices with their start and end apart: 18, of which 7 were waited for; matrix products, arithmetic and copies ran while one was open for 0% of the time, Pallas kernels for 32%

profile of v12, /device:TPU:0, one launch (start us, length us, event | category | flops | bytes accessed | tf_op | source)
XLA Modules:
  0.0 56.2 jit_solution(13677095665718141014)
XLA Ops:
  0.0 1.0 %shard_map.46 = (bf16[16,2048]{1,0:T(8,128)(2,1)S(1)}, bf16[16,2048]{1,0:T(8,128)(2,1)S(1)}) custom-call(bf16[16,2048]{1,0:T(8,128)(2,1)} %refs_0_.1, bf16[6656,2048]{1,0:T(8,128)(2,1)} %refs_5_.1), custom_call_target="tpu_custom_call" | custom-call | bytes 54525952 | tf_op jit(solution)/shard_map/pallas_call | solution.py:71
  1.0 5.1 %collective-permute-start.2 = (bf16[16,2048]{1,0:T(8,128)(2,1)S(1)}, bf16[16,2048]{1,0:T(8,128)(2,1)S(1)}, u32[]{:S(2)}, u32[]{:S(2)}) collective-permute-start(bf16[16,2048]{1,0:T(8,128)(2,1)S(1)} %get-tuple-element.42.refs_0_.refs_6_), channel_id=1, source_target_pairs={{0,6},{2,4},{4,2},{6,0},{1,7},{3,5},{5,3},{7,1},{8,14},{10,12},{12... | collective-permute-start | bytes 196616 | tf_op jit(solution)/shard_map/ppermute | solution.py:190
  6.2 0.6 %collective-permute-start = (bf16[16,2048]{1,0:T(8,128)(2,1)S(1)}, bf16[16,2048]{1,0:T(8,128)(2,1)S(1)}, u32[]{:S(2)}, u32[]{:S(2)}) collective-permute-start(bf16[16,2048]{1,0:T(8,128)(2,1)S(1)} %get-tuple-element.42.refs_0_.refs_6_), channel_id=1, source_target_pairs={{0,2},{2,0},{4,6},{6,4},{1,3},{3,1},{5,7},{7,5},{8,10},{10,8},{12,... | collective-permute-start | bytes 196616 | tf_op jit(solution)/shard_map/ppermute | solution.py:190
  6.8 1.9 %collective-permute-done.2.refs_3_ = bf16[16,2048]{1,0:T(8,128)(2,1)S(1)} collective-permute-done((bf16[16,2048]{1,0:T(8,128)(2,1)S(1)}, bf16[16,2048]{1,0:T(8,128)(2,1)S(1)}, u32[]{:S(2)}, u32[]{:S(2)}) %collective-permute-start.2) | collective-permute-done | bytes 65568 | tf_op jit(solution)/shard_map/ppermute | solution.py:190
  8.7 3.0 %collective-permute-done.1.refs_2_ = bf16[16,2048]{1,0:T(8,128)(2,1)S(1)} collective-permute-done((bf16[16,2048]{1,0:T(8,128)(2,1)S(1)}, bf16[16,2048]{1,0:T(8,128)(2,1)S(1)}, u32[]{:S(2)}, u32[]{:S(2)}) %collective-permute-start.1) | collective-permute-done | bytes 65568 | tf_op jit(solution)/shard_map/ppermute | solution.py:190
  11.8 6.4 %shard_map.47 = (f32[32,6656]{1,0:T(8,128)S(1)}, bf16[32,6656]{1,0:T(8,128)(2,1)S(1)}, bf16[64,2048]{1,0:T(8,128)(2,1)S(1)}, bf16[2048,4096]{1,0:T(8,128)(2,1)S(1)}) custom-call(bf16[16,2048]{1,0:T(8,128)(2,1)S(1)} %get-tuple-element.42.refs_0_.refs_6_, bf16[16,2048]{1,0:T(8,128)(2,1)S(1)} %collective-permute-done.refs_1_, ...), custom_call_target="tpu_custom_call" | custom-call | flops 1744830464 | bytes 33554432 | tf_op jit(solution)/shard_map/pallas_call | solution.py:71
  18.3 1.6 %shard_map.48 = (bf16[64,2048]{1,0:T(8,128)(2,1)S(1)}, bf16[512,2048]{1,0:T(8,128)(2,1)S(1)}) custom-call(bf16[64,2048]{1,0:T(8,128)(2,1)S(1)} %get-tuple-element.46.refs_0_.refs_1_, bf16[64,2048]{1,0:T(8,128)(2,1)S(1)} %get-tuple-element.46.refs_0_.refs_1_, bf16[6656,2048]{1,0:T(8,128)(2,1)} %refs_5_.1), custom_call_target="tpu_custom_call" | custom-call | bytes 4194304 | tf_op jit(solution)/shard_map/pallas_call | solution.py:71
  20.2 1.6 %collective-permute-start.4 = (bf16[32,6656]{1,0:T(8,128)(2,1)S(1)}, bf16[32,6656]{1,0:T(8,128)(2,1)S(1)}, u32[]{:S(2)}, u32[]{:S(2)}) collective-permute-start(bf16[32,6656]{1,0:T(8,128)(2,1)S(1)} %get-tuple-element.49), channel_id=1, source_target_pairs={{0,8},{8,0},{1,9},{9,1},{2,10},{10,2},{3,11},{11,3},{4,12},{12,4},... | collective-permute-start | bytes 1277960 | tf_op jit(solution)/shard_map/ppermute | solution.py:190
  21.8 4.1 %shard_map.50 = (f32[32,4096]{1,0:T(8,128)S(1)}, bf16[32,2048]{1,0:T(8,128)(2,1)S(1)}, bf16[32,2048]{1,0:T(8,128)(2,1)S(1)}, bf16[2048,2560]{1,0:T(8,128)(2,1)S(1)}) custom-call(bf16[64,2048]{1,0:T(8,128)(2,1)S(1)} %get-tuple-element.47.refs_2_.refs_0_, bf16[2048,4096]{1,0:T(8,128)(2,1)S(1)} %get-tuple-element.50.refs_1_, ...), custom_call_target="tpu_custom_call" | custom-call | flops 1073741824 | bytes 20971520 | tf_op jit(solution)/shard_map/pallas_call | solution.py:71
  26.4 2.5 %shard_map.51 = (f32[32,2560]{1,0:T(8,128)S(1)}, bf16[32,2560]{1,0:T(8,128)(2,1)S(1)}, bf16[1024,2048]{1,0:T(8,128)(2,1)S(1)}) custom-call(bf16[64,2048]{1,0:T(8,128)(2,1)S(1)} %get-tuple-element.47.refs_2_.refs_0_, bf16[2048,2560]{1,0:T(8,128)(2,1)S(1)} %get-tuple-element.51.refs_1_, bf16[32,2048]{1,0:T(8,128)(2,1)S(1)} %get-tuple-element.52.refs_2_, ...), custom_call_target="tpu_custom_call" | custom-call | flops 671088640 | bytes 8388608 | tf_op jit(solution)/shard_map/pallas_call | solution.py:71
  29.1 0.6 %collective-permute-start.9 = (bf16[32,2048]{1,0:T(8,128)(2,1)S(1)}, bf16[32,2048]{1,0:T(8,128)(2,1)S(1)}, u32[]{:S(2)}, u32[]{:S(2)}) collective-permute-start(bf16[32,2048]{1,0:T(8,128)(2,1)S(1)} %get-tuple-element.60), channel_id=1, source_target_pairs={{0,8},{8,0},{1,9},{9,1},{2,10},{10,2},{3,11},{11,3},{4,12},{12,4},... | collective-permute-start | bytes 393224 | tf_op jit(solution)/shard_map/ppermute | solution.py:190
  29.7 1.5 %collective-permute-start.12 = (bf16[32,2048]{1,0:T(8,128)(2,1)S(1)}, bf16[32,2048]{1,0:T(8,128)(2,1)S(1)}, u32[]{:S(2)}, u32[]{:S(2)}) collective-permute-start(bf16[32,2048]{1,0:T(8,128)(2,1)S(1)} %get-tuple-element.68), channel_id=1, source_target_pairs={{0,8},{8,0},{1,9},{9,1},{2,10},{10,2},{3,11},{11,3},{4,12},{12,4},... | collective-permute-start | bytes 393224 | tf_op jit(solution)/shard_map/ppermute | solution.py:190
  31.3 0.6 %collective-permute-start.8 = (bf16[32,2560]{1,0:T(8,128)(2,1)S(1)}, bf16[32,2560]{1,0:T(8,128)(2,1)S(1)}, u32[]{:S(2)}, u32[]{:S(2)}) collective-permute-start(bf16[32,2560]{1,0:T(8,128)(2,1)S(1)} %get-tuple-element.59), channel_id=1, source_target_pairs={{0,8},{8,0},{1,9},{9,1},{2,10},{10,2},{3,11},{11,3},{4,12},{12,4},... | collective-permute-start | bytes 491528 | tf_op jit(solution)/shard_map/ppermute | solution.py:190
  31.9 4.6 %shard_map.54 = (bf16[64,2048]{1,0:T(8,128)(2,1)S(1)}, bf16[512,2048]{1,0:T(8,128)(2,1)S(1)}, bf16[2048,2048]{1,0:T(8,128)(2,1)S(1)}, bf16[512,2048]{1,0:T(8,128)(2,1)S(1)}) custom-call(bf16[64,2048]{1,0:T(8,128)(2,1)S(1)} %get-tuple-element.47.refs_2_.refs_0_, f32[32,2560]{1,0:T(8,128)S(1)} %get-tuple-element.58.refs_1_.refs_2_, ...), custom_call_target="tpu_custom_call" | custom-call | tf_op jit(solution)/shard_map/pallas_call | solution.py:71
  37.3 1.0 %collective-permute-done.12.refs_3_ = bf16[32,2048]{1,0:T(8,128)(2,1)S(1)} collective-permute-done((bf16[32,2048]{1,0:T(8,128)(2,1)S(1)}, bf16[32,2048]{1,0:T(8,128)(2,1)S(1)}, u32[]{:S(2)}, u32[]{:S(2)}) %collective-permute-start.12) | collective-permute-done | bytes 131104 | tf_op jit(solution)/shard_map/ppermute | solution.py:190
  38.5 2.2 %shard_map.58 = (f32[64,2048]{1,0:T(8,128)S(1)}, bf16[1024,2048]{1,0:T(8,128)(2,1)S(1)}) custom-call(bf16[16,2048]{1,0:T(8,128)(2,1)S(1)} %get-tuple-element.62.refs_4_.refs_0_, bf16[16,2048]{1,0:T(8,128)(2,1)S(1)} %get-tuple-element.63.refs_1_, bf16[16,2048]{1,0:T(8,128)(2,1)S(1)} %collective-permute-done.10.refs_2_, ...), custom_call_target="tpu_custom_call" | custom-call | flops 536870912 | bytes 8388608 | tf_op jit(solution)/shard_map/pallas_call | solution.py:71
  40.7 0.7 %collective-permute-done.8.refs_3_ = bf16[32,2560]{1,0:T(8,128)(2,1)S(1)} collective-permute-done((bf16[32,2560]{1,0:T(8,128)(2,1)S(1)}, bf16[32,2560]{1,0:T(8,128)(2,1)S(1)}, u32[]{:S(2)}, u32[]{:S(2)}) %collective-permute-start.8) | collective-permute-done | bytes 163872 | tf_op jit(solution)/shard_map/ppermute | solution.py:190
  41.7 2.2 %shard_map.60 = (f32[64,2048]{1,0:T(8,128)S(1)}, bf16[1024,2048]{1,0:T(8,128)(2,1)S(1)}) custom-call(bf16[32,2048]{1,0:T(8,128)(2,1)S(1)} %shard_map.57.refs_7_.refs_0_, bf16[32,2048]{1,0:T(8,128)(2,1)S(1)} %collective-permute-done.14.refs_1_, bf16[2048,2048]{1,0:T(8,128)(2,1)S(1)} %get-tuple-element.72.refs_2_, ...), custom_call_target="tpu_custom_call" | custom-call | flops 536870912 | bytes 8388608 | tf_op jit(solution)/shard_map/pallas_call | solution.py:71
  43.9 2.3 %shard_map.61 = (f32[16,2048]{1,0:T(8,128)S(1)}, bf16[16,2048]{1,0:T(8,128)(2,1)S(1)}, bf16[16,2048]{1,0:T(8,128)(2,1)S(1)}, bf16[16,2048]{1,0:T(8,128)(2,1)S(1)}) custom-call(bf16[32,2560]{1,0:T(8,128)(2,1)S(1)} %shard_map.59.refs_4_.refs_0_, bf16[32,2560]{1,0:T(8,128)(2,1)S(1)} %collective-permute-done.13.refs_1_, ...), custom_call_target="tpu_custom_call" | custom-call | flops 671088640 | tf_op jit(solution)/shard_map/pallas_call | solution.py:71
  46.3 2.8 %collective-permute-start.15 = (bf16[16,2048]{1,0:T(8,128)(2,1)S(1)}, bf16[16,2048]{1,0:T(8,128)(2,1)S(1)}, u32[]{:S(2)}, u32[]{:S(2)}) collective-permute-start(bf16[16,2048]{1,0:T(8,128)(2,1)S(1)} %get-tuple-element.76), channel_id=1, source_target_pairs={{0,6},{2,4},{4,2},{6,0},{1,7},{3,5},{5,3},{7,1},{8,14},{10,12},{12... | collective-permute-start | bytes 196616 | tf_op jit(solution)/shard_map/ppermute | solution.py:190
  49.0 1.7 %collective-permute-start.17 = (bf16[16,2048]{1,0:T(8,128)(2,1)S(1)}, bf16[16,2048]{1,0:T(8,128)(2,1)S(1)}, u32[]{:S(2)}, u32[]{:S(2)}) collective-permute-start(bf16[16,2048]{1,0:T(8,128)(2,1)S(1)} %get-tuple-element.78), channel_id=1, source_target_pairs={{0,2},{2,0},{4,6},{6,4},{1,3},{3,1},{5,7},{7,5},{8,10},{10,8},{12,... | collective-permute-start | bytes 196616 | tf_op jit(solution)/shard_map/ppermute | solution.py:190
  50.7 2.4 %collective-permute-done.15 = bf16[16,2048]{1,0:T(8,128)(2,1)S(1)} collective-permute-done((bf16[16,2048]{1,0:T(8,128)(2,1)S(1)}, bf16[16,2048]{1,0:T(8,128)(2,1)S(1)}, u32[]{:S(2)}, u32[]{:S(2)}) %collective-permute-start.15) | collective-permute-done | bytes 65568 | tf_op jit(solution)/shard_map/ppermute | solution.py:190
  53.1 2.4 %collective-permute-done.16 = bf16[16,2048]{1,0:T(8,128)(2,1)S(1)} collective-permute-done((bf16[16,2048]{1,0:T(8,128)(2,1)S(1)}, bf16[16,2048]{1,0:T(8,128)(2,1)S(1)}, u32[]{:S(2)}, u32[]{:S(2)}) %collective-permute-start.16) | collective-permute-done | bytes 65568 | tf_op jit(solution)/shard_map/ppermute | solution.py:190
  55.5 0.7 %add_convert_fusion = bf16[16,2048]{1,0:T(8,128)(2,1)} fusion(bf16[16,2048]{1,0:T(8,128)(2,1)S(1)} %collective-permute-done.17, bf16[16,2048]{1,0:T(8,128)(2,1)S(1)} %collective-permute-done.16, f32[16,2048]{1,0:T(8,128)S(1)} %get-tuple-element.75, bf16[16,2048]{1,0:T(8,128)(2,1)S(1)} %collective-permute-done.15), kind=kLoop, calls=%fused_computation | loop fusion | flops 229376 | bytes 393216 | tf_op jit(solution)/shard_map/convert_element_type | solution.py:325
  (31 shorter events, 2.4 us)
Async XLA Ops:
  0.0 11.8 %copy-start = (bf16[2048,6656]{1,0:T(8,128)(2,1)S(1)}, bf16[2048,6656]{1,0:T(8,128)(2,1)}, u32[]{:S(2)}) copy-start(bf16[2048,6656]{1,0:T(8,128)(2,1)} %refs_4_.2) | copy-start | bytes 81788928
  1.0 7.7 %collective-permute-start.2 = (bf16[16,2048]{1,0:T(8,128)(2,1)S(1)}, bf16[16,2048]{1,0:T(8,128)(2,1)S(1)}, u32[]{:S(2)}, u32[]{:S(2)}) collective-permute-start(bf16[16,2048]{1,0:T(8,128)(2,1)S(1)} %get-tuple-element.42.refs_0_.refs_6_), channel_id=1, source_target_pairs={{0,6},{2,4},{4,2},{6,0},{1,7},{3,5},{5,3},{7,1},{8,14},{10,12},{12... | collective-permute-start | bytes 196616 | tf_op jit(solution)/shard_map/ppermute | solution.py:190
  6.2 5.6 %collective-permute-start.1 = (bf16[16,2048]{1,0:T(8,128)(2,1)S(1)}, bf16[16,2048]{1,0:T(8,128)(2,1)S(1)}, u32[]{:S(2)}, u32[]{:S(2)}) collective-permute-start(bf16[16,2048]{1,0:T(8,128)(2,1)S(1)} %get-tuple-element.42.refs_0_.refs_6_), channel_id=1, source_target_pairs={{0,4},{2,6},{4,0},{6,2},{1,5},{3,7},{5,1},{7,3},{8,12},{10,14},{12... | collective-permute-start | bytes 196616 | tf_op jit(solution)/shard_map/ppermute | solution.py:190
  6.2 5.6 %collective-permute-start = (bf16[16,2048]{1,0:T(8,128)(2,1)S(1)}, bf16[16,2048]{1,0:T(8,128)(2,1)S(1)}, u32[]{:S(2)}, u32[]{:S(2)}) collective-permute-start(bf16[16,2048]{1,0:T(8,128)(2,1)S(1)} %get-tuple-element.42.refs_0_.refs_6_), channel_id=1, source_target_pairs={{0,2},{2,0},{4,6},{6,4},{1,3},{3,1},{5,7},{7,5},{8,10},{10,8},{12,... | collective-permute-start | bytes 196616 | tf_op jit(solution)/shard_map/ppermute | solution.py:190
  18.2 1.8 %collective-permute-start.3 = (bf16[32,6656]{1,0:T(8,128)(2,1)S(1)}, bf16[32,6656]{1,0:T(8,128)(2,1)S(1)}, u32[]{:S(2)}, u32[]{:S(2)}) collective-permute-start(bf16[32,6656]{1,0:T(8,128)(2,1)S(1)} %get-tuple-element.45), channel_id=1, source_target_pairs={{0,1},{1,0},{2,3},{3,2},{4,5},{5,4},{6,7},{7,6},{8,9},{9,8},{10,11... | collective-permute-start | bytes 1277960 | tf_op jit(solution)/shard_map/ppermute | solution.py:190
  20.2 16.3 %collective-permute-start.4 = (bf16[32,6656]{1,0:T(8,128)(2,1)S(1)}, bf16[32,6656]{1,0:T(8,128)(2,1)S(1)}, u32[]{:S(2)}, u32[]{:S(2)}) collective-permute-start(bf16[32,6656]{1,0:T(8,128)(2,1)S(1)} %get-tuple-element.49), channel_id=1, source_target_pairs={{0,8},{8,0},{1,9},{9,1},{2,10},{10,2},{3,11},{11,3},{4,12},{12,4},... | collective-permute-start | bytes 1277960 | tf_op jit(solution)/shard_map/ppermute | solution.py:190
  25.8 3.2 %collective-permute-start.7 = (bf16[32,2048]{1,0:T(8,128)(2,1)S(1)}, bf16[32,2048]{1,0:T(8,128)(2,1)S(1)}, u32[]{:S(2)}, u32[]{:S(2)}) collective-permute-start(bf16[32,2048]{1,0:T(8,128)(2,1)S(1)} %get-tuple-element.56), channel_id=1, source_target_pairs={{0,1},{1,0},{2,3},{3,2},{4,5},{5,4},{6,7},{7,6},{8,9},{9,8},{10,11... | collective-permute-start | bytes 393224 | tf_op jit(solution)/shard_map/ppermute | solution.py:190
  25.9 3.1 %collective-permute-start.6 = (bf16[32,2048]{1,0:T(8,128)(2,1)S(1)}, bf16[32,2048]{1,0:T(8,128)(2,1)S(1)}, u32[]{:S(2)}, u32[]{:S(2)}) collective-permute-start(bf16[32,2048]{1,0:T(8,128)(2,1)S(1)} %get-tuple-element.52.refs_2_), channel_id=1, source_target_pairs={{0,1},{1,0},{2,3},{3,2},{4,5},{5,4},{6,7},{7,6},{8,9},{9,8},{10,11... | collective-permute-start | bytes 393224 | tf_op jit(solution)/shard_map/ppermute | solution.py:190
  28.9 2.3 %collective-permute-start.5 = (bf16[32,2560]{1,0:T(8,128)(2,1)S(1)}, bf16[32,2560]{1,0:T(8,128)(2,1)S(1)}, u32[]{:S(2)}, u32[]{:S(2)}) collective-permute-start(bf16[32,2560]{1,0:T(8,128)(2,1)S(1)} %get-tuple-element.54), channel_id=1, source_target_pairs={{0,1},{1,0},{2,3},{3,2},{4,5},{5,4},{6,7},{7,6},{8,9},{9,8},{10,11... | collective-permute-start | bytes 491528 | tf_op jit(solution)/shard_map/ppermute | solution.py:190
  29.1 7.5 %collective-permute-start.9 = (bf16[32,2048]{1,0:T(8,128)(2,1)S(1)}, bf16[32,2048]{1,0:T(8,128)(2,1)S(1)}, u32[]{:S(2)}, u32[]{:S(2)}) collective-permute-start(bf16[32,2048]{1,0:T(8,128)(2,1)S(1)} %get-tuple-element.60), channel_id=1, source_target_pairs={{0,8},{8,0},{1,9},{9,1},{2,10},{10,2},{3,11},{11,3},{4,12},{12,4},... | collective-permute-start | bytes 393224 | tf_op jit(solution)/shard_map/ppermute | solution.py:190
  29.7 8.6 %collective-permute-start.12 = (bf16[32,2048]{1,0:T(8,128)(2,1)S(1)}, bf16[32,2048]{1,0:T(8,128)(2,1)S(1)}, u32[]{:S(2)}, u32[]{:S(2)}) collective-permute-start(bf16[32,2048]{1,0:T(8,128)(2,1)S(1)} %get-tuple-element.68), channel_id=1, source_target_pairs={{0,8},{8,0},{1,9},{9,1},{2,10},{10,2},{3,11},{11,3},{4,12},{12,4},... | collective-permute-start | bytes 393224 | tf_op jit(solution)/shard_map/ppermute | solution.py:190
  31.3 10.2 %collective-permute-start.8 = (bf16[32,2560]{1,0:T(8,128)(2,1)S(1)}, bf16[32,2560]{1,0:T(8,128)(2,1)S(1)}, u32[]{:S(2)}, u32[]{:S(2)}) collective-permute-start(bf16[32,2560]{1,0:T(8,128)(2,1)S(1)} %get-tuple-element.59), channel_id=1, source_target_pairs={{0,8},{8,0},{1,9},{9,1},{2,10},{10,2},{3,11},{11,3},{4,12},{12,4},... | collective-permute-start | bytes 491528 | tf_op jit(solution)/shard_map/ppermute | solution.py:190
  36.7 1.8 %collective-permute-start.11 = (bf16[16,2048]{1,0:T(8,128)(2,1)S(1)}, bf16[16,2048]{1,0:T(8,128)(2,1)S(1)}, u32[]{:S(2)}, u32[]{:S(2)}) collective-permute-start(bf16[16,2048]{1,0:T(8,128)(2,1)S(1)} %get-tuple-element.63.refs_1_), channel_id=1, source_target_pairs={{0,1},{1,0},{2,3},{3,2},{4,5},{5,4},{6,7},{7,6},{8,9},{9,8},{10,11... | collective-permute-start | bytes 196616 | tf_op jit(solution)/shard_map/ppermute | solution.py:190
  36.8 1.7 %collective-permute-start.10 = (bf16[16,2048]{1,0:T(8,128)(2,1)S(1)}, bf16[16,2048]{1,0:T(8,128)(2,1)S(1)}, u32[]{:S(2)}, u32[]{:S(2)}) collective-permute-start(bf16[16,2048]{1,0:T(8,128)(2,1)S(1)} %get-tuple-element.62.refs_4_.refs_0_), channel_id=1, source_target_pairs={{0,1},{1,0},{2,3},{3,2},{4,5},{5,4},{6,7},{7,6},{8,9},{9,8},{10,11... | collective-permute-start | bytes 196616 | tf_op jit(solution)/shard_map/ppermute | solution.py:190
  38.4 3.3 %collective-permute-start.14 = (bf16[32,2048]{1,0:T(8,128)(2,1)S(1)}, bf16[32,2048]{1,0:T(8,128)(2,1)S(1)}, u32[]{:S(2)}, u32[]{:S(2)}) collective-permute-start(bf16[32,2048]{1,0:T(8,128)(2,1)S(1)} %shard_map.57.refs_7_.refs_0_), channel_id=1, source_target_pairs={{0,1},{1,0},{2,3},{3,2},{4,5},{5,4},{6,7},{7,6},{8,9},{9,8},{10,11... | collective-permute-start | bytes 393224 | tf_op jit(solution)/shard_map/ppermute | solution.py:190
  41.6 2.3 %collective-permute-start.13 = (bf16[32,2560]{1,0:T(8,128)(2,1)S(1)}, bf16[32,2560]{1,0:T(8,128)(2,1)S(1)}, u32[]{:S(2)}, u32[]{:S(2)}) collective-permute-start(bf16[32,2560]{1,0:T(8,128)(2,1)S(1)} %shard_map.59.refs_4_.refs_0_), channel_id=1, source_target_pairs={{0,1},{1,0},{2,3},{3,2},{4,5},{5,4},{6,7},{7,6},{8,9},{9,8},{10,11... | collective-permute-start | bytes 491528 | tf_op jit(solution)/shard_map/ppermute | solution.py:190
  46.3 6.9 %collective-permute-start.15 = (bf16[16,2048]{1,0:T(8,128)(2,1)S(1)}, bf16[16,2048]{1,0:T(8,128)(2,1)S(1)}, u32[]{:S(2)}, u32[]{:S(2)}) collective-permute-start(bf16[16,2048]{1,0:T(8,128)(2,1)S(1)} %get-tuple-element.76), channel_id=1, source_target_pairs={{0,6},{2,4},{4,2},{6,0},{1,7},{3,5},{5,3},{7,1},{8,14},{10,12},{12... | collective-permute-start | bytes 196616 | tf_op jit(solution)/shard_map/ppermute | solution.py:190
  49.0 6.5 %collective-permute-start.16 = (bf16[16,2048]{1,0:T(8,128)(2,1)S(1)}, bf16[16,2048]{1,0:T(8,128)(2,1)S(1)}, u32[]{:S(2)}, u32[]{:S(2)}) collective-permute-start(bf16[16,2048]{1,0:T(8,128)(2,1)S(1)} %get-tuple-element.77), channel_id=1, source_target_pairs={{0,4},{2,6},{4,0},{6,2},{1,5},{3,7},{5,1},{7,3},{8,12},{10,14},{12... | collective-permute-start | bytes 196616 | tf_op jit(solution)/shard_map/ppermute | solution.py:190
  49.0 6.5 %collective-permute-start.17 = (bf16[16,2048]{1,0:T(8,128)(2,1)S(1)}, bf16[16,2048]{1,0:T(8,128)(2,1)S(1)}, u32[]{:S(2)}, u32[]{:S(2)}) collective-permute-start(bf16[16,2048]{1,0:T(8,128)(2,1)S(1)} %get-tuple-element.78), channel_id=1, source_target_pairs={{0,2},{2,0},{4,6},{6,4},{1,3},{3,1},{5,7},{7,5},{8,10},{10,8},{12,... | collective-permute-start | bytes 196616 | tf_op jit(solution)/shard_map/ppermute | solution.py:190

commit v13 on v12

--- a/solution.py
+++ b/solution.py
@@ -284,11 +284,11 @@
             keep(name, more)
         return total
 
-    _, (tokens, *early) = call(
+    _, (staged, *early) = call(
         order, load_kernel, [], [], [(tokens, 0, 0, share), (down_weight, 0, 0, share)], [],
         0, 2 * up_weight.size * size,
     )
-    blocks = [tokens] + [send(tokens, "wide", k) for k in range(1, n_wide)]
+    blocks = [staged] + [send(tokens if k > 1 else staged, "wide", k) for k in range(1, n_wide)]
     up = pltpu.with_memory_space_constraint(up_weight, pltpu.VMEM)
     columns = gate_weight.shape[1]
     down, whole = {}, [(0, columns)]

time: 56.4 us -> 56.4 us (level)
  waiting for transfers between devices: 11.7 us -> 11 us
  Pallas kernels: 27.7 us -> 28.3 us
    ppermute x18, waiting for transfers between devices: 11.7 us -> 11 us  [send(): lax.ppermute(value, axis, [(i, i ^ k if paired else (i + k) % n) for i in...]
    pallas_call x16, Pallas kernels: 27.7 us -> 28.3 us  [call(): pl.pallas_call(kernel, out_shape=tuple(outs) + tuple(fetched), in_specs=[...]
  transfers between devices with their start and end apart: 18 -> 18, of which waited for: 7 -> 8; matrix products, arithmetic and copies ran while one was open for 0% -> 0% of each run, Pallas kernels for 32% -> 35%
where the time goes in v13:
time: 56.4 us; the launch traced here: 56.1 us
  Pallas kernels  28.3 us (50%)
  starting transfers between devices  16 us (28%)
  waiting for transfers between devices  11 us (20%)
  other arithmetic  0.66 us (1%)
    pallas_call x16, Pallas kernels, call(): pl.pallas_call(kernel, out_shape=tuple(outs) + tuple(fetched), in_specs=[...  28.3 us
    ppermute x18, starting transfers between devices, send(): lax.ppermute(value, axis, [(i, i ^ k if paired else (i + k) % n) for i in...  16 us
    ppermute x18, waiting for transfers between devices, send(): lax.ppermute(value, axis, [(i, i ^ k if paired else (i + k) % n) for i in...  11 us
  transfers between devices with their start and end apart: 18, of which 8 were waited for; matrix products, arithmetic and copies ran while one was open for 0% of the time, Pallas kernels for 35%

profile of v13, /device:TPU:0, one launch (start us, length us, event | category | flops | bytes accessed | tf_op | source)
XLA Modules:
  0.0 56.1 jit_solution(13669810190074773174)
XLA Ops:
  0.0 5.0 %collective-permute-start.2 = (bf16[16,2048]{1,0:T(8,128)(2,1)}, bf16[16,2048]{1,0:T(8,128)(2,1)S(1)}, u32[]{:S(2)}, u32[]{:S(2)}) collective-permute-start(bf16[16,2048]{1,0:T(8,128)(2,1)} %refs_0_.1), channel_id=1, source_target_pairs={{0,6},{2,4},{4,2},{6,0},{1,7},{3,5},{5,3},{7,1},{8,14},{10,12},{12... | collective-permute-start | bytes 196616 | tf_op jit(solution)/shard_map/ppermute | solution.py:190
  5.1 1.6 %shard_map.46 = (bf16[16,2048]{1,0:T(8,128)(2,1)S(1)}, bf16[16,2048]{1,0:T(8,128)(2,1)S(1)}) custom-call(bf16[16,2048]{1,0:T(8,128)(2,1)} %refs_0_.1, bf16[6656,2048]{1,0:T(8,128)(2,1)} %refs_5_.1), custom_call_target="tpu_custom_call" | custom-call | bytes 54525952 | tf_op jit(solution)/shard_map/pallas_call | solution.py:71
  6.7 0.7 %collective-permute-start = (bf16[16,2048]{1,0:T(8,128)(2,1)S(1)}, bf16[16,2048]{1,0:T(8,128)(2,1)S(1)}, u32[]{:S(2)}, u32[]{:S(2)}) collective-permute-start(bf16[16,2048]{1,0:T(8,128)(2,1)S(1)} %get-tuple-element.42.refs_0_.refs_6_), channel_id=1, source_target_pairs={{0,2},{2,0},{4,6},{6,4},{1,3},{3,1},{5,7},{7,5},{8,10},{10,8},{12,... | collective-permute-start | bytes 196616 | tf_op jit(solution)/shard_map/ppermute | solution.py:190
  7.8 3.1 %collective-permute-done.1.refs_2_ = bf16[16,2048]{1,0:T(8,128)(2,1)S(1)} collective-permute-done((bf16[16,2048]{1,0:T(8,128)(2,1)}, bf16[16,2048]{1,0:T(8,128)(2,1)S(1)}, u32[]{:S(2)}, u32[]{:S(2)}) %collective-permute-start.1) | collective-permute-done | bytes 65568 | tf_op jit(solution)/shard_map/ppermute | solution.py:190
  10.9 0.6 %collective-permute-done.refs_1_ = bf16[16,2048]{1,0:T(8,128)(2,1)S(1)} collective-permute-done((bf16[16,2048]{1,0:T(8,128)(2,1)S(1)}, bf16[16,2048]{1,0:T(8,128)(2,1)S(1)}, u32[]{:S(2)}, u32[]{:S(2)}) %collective-permute-start) | collective-permute-done | bytes 65568 | tf_op jit(solution)/shard_map/ppermute | solution.py:190
  11.6 6.4 %shard_map.47 = (f32[32,6656]{1,0:T(8,128)S(1)}, bf16[32,6656]{1,0:T(8,128)(2,1)S(1)}, bf16[64,2048]{1,0:T(8,128)(2,1)S(1)}, bf16[2048,4096]{1,0:T(8,128)(2,1)S(1)}) custom-call(bf16[16,2048]{1,0:T(8,128)(2,1)S(1)} %get-tuple-element.42.refs_0_.refs_6_, bf16[16,2048]{1,0:T(8,128)(2,1)S(1)} %collective-permute-done.refs_1_, ...), custom_call_target="tpu_custom_call" | custom-call | flops 1744830464 | bytes 33554432 | tf_op jit(solution)/shard_map/pallas_call | solution.py:71
  18.1 1.6 %shard_map.48 = (bf16[64,2048]{1,0:T(8,128)(2,1)S(1)}, bf16[512,2048]{1,0:T(8,128)(2,1)S(1)}) custom-call(bf16[64,2048]{1,0:T(8,128)(2,1)S(1)} %get-tuple-element.46.refs_0_.refs_1_, bf16[64,2048]{1,0:T(8,128)(2,1)S(1)} %get-tuple-element.46.refs_0_.refs_1_, bf16[6656,2048]{1,0:T(8,128)(2,1)} %refs_5_.1), custom_call_target="tpu_custom_call" | custom-call | bytes 4194304 | tf_op jit(solution)/shard_map/pallas_call | solution.py:71
  20.0 1.6 %collective-permute-start.4 = (bf16[32,6656]{1,0:T(8,128)(2,1)S(1)}, bf16[32,6656]{1,0:T(8,128)(2,1)S(1)}, u32[]{:S(2)}, u32[]{:S(2)}) collective-permute-start(bf16[32,6656]{1,0:T(8,128)(2,1)S(1)} %get-tuple-element.49), channel_id=1, source_target_pairs={{0,8},{8,0},{1,9},{9,1},{2,10},{10,2},{3,11},{11,3},{4,12},{12,4},... | collective-permute-start | bytes 1277960 | tf_op jit(solution)/shard_map/ppermute | solution.py:190
  21.6 4.1 %shard_map.50 = (f32[32,4096]{1,0:T(8,128)S(1)}, bf16[32,2048]{1,0:T(8,128)(2,1)S(1)}, bf16[32,2048]{1,0:T(8,128)(2,1)S(1)}, bf16[2048,2560]{1,0:T(8,128)(2,1)S(1)}) custom-call(bf16[64,2048]{1,0:T(8,128)(2,1)S(1)} %get-tuple-element.47.refs_2_.refs_0_, bf16[2048,4096]{1,0:T(8,128)(2,1)S(1)} %get-tuple-element.50.refs_1_, ...), custom_call_target="tpu_custom_call" | custom-call | flops 1073741824 | bytes 20971520 | tf_op jit(solution)/shard_map/pallas_call | solution.py:71
  26.2 2.5 %shard_map.51 = (f32[32,2560]{1,0:T(8,128)S(1)}, bf16[32,2560]{1,0:T(8,128)(2,1)S(1)}, bf16[1024,2048]{1,0:T(8,128)(2,1)S(1)}) custom-call(bf16[64,2048]{1,0:T(8,128)(2,1)S(1)} %get-tuple-element.47.refs_2_.refs_0_, bf16[2048,2560]{1,0:T(8,128)(2,1)S(1)} %get-tuple-element.51.refs_1_, bf16[32,2048]{1,0:T(8,128)(2,1)S(1)} %get-tuple-element.52.refs_2_, ...), custom_call_target="tpu_custom_call" | custom-call | flops 671088640 | bytes 8388608 | tf_op jit(solution)/shard_map/pallas_call | solution.py:71
  29.0 0.5 collective-permute-start.9
  29.5 1.6 %collective-permute-start.12 = (bf16[32,2048]{1,0:T(8,128)(2,1)S(1)}, bf16[32,2048]{1,0:T(8,128)(2,1)S(1)}, u32[]{:S(2)}, u32[]{:S(2)}) collective-permute-start(bf16[32,2048]{1,0:T(8,128)(2,1)S(1)} %get-tuple-element.68), channel_id=1, source_target_pairs={{0,8},{8,0},{1,9},{9,1},{2,10},{10,2},{3,11},{11,3},{4,12},{12,4},... | collective-permute-start | bytes 393224 | tf_op jit(solution)/shard_map/ppermute | solution.py:190
  31.1 0.5 collective-permute-start.8
  31.7 4.6 %shard_map.54 = (bf16[64,2048]{1,0:T(8,128)(2,1)S(1)}, bf16[512,2048]{1,0:T(8,128)(2,1)S(1)}, bf16[2048,2048]{1,0:T(8,128)(2,1)S(1)}, bf16[512,2048]{1,0:T(8,128)(2,1)S(1)}) custom-call(bf16[64,2048]{1,0:T(8,128)(2,1)S(1)} %get-tuple-element.47.refs_2_.refs_0_, f32[32,2560]{1,0:T(8,128)S(1)} %get-tuple-element.58.refs_1_.refs_2_, ...), custom_call_target="tpu_custom_call" | custom-call | tf_op jit(solution)/shard_map/pallas_call | solution.py:71
  37.1 1.1 %collective-permute-done.12.refs_3_ = bf16[32,2048]{1,0:T(8,128)(2,1)S(1)} collective-permute-done((bf16[32,2048]{1,0:T(8,128)(2,1)S(1)}, bf16[32,2048]{1,0:T(8,128)(2,1)S(1)}, u32[]{:S(2)}, u32[]{:S(2)}) %collective-permute-start.12) | collective-permute-done | bytes 131104 | tf_op jit(solution)/shard_map/ppermute | solution.py:190
  38.4 2.2 %shard_map.58 = (f32[64,2048]{1,0:T(8,128)S(1)}, bf16[1024,2048]{1,0:T(8,128)(2,1)S(1)}) custom-call(bf16[16,2048]{1,0:T(8,128)(2,1)S(1)} %get-tuple-element.62.refs_4_.refs_0_, bf16[16,2048]{1,0:T(8,128)(2,1)S(1)} %get-tuple-element.63.refs_1_, bf16[16,2048]{1,0:T(8,128)(2,1)S(1)} %collective-permute-done.10.refs_2_, ...), custom_call_target="tpu_custom_call" | custom-call | flops 536870912 | bytes 8388608 | tf_op jit(solution)/shard_map/pallas_call | solution.py:71
  40.6 0.7 %collective-permute-done.8.refs_3_ = bf16[32,2560]{1,0:T(8,128)(2,1)S(1)} collective-permute-done((bf16[32,2560]{1,0:T(8,128)(2,1)S(1)}, bf16[32,2560]{1,0:T(8,128)(2,1)S(1)}, u32[]{:S(2)}, u32[]{:S(2)}) %collective-permute-start.8) | collective-permute-done | bytes 163872 | tf_op jit(solution)/shard_map/ppermute | solution.py:190
  41.5 2.2 %shard_map.60 = (f32[64,2048]{1,0:T(8,128)S(1)}, bf16[1024,2048]{1,0:T(8,128)(2,1)S(1)}) custom-call(bf16[32,2048]{1,0:T(8,128)(2,1)S(1)} %shard_map.57.refs_7_.refs_0_, bf16[32,2048]{1,0:T(8,128)(2,1)S(1)} %collective-permute-done.14.refs_1_, bf16[2048,2048]{1,0:T(8,128)(2,1)S(1)} %get-tuple-element.72.refs_2_, ...), custom_call_target="tpu_custom_call" | custom-call | flops 536870912 | bytes 8388608 | tf_op jit(solution)/shard_map/pallas_call | solution.py:71
  43.7 2.3 %shard_map.61 = (f32[16,2048]{1,0:T(8,128)S(1)}, bf16[16,2048]{1,0:T(8,128)(2,1)S(1)}, bf16[16,2048]{1,0:T(8,128)(2,1)S(1)}, bf16[16,2048]{1,0:T(8,128)(2,1)S(1)}) custom-call(bf16[32,2560]{1,0:T(8,128)(2,1)S(1)} %shard_map.59.refs_4_.refs_0_, bf16[32,2560]{1,0:T(8,128)(2,1)S(1)} %collective-permute-done.13.refs_1_, ...), custom_call_target="tpu_custom_call" | custom-call | flops 671088640 | tf_op jit(solution)/shard_map/pallas_call | solution.py:71
  46.1 2.5 %collective-permute-start.15 = (bf16[16,2048]{1,0:T(8,128)(2,1)S(1)}, bf16[16,2048]{1,0:T(8,128)(2,1)S(1)}, u32[]{:S(2)}, u32[]{:S(2)}) collective-permute-start(bf16[16,2048]{1,0:T(8,128)(2,1)S(1)} %get-tuple-element.76), channel_id=1, source_target_pairs={{0,6},{2,4},{4,2},{6,0},{1,7},{3,5},{5,3},{7,1},{8,14},{10,12},{12... | collective-permute-start | bytes 196616 | tf_op jit(solution)/shard_map/ppermute | solution.py:190
  48.6 1.9 %collective-permute-start.17 = (bf16[16,2048]{1,0:T(8,128)(2,1)S(1)}, bf16[16,2048]{1,0:T(8,128)(2,1)S(1)}, u32[]{:S(2)}, u32[]{:S(2)}) collective-permute-start(bf16[16,2048]{1,0:T(8,128)(2,1)S(1)} %get-tuple-element.78), channel_id=1, source_target_pairs={{0,2},{2,0},{4,6},{6,4},{1,3},{3,1},{5,7},{7,5},{8,10},{10,8},{12,... | collective-permute-start | bytes 196616 | tf_op jit(solution)/shard_map/ppermute | solution.py:190
  50.5 2.3 %collective-permute-done.15 = bf16[16,2048]{1,0:T(8,128)(2,1)S(1)} collective-permute-done((bf16[16,2048]{1,0:T(8,128)(2,1)S(1)}, bf16[16,2048]{1,0:T(8,128)(2,1)S(1)}, u32[]{:S(2)}, u32[]{:S(2)}) %collective-permute-start.15) | collective-permute-done | bytes 65568 | tf_op jit(solution)/shard_map/ppermute | solution.py:190
  52.8 2.7 %collective-permute-done.16 = bf16[16,2048]{1,0:T(8,128)(2,1)S(1)} collective-permute-done((bf16[16,2048]{1,0:T(8,128)(2,1)S(1)}, bf16[16,2048]{1,0:T(8,128)(2,1)S(1)}, u32[]{:S(2)}, u32[]{:S(2)}) %collective-permute-start.16) | collective-permute-done | bytes 65568 | tf_op jit(solution)/shard_map/ppermute | solution.py:190
  55.5 0.7 %add_convert_fusion = bf16[16,2048]{1,0:T(8,128)(2,1)} fusion(bf16[16,2048]{1,0:T(8,128)(2,1)S(1)} %collective-permute-done.17, bf16[16,2048]{1,0:T(8,128)(2,1)S(1)} %collective-permute-done.16, f32[16,2048]{1,0:T(8,128)S(1)} %get-tuple-element.75, bf16[16,2048]{1,0:T(8,128)(2,1)S(1)} %collective-permute-done.15), kind=kLoop, calls=%fused_computation | loop fusion | flops 229376 | bytes 393216 | tf_op jit(solution)/shard_map/convert_element_type | solution.py:325
  (31 shorter events, 2.8 us)
Async XLA Ops:
  0.0 11.6 %copy-start = (bf16[2048,6656]{1,0:T(8,128)(2,1)S(1)}, bf16[2048,6656]{1,0:T(8,128)(2,1)}, u32[]{:S(2)}) copy-start(bf16[2048,6656]{1,0:T(8,128)(2,1)} %refs_4_.2) | copy-start | bytes 81788928
  0.0 7.8 %collective-permute-start.2 = (bf16[16,2048]{1,0:T(8,128)(2,1)}, bf16[16,2048]{1,0:T(8,128)(2,1)S(1)}, u32[]{:S(2)}, u32[]{:S(2)}) collective-permute-start(bf16[16,2048]{1,0:T(8,128)(2,1)} %refs_0_.1), channel_id=1, source_target_pairs={{0,6},{2,4},{4,2},{6,0},{1,7},{3,5},{5,3},{7,1},{8,14},{10,12},{12... | collective-permute-start | bytes 196616 | tf_op jit(solution)/shard_map/ppermute | solution.py:190
  5.1 5.9 %collective-permute-start.1 = (bf16[16,2048]{1,0:T(8,128)(2,1)}, bf16[16,2048]{1,0:T(8,128)(2,1)S(1)}, u32[]{:S(2)}, u32[]{:S(2)}) collective-permute-start(bf16[16,2048]{1,0:T(8,128)(2,1)} %refs_0_.1), channel_id=1, source_target_pairs={{0,4},{2,6},{4,0},{6,2},{1,5},{3,7},{5,1},{7,3},{8,12},{10,14},{12... | collective-permute-start | bytes 196616 | tf_op jit(solution)/shard_map/ppermute | solution.py:190
  6.7 4.9 %collective-permute-start = (bf16[16,2048]{1,0:T(8,128)(2,1)S(1)}, bf16[16,2048]{1,0:T(8,128)(2,1)S(1)}, u32[]{:S(2)}, u32[]{:S(2)}) collective-permute-start(bf16[16,2048]{1,0:T(8,128)(2,1)S(1)} %get-tuple-element.42.refs_0_.refs_6_), channel_id=1, source_target_pairs={{0,2},{2,0},{4,6},{6,4},{1,3},{3,1},{5,7},{7,5},{8,10},{10,8},{12,... | collective-permute-start | bytes 196616 | tf_op jit(solution)/shard_map/ppermute | solution.py:190
  18.0 1.8 %collective-permute-start.3 = (bf16[32,6656]{1,0:T(8,128)(2,1)S(1)}, bf16[32,6656]{1,0:T(8,128)(2,1)S(1)}, u32[]{:S(2)}, u32[]{:S(2)}) collective-permute-start(bf16[32,6656]{1,0:T(8,128)(2,1)S(1)} %get-tuple-element.45), channel_id=1, source_target_pairs={{0,1},{1,0},{2,3},{3,2},{4,5},{5,4},{6,7},{7,6},{8,9},{9,8},{10,11... | collective-permute-start | bytes 1277960 | tf_op jit(solution)/shard_map/ppermute | solution.py:190
  20.0 16.3 %collective-permute-start.4 = (bf16[32,6656]{1,0:T(8,128)(2,1)S(1)}, bf16[32,6656]{1,0:T(8,128)(2,1)S(1)}, u32[]{:S(2)}, u32[]{:S(2)}) collective-permute-start(bf16[32,6656]{1,0:T(8,128)(2,1)S(1)} %get-tuple-element.49), channel_id=1, source_target_pairs={{0,8},{8,0},{1,9},{9,1},{2,10},{10,2},{3,11},{11,3},{4,12},{12,4},... | collective-permute-start | bytes 1277960 | tf_op jit(solution)/shard_map/ppermute | solution.py:190
  25.7 3.2 %collective-permute-start.7 = (bf16[32,2048]{1,0:T(8,128)(2,1)S(1)}, bf16[32,2048]{1,0:T(8,128)(2,1)S(1)}, u32[]{:S(2)}, u32[]{:S(2)}) collective-permute-start(bf16[32,2048]{1,0:T(8,128)(2,1)S(1)} %get-tuple-element.56), channel_id=1, source_target_pairs={{0,1},{1,0},{2,3},{3,2},{4,5},{5,4},{6,7},{7,6},{8,9},{9,8},{10,11... | collective-permute-start | bytes 393224 | tf_op jit(solution)/shard_map/ppermute | solution.py:190
  25.8 3.1 %collective-permute-start.6 = (bf16[32,2048]{1,0:T(8,128)(2,1)S(1)}, bf16[32,2048]{1,0:T(8,128)(2,1)S(1)}, u32[]{:S(2)}, u32[]{:S(2)}) collective-permute-start(bf16[32,2048]{1,0:T(8,128)(2,1)S(1)} %get-tuple-element.52.refs_2_), channel_id=1, source_target_pairs={{0,1},{1,0},{2,3},{3,2},{4,5},{5,4},{6,7},{7,6},{8,9},{9,8},{10,11... | collective-permute-start | bytes 393224 | tf_op jit(solution)/shard_map/ppermute | solution.py:190
  28.7 2.3 %collective-permute-start.5 = (bf16[32,2560]{1,0:T(8,128)(2,1)S(1)}, bf16[32,2560]{1,0:T(8,128)(2,1)S(1)}, u32[]{:S(2)}, u32[]{:S(2)}) collective-permute-start(bf16[32,2560]{1,0:T(8,128)(2,1)S(1)} %get-tuple-element.54), channel_id=1, source_target_pairs={{0,1},{1,0},{2,3},{3,2},{4,5},{5,4},{6,7},{7,6},{8,9},{9,8},{10,11... | collective-permute-start | bytes 491528 | tf_op jit(solution)/shard_map/ppermute | solution.py:190
  29.0 7.4 %collective-permute-start.9 = (bf16[32,2048]{1,0:T(8,128)(2,1)S(1)}, bf16[32,2048]{1,0:T(8,128)(2,1)S(1)}, u32[]{:S(2)}, u32[]{:S(2)}) collective-permute-start(bf16[32,2048]{1,0:T(8,128)(2,1)S(1)} %get-tuple-element.60), channel_id=1, source_target_pairs={{0,8},{8,0},{1,9},{9,1},{2,10},{10,2},{3,11},{11,3},{4,12},{12,4},... | collective-permute-start | bytes 393224 | tf_op jit(solution)/shard_map/ppermute | solution.py:190
  29.5 8.6 %collective-permute-start.12 = (bf16[32,2048]{1,0:T(8,128)(2,1)S(1)}, bf16[32,2048]{1,0:T(8,128)(2,1)S(1)}, u32[]{:S(2)}, u32[]{:S(2)}) collective-permute-start(bf16[32,2048]{1,0:T(8,128)(2,1)S(1)} %get-tuple-element.68), channel_id=1, source_target_pairs={{0,8},{8,0},{1,9},{9,1},{2,10},{10,2},{3,11},{11,3},{4,12},{12,4},... | collective-permute-start | bytes 393224 | tf_op jit(solution)/shard_map/ppermute | solution.py:190
  31.1 10.1 %collective-permute-start.8 = (bf16[32,2560]{1,0:T(8,128)(2,1)S(1)}, bf16[32,2560]{1,0:T(8,128)(2,1)S(1)}, u32[]{:S(2)}, u32[]{:S(2)}) collective-permute-start(bf16[32,2560]{1,0:T(8,128)(2,1)S(1)} %get-tuple-element.59), channel_id=1, source_target_pairs={{0,8},{8,0},{1,9},{9,1},{2,10},{10,2},{3,11},{11,3},{4,12},{12,4},... | collective-permute-start | bytes 491528 | tf_op jit(solution)/shard_map/ppermute | solution.py:190
  36.5 1.9 %collective-permute-start.11 = (bf16[16,2048]{1,0:T(8,128)(2,1)S(1)}, bf16[16,2048]{1,0:T(8,128)(2,1)S(1)}, u32[]{:S(2)}, u32[]{:S(2)}) collective-permute-start(bf16[16,2048]{1,0:T(8,128)(2,1)S(1)} %get-tuple-element.63.refs_1_), channel_id=1, source_target_pairs={{0,1},{1,0},{2,3},{3,2},{4,5},{5,4},{6,7},{7,6},{8,9},{9,8},{10,11... | collective-permute-start | bytes 196616 | tf_op jit(solution)/shard_map/ppermute | solution.py:190
  36.6 1.8 %collective-permute-start.10 = (bf16[16,2048]{1,0:T(8,128)(2,1)S(1)}, bf16[16,2048]{1,0:T(8,128)(2,1)S(1)}, u32[]{:S(2)}, u32[]{:S(2)}) collective-permute-start(bf16[16,2048]{1,0:T(8,128)(2,1)S(1)} %get-tuple-element.62.refs_4_.refs_0_), channel_id=1, source_target_pairs={{0,1},{1,0},{2,3},{3,2},{4,5},{5,4},{6,7},{7,6},{8,9},{9,8},{10,11... | collective-permute-start | bytes 196616 | tf_op jit(solution)/shard_map/ppermute | solution.py:190
  38.3 3.2 %collective-permute-start.14 = (bf16[32,2048]{1,0:T(8,128)(2,1)S(1)}, bf16[32,2048]{1,0:T(8,128)(2,1)S(1)}, u32[]{:S(2)}, u32[]{:S(2)}) collective-permute-start(bf16[32,2048]{1,0:T(8,128)(2,1)S(1)} %shard_map.57.refs_7_.refs_0_), channel_id=1, source_target_pairs={{0,1},{1,0},{2,3},{3,2},{4,5},{5,4},{6,7},{7,6},{8,9},{9,8},{10,11... | collective-permute-start | bytes 393224 | tf_op jit(solution)/shard_map/ppermute | solution.py:190
  41.4 2.3 %collective-permute-start.13 = (bf16[32,2560]{1,0:T(8,128)(2,1)S(1)}, bf16[32,2560]{1,0:T(8,128)(2,1)S(1)}, u32[]{:S(2)}, u32[]{:S(2)}) collective-permute-start(bf16[32,2560]{1,0:T(8,128)(2,1)S(1)} %shard_map.59.refs_4_.refs_0_), channel_id=1, source_target_pairs={{0,1},{1,0},{2,3},{3,2},{4,5},{5,4},{6,7},{7,6},{8,9},{9,8},{10,11... | collective-permute-start | bytes 491528 | tf_op jit(solution)/shard_map/ppermute | solution.py:190
  46.1 6.7 %collective-permute-start.15 = (bf16[16,2048]{1,0:T(8,128)(2,1)S(1)}, bf16[16,2048]{1,0:T(8,128)(2,1)S(1)}, u32[]{:S(2)}, u32[]{:S(2)}) collective-permute-start(bf16[16,2048]{1,0:T(8,128)(2,1)S(1)} %get-tuple-element.76), channel_id=1, source_target_pairs={{0,6},{2,4},{4,2},{6,0},{1,7},{3,5},{5,3},{7,1},{8,14},{10,12},{12... | collective-permute-start | bytes 196616 | tf_op jit(solution)/shard_map/ppermute | solution.py:190
  48.6 6.9 %collective-permute-start.16 = (bf16[16,2048]{1,0:T(8,128)(2,1)S(1)}, bf16[16,2048]{1,0:T(8,128)(2,1)S(1)}, u32[]{:S(2)}, u32[]{:S(2)}) collective-permute-start(bf16[16,2048]{1,0:T(8,128)(2,1)S(1)} %get-tuple-element.77), channel_id=1, source_target_pairs={{0,4},{2,6},{4,0},{6,2},{1,5},{3,7},{5,1},{7,3},{8,12},{10,14},{12... | collective-permute-start | bytes 196616 | tf_op jit(solution)/shard_map/ppermute | solution.py:190
  48.6 6.9 %collective-permute-start.17 = (bf16[16,2048]{1,0:T(8,128)(2,1)S(1)}, bf16[16,2048]{1,0:T(8,128)(2,1)S(1)}, u32[]{:S(2)}, u32[]{:S(2)}) collective-permute-start(bf16[16,2048]{1,0:T(8,128)(2,1)S(1)} %get-tuple-element.78), channel_id=1, source_target_pairs={{0,2},{2,0},{4,6},{6,4},{1,3},{3,1},{5,7},{7,5},{8,10},{10,8},{12,... | collective-permute-start | bytes 196616 | tf_op jit(solution)/shard_map/ppermute | solution.py:190

commit v14 on v13

--- a/solution.py
+++ b/solution.py
@@ -151,8 +151,8 @@
     before = ins[-1:] if not first else []
     ins = ins[: len(ins) - len(before)]
     parts, weights = ins[:-n_weights], ins[-n_weights:]
-    (hidden,) = room
-    c = lax.axis_index("pair")
+    hidden, res = room
+    c, w = lax.axis_index("pair"), lax.axis_index("wide")
     rows = parts[0].shape[0]
     pieces = len(parts) // n_pair
     for at, part in enumerate(parts):
@@ -174,9 +174,12 @@
             total += before[0][:, at]
         if last:
             share = total.shape[0] // n_wide
+            res[...] = total
             for k in range(n_wide):
-                place = (k if n_wide & (n_wide - 1) == 0 else (n_wide - k) % n_wide) * share
-                outs[k][:, at] = total[place : place + share].astype(outs[k].dtype)
+                other = lax.rem(w + k, n_wide)
+                place = jnp.bitwise_xor(w, other) if n_wide & (n_wide - 1) == 0 else (n_wide - k) % n_wide
+                rows_of = pl.ds(pl.multiple_of(place * share, 16), share)
+                outs[k][:, at] = res[rows_of, :].astype(outs[k].dtype)
         else:
             outs[0][:, at] = total
 
@@ -184,9 +187,9 @@
 def shards(sizes, tokens, gate_weight, up_weight, down_weight):
     n_seq, n_wide, n_pair = sizes["seq"], sizes["wide"], sizes["pair"]
 
-    def send(value, axis, k):
+    def send(value, axis, k, paired=False):
         n = sizes[axis]
-        paired = axis == "wide" and n & (n - 1) == 0
+        paired = paired and n & (n - 1) == 0
         return lax.ppermute(value, axis, [(i, i ^ k if paired else (i + k) % n) for i in range(n)])
 
     share, depth = tokens.shape
@@ -276,7 +279,7 @@
             [*parts, *weights, *total],
             outs,
             fetch,
-            [pltpu.VMEM((rows, width), BF16)],
+            [pltpu.VMEM((rows, width), BF16), pltpu.VMEM((rows, tile_of(features)), F32)],
             COST * 2 * rows * width * features,
             COST * 2 * bytes_of(fetch),
         )
@@ -288,7 +291,7 @@
         order, load_kernel, [], [], [(tokens, 0, 0, share), (down_weight, 0, 0, share)], [],
         0, 2 * up_weight.size * size,
     )
-    blocks = [staged] + [send(tokens if k > 1 else staged, "wide", k) for k in range(1, n_wide)]
+    blocks = [staged] + [send(tokens if k > 1 else staged, "wide", k, True) for k in range(1, n_wide)]
     up = pltpu.with_memory_space_constraint(up_weight, pltpu.VMEM)
     columns = gate_weight.shape[1]
     down, whole = {}, [(0, columns)]
@@ -320,7 +323,7 @@
         total = multiply_down(j, hiddens[j], total)
 
     result = total[0]
-    for k in reversed(range(1, n_wide)):
+    for k in range(1, n_wide):
         result = result + send(total[k], "wide", k).astype(F32)
     return result.astype(BF16)
 

time: 56.4 us -> 56 us (level)
  waiting for transfers between devices: 11 us -> 9.72 us
  starting transfers between devices: 16 us -> 16.9 us
    ppermute x18, waiting for transfers between devices: 11 us -> 9.72 us  [send(): lax.ppermute(value, axis, [(i, i ^ k if paired else (i + k) % n) for i in...]
    ppermute x18, starting transfers between devices: 16 us -> 16.9 us  [send(): lax.ppermute(value, axis, [(i, i ^ k if paired else (i + k) % n) for i in...]
where the time goes in v14:
time: 56 us; the launch traced here: 55.8 us
  Pallas kernels  28.3 us (51%)
  starting transfers between devices  16.9 us (30%)
  waiting for transfers between devices  9.72 us (17%)
  other arithmetic  0.66 us (1%)
    pallas_call x16, Pallas kernels, call(): pl.pallas_call(kernel, out_shape=tuple(outs) + tuple(fetched), in_specs=[...  28.3 us
    ppermute x18, starting transfers between devices, send(): lax.ppermute(value, axis, [(i, i ^ k if paired else (i + k) % n) for i in...  16.9 us
    ppermute x18, waiting for transfers between devices, send(): lax.ppermute(value, axis, [(i, i ^ k if paired else (i + k) % n) for i in...  9.72 us
  transfers between devices with their start and end apart: 18, of which 8 were waited for; matrix products, arithmetic and copies ran while one was open for 0% of the time, Pallas kernels for 35%

profile of v14, /device:TPU:0, one launch (start us, length us, event | category | flops | bytes accessed | tf_op | source)
XLA Modules:
  0.0 55.8 jit_solution(2541204484441847856)
XLA Ops:
  0.0 5.0 %collective-permute-start.2 = (bf16[16,2048]{1,0:T(8,128)(2,1)}, bf16[16,2048]{1,0:T(8,128)(2,1)S(1)}, u32[]{:S(2)}, u32[]{:S(2)}) collective-permute-start(bf16[16,2048]{1,0:T(8,128)(2,1)} %refs_0_.1), channel_id=1, source_target_pairs={{0,6},{2,4},{4,2},{6,0},{1,7},{3,5},{5,3},{7,1},{8,14},{10,12},{12... | collective-permute-start | bytes 196616 | tf_op jit(solution)/shard_map/ppermute | solution.py:193
  5.1 1.6 %shard_map.46 = (bf16[16,2048]{1,0:T(8,128)(2,1)S(1)}, bf16[16,2048]{1,0:T(8,128)(2,1)S(1)}) custom-call(bf16[16,2048]{1,0:T(8,128)(2,1)} %refs_0_.1, bf16[6656,2048]{1,0:T(8,128)(2,1)} %refs_5_.1), custom_call_target="tpu_custom_call" | custom-call | bytes 54525952 | tf_op jit(solution)/shard_map/pallas_call | solution.py:71
  6.7 0.7 %collective-permute-start = (bf16[16,2048]{1,0:T(8,128)(2,1)S(1)}, bf16[16,2048]{1,0:T(8,128)(2,1)S(1)}, u32[]{:S(2)}, u32[]{:S(2)}) collective-permute-start(bf16[16,2048]{1,0:T(8,128)(2,1)S(1)} %get-tuple-element.42.refs_0_.refs_6_), channel_id=1, source_target_pairs={{0,2},{2,0},{4,6},{6,4},{1,3},{3,1},{5,7},{7,5},{8,10},{10,8},{12,... | collective-permute-start | bytes 196616 | tf_op jit(solution)/shard_map/ppermute | solution.py:193
  7.8 3.1 %collective-permute-done.1.refs_2_ = bf16[16,2048]{1,0:T(8,128)(2,1)S(1)} collective-permute-done((bf16[16,2048]{1,0:T(8,128)(2,1)}, bf16[16,2048]{1,0:T(8,128)(2,1)S(1)}, u32[]{:S(2)}, u32[]{:S(2)}) %collective-permute-start.1) | collective-permute-done | bytes 65568 | tf_op jit(solution)/shard_map/ppermute | solution.py:193
  10.9 0.6 %collective-permute-done.refs_1_ = bf16[16,2048]{1,0:T(8,128)(2,1)S(1)} collective-permute-done((bf16[16,2048]{1,0:T(8,128)(2,1)S(1)}, bf16[16,2048]{1,0:T(8,128)(2,1)S(1)}, u32[]{:S(2)}, u32[]{:S(2)}) %collective-permute-start) | collective-permute-done | bytes 65568 | tf_op jit(solution)/shard_map/ppermute | solution.py:193
  11.6 6.4 %shard_map.47 = (f32[32,6656]{1,0:T(8,128)S(1)}, bf16[32,6656]{1,0:T(8,128)(2,1)S(1)}, bf16[64,2048]{1,0:T(8,128)(2,1)S(1)}, bf16[2048,4096]{1,0:T(8,128)(2,1)S(1)}) custom-call(bf16[16,2048]{1,0:T(8,128)(2,1)S(1)} %get-tuple-element.42.refs_0_.refs_6_, bf16[16,2048]{1,0:T(8,128)(2,1)S(1)} %collective-permute-done.refs_1_, ...), custom_call_target="tpu_custom_call" | custom-call | flops 1744830464 | bytes 33554432 | tf_op jit(solution)/shard_map/pallas_call | solution.py:71
  18.1 1.6 %shard_map.48 = (bf16[64,2048]{1,0:T(8,128)(2,1)S(1)}, bf16[512,2048]{1,0:T(8,128)(2,1)S(1)}) custom-call(bf16[64,2048]{1,0:T(8,128)(2,1)S(1)} %get-tuple-element.46.refs_0_.refs_1_, bf16[64,2048]{1,0:T(8,128)(2,1)S(1)} %get-tuple-element.46.refs_0_.refs_1_, bf16[6656,2048]{1,0:T(8,128)(2,1)} %refs_5_.1), custom_call_target="tpu_custom_call" | custom-call | bytes 4194304 | tf_op jit(solution)/shard_map/pallas_call | solution.py:71
  20.0 1.6 %collective-permute-start.4 = (bf16[32,6656]{1,0:T(8,128)(2,1)S(1)}, bf16[32,6656]{1,0:T(8,128)(2,1)S(1)}, u32[]{:S(2)}, u32[]{:S(2)}) collective-permute-start(bf16[32,6656]{1,0:T(8,128)(2,1)S(1)} %get-tuple-element.49), channel_id=1, source_target_pairs={{0,8},{8,0},{1,9},{9,1},{2,10},{10,2},{3,11},{11,3},{4,12},{12,4},... | collective-permute-start | bytes 1277960 | tf_op jit(solution)/shard_map/ppermute | solution.py:193
  21.6 4.1 %shard_map.50 = (f32[32,4096]{1,0:T(8,128)S(1)}, bf16[32,2048]{1,0:T(8,128)(2,1)S(1)}, bf16[32,2048]{1,0:T(8,128)(2,1)S(1)}, bf16[2048,2560]{1,0:T(8,128)(2,1)S(1)}) custom-call(bf16[64,2048]{1,0:T(8,128)(2,1)S(1)} %get-tuple-element.47.refs_2_.refs_0_, bf16[2048,4096]{1,0:T(8,128)(2,1)S(1)} %get-tuple-element.50.refs_1_, ...), custom_call_target="tpu_custom_call" | custom-call | flops 1073741824 | bytes 20971520 | tf_op jit(solution)/shard_map/pallas_call | solution.py:71
  26.2 2.5 %shard_map.51 = (f32[32,2560]{1,0:T(8,128)S(1)}, bf16[32,2560]{1,0:T(8,128)(2,1)S(1)}, bf16[1024,2048]{1,0:T(8,128)(2,1)S(1)}) custom-call(bf16[64,2048]{1,0:T(8,128)(2,1)S(1)} %get-tuple-element.47.refs_2_.refs_0_, bf16[2048,2560]{1,0:T(8,128)(2,1)S(1)} %get-tuple-element.51.refs_1_, bf16[32,2048]{1,0:T(8,128)(2,1)S(1)} %get-tuple-element.52.refs_2_, ...), custom_call_target="tpu_custom_call" | custom-call | flops 671088640 | bytes 8388608 | tf_op jit(solution)/shard_map/pallas_call | solution.py:71
  29.0 0.5 collective-permute-start.9
  29.5 1.6 %collective-permute-start.12 = (bf16[32,2048]{1,0:T(8,128)(2,1)S(1)}, bf16[32,2048]{1,0:T(8,128)(2,1)S(1)}, u32[]{:S(2)}, u32[]{:S(2)}) collective-permute-start(bf16[32,2048]{1,0:T(8,128)(2,1)S(1)} %get-tuple-element.68), channel_id=1, source_target_pairs={{0,8},{8,0},{1,9},{9,1},{2,10},{10,2},{3,11},{11,3},{4,12},{12,4},... | collective-permute-start | bytes 393224 | tf_op jit(solution)/shard_map/ppermute | solution.py:193
  31.1 0.5 collective-permute-start.8
  31.7 4.6 %shard_map.54 = (bf16[64,2048]{1,0:T(8,128)(2,1)S(1)}, bf16[512,2048]{1,0:T(8,128)(2,1)S(1)}, bf16[2048,2048]{1,0:T(8,128)(2,1)S(1)}, bf16[512,2048]{1,0:T(8,128)(2,1)S(1)}) custom-call(bf16[64,2048]{1,0:T(8,128)(2,1)S(1)} %get-tuple-element.47.refs_2_.refs_0_, f32[32,2560]{1,0:T(8,128)S(1)} %get-tuple-element.58.refs_1_.refs_2_, ...), custom_call_target="tpu_custom_call" | custom-call | tf_op jit(solution)/shard_map/pallas_call | solution.py:71
  37.1 1.1 %collective-permute-done.12.refs_3_ = bf16[32,2048]{1,0:T(8,128)(2,1)S(1)} collective-permute-done((bf16[32,2048]{1,0:T(8,128)(2,1)S(1)}, bf16[32,2048]{1,0:T(8,128)(2,1)S(1)}, u32[]{:S(2)}, u32[]{:S(2)}) %collective-permute-start.12) | collective-permute-done | bytes 131104 | tf_op jit(solution)/shard_map/ppermute | solution.py:193
  38.4 2.2 %shard_map.58 = (f32[64,2048]{1,0:T(8,128)S(1)}, bf16[1024,2048]{1,0:T(8,128)(2,1)S(1)}) custom-call(bf16[16,2048]{1,0:T(8,128)(2,1)S(1)} %get-tuple-element.62.refs_4_.refs_0_, bf16[16,2048]{1,0:T(8,128)(2,1)S(1)} %get-tuple-element.63.refs_1_, bf16[16,2048]{1,0:T(8,128)(2,1)S(1)} %collective-permute-done.10.refs_2_, ...), custom_call_target="tpu_custom_call" | custom-call | flops 536870912 | bytes 8388608 | tf_op jit(solution)/shard_map/pallas_call | solution.py:71
  40.6 0.7 %collective-permute-done.8.refs_3_ = bf16[32,2560]{1,0:T(8,128)(2,1)S(1)} collective-permute-done((bf16[32,2560]{1,0:T(8,128)(2,1)S(1)}, bf16[32,2560]{1,0:T(8,128)(2,1)S(1)}, u32[]{:S(2)}, u32[]{:S(2)}) %collective-permute-start.8) | collective-permute-done | bytes 163872 | tf_op jit(solution)/shard_map/ppermute | solution.py:193
  41.5 2.2 %shard_map.60 = (f32[64,2048]{1,0:T(8,128)S(1)}, bf16[1024,2048]{1,0:T(8,128)(2,1)S(1)}) custom-call(bf16[32,2048]{1,0:T(8,128)(2,1)S(1)} %shard_map.57.refs_7_.refs_0_, bf16[32,2048]{1,0:T(8,128)(2,1)S(1)} %collective-permute-done.14.refs_1_, bf16[2048,2048]{1,0:T(8,128)(2,1)S(1)} %get-tuple-element.72.refs_2_, ...), custom_call_target="tpu_custom_call" | custom-call | flops 536870912 | bytes 8388608 | tf_op jit(solution)/shard_map/pallas_call | solution.py:71
  43.7 2.4 %shard_map.61 = (f32[16,2048]{1,0:T(8,128)S(1)}, bf16[16,2048]{1,0:T(8,128)(2,1)S(1)}, bf16[16,2048]{1,0:T(8,128)(2,1)S(1)}, bf16[16,2048]{1,0:T(8,128)(2,1)S(1)}) custom-call(bf16[32,2560]{1,0:T(8,128)(2,1)S(1)} %shard_map.59.refs_4_.refs_0_, bf16[32,2560]{1,0:T(8,128)(2,1)S(1)} %collective-permute-done.13.refs_1_, ...), custom_call_target="tpu_custom_call" | custom-call | flops 671088640 | tf_op jit(solution)/shard_map/pallas_call | solution.py:71
  46.5 2.6 %collective-permute-start.16 = (bf16[16,2048]{1,0:T(8,128)(2,1)S(1)}, bf16[16,2048]{1,0:T(8,128)(2,1)S(1)}, u32[]{:S(2)}, u32[]{:S(2)}) collective-permute-start(bf16[16,2048]{1,0:T(8,128)(2,1)S(1)} %get-tuple-element.77), channel_id=1, source_target_pairs={{0,4},{2,6},{4,0},{6,2},{1,5},{3,7},{5,1},{7,3},{8,12},{10,14},{12... | collective-permute-start | bytes 196616 | tf_op jit(solution)/shard_map/ppermute | solution.py:193
  49.2 2.3 %collective-permute-start.17 = (bf16[16,2048]{1,0:T(8,128)(2,1)S(1)}, bf16[16,2048]{1,0:T(8,128)(2,1)S(1)}, u32[]{:S(2)}, u32[]{:S(2)}) collective-permute-start(bf16[16,2048]{1,0:T(8,128)(2,1)S(1)} %get-tuple-element.78), channel_id=1, source_target_pairs={{0,6},{2,0},{4,2},{6,4},{1,7},{3,1},{5,3},{7,5},{8,14},{10,8},{12,... | collective-permute-start | bytes 196616 | tf_op jit(solution)/shard_map/ppermute | solution.py:193
  51.5 1.3 %collective-permute-done.15 = bf16[16,2048]{1,0:T(8,128)(2,1)S(1)} collective-permute-done((bf16[16,2048]{1,0:T(8,128)(2,1)S(1)}, bf16[16,2048]{1,0:T(8,128)(2,1)S(1)}, u32[]{:S(2)}, u32[]{:S(2)}) %collective-permute-start.15) | collective-permute-done | bytes 65568 | tf_op jit(solution)/shard_map/ppermute | solution.py:193
  52.8 2.3 %collective-permute-done.16 = bf16[16,2048]{1,0:T(8,128)(2,1)S(1)} collective-permute-done((bf16[16,2048]{1,0:T(8,128)(2,1)S(1)}, bf16[16,2048]{1,0:T(8,128)(2,1)S(1)}, u32[]{:S(2)}, u32[]{:S(2)}) %collective-permute-start.16) | collective-permute-done | bytes 65568 | tf_op jit(solution)/shard_map/ppermute | solution.py:193
  55.1 0.7 %add_convert_fusion = bf16[16,2048]{1,0:T(8,128)(2,1)} fusion(bf16[16,2048]{1,0:T(8,128)(2,1)S(1)} %collective-permute-done.17, bf16[16,2048]{1,0:T(8,128)(2,1)S(1)} %collective-permute-done.16, f32[16,2048]{1,0:T(8,128)S(1)} %get-tuple-element.75, bf16[16,2048]{1,0:T(8,128)(2,1)S(1)} %collective-permute-done.15), kind=kLoop, calls=%fused_computation | loop fusion | flops 229376 | bytes 393216 | tf_op jit(solution)/shard_map/convert_element_type | solution.py:328
  (31 shorter events, 3.2 us)
Async XLA Ops:
  0.0 11.6 %copy-start = (bf16[2048,6656]{1,0:T(8,128)(2,1)S(1)}, bf16[2048,6656]{1,0:T(8,128)(2,1)}, u32[]{:S(2)}) copy-start(bf16[2048,6656]{1,0:T(8,128)(2,1)} %refs_4_.2) | copy-start | bytes 81788928
  0.0 7.8 %collective-permute-start.2 = (bf16[16,2048]{1,0:T(8,128)(2,1)}, bf16[16,2048]{1,0:T(8,128)(2,1)S(1)}, u32[]{:S(2)}, u32[]{:S(2)}) collective-permute-start(bf16[16,2048]{1,0:T(8,128)(2,1)} %refs_0_.1), channel_id=1, source_target_pairs={{0,6},{2,4},{4,2},{6,0},{1,7},{3,5},{5,3},{7,1},{8,14},{10,12},{12... | collective-permute-start | bytes 196616 | tf_op jit(solution)/shard_map/ppermute | solution.py:193
  5.1 5.9 %collective-permute-start.1 = (bf16[16,2048]{1,0:T(8,128)(2,1)}, bf16[16,2048]{1,0:T(8,128)(2,1)S(1)}, u32[]{:S(2)}, u32[]{:S(2)}) collective-permute-start(bf16[16,2048]{1,0:T(8,128)(2,1)} %refs_0_.1), channel_id=1, source_target_pairs={{0,4},{2,6},{4,0},{6,2},{1,5},{3,7},{5,1},{7,3},{8,12},{10,14},{12... | collective-permute-start | bytes 196616 | tf_op jit(solution)/shard_map/ppermute | solution.py:193
  6.7 4.9 %collective-permute-start = (bf16[16,2048]{1,0:T(8,128)(2,1)S(1)}, bf16[16,2048]{1,0:T(8,128)(2,1)S(1)}, u32[]{:S(2)}, u32[]{:S(2)}) collective-permute-start(bf16[16,2048]{1,0:T(8,128)(2,1)S(1)} %get-tuple-element.42.refs_0_.refs_6_), channel_id=1, source_target_pairs={{0,2},{2,0},{4,6},{6,4},{1,3},{3,1},{5,7},{7,5},{8,10},{10,8},{12,... | collective-permute-start | bytes 196616 | tf_op jit(solution)/shard_map/ppermute | solution.py:193
  18.0 1.8 %collective-permute-start.3 = (bf16[32,6656]{1,0:T(8,128)(2,1)S(1)}, bf16[32,6656]{1,0:T(8,128)(2,1)S(1)}, u32[]{:S(2)}, u32[]{:S(2)}) collective-permute-start(bf16[32,6656]{1,0:T(8,128)(2,1)S(1)} %get-tuple-element.45), channel_id=1, source_target_pairs={{0,1},{1,0},{2,3},{3,2},{4,5},{5,4},{6,7},{7,6},{8,9},{9,8},{10,11... | collective-permute-start | bytes 1277960 | tf_op jit(solution)/shard_map/ppermute | solution.py:193
  20.0 16.3 %collective-permute-start.4 = (bf16[32,6656]{1,0:T(8,128)(2,1)S(1)}, bf16[32,6656]{1,0:T(8,128)(2,1)S(1)}, u32[]{:S(2)}, u32[]{:S(2)}) collective-permute-start(bf16[32,6656]{1,0:T(8,128)(2,1)S(1)} %get-tuple-element.49), channel_id=1, source_target_pairs={{0,8},{8,0},{1,9},{9,1},{2,10},{10,2},{3,11},{11,3},{4,12},{12,4},... | collective-permute-start | bytes 1277960 | tf_op jit(solution)/shard_map/ppermute | solution.py:193
  25.7 3.2 %collective-permute-start.7 = (bf16[32,2048]{1,0:T(8,128)(2,1)S(1)}, bf16[32,2048]{1,0:T(8,128)(2,1)S(1)}, u32[]{:S(2)}, u32[]{:S(2)}) collective-permute-start(bf16[32,2048]{1,0:T(8,128)(2,1)S(1)} %get-tuple-element.56), channel_id=1, source_target_pairs={{0,1},{1,0},{2,3},{3,2},{4,5},{5,4},{6,7},{7,6},{8,9},{9,8},{10,11... | collective-permute-start | bytes 393224 | tf_op jit(solution)/shard_map/ppermute | solution.py:193
  25.8 3.1 %collective-permute-start.6 = (bf16[32,2048]{1,0:T(8,128)(2,1)S(1)}, bf16[32,2048]{1,0:T(8,128)(2,1)S(1)}, u32[]{:S(2)}, u32[]{:S(2)}) collective-permute-start(bf16[32,2048]{1,0:T(8,128)(2,1)S(1)} %get-tuple-element.52.refs_2_), channel_id=1, source_target_pairs={{0,1},{1,0},{2,3},{3,2},{4,5},{5,4},{6,7},{7,6},{8,9},{9,8},{10,11... | collective-permute-start | bytes 393224 | tf_op jit(solution)/shard_map/ppermute | solution.py:193
  28.7 2.3 %collective-permute-start.5 = (bf16[32,2560]{1,0:T(8,128)(2,1)S(1)}, bf16[32,2560]{1,0:T(8,128)(2,1)S(1)}, u32[]{:S(2)}, u32[]{:S(2)}) collective-permute-start(bf16[32,2560]{1,0:T(8,128)(2,1)S(1)} %get-tuple-element.54), channel_id=1, source_target_pairs={{0,1},{1,0},{2,3},{3,2},{4,5},{5,4},{6,7},{7,6},{8,9},{9,8},{10,11... | collective-permute-start | bytes 491528 | tf_op jit(solution)/shard_map/ppermute | solution.py:193
  29.0 7.4 %collective-permute-start.9 = (bf16[32,2048]{1,0:T(8,128)(2,1)S(1)}, bf16[32,2048]{1,0:T(8,128)(2,1)S(1)}, u32[]{:S(2)}, u32[]{:S(2)}) collective-permute-start(bf16[32,2048]{1,0:T(8,128)(2,1)S(1)} %get-tuple-element.60), channel_id=1, source_target_pairs={{0,8},{8,0},{1,9},{9,1},{2,10},{10,2},{3,11},{11,3},{4,12},{12,4},... | collective-permute-start | bytes 393224 | tf_op jit(solution)/shard_map/ppermute | solution.py:193
  29.5 8.6 %collective-permute-start.12 = (bf16[32,2048]{1,0:T(8,128)(2,1)S(1)}, bf16[32,2048]{1,0:T(8,128)(2,1)S(1)}, u32[]{:S(2)}, u32[]{:S(2)}) collective-permute-start(bf16[32,2048]{1,0:T(8,128)(2,1)S(1)} %get-tuple-element.68), channel_id=1, source_target_pairs={{0,8},{8,0},{1,9},{9,1},{2,10},{10,2},{3,11},{11,3},{4,12},{12,4},... | collective-permute-start | bytes 393224 | tf_op jit(solution)/shard_map/ppermute | solution.py:193
  31.1 10.1 %collective-permute-start.8 = (bf16[32,2560]{1,0:T(8,128)(2,1)S(1)}, bf16[32,2560]{1,0:T(8,128)(2,1)S(1)}, u32[]{:S(2)}, u32[]{:S(2)}) collective-permute-start(bf16[32,2560]{1,0:T(8,128)(2,1)S(1)} %get-tuple-element.59), channel_id=1, source_target_pairs={{0,8},{8,0},{1,9},{9,1},{2,10},{10,2},{3,11},{11,3},{4,12},{12,4},... | collective-permute-start | bytes 491528 | tf_op jit(solution)/shard_map/ppermute | solution.py:193
  36.5 1.9 %collective-permute-start.11 = (bf16[16,2048]{1,0:T(8,128)(2,1)S(1)}, bf16[16,2048]{1,0:T(8,128)(2,1)S(1)}, u32[]{:S(2)}, u32[]{:S(2)}) collective-permute-start(bf16[16,2048]{1,0:T(8,128)(2,1)S(1)} %get-tuple-element.63.refs_1_), channel_id=1, source_target_pairs={{0,1},{1,0},{2,3},{3,2},{4,5},{5,4},{6,7},{7,6},{8,9},{9,8},{10,11... | collective-permute-start | bytes 196616 | tf_op jit(solution)/shard_map/ppermute | solution.py:193
  36.6 1.8 %collective-permute-start.10 = (bf16[16,2048]{1,0:T(8,128)(2,1)S(1)}, bf16[16,2048]{1,0:T(8,128)(2,1)S(1)}, u32[]{:S(2)}, u32[]{:S(2)}) collective-permute-start(bf16[16,2048]{1,0:T(8,128)(2,1)S(1)} %get-tuple-element.62.refs_4_.refs_0_), channel_id=1, source_target_pairs={{0,1},{1,0},{2,3},{3,2},{4,5},{5,4},{6,7},{7,6},{8,9},{9,8},{10,11... | collective-permute-start | bytes 196616 | tf_op jit(solution)/shard_map/ppermute | solution.py:193
  38.3 3.2 %collective-permute-start.14 = (bf16[32,2048]{1,0:T(8,128)(2,1)S(1)}, bf16[32,2048]{1,0:T(8,128)(2,1)S(1)}, u32[]{:S(2)}, u32[]{:S(2)}) collective-permute-start(bf16[32,2048]{1,0:T(8,128)(2,1)S(1)} %shard_map.57.refs_7_.refs_0_), channel_id=1, source_target_pairs={{0,1},{1,0},{2,3},{3,2},{4,5},{5,4},{6,7},{7,6},{8,9},{9,8},{10,11... | collective-permute-start | bytes 393224 | tf_op jit(solution)/shard_map/ppermute | solution.py:193
  41.4 2.3 %collective-permute-start.13 = (bf16[32,2560]{1,0:T(8,128)(2,1)S(1)}, bf16[32,2560]{1,0:T(8,128)(2,1)S(1)}, u32[]{:S(2)}, u32[]{:S(2)}) collective-permute-start(bf16[32,2560]{1,0:T(8,128)(2,1)S(1)} %shard_map.59.refs_4_.refs_0_), channel_id=1, source_target_pairs={{0,1},{1,0},{2,3},{3,2},{4,5},{5,4},{6,7},{7,6},{8,9},{9,8},{10,11... | collective-permute-start | bytes 491528 | tf_op jit(solution)/shard_map/ppermute | solution.py:193
  46.1 6.7 %collective-permute-start.15 = (bf16[16,2048]{1,0:T(8,128)(2,1)S(1)}, bf16[16,2048]{1,0:T(8,128)(2,1)S(1)}, u32[]{:S(2)}, u32[]{:S(2)}) collective-permute-start(bf16[16,2048]{1,0:T(8,128)(2,1)S(1)} %get-tuple-element.76), channel_id=1, source_target_pairs={{0,2},{2,4},{4,6},{6,0},{1,3},{3,5},{5,7},{7,1},{8,10},{10,12},{12... | collective-permute-start | bytes 196616 | tf_op jit(solution)/shard_map/ppermute | solution.py:193
  46.5 8.6 %collective-permute-start.16 = (bf16[16,2048]{1,0:T(8,128)(2,1)S(1)}, bf16[16,2048]{1,0:T(8,128)(2,1)S(1)}, u32[]{:S(2)}, u32[]{:S(2)}) collective-permute-start(bf16[16,2048]{1,0:T(8,128)(2,1)S(1)} %get-tuple-element.77), channel_id=1, source_target_pairs={{0,4},{2,6},{4,0},{6,2},{1,5},{3,7},{5,1},{7,3},{8,12},{10,14},{12... | collective-permute-start | bytes 196616 | tf_op jit(solution)/shard_map/ppermute | solution.py:193
  49.2 5.9 %collective-permute-start.17 = (bf16[16,2048]{1,0:T(8,128)(2,1)S(1)}, bf16[16,2048]{1,0:T(8,128)(2,1)S(1)}, u32[]{:S(2)}, u32[]{:S(2)}) collective-permute-start(bf16[16,2048]{1,0:T(8,128)(2,1)S(1)} %get-tuple-element.78), channel_id=1, source_target_pairs={{0,6},{2,0},{4,2},{6,4},{1,7},{3,1},{5,3},{7,5},{8,14},{10,8},{12,... | collective-permute-start | bytes 196616 | tf_op jit(solution)/shard_map/ppermute | solution.py:193

commit v15 on v14

--- a/solution.py
+++ b/solution.py
@@ -291,7 +291,7 @@
         order, load_kernel, [], [], [(tokens, 0, 0, share), (down_weight, 0, 0, share)], [],
         0, 2 * up_weight.size * size,
     )
-    blocks = [staged] + [send(tokens if k > 1 else staged, "wide", k, True) for k in range(1, n_wide)]
+    blocks = [staged] + [send(tokens, "wide", k, True) for k in range(1, n_wide)]
     up = pltpu.with_memory_space_constraint(up_weight, pltpu.VMEM)
     columns = gate_weight.shape[1]
     down, whole = {}, [(0, columns)]

time: 56 us -> 56.3 us (level)
  waiting for transfers between devices: 9.72 us -> 11.7 us
  starting transfers between devices: 16.9 us -> 15.3 us
    ppermute x18, waiting for transfers between devices: 9.72 us -> 11.7 us  [send(): lax.ppermute(value, axis, [(i, i ^ k if paired else (i + k) % n) for i in...]
    ppermute x18, starting transfers between devices: 16.9 us -> 15.3 us  [send(): lax.ppermute(value, axis, [(i, i ^ k if paired else (i + k) % n) for i in...]
  transfers between devices with their start and end apart: 18 -> 18, of which waited for: 8 -> 7; matrix products, arithmetic and copies ran while one was open for 0% -> 0% of each run, Pallas kernels for 35% -> 34%
where the time goes in v15:
time: 56.3 us; the launch traced here: 56.1 us
  Pallas kernels  28.3 us (50%)
  starting transfers between devices  15.3 us (27%)
  waiting for transfers between devices  11.7 us (21%)
  other arithmetic  0.66 us (1%)
    pallas_call x16, Pallas kernels, call(): pl.pallas_call(kernel, out_shape=tuple(outs) + tuple(fetched), in_specs=[...  28.3 us
    ppermute x18, starting transfers between devices, send(): lax.ppermute(value, axis, [(i, i ^ k if paired else (i + k) % n) for i in...  15.3 us
    ppermute x18, waiting for transfers between devices, send(): lax.ppermute(value, axis, [(i, i ^ k if paired else (i + k) % n) for i in...  11.7 us
  transfers between devices with their start and end apart: 18, of which 7 were waited for; matrix products, arithmetic and copies ran while one was open for 0% of the time, Pallas kernels for 34%

profile of v15, /device:TPU:0, one launch (start us, length us, event | category | flops | bytes accessed | tf_op | source)
XLA Modules:
  0.0 56.1 jit_solution(8585402320725223154)
XLA Ops:
  0.0 3.0 %collective-permute-start = (bf16[16,2048]{1,0:T(8,128)(2,1)}, bf16[16,2048]{1,0:T(8,128)(2,1)S(1)}, u32[]{:S(2)}, u32[]{:S(2)}) collective-permute-start(bf16[16,2048]{1,0:T(8,128)(2,1)} %refs_0_.1), channel_id=1, source_target_pairs={{0,2},{2,0},{4,6},{6,4},{1,3},{3,1},{5,7},{7,5},{8,10},{10,8},{12,... | collective-permute-start | bytes 196616 | tf_op jit(solution)/shard_map/ppermute | solution.py:193
  3.0 2.5 %collective-permute-start.2 = (bf16[16,2048]{1,0:T(8,128)(2,1)}, bf16[16,2048]{1,0:T(8,128)(2,1)S(1)}, u32[]{:S(2)}, u32[]{:S(2)}) collective-permute-start(bf16[16,2048]{1,0:T(8,128)(2,1)} %refs_0_.1), channel_id=1, source_target_pairs={{0,6},{2,4},{4,2},{6,0},{1,7},{3,5},{5,3},{7,1},{8,14},{10,12},{12... | collective-permute-start | bytes 196616 | tf_op jit(solution)/shard_map/ppermute | solution.py:193
  5.6 1.6 %shard_map.46 = (bf16[16,2048]{1,0:T(8,128)(2,1)S(1)}, bf16[16,2048]{1,0:T(8,128)(2,1)S(1)}) custom-call(bf16[16,2048]{1,0:T(8,128)(2,1)} %refs_0_.1, bf16[6656,2048]{1,0:T(8,128)(2,1)} %refs_5_.1), custom_call_target="tpu_custom_call" | custom-call | bytes 54525952 | tf_op jit(solution)/shard_map/pallas_call | solution.py:71
  7.3 2.8 %collective-permute-done.2.refs_3_ = bf16[16,2048]{1,0:T(8,128)(2,1)S(1)} collective-permute-done((bf16[16,2048]{1,0:T(8,128)(2,1)}, bf16[16,2048]{1,0:T(8,128)(2,1)S(1)}, u32[]{:S(2)}, u32[]{:S(2)}) %collective-permute-start.2) | collective-permute-done | bytes 65568 | tf_op jit(solution)/shard_map/ppermute | solution.py:193
  10.1 2.1 %collective-permute-done.1.refs_2_ = bf16[16,2048]{1,0:T(8,128)(2,1)S(1)} collective-permute-done((bf16[16,2048]{1,0:T(8,128)(2,1)}, bf16[16,2048]{1,0:T(8,128)(2,1)S(1)}, u32[]{:S(2)}, u32[]{:S(2)}) %collective-permute-start.1) | collective-permute-done | bytes 65568 | tf_op jit(solution)/shard_map/ppermute | solution.py:193
  12.2 6.4 %shard_map.47 = (f32[32,6656]{1,0:T(8,128)S(1)}, bf16[32,6656]{1,0:T(8,128)(2,1)S(1)}, bf16[64,2048]{1,0:T(8,128)(2,1)S(1)}, bf16[2048,4096]{1,0:T(8,128)(2,1)S(1)}) custom-call(bf16[16,2048]{1,0:T(8,128)(2,1)S(1)} %get-tuple-element.42.refs_0_.refs_6_, bf16[16,2048]{1,0:T(8,128)(2,1)S(1)} %collective-permute-done.refs_1_, ...), custom_call_target="tpu_custom_call" | custom-call | flops 1744830464 | bytes 33554432 | tf_op jit(solution)/shard_map/pallas_call | solution.py:71
  18.7 1.6 %shard_map.48 = (bf16[64,2048]{1,0:T(8,128)(2,1)S(1)}, bf16[512,2048]{1,0:T(8,128)(2,1)S(1)}) custom-call(bf16[64,2048]{1,0:T(8,128)(2,1)S(1)} %get-tuple-element.46.refs_0_.refs_1_, bf16[64,2048]{1,0:T(8,128)(2,1)S(1)} %get-tuple-element.46.refs_0_.refs_1_, bf16[6656,2048]{1,0:T(8,128)(2,1)} %refs_5_.1), custom_call_target="tpu_custom_call" | custom-call | bytes 4194304 | tf_op jit(solution)/shard_map/pallas_call | solution.py:71
  20.6 1.6 %collective-permute-start.4 = (bf16[32,6656]{1,0:T(8,128)(2,1)S(1)}, bf16[32,6656]{1,0:T(8,128)(2,1)S(1)}, u32[]{:S(2)}, u32[]{:S(2)}) collective-permute-start(bf16[32,6656]{1,0:T(8,128)(2,1)S(1)} %get-tuple-element.49), channel_id=1, source_target_pairs={{0,8},{8,0},{1,9},{9,1},{2,10},{10,2},{3,11},{11,3},{4,12},{12,4},... | collective-permute-start | bytes 1277960 | tf_op jit(solution)/shard_map/ppermute | solution.py:193
  22.2 4.1 %shard_map.50 = (f32[32,4096]{1,0:T(8,128)S(1)}, bf16[32,2048]{1,0:T(8,128)(2,1)S(1)}, bf16[32,2048]{1,0:T(8,128)(2,1)S(1)}, bf16[2048,2560]{1,0:T(8,128)(2,1)S(1)}) custom-call(bf16[64,2048]{1,0:T(8,128)(2,1)S(1)} %get-tuple-element.47.refs_2_.refs_0_, bf16[2048,4096]{1,0:T(8,128)(2,1)S(1)} %get-tuple-element.50.refs_1_, ...), custom_call_target="tpu_custom_call" | custom-call | flops 1073741824 | bytes 20971520 | tf_op jit(solution)/shard_map/pallas_call | solution.py:71
  26.8 2.5 %shard_map.51 = (f32[32,2560]{1,0:T(8,128)S(1)}, bf16[32,2560]{1,0:T(8,128)(2,1)S(1)}, bf16[1024,2048]{1,0:T(8,128)(2,1)S(1)}) custom-call(bf16[64,2048]{1,0:T(8,128)(2,1)S(1)} %get-tuple-element.47.refs_2_.refs_0_, bf16[2048,2560]{1,0:T(8,128)(2,1)S(1)} %get-tuple-element.51.refs_1_, bf16[32,2048]{1,0:T(8,128)(2,1)S(1)} %get-tuple-element.52.refs_2_, ...), custom_call_target="tpu_custom_call" | custom-call | flops 671088640 | bytes 8388608 | tf_op jit(solution)/shard_map/pallas_call | solution.py:71
  29.5 0.6 %collective-permute-start.9 = (bf16[32,2048]{1,0:T(8,128)(2,1)S(1)}, bf16[32,2048]{1,0:T(8,128)(2,1)S(1)}, u32[]{:S(2)}, u32[]{:S(2)}) collective-permute-start(bf16[32,2048]{1,0:T(8,128)(2,1)S(1)} %get-tuple-element.60), channel_id=1, source_target_pairs={{0,8},{8,0},{1,9},{9,1},{2,10},{10,2},{3,11},{11,3},{4,12},{12,4},... | collective-permute-start | bytes 393224 | tf_op jit(solution)/shard_map/ppermute | solution.py:193
  30.1 1.5 %collective-permute-start.12 = (bf16[32,2048]{1,0:T(8,128)(2,1)S(1)}, bf16[32,2048]{1,0:T(8,128)(2,1)S(1)}, u32[]{:S(2)}, u32[]{:S(2)}) collective-permute-start(bf16[32,2048]{1,0:T(8,128)(2,1)S(1)} %get-tuple-element.68), channel_id=1, source_target_pairs={{0,8},{8,0},{1,9},{9,1},{2,10},{10,2},{3,11},{11,3},{4,12},{12,4},... | collective-permute-start | bytes 393224 | tf_op jit(solution)/shard_map/ppermute | solution.py:193
  31.7 0.6 %collective-permute-start.8 = (bf16[32,2560]{1,0:T(8,128)(2,1)S(1)}, bf16[32,2560]{1,0:T(8,128)(2,1)S(1)}, u32[]{:S(2)}, u32[]{:S(2)}) collective-permute-start(bf16[32,2560]{1,0:T(8,128)(2,1)S(1)} %get-tuple-element.59), channel_id=1, source_target_pairs={{0,8},{8,0},{1,9},{9,1},{2,10},{10,2},{3,11},{11,3},{4,12},{12,4},... | collective-permute-start | bytes 491528 | tf_op jit(solution)/shard_map/ppermute | solution.py:193
  32.3 4.6 %shard_map.54 = (bf16[64,2048]{1,0:T(8,128)(2,1)S(1)}, bf16[512,2048]{1,0:T(8,128)(2,1)S(1)}, bf16[2048,2048]{1,0:T(8,128)(2,1)S(1)}, bf16[512,2048]{1,0:T(8,128)(2,1)S(1)}) custom-call(bf16[64,2048]{1,0:T(8,128)(2,1)S(1)} %get-tuple-element.47.refs_2_.refs_0_, f32[32,2560]{1,0:T(8,128)S(1)} %get-tuple-element.58.refs_1_.refs_2_, ...), custom_call_target="tpu_custom_call" | custom-call | tf_op jit(solution)/shard_map/pallas_call | solution.py:71
  37.7 1.0 %collective-permute-done.12.refs_3_ = bf16[32,2048]{1,0:T(8,128)(2,1)S(1)} collective-permute-done((bf16[32,2048]{1,0:T(8,128)(2,1)S(1)}, bf16[32,2048]{1,0:T(8,128)(2,1)S(1)}, u32[]{:S(2)}, u32[]{:S(2)}) %collective-permute-start.12) | collective-permute-done | bytes 131104 | tf_op jit(solution)/shard_map/ppermute | solution.py:193
  38.9 2.2 %shard_map.58 = (f32[64,2048]{1,0:T(8,128)S(1)}, bf16[1024,2048]{1,0:T(8,128)(2,1)S(1)}) custom-call(bf16[16,2048]{1,0:T(8,128)(2,1)S(1)} %get-tuple-element.62.refs_4_.refs_0_, bf16[16,2048]{1,0:T(8,128)(2,1)S(1)} %get-tuple-element.63.refs_1_, bf16[16,2048]{1,0:T(8,128)(2,1)S(1)} %collective-permute-done.10.refs_2_, ...), custom_call_target="tpu_custom_call" | custom-call | flops 536870912 | bytes 8388608 | tf_op jit(solution)/shard_map/pallas_call | solution.py:71
  41.1 0.7 %collective-permute-done.8.refs_3_ = bf16[32,2560]{1,0:T(8,128)(2,1)S(1)} collective-permute-done((bf16[32,2560]{1,0:T(8,128)(2,1)S(1)}, bf16[32,2560]{1,0:T(8,128)(2,1)S(1)}, u32[]{:S(2)}, u32[]{:S(2)}) %collective-permute-start.8) | collective-permute-done | bytes 163872 | tf_op jit(solution)/shard_map/ppermute | solution.py:193
  42.1 2.2 %shard_map.60 = (f32[64,2048]{1,0:T(8,128)S(1)}, bf16[1024,2048]{1,0:T(8,128)(2,1)S(1)}) custom-call(bf16[32,2048]{1,0:T(8,128)(2,1)S(1)} %shard_map.57.refs_7_.refs_0_, bf16[32,2048]{1,0:T(8,128)(2,1)S(1)} %collective-permute-done.14.refs_1_, bf16[2048,2048]{1,0:T(8,128)(2,1)S(1)} %get-tuple-element.72.refs_2_, ...), custom_call_target="tpu_custom_call" | custom-call | flops 536870912 | bytes 8388608 | tf_op jit(solution)/shard_map/pallas_call | solution.py:71
  44.3 2.4 %shard_map.61 = (f32[16,2048]{1,0:T(8,128)S(1)}, bf16[16,2048]{1,0:T(8,128)(2,1)S(1)}, bf16[16,2048]{1,0:T(8,128)(2,1)S(1)}, bf16[16,2048]{1,0:T(8,128)(2,1)S(1)}) custom-call(bf16[32,2560]{1,0:T(8,128)(2,1)S(1)} %shard_map.59.refs_4_.refs_0_, bf16[32,2560]{1,0:T(8,128)(2,1)S(1)} %collective-permute-done.13.refs_1_, ...), custom_call_target="tpu_custom_call" | custom-call | flops 671088640 | tf_op jit(solution)/shard_map/pallas_call | solution.py:71
  46.8 3.0 %collective-permute-start.16 = (bf16[16,2048]{1,0:T(8,128)(2,1)S(1)}, bf16[16,2048]{1,0:T(8,128)(2,1)S(1)}, u32[]{:S(2)}, u32[]{:S(2)}) collective-permute-start(bf16[16,2048]{1,0:T(8,128)(2,1)S(1)} %get-tuple-element.77), channel_id=1, source_target_pairs={{0,4},{2,6},{4,0},{6,2},{1,5},{3,7},{5,1},{7,3},{8,12},{10,14},{12... | collective-permute-start | bytes 196616 | tf_op jit(solution)/shard_map/ppermute | solution.py:193
  49.7 0.9 %collective-permute-start.17 = (bf16[16,2048]{1,0:T(8,128)(2,1)S(1)}, bf16[16,2048]{1,0:T(8,128)(2,1)S(1)}, u32[]{:S(2)}, u32[]{:S(2)}) collective-permute-start(bf16[16,2048]{1,0:T(8,128)(2,1)S(1)} %get-tuple-element.78), channel_id=1, source_target_pairs={{0,6},{2,0},{4,2},{6,4},{1,7},{3,1},{5,3},{7,5},{8,14},{10,8},{12,... | collective-permute-start | bytes 196616 | tf_op jit(solution)/shard_map/ppermute | solution.py:193
  50.6 3.0 %collective-permute-done.15 = bf16[16,2048]{1,0:T(8,128)(2,1)S(1)} collective-permute-done((bf16[16,2048]{1,0:T(8,128)(2,1)S(1)}, bf16[16,2048]{1,0:T(8,128)(2,1)S(1)}, u32[]{:S(2)}, u32[]{:S(2)}) %collective-permute-start.15) | collective-permute-done | bytes 65568 | tf_op jit(solution)/shard_map/ppermute | solution.py:193
  53.5 1.9 %collective-permute-done.16 = bf16[16,2048]{1,0:T(8,128)(2,1)S(1)} collective-permute-done((bf16[16,2048]{1,0:T(8,128)(2,1)S(1)}, bf16[16,2048]{1,0:T(8,128)(2,1)S(1)}, u32[]{:S(2)}, u32[]{:S(2)}) %collective-permute-start.16) | collective-permute-done | bytes 65568 | tf_op jit(solution)/shard_map/ppermute | solution.py:193
  55.4 0.7 %add_convert_fusion = bf16[16,2048]{1,0:T(8,128)(2,1)} fusion(bf16[16,2048]{1,0:T(8,128)(2,1)S(1)} %collective-permute-done.17, bf16[16,2048]{1,0:T(8,128)(2,1)S(1)} %collective-permute-done.16, f32[16,2048]{1,0:T(8,128)S(1)} %get-tuple-element.75, bf16[16,2048]{1,0:T(8,128)(2,1)S(1)} %collective-permute-done.15), kind=kLoop, calls=%fused_computation | loop fusion | flops 229376 | bytes 393216 | tf_op jit(solution)/shard_map/convert_element_type | solution.py:328
  (31 shorter events, 2.5 us)
Async XLA Ops:
  0.0 12.2 %copy-start = (bf16[2048,6656]{1,0:T(8,128)(2,1)S(1)}, bf16[2048,6656]{1,0:T(8,128)(2,1)}, u32[]{:S(2)}) copy-start(bf16[2048,6656]{1,0:T(8,128)(2,1)} %refs_4_.2) | copy-start | bytes 81788928
  0.0 7.3 %collective-permute-start = (bf16[16,2048]{1,0:T(8,128)(2,1)}, bf16[16,2048]{1,0:T(8,128)(2,1)S(1)}, u32[]{:S(2)}, u32[]{:S(2)}) collective-permute-start(bf16[16,2048]{1,0:T(8,128)(2,1)} %refs_0_.1), channel_id=1, source_target_pairs={{0,2},{2,0},{4,6},{6,4},{1,3},{3,1},{5,7},{7,5},{8,10},{10,8},{12,... | collective-permute-start | bytes 196616 | tf_op jit(solution)/shard_map/ppermute | solution.py:193
  3.0 7.1 %collective-permute-start.2 = (bf16[16,2048]{1,0:T(8,128)(2,1)}, bf16[16,2048]{1,0:T(8,128)(2,1)S(1)}, u32[]{:S(2)}, u32[]{:S(2)}) collective-permute-start(bf16[16,2048]{1,0:T(8,128)(2,1)} %refs_0_.1), channel_id=1, source_target_pairs={{0,6},{2,4},{4,2},{6,0},{1,7},{3,5},{5,3},{7,1},{8,14},{10,12},{12... | collective-permute-start | bytes 196616 | tf_op jit(solution)/shard_map/ppermute | solution.py:193
  5.5 6.7 %collective-permute-start.1 = (bf16[16,2048]{1,0:T(8,128)(2,1)}, bf16[16,2048]{1,0:T(8,128)(2,1)S(1)}, u32[]{:S(2)}, u32[]{:S(2)}) collective-permute-start(bf16[16,2048]{1,0:T(8,128)(2,1)} %refs_0_.1), channel_id=1, source_target_pairs={{0,4},{2,6},{4,0},{6,2},{1,5},{3,7},{5,1},{7,3},{8,12},{10,14},{12... | collective-permute-start | bytes 196616 | tf_op jit(solution)/shard_map/ppermute | solution.py:193
  18.6 1.8 %collective-permute-start.3 = (bf16[32,6656]{1,0:T(8,128)(2,1)S(1)}, bf16[32,6656]{1,0:T(8,128)(2,1)S(1)}, u32[]{:S(2)}, u32[]{:S(2)}) collective-permute-start(bf16[32,6656]{1,0:T(8,128)(2,1)S(1)} %get-tuple-element.45), channel_id=1, source_target_pairs={{0,1},{1,0},{2,3},{3,2},{4,5},{5,4},{6,7},{7,6},{8,9},{9,8},{10,11... | collective-permute-start | bytes 1277960 | tf_op jit(solution)/shard_map/ppermute | solution.py:193
  20.6 16.3 %collective-permute-start.4 = (bf16[32,6656]{1,0:T(8,128)(2,1)S(1)}, bf16[32,6656]{1,0:T(8,128)(2,1)S(1)}, u32[]{:S(2)}, u32[]{:S(2)}) collective-permute-start(bf16[32,6656]{1,0:T(8,128)(2,1)S(1)} %get-tuple-element.49), channel_id=1, source_target_pairs={{0,8},{8,0},{1,9},{9,1},{2,10},{10,2},{3,11},{11,3},{4,12},{12,4},... | collective-permute-start | bytes 1277960 | tf_op jit(solution)/shard_map/ppermute | solution.py:193
  26.2 3.2 %collective-permute-start.7 = (bf16[32,2048]{1,0:T(8,128)(2,1)S(1)}, bf16[32,2048]{1,0:T(8,128)(2,1)S(1)}, u32[]{:S(2)}, u32[]{:S(2)}) collective-permute-start(bf16[32,2048]{1,0:T(8,128)(2,1)S(1)} %get-tuple-element.56), channel_id=1, source_target_pairs={{0,1},{1,0},{2,3},{3,2},{4,5},{5,4},{6,7},{7,6},{8,9},{9,8},{10,11... | collective-permute-start | bytes 393224 | tf_op jit(solution)/shard_map/ppermute | solution.py:193
  26.3 3.1 %collective-permute-start.6 = (bf16[32,2048]{1,0:T(8,128)(2,1)S(1)}, bf16[32,2048]{1,0:T(8,128)(2,1)S(1)}, u32[]{:S(2)}, u32[]{:S(2)}) collective-permute-start(bf16[32,2048]{1,0:T(8,128)(2,1)S(1)} %get-tuple-element.52.refs_2_), channel_id=1, source_target_pairs={{0,1},{1,0},{2,3},{3,2},{4,5},{5,4},{6,7},{7,6},{8,9},{9,8},{10,11... | collective-permute-start | bytes 393224 | tf_op jit(solution)/shard_map/ppermute | solution.py:193
  29.3 2.3 %collective-permute-start.5 = (bf16[32,2560]{1,0:T(8,128)(2,1)S(1)}, bf16[32,2560]{1,0:T(8,128)(2,1)S(1)}, u32[]{:S(2)}, u32[]{:S(2)}) collective-permute-start(bf16[32,2560]{1,0:T(8,128)(2,1)S(1)} %get-tuple-element.54), channel_id=1, source_target_pairs={{0,1},{1,0},{2,3},{3,2},{4,5},{5,4},{6,7},{7,6},{8,9},{9,8},{10,11... | collective-permute-start | bytes 491528 | tf_op jit(solution)/shard_map/ppermute | solution.py:193
  29.5 7.5 %collective-permute-start.9 = (bf16[32,2048]{1,0:T(8,128)(2,1)S(1)}, bf16[32,2048]{1,0:T(8,128)(2,1)S(1)}, u32[]{:S(2)}, u32[]{:S(2)}) collective-permute-start(bf16[32,2048]{1,0:T(8,128)(2,1)S(1)} %get-tuple-element.60), channel_id=1, source_target_pairs={{0,8},{8,0},{1,9},{9,1},{2,10},{10,2},{3,11},{11,3},{4,12},{12,4},... | collective-permute-start | bytes 393224 | tf_op jit(solution)/shard_map/ppermute | solution.py:193
  30.1 8.6 %collective-permute-start.12 = (bf16[32,2048]{1,0:T(8,128)(2,1)S(1)}, bf16[32,2048]{1,0:T(8,128)(2,1)S(1)}, u32[]{:S(2)}, u32[]{:S(2)}) collective-permute-start(bf16[32,2048]{1,0:T(8,128)(2,1)S(1)} %get-tuple-element.68), channel_id=1, source_target_pairs={{0,8},{8,0},{1,9},{9,1},{2,10},{10,2},{3,11},{11,3},{4,12},{12,4},... | collective-permute-start | bytes 393224 | tf_op jit(solution)/shard_map/ppermute | solution.py:193
  31.7 10.2 %collective-permute-start.8 = (bf16[32,2560]{1,0:T(8,128)(2,1)S(1)}, bf16[32,2560]{1,0:T(8,128)(2,1)S(1)}, u32[]{:S(2)}, u32[]{:S(2)}) collective-permute-start(bf16[32,2560]{1,0:T(8,128)(2,1)S(1)} %get-tuple-element.59), channel_id=1, source_target_pairs={{0,8},{8,0},{1,9},{9,1},{2,10},{10,2},{3,11},{11,3},{4,12},{12,4},... | collective-permute-start | bytes 491528 | tf_op jit(solution)/shard_map/ppermute | solution.py:193
  37.1 1.8 %collective-permute-start.11 = (bf16[16,2048]{1,0:T(8,128)(2,1)S(1)}, bf16[16,2048]{1,0:T(8,128)(2,1)S(1)}, u32[]{:S(2)}, u32[]{:S(2)}) collective-permute-start(bf16[16,2048]{1,0:T(8,128)(2,1)S(1)} %get-tuple-element.63.refs_1_), channel_id=1, source_target_pairs={{0,1},{1,0},{2,3},{3,2},{4,5},{5,4},{6,7},{7,6},{8,9},{9,8},{10,11... | collective-permute-start | bytes 196616 | tf_op jit(solution)/shard_map/ppermute | solution.py:193
  37.2 1.7 %collective-permute-start.10 = (bf16[16,2048]{1,0:T(8,128)(2,1)S(1)}, bf16[16,2048]{1,0:T(8,128)(2,1)S(1)}, u32[]{:S(2)}, u32[]{:S(2)}) collective-permute-start(bf16[16,2048]{1,0:T(8,128)(2,1)S(1)} %get-tuple-element.62.refs_4_.refs_0_), channel_id=1, source_target_pairs={{0,1},{1,0},{2,3},{3,2},{4,5},{5,4},{6,7},{7,6},{8,9},{9,8},{10,11... | collective-permute-start | bytes 196616 | tf_op jit(solution)/shard_map/ppermute | solution.py:193
  38.8 3.3 %collective-permute-start.14 = (bf16[32,2048]{1,0:T(8,128)(2,1)S(1)}, bf16[32,2048]{1,0:T(8,128)(2,1)S(1)}, u32[]{:S(2)}, u32[]{:S(2)}) collective-permute-start(bf16[32,2048]{1,0:T(8,128)(2,1)S(1)} %shard_map.57.refs_7_.refs_0_), channel_id=1, source_target_pairs={{0,1},{1,0},{2,3},{3,2},{4,5},{5,4},{6,7},{7,6},{8,9},{9,8},{10,11... | collective-permute-start | bytes 393224 | tf_op jit(solution)/shard_map/ppermute | solution.py:193
  42.0 2.3 %collective-permute-start.13 = (bf16[32,2560]{1,0:T(8,128)(2,1)S(1)}, bf16[32,2560]{1,0:T(8,128)(2,1)S(1)}, u32[]{:S(2)}, u32[]{:S(2)}) collective-permute-start(bf16[32,2560]{1,0:T(8,128)(2,1)S(1)} %shard_map.59.refs_4_.refs_0_), channel_id=1, source_target_pairs={{0,1},{1,0},{2,3},{3,2},{4,5},{5,4},{6,7},{7,6},{8,9},{9,8},{10,11... | collective-permute-start | bytes 491528 | tf_op jit(solution)/shard_map/ppermute | solution.py:193
  46.7 6.8 %collective-permute-start.15 = (bf16[16,2048]{1,0:T(8,128)(2,1)S(1)}, bf16[16,2048]{1,0:T(8,128)(2,1)S(1)}, u32[]{:S(2)}, u32[]{:S(2)}) collective-permute-start(bf16[16,2048]{1,0:T(8,128)(2,1)S(1)} %get-tuple-element.76), channel_id=1, source_target_pairs={{0,2},{2,4},{4,6},{6,0},{1,3},{3,5},{5,7},{7,1},{8,10},{10,12},{12... | collective-permute-start | bytes 196616 | tf_op jit(solution)/shard_map/ppermute | solution.py:193
  46.8 8.7 %collective-permute-start.16 = (bf16[16,2048]{1,0:T(8,128)(2,1)S(1)}, bf16[16,2048]{1,0:T(8,128)(2,1)S(1)}, u32[]{:S(2)}, u32[]{:S(2)}) collective-permute-start(bf16[16,2048]{1,0:T(8,128)(2,1)S(1)} %get-tuple-element.77), channel_id=1, source_target_pairs={{0,4},{2,6},{4,0},{6,2},{1,5},{3,7},{5,1},{7,3},{8,12},{10,14},{12... | collective-permute-start | bytes 196616 | tf_op jit(solution)/shard_map/ppermute | solution.py:193
  49.7 5.7 %collective-permute-start.17 = (bf16[16,2048]{1,0:T(8,128)(2,1)S(1)}, bf16[16,2048]{1,0:T(8,128)(2,1)S(1)}, u32[]{:S(2)}, u32[]{:S(2)}) collective-permute-start(bf16[16,2048]{1,0:T(8,128)(2,1)S(1)} %get-tuple-element.78), channel_id=1, source_target_pairs={{0,6},{2,0},{4,2},{6,4},{1,7},{3,1},{5,3},{7,5},{8,14},{10,8},{12,... | collective-permute-start | bytes 196616 | tf_op jit(solution)/shard_map/ppermute | solution.py:193

commit v16 on v14

--- a/solution.py
+++ b/solution.py
@@ -323,7 +323,7 @@
         total = multiply_down(j, hiddens[j], total)
 
     result = total[0]
-    for k in range(1, n_wide):
+    for k in sorted(range(1, n_wide), key=lambda k: -min(k, n_wide - k)):
         result = result + send(total[k], "wide", k).astype(F32)
     return result.astype(BF16)
 

time: 56 us -> 56.5 us (level)
  starting transfers between devices: 16.9 us -> 17.8 us
    ppermute x18, starting transfers between devices: 16.9 us -> 17.8 us  [send(): lax.ppermute(value, axis, [(i, i ^ k if paired else (i + k) % n) for i in...]
  transfers between devices with their start and end apart: 18 -> 18, of which waited for: 8 -> 9; matrix products, arithmetic and copies ran while one was open for 0% -> 0% of each run, Pallas kernels for 35% -> 34%
where the time goes in v16:
time: 56.5 us; the launch traced here: 56.2 us
  Pallas kernels  28.3 us (50%)
  starting transfers between devices  17.8 us (32%)
  waiting for transfers between devices  9.3 us (16%)
  other arithmetic  0.66 us (1%)
    pallas_call x16, Pallas kernels, call(): pl.pallas_call(kernel, out_shape=tuple(outs) + tuple(fetched), in_specs=[...  28.3 us
    ppermute x18, starting transfers between devices, send(): lax.ppermute(value, axis, [(i, i ^ k if paired else (i + k) % n) for i in...  17.8 us
    ppermute x18, waiting for transfers between devices, send(): lax.ppermute(value, axis, [(i, i ^ k if paired else (i + k) % n) for i in...  9.3 us
  transfers between devices with their start and end apart: 18, of which 9 were waited for; matrix products, arithmetic and copies ran while one was open for 0% of the time, Pallas kernels for 34%

profile of v16, /device:TPU:0, one launch (start us, length us, event | category | flops | bytes accessed | tf_op | source)
XLA Modules:
  0.0 56.2 jit_solution(8731556215763153869)
XLA Ops:
  0.0 5.0 %collective-permute-start.2 = (bf16[16,2048]{1,0:T(8,128)(2,1)}, bf16[16,2048]{1,0:T(8,128)(2,1)S(1)}, u32[]{:S(2)}, u32[]{:S(2)}) collective-permute-start(bf16[16,2048]{1,0:T(8,128)(2,1)} %refs_0_.1), channel_id=1, source_target_pairs={{0,6},{2,4},{4,2},{6,0},{1,7},{3,5},{5,3},{7,1},{8,14},{10,12},{12... | collective-permute-start | bytes 196616 | tf_op jit(solution)/shard_map/ppermute | solution.py:193
  5.1 1.6 %shard_map.46 = (bf16[16,2048]{1,0:T(8,128)(2,1)S(1)}, bf16[16,2048]{1,0:T(8,128)(2,1)S(1)}) custom-call(bf16[16,2048]{1,0:T(8,128)(2,1)} %refs_0_.1, bf16[6656,2048]{1,0:T(8,128)(2,1)} %refs_5_.1), custom_call_target="tpu_custom_call" | custom-call | bytes 54525952 | tf_op jit(solution)/shard_map/pallas_call | solution.py:71
  6.7 0.7 %collective-permute-start = (bf16[16,2048]{1,0:T(8,128)(2,1)S(1)}, bf16[16,2048]{1,0:T(8,128)(2,1)S(1)}, u32[]{:S(2)}, u32[]{:S(2)}) collective-permute-start(bf16[16,2048]{1,0:T(8,128)(2,1)S(1)} %get-tuple-element.42.refs_0_.refs_6_), channel_id=1, source_target_pairs={{0,2},{2,0},{4,6},{6,4},{1,3},{3,1},{5,7},{7,5},{8,10},{10,8},{12,... | collective-permute-start | bytes 196616 | tf_op jit(solution)/shard_map/ppermute | solution.py:193
  7.8 3.1 %collective-permute-done.1.refs_2_ = bf16[16,2048]{1,0:T(8,128)(2,1)S(1)} collective-permute-done((bf16[16,2048]{1,0:T(8,128)(2,1)}, bf16[16,2048]{1,0:T(8,128)(2,1)S(1)}, u32[]{:S(2)}, u32[]{:S(2)}) %collective-permute-start.1) | collective-permute-done | bytes 65568 | tf_op jit(solution)/shard_map/ppermute | solution.py:193
  10.9 0.6 %collective-permute-done.refs_1_ = bf16[16,2048]{1,0:T(8,128)(2,1)S(1)} collective-permute-done((bf16[16,2048]{1,0:T(8,128)(2,1)S(1)}, bf16[16,2048]{1,0:T(8,128)(2,1)S(1)}, u32[]{:S(2)}, u32[]{:S(2)}) %collective-permute-start) | collective-permute-done | bytes 65568 | tf_op jit(solution)/shard_map/ppermute | solution.py:193
  11.6 6.4 %shard_map.47 = (f32[32,6656]{1,0:T(8,128)S(1)}, bf16[32,6656]{1,0:T(8,128)(2,1)S(1)}, bf16[64,2048]{1,0:T(8,128)(2,1)S(1)}, bf16[2048,4096]{1,0:T(8,128)(2,1)S(1)}) custom-call(bf16[16,2048]{1,0:T(8,128)(2,1)S(1)} %get-tuple-element.42.refs_0_.refs_6_, bf16[16,2048]{1,0:T(8,128)(2,1)S(1)} %collective-permute-done.refs_1_, ...), custom_call_target="tpu_custom_call" | custom-call | flops 1744830464 | bytes 33554432 | tf_op jit(solution)/shard_map/pallas_call | solution.py:71
  18.1 1.6 %shard_map.48 = (bf16[64,2048]{1,0:T(8,128)(2,1)S(1)}, bf16[512,2048]{1,0:T(8,128)(2,1)S(1)}) custom-call(bf16[64,2048]{1,0:T(8,128)(2,1)S(1)} %get-tuple-element.46.refs_0_.refs_1_, bf16[64,2048]{1,0:T(8,128)(2,1)S(1)} %get-tuple-element.46.refs_0_.refs_1_, bf16[6656,2048]{1,0:T(8,128)(2,1)} %refs_5_.1), custom_call_target="tpu_custom_call" | custom-call | bytes 4194304 | tf_op jit(solution)/shard_map/pallas_call | solution.py:71
  20.0 1.6 %collective-permute-start.4 = (bf16[32,6656]{1,0:T(8,128)(2,1)S(1)}, bf16[32,6656]{1,0:T(8,128)(2,1)S(1)}, u32[]{:S(2)}, u32[]{:S(2)}) collective-permute-start(bf16[32,6656]{1,0:T(8,128)(2,1)S(1)} %get-tuple-element.49), channel_id=1, source_target_pairs={{0,8},{8,0},{1,9},{9,1},{2,10},{10,2},{3,11},{11,3},{4,12},{12,4},... | collective-permute-start | bytes 1277960 | tf_op jit(solution)/shard_map/ppermute | solution.py:193
  21.6 4.1 %shard_map.50 = (f32[32,4096]{1,0:T(8,128)S(1)}, bf16[32,2048]{1,0:T(8,128)(2,1)S(1)}, bf16[32,2048]{1,0:T(8,128)(2,1)S(1)}, bf16[2048,2560]{1,0:T(8,128)(2,1)S(1)}) custom-call(bf16[64,2048]{1,0:T(8,128)(2,1)S(1)} %get-tuple-element.47.refs_2_.refs_0_, bf16[2048,4096]{1,0:T(8,128)(2,1)S(1)} %get-tuple-element.50.refs_1_, ...), custom_call_target="tpu_custom_call" | custom-call | flops 1073741824 | bytes 20971520 | tf_op jit(solution)/shard_map/pallas_call | solution.py:71
  26.2 2.5 %shard_map.51 = (f32[32,2560]{1,0:T(8,128)S(1)}, bf16[32,2560]{1,0:T(8,128)(2,1)S(1)}, bf16[1024,2048]{1,0:T(8,128)(2,1)S(1)}) custom-call(bf16[64,2048]{1,0:T(8,128)(2,1)S(1)} %get-tuple-element.47.refs_2_.refs_0_, bf16[2048,2560]{1,0:T(8,128)(2,1)S(1)} %get-tuple-element.51.refs_1_, bf16[32,2048]{1,0:T(8,128)(2,1)S(1)} %get-tuple-element.52.refs_2_, ...), custom_call_target="tpu_custom_call" | custom-call | flops 671088640 | bytes 8388608 | tf_op jit(solution)/shard_map/pallas_call | solution.py:71
  29.0 0.5 collective-permute-start.9
  29.5 1.6 %collective-permute-start.12 = (bf16[32,2048]{1,0:T(8,128)(2,1)S(1)}, bf16[32,2048]{1,0:T(8,128)(2,1)S(1)}, u32[]{:S(2)}, u32[]{:S(2)}) collective-permute-start(bf16[32,2048]{1,0:T(8,128)(2,1)S(1)} %get-tuple-element.68), channel_id=1, source_target_pairs={{0,8},{8,0},{1,9},{9,1},{2,10},{10,2},{3,11},{11,3},{4,12},{12,4},... | collective-permute-start | bytes 393224 | tf_op jit(solution)/shard_map/ppermute | solution.py:193
  31.1 0.5 collective-permute-start.8
  31.7 4.6 %shard_map.54 = (bf16[64,2048]{1,0:T(8,128)(2,1)S(1)}, bf16[512,2048]{1,0:T(8,128)(2,1)S(1)}, bf16[2048,2048]{1,0:T(8,128)(2,1)S(1)}, bf16[512,2048]{1,0:T(8,128)(2,1)S(1)}) custom-call(bf16[64,2048]{1,0:T(8,128)(2,1)S(1)} %get-tuple-element.47.refs_2_.refs_0_, f32[32,2560]{1,0:T(8,128)S(1)} %get-tuple-element.58.refs_1_.refs_2_, ...), custom_call_target="tpu_custom_call" | custom-call | tf_op jit(solution)/shard_map/pallas_call | solution.py:71
  37.1 1.1 %collective-permute-done.12.refs_3_ = bf16[32,2048]{1,0:T(8,128)(2,1)S(1)} collective-permute-done((bf16[32,2048]{1,0:T(8,128)(2,1)S(1)}, bf16[32,2048]{1,0:T(8,128)(2,1)S(1)}, u32[]{:S(2)}, u32[]{:S(2)}) %collective-permute-start.12) | collective-permute-done | bytes 131104 | tf_op jit(solution)/shard_map/ppermute | solution.py:193
  38.4 2.2 %shard_map.58 = (f32[64,2048]{1,0:T(8,128)S(1)}, bf16[1024,2048]{1,0:T(8,128)(2,1)S(1)}) custom-call(bf16[16,2048]{1,0:T(8,128)(2,1)S(1)} %get-tuple-element.62.refs_4_.refs_0_, bf16[16,2048]{1,0:T(8,128)(2,1)S(1)} %get-tuple-element.63.refs_1_, bf16[16,2048]{1,0:T(8,128)(2,1)S(1)} %collective-permute-done.10.refs_2_, ...), custom_call_target="tpu_custom_call" | custom-call | flops 536870912 | bytes 8388608 | tf_op jit(solution)/shard_map/pallas_call | solution.py:71
  40.6 0.7 %collective-permute-done.8.refs_3_ = bf16[32,2560]{1,0:T(8,128)(2,1)S(1)} collective-permute-done((bf16[32,2560]{1,0:T(8,128)(2,1)S(1)}, bf16[32,2560]{1,0:T(8,128)(2,1)S(1)}, u32[]{:S(2)}, u32[]{:S(2)}) %collective-permute-start.8) | collective-permute-done | bytes 163872 | tf_op jit(solution)/shard_map/ppermute | solution.py:193
  41.5 2.2 %shard_map.60 = (f32[64,2048]{1,0:T(8,128)S(1)}, bf16[1024,2048]{1,0:T(8,128)(2,1)S(1)}) custom-call(bf16[32,2048]{1,0:T(8,128)(2,1)S(1)} %shard_map.57.refs_7_.refs_0_, bf16[32,2048]{1,0:T(8,128)(2,1)S(1)} %collective-permute-done.14.refs_1_, bf16[2048,2048]{1,0:T(8,128)(2,1)S(1)} %get-tuple-element.72.refs_2_, ...), custom_call_target="tpu_custom_call" | custom-call | flops 536870912 | bytes 8388608 | tf_op jit(solution)/shard_map/pallas_call | solution.py:71
  43.7 2.4 %shard_map.61 = (f32[16,2048]{1,0:T(8,128)S(1)}, bf16[16,2048]{1,0:T(8,128)(2,1)S(1)}, bf16[16,2048]{1,0:T(8,128)(2,1)S(1)}, bf16[16,2048]{1,0:T(8,128)(2,1)S(1)}) custom-call(bf16[32,2560]{1,0:T(8,128)(2,1)S(1)} %shard_map.59.refs_4_.refs_0_, bf16[32,2560]{1,0:T(8,128)(2,1)S(1)} %collective-permute-done.13.refs_1_, ...), custom_call_target="tpu_custom_call" | custom-call | flops 671088640 | tf_op jit(solution)/shard_map/pallas_call | solution.py:71
  46.1 2.5 %collective-permute-start.15 = (bf16[16,2048]{1,0:T(8,128)(2,1)S(1)}, bf16[16,2048]{1,0:T(8,128)(2,1)S(1)}, u32[]{:S(2)}, u32[]{:S(2)}) collective-permute-start(bf16[16,2048]{1,0:T(8,128)(2,1)S(1)} %get-tuple-element.76), channel_id=1, source_target_pairs={{0,4},{2,6},{4,0},{6,2},{1,5},{3,7},{5,1},{7,3},{8,12},{10,14},{12... | collective-permute-start | bytes 196616 | tf_op jit(solution)/shard_map/ppermute | solution.py:193
  48.5 0.6 %collective-permute-start.16 = (bf16[16,2048]{1,0:T(8,128)(2,1)S(1)}, bf16[16,2048]{1,0:T(8,128)(2,1)S(1)}, u32[]{:S(2)}, u32[]{:S(2)}) collective-permute-start(bf16[16,2048]{1,0:T(8,128)(2,1)S(1)} %get-tuple-element.77), channel_id=1, source_target_pairs={{0,2},{2,4},{4,6},{6,0},{1,3},{3,5},{5,7},{7,1},{8,10},{10,12},{12... | collective-permute-start | bytes 196616 | tf_op jit(solution)/shard_map/ppermute | solution.py:193
  49.2 3.2 %collective-permute-start.17 = (bf16[16,2048]{1,0:T(8,128)(2,1)S(1)}, bf16[16,2048]{1,0:T(8,128)(2,1)S(1)}, u32[]{:S(2)}, u32[]{:S(2)}) collective-permute-start(bf16[16,2048]{1,0:T(8,128)(2,1)S(1)} %get-tuple-element.78), channel_id=1, source_target_pairs={{0,6},{2,0},{4,2},{6,4},{1,7},{3,1},{5,3},{7,5},{8,14},{10,8},{12,... | collective-permute-start | bytes 196616 | tf_op jit(solution)/shard_map/ppermute | solution.py:193
  52.9 2.4 %collective-permute-done.16 = bf16[16,2048]{1,0:T(8,128)(2,1)S(1)} collective-permute-done((bf16[16,2048]{1,0:T(8,128)(2,1)S(1)}, bf16[16,2048]{1,0:T(8,128)(2,1)S(1)}, u32[]{:S(2)}, u32[]{:S(2)}) %collective-permute-start.16) | collective-permute-done | bytes 65568 | tf_op jit(solution)/shard_map/ppermute | solution.py:193
  55.6 0.7 %add_convert_fusion = bf16[16,2048]{1,0:T(8,128)(2,1)} fusion(bf16[16,2048]{1,0:T(8,128)(2,1)S(1)} %collective-permute-done.17, bf16[16,2048]{1,0:T(8,128)(2,1)S(1)} %collective-permute-done.16, f32[16,2048]{1,0:T(8,128)S(1)} %get-tuple-element.75, bf16[16,2048]{1,0:T(8,128)(2,1)S(1)} %collective-permute-done.15), kind=kLoop, calls=%fused_computation | loop fusion | flops 229376 | bytes 393216 | tf_op jit(solution)/shard_map/convert_element_type | solution.py:328
  (31 shorter events, 3.6 us)
Async XLA Ops:
  0.0 11.6 %copy-start = (bf16[2048,6656]{1,0:T(8,128)(2,1)S(1)}, bf16[2048,6656]{1,0:T(8,128)(2,1)}, u32[]{:S(2)}) copy-start(bf16[2048,6656]{1,0:T(8,128)(2,1)} %refs_4_.2) | copy-start | bytes 81788928
  0.0 7.8 %collective-permute-start.2 = (bf16[16,2048]{1,0:T(8,128)(2,1)}, bf16[16,2048]{1,0:T(8,128)(2,1)S(1)}, u32[]{:S(2)}, u32[]{:S(2)}) collective-permute-start(bf16[16,2048]{1,0:T(8,128)(2,1)} %refs_0_.1), channel_id=1, source_target_pairs={{0,6},{2,4},{4,2},{6,0},{1,7},{3,5},{5,3},{7,1},{8,14},{10,12},{12... | collective-permute-start | bytes 196616 | tf_op jit(solution)/shard_map/ppermute | solution.py:193
  5.1 5.9 %collective-permute-start.1 = (bf16[16,2048]{1,0:T(8,128)(2,1)}, bf16[16,2048]{1,0:T(8,128)(2,1)S(1)}, u32[]{:S(2)}, u32[]{:S(2)}) collective-permute-start(bf16[16,2048]{1,0:T(8,128)(2,1)} %refs_0_.1), channel_id=1, source_target_pairs={{0,4},{2,6},{4,0},{6,2},{1,5},{3,7},{5,1},{7,3},{8,12},{10,14},{12... | collective-permute-start | bytes 196616 | tf_op jit(solution)/shard_map/ppermute | solution.py:193
  6.7 4.9 %collective-permute-start = (bf16[16,2048]{1,0:T(8,128)(2,1)S(1)}, bf16[16,2048]{1,0:T(8,128)(2,1)S(1)}, u32[]{:S(2)}, u32[]{:S(2)}) collective-permute-start(bf16[16,2048]{1,0:T(8,128)(2,1)S(1)} %get-tuple-element.42.refs_0_.refs_6_), channel_id=1, source_target_pairs={{0,2},{2,0},{4,6},{6,4},{1,3},{3,1},{5,7},{7,5},{8,10},{10,8},{12,... | collective-permute-start | bytes 196616 | tf_op jit(solution)/shard_map/ppermute | solution.py:193
  18.0 1.8 %collective-permute-start.3 = (bf16[32,6656]{1,0:T(8,128)(2,1)S(1)}, bf16[32,6656]{1,0:T(8,128)(2,1)S(1)}, u32[]{:S(2)}, u32[]{:S(2)}) collective-permute-start(bf16[32,6656]{1,0:T(8,128)(2,1)S(1)} %get-tuple-element.45), channel_id=1, source_target_pairs={{0,1},{1,0},{2,3},{3,2},{4,5},{5,4},{6,7},{7,6},{8,9},{9,8},{10,11... | collective-permute-start | bytes 1277960 | tf_op jit(solution)/shard_map/ppermute | solution.py:193
  20.0 16.3 %collective-permute-start.4 = (bf16[32,6656]{1,0:T(8,128)(2,1)S(1)}, bf16[32,6656]{1,0:T(8,128)(2,1)S(1)}, u32[]{:S(2)}, u32[]{:S(2)}) collective-permute-start(bf16[32,6656]{1,0:T(8,128)(2,1)S(1)} %get-tuple-element.49), channel_id=1, source_target_pairs={{0,8},{8,0},{1,9},{9,1},{2,10},{10,2},{3,11},{11,3},{4,12},{12,4},... | collective-permute-start | bytes 1277960 | tf_op jit(solution)/shard_map/ppermute | solution.py:193
  25.7 3.2 %collective-permute-start.7 = (bf16[32,2048]{1,0:T(8,128)(2,1)S(1)}, bf16[32,2048]{1,0:T(8,128)(2,1)S(1)}, u32[]{:S(2)}, u32[]{:S(2)}) collective-permute-start(bf16[32,2048]{1,0:T(8,128)(2,1)S(1)} %get-tuple-element.56), channel_id=1, source_target_pairs={{0,1},{1,0},{2,3},{3,2},{4,5},{5,4},{6,7},{7,6},{8,9},{9,8},{10,11... | collective-permute-start | bytes 393224 | tf_op jit(solution)/shard_map/ppermute | solution.py:193
  25.8 3.1 %collective-permute-start.6 = (bf16[32,2048]{1,0:T(8,128)(2,1)S(1)}, bf16[32,2048]{1,0:T(8,128)(2,1)S(1)}, u32[]{:S(2)}, u32[]{:S(2)}) collective-permute-start(bf16[32,2048]{1,0:T(8,128)(2,1)S(1)} %get-tuple-element.52.refs_2_), channel_id=1, source_target_pairs={{0,1},{1,0},{2,3},{3,2},{4,5},{5,4},{6,7},{7,6},{8,9},{9,8},{10,11... | collective-permute-start | bytes 393224 | tf_op jit(solution)/shard_map/ppermute | solution.py:193
  28.7 2.3 %collective-permute-start.5 = (bf16[32,2560]{1,0:T(8,128)(2,1)S(1)}, bf16[32,2560]{1,0:T(8,128)(2,1)S(1)}, u32[]{:S(2)}, u32[]{:S(2)}) collective-permute-start(bf16[32,2560]{1,0:T(8,128)(2,1)S(1)} %get-tuple-element.54), channel_id=1, source_target_pairs={{0,1},{1,0},{2,3},{3,2},{4,5},{5,4},{6,7},{7,6},{8,9},{9,8},{10,11... | collective-permute-start | bytes 491528 | tf_op jit(solution)/shard_map/ppermute | solution.py:193
  29.0 7.4 %collective-permute-start.9 = (bf16[32,2048]{1,0:T(8,128)(2,1)S(1)}, bf16[32,2048]{1,0:T(8,128)(2,1)S(1)}, u32[]{:S(2)}, u32[]{:S(2)}) collective-permute-start(bf16[32,2048]{1,0:T(8,128)(2,1)S(1)} %get-tuple-element.60), channel_id=1, source_target_pairs={{0,8},{8,0},{1,9},{9,1},{2,10},{10,2},{3,11},{11,3},{4,12},{12,4},... | collective-permute-start | bytes 393224 | tf_op jit(solution)/shard_map/ppermute | solution.py:193
  29.5 8.6 %collective-permute-start.12 = (bf16[32,2048]{1,0:T(8,128)(2,1)S(1)}, bf16[32,2048]{1,0:T(8,128)(2,1)S(1)}, u32[]{:S(2)}, u32[]{:S(2)}) collective-permute-start(bf16[32,2048]{1,0:T(8,128)(2,1)S(1)} %get-tuple-element.68), channel_id=1, source_target_pairs={{0,8},{8,0},{1,9},{9,1},{2,10},{10,2},{3,11},{11,3},{4,12},{12,4},... | collective-permute-start | bytes 393224 | tf_op jit(solution)/shard_map/ppermute | solution.py:193
  31.1 10.1 %collective-permute-start.8 = (bf16[32,2560]{1,0:T(8,128)(2,1)S(1)}, bf16[32,2560]{1,0:T(8,128)(2,1)S(1)}, u32[]{:S(2)}, u32[]{:S(2)}) collective-permute-start(bf16[32,2560]{1,0:T(8,128)(2,1)S(1)} %get-tuple-element.59), channel_id=1, source_target_pairs={{0,8},{8,0},{1,9},{9,1},{2,10},{10,2},{3,11},{11,3},{4,12},{12,4},... | collective-permute-start | bytes 491528 | tf_op jit(solution)/shard_map/ppermute | solution.py:193
  36.5 1.9 %collective-permute-start.11 = (bf16[16,2048]{1,0:T(8,128)(2,1)S(1)}, bf16[16,2048]{1,0:T(8,128)(2,1)S(1)}, u32[]{:S(2)}, u32[]{:S(2)}) collective-permute-start(bf16[16,2048]{1,0:T(8,128)(2,1)S(1)} %get-tuple-element.63.refs_1_), channel_id=1, source_target_pairs={{0,1},{1,0},{2,3},{3,2},{4,5},{5,4},{6,7},{7,6},{8,9},{9,8},{10,11... | collective-permute-start | bytes 196616 | tf_op jit(solution)/shard_map/ppermute | solution.py:193
  36.6 1.8 %collective-permute-start.10 = (bf16[16,2048]{1,0:T(8,128)(2,1)S(1)}, bf16[16,2048]{1,0:T(8,128)(2,1)S(1)}, u32[]{:S(2)}, u32[]{:S(2)}) collective-permute-start(bf16[16,2048]{1,0:T(8,128)(2,1)S(1)} %get-tuple-element.62.refs_4_.refs_0_), channel_id=1, source_target_pairs={{0,1},{1,0},{2,3},{3,2},{4,5},{5,4},{6,7},{7,6},{8,9},{9,8},{10,11... | collective-permute-start | bytes 196616 | tf_op jit(solution)/shard_map/ppermute | solution.py:193
  38.3 3.2 %collective-permute-start.14 = (bf16[32,2048]{1,0:T(8,128)(2,1)S(1)}, bf16[32,2048]{1,0:T(8,128)(2,1)S(1)}, u32[]{:S(2)}, u32[]{:S(2)}) collective-permute-start(bf16[32,2048]{1,0:T(8,128)(2,1)S(1)} %shard_map.57.refs_7_.refs_0_), channel_id=1, source_target_pairs={{0,1},{1,0},{2,3},{3,2},{4,5},{5,4},{6,7},{7,6},{8,9},{9,8},{10,11... | collective-permute-start | bytes 393224 | tf_op jit(solution)/shard_map/ppermute | solution.py:193
  41.4 2.3 %collective-permute-start.13 = (bf16[32,2560]{1,0:T(8,128)(2,1)S(1)}, bf16[32,2560]{1,0:T(8,128)(2,1)S(1)}, u32[]{:S(2)}, u32[]{:S(2)}) collective-permute-start(bf16[32,2560]{1,0:T(8,128)(2,1)S(1)} %shard_map.59.refs_4_.refs_0_), channel_id=1, source_target_pairs={{0,1},{1,0},{2,3},{3,2},{4,5},{5,4},{6,7},{7,6},{8,9},{9,8},{10,11... | collective-permute-start | bytes 491528 | tf_op jit(solution)/shard_map/ppermute | solution.py:193
  46.1 6.8 %collective-permute-start.15 = (bf16[16,2048]{1,0:T(8,128)(2,1)S(1)}, bf16[16,2048]{1,0:T(8,128)(2,1)S(1)}, u32[]{:S(2)}, u32[]{:S(2)}) collective-permute-start(bf16[16,2048]{1,0:T(8,128)(2,1)S(1)} %get-tuple-element.76), channel_id=1, source_target_pairs={{0,4},{2,6},{4,0},{6,2},{1,5},{3,7},{5,1},{7,3},{8,12},{10,14},{12... | collective-permute-start | bytes 196616 | tf_op jit(solution)/shard_map/ppermute | solution.py:193
  48.5 6.7 %collective-permute-start.16 = (bf16[16,2048]{1,0:T(8,128)(2,1)S(1)}, bf16[16,2048]{1,0:T(8,128)(2,1)S(1)}, u32[]{:S(2)}, u32[]{:S(2)}) collective-permute-start(bf16[16,2048]{1,0:T(8,128)(2,1)S(1)} %get-tuple-element.77), channel_id=1, source_target_pairs={{0,2},{2,4},{4,6},{6,0},{1,3},{3,5},{5,7},{7,1},{8,10},{10,12},{12... | collective-permute-start | bytes 196616 | tf_op jit(solution)/shard_map/ppermute | solution.py:193
  49.2 6.4 %collective-permute-start.17 = (bf16[16,2048]{1,0:T(8,128)(2,1)S(1)}, bf16[16,2048]{1,0:T(8,128)(2,1)S(1)}, u32[]{:S(2)}, u32[]{:S(2)}) collective-permute-start(bf16[16,2048]{1,0:T(8,128)(2,1)S(1)} %get-tuple-element.78), channel_id=1, source_target_pairs={{0,6},{2,0},{4,2},{6,4},{1,7},{3,1},{5,3},{7,5},{8,14},{10,8},{12,... | collective-permute-start | bytes 196616 | tf_op jit(solution)/shard_map/ppermute | solution.py:193

commit v17 on v14

--- a/solution.py
+++ b/solution.py
@@ -11,7 +11,7 @@
 TILE = 512
 GATE = (8, 5)
 DOWN = (4, 4, 5)
-DOWN_LOADS = dict(wait=((0, 1),), rest=((1, 2),), late=((3, 1), (4, 4), (8, 1)), first=((9, 2),), second=((11, 2),))
+DOWN_LOADS = dict(wait=((0, 1),), rest=((1, 2),), late=((3, 1), (4, 4), (8, 2)), first=((10, 3),), second=())
 PAIR_TYPE = BF16
 COST = 1
 SPLIT = 2

time: 56 us -> 55.9 us (level)
  waiting for transfers between devices: 9.72 us -> 8.37 us
  Pallas kernels: 28.3 us -> 29.2 us
    ppermute x18, waiting for transfers between devices: 9.72 us -> 8.37 us  [send(): lax.ppermute(value, axis, [(i, i ^ k if paired else (i + k) % n) for i in...]
    pallas_call x16, Pallas kernels: 28.3 us -> 29.2 us  [call(): pl.pallas_call(kernel, out_shape=tuple(outs) + tuple(fetched), in_specs=[...]
  transfers between devices with their start and end apart: 18 -> 18, of which waited for: 8 -> 9; matrix products, arithmetic and copies ran while one was open for 0% -> 0% of each run, Pallas kernels for 35% -> 36%
where the time goes in v17:
time: 55.9 us; the launch traced here: 55.7 us
  Pallas kernels  29.2 us (52%)
  starting transfers between devices  17.2 us (31%)
  waiting for transfers between devices  8.37 us (15%)
  other arithmetic  0.66 us (1%)
    pallas_call x16, Pallas kernels, call(): pl.pallas_call(kernel, out_shape=tuple(outs) + tuple(fetched), in_specs=[...  29.2 us
    ppermute x18, starting transfers between devices, send(): lax.ppermute(value, axis, [(i, i ^ k if paired else (i + k) % n) for i in...  17.2 us
    ppermute x18, waiting for transfers between devices, send(): lax.ppermute(value, axis, [(i, i ^ k if paired else (i + k) % n) for i in...  8.37 us
  transfers between devices with their start and end apart: 18, of which 9 were waited for; matrix products, arithmetic and copies ran while one was open for 0% of the time, Pallas kernels for 36%

profile of v17, /device:TPU:0, one launch (start us, length us, event | category | flops | bytes accessed | tf_op | source)
XLA Modules:
  0.0 55.7 jit_solution(4123614682945081410)
XLA Ops:
  0.0 5.0 %collective-permute-start.2 = (bf16[16,2048]{1,0:T(8,128)(2,1)}, bf16[16,2048]{1,0:T(8,128)(2,1)S(1)}, u32[]{:S(2)}, u32[]{:S(2)}) collective-permute-start(bf16[16,2048]{1,0:T(8,128)(2,1)} %refs_0_.1), channel_id=1, source_target_pairs={{0,6},{2,4},{4,2},{6,0},{1,7},{3,5},{5,3},{7,1},{8,14},{10,12},{12... | collective-permute-start | bytes 196616 | tf_op jit(solution)/shard_map/ppermute | solution.py:193
  5.1 1.6 %shard_map.46 = (bf16[16,2048]{1,0:T(8,128)(2,1)S(1)}, bf16[16,2048]{1,0:T(8,128)(2,1)S(1)}) custom-call(bf16[16,2048]{1,0:T(8,128)(2,1)} %refs_0_.1, bf16[6656,2048]{1,0:T(8,128)(2,1)} %refs_8_.1), custom_call_target="tpu_custom_call" | custom-call | bytes 54525952 | tf_op jit(solution)/shard_map/pallas_call | solution.py:71
  6.7 0.7 %collective-permute-start = (bf16[16,2048]{1,0:T(8,128)(2,1)S(1)}, bf16[16,2048]{1,0:T(8,128)(2,1)S(1)}, u32[]{:S(2)}, u32[]{:S(2)}) collective-permute-start(bf16[16,2048]{1,0:T(8,128)(2,1)S(1)} %get-tuple-element.40.refs_0_.refs_6_), channel_id=1, source_target_pairs={{0,2},{2,0},{4,6},{6,4},{1,3},{3,1},{5,7},{7,5},{8,10},{10,8},{12,... | collective-permute-start | bytes 196616 | tf_op jit(solution)/shard_map/ppermute | solution.py:193
  7.8 3.1 %collective-permute-done.1.refs_2_ = bf16[16,2048]{1,0:T(8,128)(2,1)S(1)} collective-permute-done((bf16[16,2048]{1,0:T(8,128)(2,1)}, bf16[16,2048]{1,0:T(8,128)(2,1)S(1)}, u32[]{:S(2)}, u32[]{:S(2)}) %collective-permute-start.1) | collective-permute-done | bytes 65568 | tf_op jit(solution)/shard_map/ppermute | solution.py:193
  10.9 0.6 %collective-permute-done.refs_1_ = bf16[16,2048]{1,0:T(8,128)(2,1)S(1)} collective-permute-done((bf16[16,2048]{1,0:T(8,128)(2,1)S(1)}, bf16[16,2048]{1,0:T(8,128)(2,1)S(1)}, u32[]{:S(2)}, u32[]{:S(2)}) %collective-permute-start) | collective-permute-done | bytes 65568 | tf_op jit(solution)/shard_map/ppermute | solution.py:193
  11.6 6.4 %shard_map.47 = (f32[32,6656]{1,0:T(8,128)S(1)}, bf16[32,6656]{1,0:T(8,128)(2,1)S(1)}, bf16[64,2048]{1,0:T(8,128)(2,1)S(1)}, bf16[2048,4096]{1,0:T(8,128)(2,1)S(1)}) custom-call(bf16[16,2048]{1,0:T(8,128)(2,1)S(1)} %get-tuple-element.40.refs_0_.refs_6_, bf16[16,2048]{1,0:T(8,128)(2,1)S(1)} %collective-permute-done.refs_1_, ...), custom_call_target="tpu_custom_call" | custom-call | flops 1744830464 | bytes 33554432 | tf_op jit(solution)/shard_map/pallas_call | solution.py:71
  18.1 1.6 %shard_map.48 = (bf16[64,2048]{1,0:T(8,128)(2,1)S(1)}, bf16[512,2048]{1,0:T(8,128)(2,1)S(1)}) custom-call(bf16[64,2048]{1,0:T(8,128)(2,1)S(1)} %get-tuple-element.44.refs_0_.refs_1_, bf16[64,2048]{1,0:T(8,128)(2,1)S(1)} %get-tuple-element.44.refs_0_.refs_1_, bf16[6656,2048]{1,0:T(8,128)(2,1)} %refs_8_.1), custom_call_target="tpu_custom_call" | custom-call | bytes 4194304 | tf_op jit(solution)/shard_map/pallas_call | solution.py:71
  20.0 1.6 %collective-permute-start.4 = (bf16[32,6656]{1,0:T(8,128)(2,1)S(1)}, bf16[32,6656]{1,0:T(8,128)(2,1)S(1)}, u32[]{:S(2)}, u32[]{:S(2)}) collective-permute-start(bf16[32,6656]{1,0:T(8,128)(2,1)S(1)} %get-tuple-element.47), channel_id=1, source_target_pairs={{0,8},{8,0},{1,9},{9,1},{2,10},{10,2},{3,11},{11,3},{4,12},{12,4},... | collective-permute-start | bytes 1277960 | tf_op jit(solution)/shard_map/ppermute | solution.py:193
  21.6 4.1 %shard_map.50 = (f32[32,4096]{1,0:T(8,128)S(1)}, bf16[32,2048]{1,0:T(8,128)(2,1)S(1)}, bf16[32,2048]{1,0:T(8,128)(2,1)S(1)}, bf16[2048,2560]{1,0:T(8,128)(2,1)S(1)}) custom-call(bf16[64,2048]{1,0:T(8,128)(2,1)S(1)} %get-tuple-element.45.refs_2_.refs_0_, bf16[2048,4096]{1,0:T(8,128)(2,1)S(1)} %get-tuple-element.48.refs_1_, ...), custom_call_target="tpu_custom_call" | custom-call | flops 1073741824 | bytes 20971520 | tf_op jit(solution)/shard_map/pallas_call | solution.py:71
  26.2 2.5 %shard_map.51 = (f32[32,2560]{1,0:T(8,128)S(1)}, bf16[32,2560]{1,0:T(8,128)(2,1)S(1)}, bf16[1024,2048]{1,0:T(8,128)(2,1)S(1)}) custom-call(bf16[64,2048]{1,0:T(8,128)(2,1)S(1)} %get-tuple-element.45.refs_2_.refs_0_, bf16[2048,2560]{1,0:T(8,128)(2,1)S(1)} %get-tuple-element.49.refs_1_, bf16[32,2048]{1,0:T(8,128)(2,1)S(1)} %get-tuple-element.50.refs_2_, ...), custom_call_target="tpu_custom_call" | custom-call | flops 671088640 | bytes 8388608 | tf_op jit(solution)/shard_map/pallas_call | solution.py:71
  29.0 0.5 collective-permute-start.9
  29.5 1.6 %collective-permute-start.12 = (bf16[32,2048]{1,0:T(8,128)(2,1)S(1)}, bf16[32,2048]{1,0:T(8,128)(2,1)S(1)}, u32[]{:S(2)}, u32[]{:S(2)}) collective-permute-start(bf16[32,2048]{1,0:T(8,128)(2,1)S(1)} %get-tuple-element.66), channel_id=1, source_target_pairs={{0,8},{8,0},{1,9},{9,1},{2,10},{10,2},{3,11},{11,3},{4,12},{12,4},... | collective-permute-start | bytes 393224 | tf_op jit(solution)/shard_map/ppermute | solution.py:193
  31.1 0.5 collective-permute-start.8
  31.7 5.2 %shard_map.54 = (bf16[64,2048]{1,0:T(8,128)(2,1)S(1)}, bf16[512,2048]{1,0:T(8,128)(2,1)S(1)}, bf16[2048,2048]{1,0:T(8,128)(2,1)S(1)}, bf16[1024,2048]{1,0:T(8,128)(2,1)S(1)}) custom-call(bf16[64,2048]{1,0:T(8,128)(2,1)S(1)} %get-tuple-element.45.refs_2_.refs_0_, f32[32,2560]{1,0:T(8,128)S(1)} %get-tuple-element.56.refs_1_.refs_2_, ...), custom_call_target="tpu_custom_call" | custom-call | tf_op jit(solution)/shard_map/pallas_call | solution.py:71
  37.2 0.5 collective-permute-start.10
  37.7 0.5 collective-permute-done.12.refs_3_
  38.6 2.8 %shard_map.58 = (f32[64,2048]{1,0:T(8,128)S(1)}, bf16[1536,2048]{1,0:T(8,128)(2,1)S(1)}) custom-call(bf16[16,2048]{1,0:T(8,128)(2,1)S(1)} %get-tuple-element.60.refs_4_.refs_0_, bf16[16,2048]{1,0:T(8,128)(2,1)S(1)} %get-tuple-element.61.refs_1_, bf16[16,2048]{1,0:T(8,128)(2,1)S(1)} %collective-permute-done.10.refs_2_, ...), custom_call_target="tpu_custom_call" | custom-call | flops 536870912 | bytes 12582912 | tf_op jit(solution)/shard_map/pallas_call | solution.py:71
  42.0 2.0 %shard_map.60.refs_4_.refs_5_ = f32[64,2048]{1,0:T(8,128)S(1)} custom-call(bf16[32,2048]{1,0:T(8,128)(2,1)S(1)} %shard_map.57.refs_7_.refs_0_, bf16[32,2048]{1,0:T(8,128)(2,1)S(1)} %collective-permute-done.14.refs_1_, bf16[2048,2048]{1,0:T(8,128)(2,1)S(1)} %get-tuple-element.70.refs_2_, f32[64,2048]{1,0:T(8,128)S(1)} %get-tuple-element.67.refs_4_.refs_3_, ...), custom_call_target="tpu_custom_call" | custom-call | flops 536870912 | tf_op jit(solution)/shard_map/pallas_call | solution.py:71
  44.0 2.4 %shard_map.61 = (f32[16,2048]{1,0:T(8,128)S(1)}, bf16[16,2048]{1,0:T(8,128)(2,1)S(1)}, bf16[16,2048]{1,0:T(8,128)(2,1)S(1)}, bf16[16,2048]{1,0:T(8,128)(2,1)S(1)}) custom-call(bf16[32,2560]{1,0:T(8,128)(2,1)S(1)} %shard_map.59.refs_4_.refs_0_, bf16[32,2560]{1,0:T(8,128)(2,1)S(1)} %collective-permute-done.13.refs_1_, ...), custom_call_target="tpu_custom_call" | custom-call | flops 671088640 | tf_op jit(solution)/shard_map/pallas_call | solution.py:71
  46.8 2.6 %collective-permute-start.16 = (bf16[16,2048]{1,0:T(8,128)(2,1)S(1)}, bf16[16,2048]{1,0:T(8,128)(2,1)S(1)}, u32[]{:S(2)}, u32[]{:S(2)}) collective-permute-start(bf16[16,2048]{1,0:T(8,128)(2,1)S(1)} %get-tuple-element.73), channel_id=1, source_target_pairs={{0,4},{2,6},{4,0},{6,2},{1,5},{3,7},{5,1},{7,3},{8,12},{10,14},{12... | collective-permute-start | bytes 196616 | tf_op jit(solution)/shard_map/ppermute | solution.py:193
  49.4 2.3 %collective-permute-start.17 = (bf16[16,2048]{1,0:T(8,128)(2,1)S(1)}, bf16[16,2048]{1,0:T(8,128)(2,1)S(1)}, u32[]{:S(2)}, u32[]{:S(2)}) collective-permute-start(bf16[16,2048]{1,0:T(8,128)(2,1)S(1)} %get-tuple-element.74), channel_id=1, source_target_pairs={{0,6},{2,0},{4,2},{6,4},{1,7},{3,1},{5,3},{7,5},{8,14},{10,8},{12,... | collective-permute-start | bytes 196616 | tf_op jit(solution)/shard_map/ppermute | solution.py:193
  51.7 1.1 %collective-permute-done.15 = bf16[16,2048]{1,0:T(8,128)(2,1)S(1)} collective-permute-done((bf16[16,2048]{1,0:T(8,128)(2,1)S(1)}, bf16[16,2048]{1,0:T(8,128)(2,1)S(1)}, u32[]{:S(2)}, u32[]{:S(2)}) %collective-permute-start.15) | collective-permute-done | bytes 65568 | tf_op jit(solution)/shard_map/ppermute | solution.py:193
  52.8 2.2 %collective-permute-done.16 = bf16[16,2048]{1,0:T(8,128)(2,1)S(1)} collective-permute-done((bf16[16,2048]{1,0:T(8,128)(2,1)S(1)}, bf16[16,2048]{1,0:T(8,128)(2,1)S(1)}, u32[]{:S(2)}, u32[]{:S(2)}) %collective-permute-start.16) | collective-permute-done | bytes 65568 | tf_op jit(solution)/shard_map/ppermute | solution.py:193
  55.0 0.7 %add_convert_fusion = bf16[16,2048]{1,0:T(8,128)(2,1)} fusion(bf16[16,2048]{1,0:T(8,128)(2,1)S(1)} %collective-permute-done.17, bf16[16,2048]{1,0:T(8,128)(2,1)S(1)} %collective-permute-done.16, f32[16,2048]{1,0:T(8,128)S(1)} %get-tuple-element.71, bf16[16,2048]{1,0:T(8,128)(2,1)S(1)} %collective-permute-done.15), kind=kLoop, calls=%fused_computation | loop fusion | flops 229376 | bytes 393216 | tf_op jit(solution)/shard_map/convert_element_type | solution.py:328
  (31 shorter events, 3.3 us)
Async XLA Ops:
  0.0 11.6 %copy-start = (bf16[2048,6656]{1,0:T(8,128)(2,1)S(1)}, bf16[2048,6656]{1,0:T(8,128)(2,1)}, u32[]{:S(2)}) copy-start(bf16[2048,6656]{1,0:T(8,128)(2,1)} %refs_4_.2) | copy-start | bytes 81788928
  0.0 7.8 %collective-permute-start.2 = (bf16[16,2048]{1,0:T(8,128)(2,1)}, bf16[16,2048]{1,0:T(8,128)(2,1)S(1)}, u32[]{:S(2)}, u32[]{:S(2)}) collective-permute-start(bf16[16,2048]{1,0:T(8,128)(2,1)} %refs_0_.1), channel_id=1, source_target_pairs={{0,6},{2,4},{4,2},{6,0},{1,7},{3,5},{5,3},{7,1},{8,14},{10,12},{12... | collective-permute-start | bytes 196616 | tf_op jit(solution)/shard_map/ppermute | solution.py:193
  5.1 5.9 %collective-permute-start.1 = (bf16[16,2048]{1,0:T(8,128)(2,1)}, bf16[16,2048]{1,0:T(8,128)(2,1)S(1)}, u32[]{:S(2)}, u32[]{:S(2)}) collective-permute-start(bf16[16,2048]{1,0:T(8,128)(2,1)} %refs_0_.1), channel_id=1, source_target_pairs={{0,4},{2,6},{4,0},{6,2},{1,5},{3,7},{5,1},{7,3},{8,12},{10,14},{12... | collective-permute-start | bytes 196616 | tf_op jit(solution)/shard_map/ppermute | solution.py:193
  6.7 4.9 %collective-permute-start = (bf16[16,2048]{1,0:T(8,128)(2,1)S(1)}, bf16[16,2048]{1,0:T(8,128)(2,1)S(1)}, u32[]{:S(2)}, u32[]{:S(2)}) collective-permute-start(bf16[16,2048]{1,0:T(8,128)(2,1)S(1)} %get-tuple-element.40.refs_0_.refs_6_), channel_id=1, source_target_pairs={{0,2},{2,0},{4,6},{6,4},{1,3},{3,1},{5,7},{7,5},{8,10},{10,8},{12,... | collective-permute-start | bytes 196616 | tf_op jit(solution)/shard_map/ppermute | solution.py:193
  18.0 1.8 %collective-permute-start.3 = (bf16[32,6656]{1,0:T(8,128)(2,1)S(1)}, bf16[32,6656]{1,0:T(8,128)(2,1)S(1)}, u32[]{:S(2)}, u32[]{:S(2)}) collective-permute-start(bf16[32,6656]{1,0:T(8,128)(2,1)S(1)} %get-tuple-element.43), channel_id=1, source_target_pairs={{0,1},{1,0},{2,3},{3,2},{4,5},{5,4},{6,7},{7,6},{8,9},{9,8},{10,11... | collective-permute-start | bytes 1277960 | tf_op jit(solution)/shard_map/ppermute | solution.py:193
  20.0 16.9 %collective-permute-start.4 = (bf16[32,6656]{1,0:T(8,128)(2,1)S(1)}, bf16[32,6656]{1,0:T(8,128)(2,1)S(1)}, u32[]{:S(2)}, u32[]{:S(2)}) collective-permute-start(bf16[32,6656]{1,0:T(8,128)(2,1)S(1)} %get-tuple-element.47), channel_id=1, source_target_pairs={{0,8},{8,0},{1,9},{9,1},{2,10},{10,2},{3,11},{11,3},{4,12},{12,4},... | collective-permute-start | bytes 1277960 | tf_op jit(solution)/shard_map/ppermute | solution.py:193
  25.7 3.2 %collective-permute-start.7 = (bf16[32,2048]{1,0:T(8,128)(2,1)S(1)}, bf16[32,2048]{1,0:T(8,128)(2,1)S(1)}, u32[]{:S(2)}, u32[]{:S(2)}) collective-permute-start(bf16[32,2048]{1,0:T(8,128)(2,1)S(1)} %get-tuple-element.54), channel_id=1, source_target_pairs={{0,1},{1,0},{2,3},{3,2},{4,5},{5,4},{6,7},{7,6},{8,9},{9,8},{10,11... | collective-permute-start | bytes 393224 | tf_op jit(solution)/shard_map/ppermute | solution.py:193
  25.8 3.1 %collective-permute-start.6 = (bf16[32,2048]{1,0:T(8,128)(2,1)S(1)}, bf16[32,2048]{1,0:T(8,128)(2,1)S(1)}, u32[]{:S(2)}, u32[]{:S(2)}) collective-permute-start(bf16[32,2048]{1,0:T(8,128)(2,1)S(1)} %get-tuple-element.50.refs_2_), channel_id=1, source_target_pairs={{0,1},{1,0},{2,3},{3,2},{4,5},{5,4},{6,7},{7,6},{8,9},{9,8},{10,11... | collective-permute-start | bytes 393224 | tf_op jit(solution)/shard_map/ppermute | solution.py:193
  28.7 2.3 %collective-permute-start.5 = (bf16[32,2560]{1,0:T(8,128)(2,1)S(1)}, bf16[32,2560]{1,0:T(8,128)(2,1)S(1)}, u32[]{:S(2)}, u32[]{:S(2)}) collective-permute-start(bf16[32,2560]{1,0:T(8,128)(2,1)S(1)} %get-tuple-element.52), channel_id=1, source_target_pairs={{0,1},{1,0},{2,3},{3,2},{4,5},{5,4},{6,7},{7,6},{8,9},{9,8},{10,11... | collective-permute-start | bytes 491528 | tf_op jit(solution)/shard_map/ppermute | solution.py:193
  29.0 8.0 %collective-permute-start.9 = (bf16[32,2048]{1,0:T(8,128)(2,1)S(1)}, bf16[32,2048]{1,0:T(8,128)(2,1)S(1)}, u32[]{:S(2)}, u32[]{:S(2)}) collective-permute-start(bf16[32,2048]{1,0:T(8,128)(2,1)S(1)} %get-tuple-element.58), channel_id=1, source_target_pairs={{0,8},{8,0},{1,9},{9,1},{2,10},{10,2},{3,11},{11,3},{4,12},{12,4},... | collective-permute-start | bytes 393224 | tf_op jit(solution)/shard_map/ppermute | solution.py:193
  29.5 8.6 %collective-permute-start.12 = (bf16[32,2048]{1,0:T(8,128)(2,1)S(1)}, bf16[32,2048]{1,0:T(8,128)(2,1)S(1)}, u32[]{:S(2)}, u32[]{:S(2)}) collective-permute-start(bf16[32,2048]{1,0:T(8,128)(2,1)S(1)} %get-tuple-element.66), channel_id=1, source_target_pairs={{0,8},{8,0},{1,9},{9,1},{2,10},{10,2},{3,11},{11,3},{4,12},{12,4},... | collective-permute-start | bytes 393224 | tf_op jit(solution)/shard_map/ppermute | solution.py:193
  31.1 10.2 %collective-permute-start.8 = (bf16[32,2560]{1,0:T(8,128)(2,1)S(1)}, bf16[32,2560]{1,0:T(8,128)(2,1)S(1)}, u32[]{:S(2)}, u32[]{:S(2)}) collective-permute-start(bf16[32,2560]{1,0:T(8,128)(2,1)S(1)} %get-tuple-element.57), channel_id=1, source_target_pairs={{0,8},{8,0},{1,9},{9,1},{2,10},{10,2},{3,11},{11,3},{4,12},{12,4},... | collective-permute-start | bytes 491528 | tf_op jit(solution)/shard_map/ppermute | solution.py:193
  37.1 1.3 %collective-permute-start.11 = (bf16[16,2048]{1,0:T(8,128)(2,1)S(1)}, bf16[16,2048]{1,0:T(8,128)(2,1)S(1)}, u32[]{:S(2)}, u32[]{:S(2)}) collective-permute-start(bf16[16,2048]{1,0:T(8,128)(2,1)S(1)} %get-tuple-element.61.refs_1_), channel_id=1, source_target_pairs={{0,1},{1,0},{2,3},{3,2},{4,5},{5,4},{6,7},{7,6},{8,9},{9,8},{10,11... | collective-permute-start | bytes 196616 | tf_op jit(solution)/shard_map/ppermute | solution.py:193
  37.2 1.4 %collective-permute-start.10 = (bf16[16,2048]{1,0:T(8,128)(2,1)S(1)}, bf16[16,2048]{1,0:T(8,128)(2,1)S(1)}, u32[]{:S(2)}, u32[]{:S(2)}) collective-permute-start(bf16[16,2048]{1,0:T(8,128)(2,1)S(1)} %get-tuple-element.60.refs_4_.refs_0_), channel_id=1, source_target_pairs={{0,1},{1,0},{2,3},{3,2},{4,5},{5,4},{6,7},{7,6},{8,9},{9,8},{10,11... | collective-permute-start | bytes 196616 | tf_op jit(solution)/shard_map/ppermute | solution.py:193
  38.3 3.7 %collective-permute-start.14 = (bf16[32,2048]{1,0:T(8,128)(2,1)S(1)}, bf16[32,2048]{1,0:T(8,128)(2,1)S(1)}, u32[]{:S(2)}, u32[]{:S(2)}) collective-permute-start(bf16[32,2048]{1,0:T(8,128)(2,1)S(1)} %shard_map.57.refs_7_.refs_0_), channel_id=1, source_target_pairs={{0,1},{1,0},{2,3},{3,2},{4,5},{5,4},{6,7},{7,6},{8,9},{9,8},{10,11... | collective-permute-start | bytes 393224 | tf_op jit(solution)/shard_map/ppermute | solution.py:193
  41.5 2.4 %collective-permute-start.13 = (bf16[32,2560]{1,0:T(8,128)(2,1)S(1)}, bf16[32,2560]{1,0:T(8,128)(2,1)S(1)}, u32[]{:S(2)}, u32[]{:S(2)}) collective-permute-start(bf16[32,2560]{1,0:T(8,128)(2,1)S(1)} %shard_map.59.refs_4_.refs_0_), channel_id=1, source_target_pairs={{0,1},{1,0},{2,3},{3,2},{4,5},{5,4},{6,7},{7,6},{8,9},{9,8},{10,11... | collective-permute-start | bytes 491528 | tf_op jit(solution)/shard_map/ppermute | solution.py:193
  46.3 6.5 %collective-permute-start.15 = (bf16[16,2048]{1,0:T(8,128)(2,1)S(1)}, bf16[16,2048]{1,0:T(8,128)(2,1)S(1)}, u32[]{:S(2)}, u32[]{:S(2)}) collective-permute-start(bf16[16,2048]{1,0:T(8,128)(2,1)S(1)} %get-tuple-element.72), channel_id=1, source_target_pairs={{0,2},{2,4},{4,6},{6,0},{1,3},{3,5},{5,7},{7,1},{8,10},{10,12},{12... | collective-permute-start | bytes 196616 | tf_op jit(solution)/shard_map/ppermute | solution.py:193
  46.8 8.3 %collective-permute-start.16 = (bf16[16,2048]{1,0:T(8,128)(2,1)S(1)}, bf16[16,2048]{1,0:T(8,128)(2,1)S(1)}, u32[]{:S(2)}, u32[]{:S(2)}) collective-permute-start(bf16[16,2048]{1,0:T(8,128)(2,1)S(1)} %get-tuple-element.73), channel_id=1, source_target_pairs={{0,4},{2,6},{4,0},{6,2},{1,5},{3,7},{5,1},{7,3},{8,12},{10,14},{12... | collective-permute-start | bytes 196616 | tf_op jit(solution)/shard_map/ppermute | solution.py:193
  49.4 5.6 %collective-permute-start.17 = (bf16[16,2048]{1,0:T(8,128)(2,1)S(1)}, bf16[16,2048]{1,0:T(8,128)(2,1)S(1)}, u32[]{:S(2)}, u32[]{:S(2)}) collective-permute-start(bf16[16,2048]{1,0:T(8,128)(2,1)S(1)} %get-tuple-element.74), channel_id=1, source_target_pairs={{0,6},{2,0},{4,2},{6,4},{1,7},{3,1},{5,3},{7,5},{8,14},{10,8},{12,... | collective-permute-start | bytes 196616 | tf_op jit(solution)/shard_map/ppermute | solution.py:193

commit v18 on v17

--- a/solution.py
+++ b/solution.py
@@ -11,7 +11,7 @@
 TILE = 512
 GATE = (8, 5)
 DOWN = (4, 4, 5)
-DOWN_LOADS = dict(wait=((0, 1),), rest=((1, 2),), late=((3, 1), (4, 4), (8, 2)), first=((10, 3),), second=())
+DOWN_LOADS = dict(rest=((1, 2),), late=((0, 1), (3, 1), (4, 4), (8, 1)), first=((9, 2),), second=((11, 2),))
 PAIR_TYPE = BF16
 COST = 1
 SPLIT = 2
@@ -291,7 +291,8 @@
         order, load_kernel, [], [], [(tokens, 0, 0, share), (down_weight, 0, 0, share)], [],
         0, 2 * up_weight.size * size,
     )
-    blocks = [staged] + [send(tokens if k > 1 else staged, "wide", k, True) for k in range(1, n_wide)]
+    away = {k: send(tokens, "wide", k, True) for k in reversed(range(1, n_wide))}
+    blocks = [staged] + [away[k] for k in range(1, n_wide)]
     up = pltpu.with_memory_space_constraint(up_weight, pltpu.VMEM)
     columns = gate_weight.shape[1]
     down, whole = {}, [(0, columns)]
@@ -301,10 +302,9 @@
         parts, _, (down[0],) = project([x], gate, chunks, [(down_weight, 0, 0, columns)])
         sums = pair_sum(parts, chunks, chunks)
     else:
-        ups, x, first = project(blocks, [up], whole, gate_of(0), early)
-        x, more = load(x, down_of("wait"), COST * 2 * bytes_of(down_of("wait")))
-        keep("wait", more)
-        (ups,) = pair_sum(ups, whole, whole)
+        ups, x, first = project(blocks, [up], loads, gate_of(0), early)
+        x, _ = load(x, [], 0)
+        (ups,) = pair_sum(ups, loads, whole)
         edge = loads[1][0]
         inner = [chunk for chunk in chunks if chunk[0] < edge]
         parts, _, (second,) = project([x], first, inner, gate_of(1))
@@ -323,7 +323,7 @@
         total = multiply_down(j, hiddens[j], total)
 
     result = total[0]
-    for k in range(1, n_wide):
+    for k in reversed(range(1, n_wide)):
         result = result + send(total[k], "wide", k).astype(F32)
     return result.astype(BF16)
 

time: 55.9 us -> 56 us (level)
  waiting for transfers between devices: 8.37 us -> 11.1 us
  Pallas kernels: 29.2 us -> 27.3 us
  starting transfers between devices: 17.2 us -> 16.4 us
    ppermute x18 -> x19, waiting for transfers between devices: 8.37 us -> 11.1 us  [send(): lax.ppermute(value, axis, [(i, i ^ k if paired else (i + k) % n) for i in...]
    pallas_call x16, Pallas kernels: 29.2 us -> 27.3 us  [call(): pl.pallas_call(kernel, out_shape=tuple(outs) + tuple(fetched), in_specs=[...]
    ppermute x18 -> x19, starting transfers between devices: 17.2 us -> 16.4 us  [send(): lax.ppermute(value, axis, [(i, i ^ k if paired else (i + k) % n) for i in...]
  transfers between devices with their start and end apart: 18 -> 19, of which waited for: 9 -> 9; matrix products, arithmetic and copies ran while one was open for 0% -> 0% of each run, Pallas kernels for 36% -> 33%
where the time goes in v18:
time: 56 us; the launch traced here: 55.8 us
  Pallas kernels  27.3 us (49%)
  starting transfers between devices  16.4 us (29%)
  waiting for transfers between devices  11.1 us (20%)
  other arithmetic  0.66 us (1%)
    pallas_call x16, Pallas kernels, call(): pl.pallas_call(kernel, out_shape=tuple(outs) + tuple(fetched), in_specs=[...  27.3 us
    ppermute x19, starting transfers between devices, send(): lax.ppermute(value, axis, [(i, i ^ k if paired else (i + k) % n) for i in...  16.4 us
    ppermute x19, waiting for transfers between devices, send(): lax.ppermute(value, axis, [(i, i ^ k if paired else (i + k) % n) for i in...  11.1 us
  transfers between devices with their start and end apart: 19, of which 9 were waited for; matrix products, arithmetic and copies ran while one was open for 0% of the time, Pallas kernels for 33%

profile of v18, /device:TPU:0, one launch (start us, length us, event | category | flops | bytes accessed | tf_op | source)
XLA Modules:
  0.0 55.8 jit_solution(15778992267288605070)
XLA Ops:
  0.0 3.0 %collective-permute-start = (bf16[16,2048]{1,0:T(8,128)(2,1)}, bf16[16,2048]{1,0:T(8,128)(2,1)S(1)}, u32[]{:S(2)}, u32[]{:S(2)}) collective-permute-start(bf16[16,2048]{1,0:T(8,128)(2,1)} %refs_0_.1), channel_id=1, source_target_pairs={{0,2},{2,0},{4,6},{6,4},{1,3},{3,1},{5,7},{7,5},{8,10},{10,8},{12,... | collective-permute-start | bytes 196616 | tf_op jit(solution)/shard_map/ppermute | solution.py:193
  3.0 2.6 %collective-permute-start.1 = (bf16[16,2048]{1,0:T(8,128)(2,1)}, bf16[16,2048]{1,0:T(8,128)(2,1)S(1)}, u32[]{:S(2)}, u32[]{:S(2)}) collective-permute-start(bf16[16,2048]{1,0:T(8,128)(2,1)} %refs_0_.1), channel_id=1, source_target_pairs={{0,4},{2,6},{4,0},{6,2},{1,5},{3,7},{5,1},{7,3},{8,12},{10,14},{12... | collective-permute-start | bytes 196616 | tf_op jit(solution)/shard_map/ppermute | solution.py:193
  5.6 1.6 %shard_map.46 = (bf16[16,2048]{1,0:T(8,128)(2,1)S(1)}, bf16[16,2048]{1,0:T(8,128)(2,1)S(1)}) custom-call(bf16[16,2048]{1,0:T(8,128)(2,1)} %refs_0_.1, bf16[6656,2048]{1,0:T(8,128)(2,1)} %refs_5_.3), custom_call_target="tpu_custom_call" | custom-call | bytes 54525952 | tf_op jit(solution)/shard_map/pallas_call | solution.py:71
  7.3 3.2 %collective-permute-done.1.refs_2_ = bf16[16,2048]{1,0:T(8,128)(2,1)S(1)} collective-permute-done((bf16[16,2048]{1,0:T(8,128)(2,1)}, bf16[16,2048]{1,0:T(8,128)(2,1)S(1)}, u32[]{:S(2)}, u32[]{:S(2)}) %collective-permute-start.1) | collective-permute-done | bytes 65568 | tf_op jit(solution)/shard_map/ppermute | solution.py:193
  10.5 1.4 %collective-permute-done.2.refs_3_ = bf16[16,2048]{1,0:T(8,128)(2,1)S(1)} collective-permute-done((bf16[16,2048]{1,0:T(8,128)(2,1)}, bf16[16,2048]{1,0:T(8,128)(2,1)S(1)}, u32[]{:S(2)}, u32[]{:S(2)}) %collective-permute-start.2) | collective-permute-done | bytes 65568 | tf_op jit(solution)/shard_map/ppermute | solution.py:193
  11.9 6.4 %shard_map.47 = (f32[32,6656]{1,0:T(8,128)S(1)}, bf16[32,4096]{1,0:T(8,128)(2,1)S(1)}, bf16[32,2560]{1,0:T(8,128)(2,1)S(1)}, bf16[64,2048]{1,0:T(8,128)(2,1)S(1)}, bf16[2048,4096]{1,0:T(8,128)(2,1)S(1)}) custom-call(bf16[16,2048]{1,0:T(8,128)(2,1)S(1)} %get-tuple-element.42.refs_0_.refs_6_, bf16[16,2048]{1,0:T(8,128)(2,1)S(1)} %collective-permute-done.refs_1_, ...), custom_call_target="tpu_custom_call" | custom-call | flops 1744830464 | bytes 33554432 | tf_op jit(solution)/shard_map/pallas_call | solution.py:71
  18.4 0.5 collective-permute-start.4
  19.0 1.2 %collective-permute-done.4.refs_2_ = bf16[32,2560]{1,0:T(8,128)(2,1)S(1)} collective-permute-done((bf16[32,2560]{1,0:T(8,128)(2,1)S(1)}, bf16[32,2560]{1,0:T(8,128)(2,1)S(1)}, u32[]{:S(2)}, u32[]{:S(2)}) %collective-permute-start.4) | collective-permute-done | bytes 163872 | tf_op jit(solution)/shard_map/ppermute | solution.py:193
  20.3 1.6 %collective-permute-start.5 = (bf16[32,6656]{1,0:T(8,128)(2,1)S(1)}, bf16[32,6656]{1,0:T(8,128)(2,1)S(1)}, u32[]{:S(2)}, u32[]{:S(2)}) collective-permute-start(bf16[32,6656]{1,0:T(8,128)(2,1)S(1)} %get-tuple-element.49), channel_id=1, source_target_pairs={{0,8},{8,0},{1,9},{9,1},{2,10},{10,2},{3,11},{11,3},{4,12},{12,4},... | collective-permute-start | bytes 1277960 | tf_op jit(solution)/shard_map/ppermute | solution.py:193
  21.9 4.1 %shard_map.50 = (f32[32,4096]{1,0:T(8,128)S(1)}, bf16[32,2048]{1,0:T(8,128)(2,1)S(1)}, bf16[32,2048]{1,0:T(8,128)(2,1)S(1)}, bf16[2048,2560]{1,0:T(8,128)(2,1)S(1)}) custom-call(bf16[64,2048]{1,0:T(8,128)(2,1)S(1)} %shard_map.48.refs_3_.refs_0_, bf16[2048,4096]{1,0:T(8,128)(2,1)S(1)} %get-tuple-element.50.refs_1_, ...), custom_call_target="tpu_custom_call" | custom-call | flops 1073741824 | bytes 20971520 | tf_op jit(solution)/shard_map/pallas_call | solution.py:71
  26.0 0.5 collective-permute-start.8
  26.5 2.5 %shard_map.51 = (f32[32,2560]{1,0:T(8,128)S(1)}, bf16[32,2560]{1,0:T(8,128)(2,1)S(1)}, bf16[1024,2048]{1,0:T(8,128)(2,1)S(1)}) custom-call(bf16[64,2048]{1,0:T(8,128)(2,1)S(1)} %shard_map.48.refs_3_.refs_0_, bf16[2048,2560]{1,0:T(8,128)(2,1)S(1)} %get-tuple-element.51.refs_1_, bf16[32,2048]{1,0:T(8,128)(2,1)S(1)} %get-tuple-element.52.refs_2_, ...), custom_call_target="tpu_custom_call" | custom-call | flops 671088640 | bytes 8388608 | tf_op jit(solution)/shard_map/pallas_call | solution.py:71
  29.3 0.6 %collective-permute-start.10 = (bf16[32,2048]{1,0:T(8,128)(2,1)S(1)}, bf16[32,2048]{1,0:T(8,128)(2,1)S(1)}, u32[]{:S(2)}, u32[]{:S(2)}) collective-permute-start(bf16[32,2048]{1,0:T(8,128)(2,1)S(1)} %get-tuple-element.60), channel_id=1, source_target_pairs={{0,8},{8,0},{1,9},{9,1},{2,10},{10,2},{3,11},{11,3},{4,12},{12,4},... | collective-permute-start | bytes 393224 | tf_op jit(solution)/shard_map/ppermute | solution.py:193
  29.9 1.5 %collective-permute-start.13 = (bf16[32,2048]{1,0:T(8,128)(2,1)S(1)}, bf16[32,2048]{1,0:T(8,128)(2,1)S(1)}, u32[]{:S(2)}, u32[]{:S(2)}) collective-permute-start(bf16[32,2048]{1,0:T(8,128)(2,1)S(1)} %get-tuple-element.68), channel_id=1, source_target_pairs={{0,8},{8,0},{1,9},{9,1},{2,10},{10,2},{3,11},{11,3},{4,12},{12,4},... | collective-permute-start | bytes 393224 | tf_op jit(solution)/shard_map/ppermute | solution.py:193
  31.4 0.6 %collective-permute-start.9 = (bf16[32,2560]{1,0:T(8,128)(2,1)S(1)}, bf16[32,2560]{1,0:T(8,128)(2,1)S(1)}, u32[]{:S(2)}, u32[]{:S(2)}) collective-permute-start(bf16[32,2560]{1,0:T(8,128)(2,1)S(1)} %get-tuple-element.59), channel_id=1, source_target_pairs={{0,8},{8,0},{1,9},{9,1},{2,10},{10,2},{3,11},{11,3},{4,12},{12,4},... | collective-permute-start | bytes 491528 | tf_op jit(solution)/shard_map/ppermute | solution.py:193
  32.0 5.3 %shard_map.54 = (bf16[64,2048]{1,0:T(8,128)(2,1)S(1)}, bf16[512,2048]{1,0:T(8,128)(2,1)S(1)}, bf16[512,2048]{1,0:T(8,128)(2,1)S(1)}, bf16[2048,2048]{1,0:T(8,128)(2,1)S(1)}, bf16[512,2048]{1,0:T(8,128)(2,1)S(1)}) custom-call(bf16[64,2048]{1,0:T(8,128)(2,1)S(1)} %shard_map.48.refs_3_.refs_0_, f32[32,2560]{1,0:T(8,128)S(1)} %get-tuple-element.58.refs_1_.refs_2_, ...), custom_call_target="tpu_custom_call" | custom-call | tf_op jit(solution)/shard_map/pallas_call | solution.py:71
  39.0 2.2 %shard_map.58 = (f32[64,2048]{1,0:T(8,128)S(1)}, bf16[1024,2048]{1,0:T(8,128)(2,1)S(1)}) custom-call(bf16[16,2048]{1,0:T(8,128)(2,1)S(1)} %get-tuple-element.62.refs_4_.refs_0_, bf16[16,2048]{1,0:T(8,128)(2,1)S(1)} %get-tuple-element.63.refs_1_, bf16[16,2048]{1,0:T(8,128)(2,1)S(1)} %collective-permute-done.11.refs_2_, ...), custom_call_target="tpu_custom_call" | custom-call | flops 536870912 | bytes 8388608 | tf_op jit(solution)/shard_map/pallas_call | solution.py:71
  41.8 2.2 %shard_map.60 = (f32[64,2048]{1,0:T(8,128)S(1)}, bf16[1024,2048]{1,0:T(8,128)(2,1)S(1)}) custom-call(bf16[32,2048]{1,0:T(8,128)(2,1)S(1)} %shard_map.57.refs_7_.refs_0_, bf16[32,2048]{1,0:T(8,128)(2,1)S(1)} %collective-permute-done.15.refs_1_, bf16[2048,2048]{1,0:T(8,128)(2,1)S(1)} %get-tuple-element.72.refs_2_, ...), custom_call_target="tpu_custom_call" | custom-call | flops 536870912 | bytes 8388608 | tf_op jit(solution)/shard_map/pallas_call | solution.py:71
  44.0 2.4 %shard_map.61 = (f32[16,2048]{1,0:T(8,128)S(1)}, bf16[16,2048]{1,0:T(8,128)(2,1)S(1)}, bf16[16,2048]{1,0:T(8,128)(2,1)S(1)}, bf16[16,2048]{1,0:T(8,128)(2,1)S(1)}) custom-call(bf16[32,2560]{1,0:T(8,128)(2,1)S(1)} %shard_map.59.refs_4_.refs_0_, bf16[32,2560]{1,0:T(8,128)(2,1)S(1)} %collective-permute-done.14.refs_1_, ...), custom_call_target="tpu_custom_call" | custom-call | flops 671088640 | tf_op jit(solution)/shard_map/pallas_call | solution.py:71
  46.4 2.5 %collective-permute-start.17 = (bf16[16,2048]{1,0:T(8,128)(2,1)S(1)}, bf16[16,2048]{1,0:T(8,128)(2,1)S(1)}, u32[]{:S(2)}, u32[]{:S(2)}) collective-permute-start(bf16[16,2048]{1,0:T(8,128)(2,1)S(1)} %get-tuple-element.77), channel_id=1, source_target_pairs={{0,4},{2,6},{4,0},{6,2},{1,5},{3,7},{5,1},{7,3},{8,12},{10,14},{12... | collective-permute-start | bytes 196616 | tf_op jit(solution)/shard_map/ppermute | solution.py:193
  48.9 2.0 %collective-permute-start.16 = (bf16[16,2048]{1,0:T(8,128)(2,1)S(1)}, bf16[16,2048]{1,0:T(8,128)(2,1)S(1)}, u32[]{:S(2)}, u32[]{:S(2)}) collective-permute-start(bf16[16,2048]{1,0:T(8,128)(2,1)S(1)} %get-tuple-element.76), channel_id=1, source_target_pairs={{0,6},{2,0},{4,2},{6,4},{1,7},{3,1},{5,3},{7,5},{8,14},{10,8},{12,... | collective-permute-start | bytes 196616 | tf_op jit(solution)/shard_map/ppermute | solution.py:193
  50.9 2.3 %collective-permute-done.18 = bf16[16,2048]{1,0:T(8,128)(2,1)S(1)} collective-permute-done((bf16[16,2048]{1,0:T(8,128)(2,1)S(1)}, bf16[16,2048]{1,0:T(8,128)(2,1)S(1)}, u32[]{:S(2)}, u32[]{:S(2)}) %collective-permute-start.18) | collective-permute-done | bytes 65568 | tf_op jit(solution)/shard_map/ppermute | solution.py:193
  53.2 1.9 %collective-permute-done.17 = bf16[16,2048]{1,0:T(8,128)(2,1)S(1)} collective-permute-done((bf16[16,2048]{1,0:T(8,128)(2,1)S(1)}, bf16[16,2048]{1,0:T(8,128)(2,1)S(1)}, u32[]{:S(2)}, u32[]{:S(2)}) %collective-permute-start.17) | collective-permute-done | bytes 65568 | tf_op jit(solution)/shard_map/ppermute | solution.py:193
  55.1 0.7 %add_convert_fusion = bf16[16,2048]{1,0:T(8,128)(2,1)} fusion(bf16[16,2048]{1,0:T(8,128)(2,1)S(1)} %collective-permute-done.18, bf16[16,2048]{1,0:T(8,128)(2,1)S(1)} %collective-permute-done.17, f32[16,2048]{1,0:T(8,128)S(1)} %get-tuple-element.75, bf16[16,2048]{1,0:T(8,128)(2,1)S(1)} %collective-permute-done.16), kind=kLoop, calls=%fused_computation | loop fusion | flops 229376 | bytes 393216 | tf_op jit(solution)/shard_map/convert_element_type | solution.py:328
  (33 shorter events, 2.8 us)
Async XLA Ops:
  0.0 11.9 %copy-start = (bf16[2048,6656]{1,0:T(8,128)(2,1)S(1)}, bf16[2048,6656]{1,0:T(8,128)(2,1)}, u32[]{:S(2)}) copy-start(bf16[2048,6656]{1,0:T(8,128)(2,1)} %refs_4_.2) | copy-start | bytes 81788928
  0.0 7.3 %collective-permute-start = (bf16[16,2048]{1,0:T(8,128)(2,1)}, bf16[16,2048]{1,0:T(8,128)(2,1)S(1)}, u32[]{:S(2)}, u32[]{:S(2)}) collective-permute-start(bf16[16,2048]{1,0:T(8,128)(2,1)} %refs_0_.1), channel_id=1, source_target_pairs={{0,2},{2,0},{4,6},{6,4},{1,3},{3,1},{5,7},{7,5},{8,10},{10,8},{12,... | collective-permute-start | bytes 196616 | tf_op jit(solution)/shard_map/ppermute | solution.py:193
  3.0 7.5 %collective-permute-start.1 = (bf16[16,2048]{1,0:T(8,128)(2,1)}, bf16[16,2048]{1,0:T(8,128)(2,1)S(1)}, u32[]{:S(2)}, u32[]{:S(2)}) collective-permute-start(bf16[16,2048]{1,0:T(8,128)(2,1)} %refs_0_.1), channel_id=1, source_target_pairs={{0,4},{2,6},{4,0},{6,2},{1,5},{3,7},{5,1},{7,3},{8,12},{10,14},{12... | collective-permute-start | bytes 196616 | tf_op jit(solution)/shard_map/ppermute | solution.py:193
  5.6 6.3 %collective-permute-start.2 = (bf16[16,2048]{1,0:T(8,128)(2,1)}, bf16[16,2048]{1,0:T(8,128)(2,1)S(1)}, u32[]{:S(2)}, u32[]{:S(2)}) collective-permute-start(bf16[16,2048]{1,0:T(8,128)(2,1)} %refs_0_.1), channel_id=1, source_target_pairs={{0,6},{2,4},{4,2},{6,0},{1,7},{3,5},{5,3},{7,1},{8,14},{10,12},{12... | collective-permute-start | bytes 196616 | tf_op jit(solution)/shard_map/ppermute | solution.py:193
  18.4 1.8 %collective-permute-start.3 = (bf16[32,4096]{1,0:T(8,128)(2,1)S(1)}, bf16[32,4096]{1,0:T(8,128)(2,1)S(1)}, u32[]{:S(2)}, u32[]{:S(2)}) collective-permute-start(bf16[32,4096]{1,0:T(8,128)(2,1)S(1)} %get-tuple-element.45), channel_id=1, source_target_pairs={{0,1},{1,0},{2,3},{3,2},{4,5},{5,4},{6,7},{7,6},{8,9},{9,8},{10,11... | collective-permute-start | bytes 786440 | tf_op jit(solution)/shard_map/ppermute | solution.py:193
  18.4 1.8 %collective-permute-start.4 = (bf16[32,2560]{1,0:T(8,128)(2,1)S(1)}, bf16[32,2560]{1,0:T(8,128)(2,1)S(1)}, u32[]{:S(2)}, u32[]{:S(2)}) collective-permute-start(bf16[32,2560]{1,0:T(8,128)(2,1)S(1)} %get-tuple-element.46.refs_1_), channel_id=1, source_target_pairs={{0,1},{1,0},{2,3},{3,2},{4,5},{5,4},{6,7},{7,6},{8,9},{9,8},{10,11... | collective-permute-start | bytes 491528 | tf_op jit(solution)/shard_map/ppermute | solution.py:193
  20.3 17.0 %collective-permute-start.5 = (bf16[32,6656]{1,0:T(8,128)(2,1)S(1)}, bf16[32,6656]{1,0:T(8,128)(2,1)S(1)}, u32[]{:S(2)}, u32[]{:S(2)}) collective-permute-start(bf16[32,6656]{1,0:T(8,128)(2,1)S(1)} %get-tuple-element.49), channel_id=1, source_target_pairs={{0,8},{8,0},{1,9},{9,1},{2,10},{10,2},{3,11},{11,3},{4,12},{12,4},... | collective-permute-start | bytes 1277960 | tf_op jit(solution)/shard_map/ppermute | solution.py:193
  26.0 3.2 %collective-permute-start.7 = (bf16[32,2048]{1,0:T(8,128)(2,1)S(1)}, bf16[32,2048]{1,0:T(8,128)(2,1)S(1)}, u32[]{:S(2)}, u32[]{:S(2)}) collective-permute-start(bf16[32,2048]{1,0:T(8,128)(2,1)S(1)} %get-tuple-element.52.refs_2_), channel_id=1, source_target_pairs={{0,1},{1,0},{2,3},{3,2},{4,5},{5,4},{6,7},{7,6},{8,9},{9,8},{10,11... | collective-permute-start | bytes 393224 | tf_op jit(solution)/shard_map/ppermute | solution.py:193
  26.0 3.1 %collective-permute-start.8 = (bf16[32,2048]{1,0:T(8,128)(2,1)S(1)}, bf16[32,2048]{1,0:T(8,128)(2,1)S(1)}, u32[]{:S(2)}, u32[]{:S(2)}) collective-permute-start(bf16[32,2048]{1,0:T(8,128)(2,1)S(1)} %get-tuple-element.56), channel_id=1, source_target_pairs={{0,1},{1,0},{2,3},{3,2},{4,5},{5,4},{6,7},{7,6},{8,9},{9,8},{10,11... | collective-permute-start | bytes 393224 | tf_op jit(solution)/shard_map/ppermute | solution.py:193
  29.0 2.3 %collective-permute-start.6 = (bf16[32,2560]{1,0:T(8,128)(2,1)S(1)}, bf16[32,2560]{1,0:T(8,128)(2,1)S(1)}, u32[]{:S(2)}, u32[]{:S(2)}) collective-permute-start(bf16[32,2560]{1,0:T(8,128)(2,1)S(1)} %get-tuple-element.54), channel_id=1, source_target_pairs={{0,1},{1,0},{2,3},{3,2},{4,5},{5,4},{6,7},{7,6},{8,9},{9,8},{10,11... | collective-permute-start | bytes 491528 | tf_op jit(solution)/shard_map/ppermute | solution.py:193
  29.3 8.1 %collective-permute-start.10 = (bf16[32,2048]{1,0:T(8,128)(2,1)S(1)}, bf16[32,2048]{1,0:T(8,128)(2,1)S(1)}, u32[]{:S(2)}, u32[]{:S(2)}) collective-permute-start(bf16[32,2048]{1,0:T(8,128)(2,1)S(1)} %get-tuple-element.60), channel_id=1, source_target_pairs={{0,8},{8,0},{1,9},{9,1},{2,10},{10,2},{3,11},{11,3},{4,12},{12,4},... | collective-permute-start | bytes 393224 | tf_op jit(solution)/shard_map/ppermute | solution.py:193
  29.9 8.6 %collective-permute-start.13 = (bf16[32,2048]{1,0:T(8,128)(2,1)S(1)}, bf16[32,2048]{1,0:T(8,128)(2,1)S(1)}, u32[]{:S(2)}, u32[]{:S(2)}) collective-permute-start(bf16[32,2048]{1,0:T(8,128)(2,1)S(1)} %get-tuple-element.68), channel_id=1, source_target_pairs={{0,8},{8,0},{1,9},{9,1},{2,10},{10,2},{3,11},{11,3},{4,12},{12,4},... | collective-permute-start | bytes 393224 | tf_op jit(solution)/shard_map/ppermute | solution.py:193
  31.4 10.1 %collective-permute-start.9 = (bf16[32,2560]{1,0:T(8,128)(2,1)S(1)}, bf16[32,2560]{1,0:T(8,128)(2,1)S(1)}, u32[]{:S(2)}, u32[]{:S(2)}) collective-permute-start(bf16[32,2560]{1,0:T(8,128)(2,1)S(1)} %get-tuple-element.59), channel_id=1, source_target_pairs={{0,8},{8,0},{1,9},{9,1},{2,10},{10,2},{3,11},{11,3},{4,12},{12,4},... | collective-permute-start | bytes 491528 | tf_op jit(solution)/shard_map/ppermute | solution.py:193
  37.5 1.3 %collective-permute-start.11 = (bf16[16,2048]{1,0:T(8,128)(2,1)S(1)}, bf16[16,2048]{1,0:T(8,128)(2,1)S(1)}, u32[]{:S(2)}, u32[]{:S(2)}) collective-permute-start(bf16[16,2048]{1,0:T(8,128)(2,1)S(1)} %get-tuple-element.62.refs_4_.refs_0_), channel_id=1, source_target_pairs={{0,1},{1,0},{2,3},{3,2},{4,5},{5,4},{6,7},{7,6},{8,9},{9,8},{10,11... | collective-permute-start | bytes 196616 | tf_op jit(solution)/shard_map/ppermute | solution.py:193
  37.6 1.4 %collective-permute-start.12 = (bf16[16,2048]{1,0:T(8,128)(2,1)S(1)}, bf16[16,2048]{1,0:T(8,128)(2,1)S(1)}, u32[]{:S(2)}, u32[]{:S(2)}) collective-permute-start(bf16[16,2048]{1,0:T(8,128)(2,1)S(1)} %get-tuple-element.63.refs_1_), channel_id=1, source_target_pairs={{0,1},{1,0},{2,3},{3,2},{4,5},{5,4},{6,7},{7,6},{8,9},{9,8},{10,11... | collective-permute-start | bytes 196616 | tf_op jit(solution)/shard_map/ppermute | solution.py:193
  38.6 3.2 %collective-permute-start.15 = (bf16[32,2048]{1,0:T(8,128)(2,1)S(1)}, bf16[32,2048]{1,0:T(8,128)(2,1)S(1)}, u32[]{:S(2)}, u32[]{:S(2)}) collective-permute-start(bf16[32,2048]{1,0:T(8,128)(2,1)S(1)} %shard_map.57.refs_7_.refs_0_), channel_id=1, source_target_pairs={{0,1},{1,0},{2,3},{3,2},{4,5},{5,4},{6,7},{7,6},{8,9},{9,8},{10,11... | collective-permute-start | bytes 393224 | tf_op jit(solution)/shard_map/ppermute | solution.py:193
  41.6 2.3 %collective-permute-start.14 = (bf16[32,2560]{1,0:T(8,128)(2,1)S(1)}, bf16[32,2560]{1,0:T(8,128)(2,1)S(1)}, u32[]{:S(2)}, u32[]{:S(2)}) collective-permute-start(bf16[32,2560]{1,0:T(8,128)(2,1)S(1)} %shard_map.59.refs_4_.refs_0_), channel_id=1, source_target_pairs={{0,1},{1,0},{2,3},{3,2},{4,5},{5,4},{6,7},{7,6},{8,9},{9,8},{10,11... | collective-permute-start | bytes 491528 | tf_op jit(solution)/shard_map/ppermute | solution.py:193
  46.4 6.8 %collective-permute-start.18 = (bf16[16,2048]{1,0:T(8,128)(2,1)S(1)}, bf16[16,2048]{1,0:T(8,128)(2,1)S(1)}, u32[]{:S(2)}, u32[]{:S(2)}) collective-permute-start(bf16[16,2048]{1,0:T(8,128)(2,1)S(1)} %get-tuple-element.78), channel_id=1, source_target_pairs={{0,2},{2,4},{4,6},{6,0},{1,3},{3,5},{5,7},{7,1},{8,10},{10,12},{12... | collective-permute-start | bytes 196616 | tf_op jit(solution)/shard_map/ppermute | solution.py:193
  46.4 8.7 %collective-permute-start.17 = (bf16[16,2048]{1,0:T(8,128)(2,1)S(1)}, bf16[16,2048]{1,0:T(8,128)(2,1)S(1)}, u32[]{:S(2)}, u32[]{:S(2)}) collective-permute-start(bf16[16,2048]{1,0:T(8,128)(2,1)S(1)} %get-tuple-element.77), channel_id=1, source_target_pairs={{0,4},{2,6},{4,0},{6,2},{1,5},{3,7},{5,1},{7,3},{8,12},{10,14},{12... | collective-permute-start | bytes 196616 | tf_op jit(solution)/shard_map/ppermute | solution.py:193
  48.9 6.2 %collective-permute-start.16 = (bf16[16,2048]{1,0:T(8,128)(2,1)S(1)}, bf16[16,2048]{1,0:T(8,128)(2,1)S(1)}, u32[]{:S(2)}, u32[]{:S(2)}) collective-permute-start(bf16[16,2048]{1,0:T(8,128)(2,1)S(1)} %get-tuple-element.76), channel_id=1, source_target_pairs={{0,6},{2,0},{4,2},{6,4},{1,7},{3,1},{5,3},{7,5},{8,14},{10,8},{12,... | collective-permute-start | bytes 196616 | tf_op jit(solution)/shard_map/ppermute | solution.py:193
